TPU v7x, 512 devices: a whole 4x8x8 slice. The times are simulated.
512 devices in a mesh: row: 16 (over z, core), col: 32 (over y, x).
Axes of the slice: x: 4, y: 8, z: 8, core: 2. Of those that a mesh axis runs over, the one named last changes fastest.
Arguments:
- train_embed: bfloat16 [8192, 256], P(('row', 'col')), may hold values from -16 to 16
- valid_embed: bfloat16 [65536, 256], P(('row', 'col')), may hold values from -16 to 16
- train_labels: int32 [8192], P(('row', 'col')), may hold values from 0 to 99
- valid_labels: int32 [65536], P(('row', 'col')), may hold values from 0 to 99
- pair_level: int32 [100, 100], replicated, may hold values from 0 to 3
- level_cost: float32 [4], replicated, may hold values from 0.05 to 1
Outputs:
- calibrated: float32 [8192], P('row')
All inputs are finite; a program needn't handle non-finite values.
Results may differ from a plain program's by a relative error of at most 0.0003.
Values may be sent and summed in bfloat16 or wider, within the bound.
No kernel may reach another device: no remote copies, remote signals or barrier semaphores. Data moves between devices by JAX's collectives and lax.ppermute only.
A program may use at most 64 MiB of HBM per device.

v0:
```python
import math

import jax
import jax.numpy as jnp
from jax import lax
from jax.sharding import PartitionSpec as P

ITERS = 4


entropy_scale = 0.05


def inner_products(left_rows, right_rows):
    return lax.dot_general(
        left_rows, right_rows, (((1,), (1,)), ((), ())), preferred_element_type=jnp.float32
    )


def squared_norms(embeddings):
    widened = embeddings.astype(jnp.float32)
    return jnp.sum(widened * widened, axis=1)


def class_costs(pair_level, level_cost):
    num_levels = level_cost.shape[0]
    selected = (
        pair_level[:, :, None] == jnp.arange(num_levels, dtype=jnp.int32)[None, None, :]
    ).astype(jnp.float32)
    return jnp.sum(selected * level_cost[None, None, :], axis=2)


def label_costs(row_labels, class_ids, labels_y):
    col_hot = (class_ids[:, None] == labels_y[None, :]).astype(jnp.float32)
    return jnp.dot(
        row_labels, col_hot, precision=lax.Precision.HIGHEST, preferred_element_type=jnp.float32
    )


def shards(train_embed, valid_embed, train_labels, valid_labels, pair_level, level_cost):
    rows_x, labels_x = (
        lax.all_gather(train_embed, "col", axis=0, tiled=True),
        lax.all_gather(train_labels, "col", axis=0, tiled=True),
    )
    width_d = rows_x.shape[1]
    classes = pair_level.shape[0]
    class_table = class_costs(pair_level, level_cost)
    class_ids = jnp.arange(classes, dtype=jnp.int32)
    train_hot = (labels_x[:, None] == class_ids[None, :]).astype(jnp.float32)
    row_labels = jnp.dot(
        train_hot, class_table, precision=lax.Precision.HIGHEST, preferred_element_type=jnp.float32
    )
    train_sq = squared_norms(rows_x)
    cols_y, labels_y = (
        lax.all_gather(valid_embed, "row", axis=0, tiled=True),
        lax.all_gather(valid_labels, "row", axis=0, tiled=True),
    )
    valid_sq = squared_norms(cols_y)
    label_full = label_costs(row_labels, class_ids, labels_y)

    def cost_block(offset, block_cols):
        block_y = lax.dynamic_slice_in_dim(cols_y, offset, block_cols, 0)
        block_sq = lax.dynamic_slice_in_dim(valid_sq, offset, block_cols, 0)
        label_slice = lax.dynamic_slice_in_dim(label_full, offset, block_cols, 1)
        return (
            train_sq[:, None] + block_sq[None, :] - 2.0 * inner_products(rows_x, block_y)
        ) / width_d + label_slice

    row_count = rows_x.shape[0]
    col_count = labels_y.shape[0]
    block_cols = min(512, col_count)
    block_count = col_count // block_cols
    block_ids = jnp.arange(block_count, dtype=jnp.int32)

    def scores(block_index, row_pot, col_pot):
        offset = block_index * block_cols
        cost_tile = cost_block(offset, block_cols)
        block_pot = lax.dynamic_slice_in_dim(col_pot, offset, block_cols, 0)
        return (
            (block_pot[None, :] - cost_tile) / entropy_scale,
            (row_pot[:, None] - cost_tile) / entropy_scale,
        )

    row_pot = jnp.zeros((row_count,), jnp.float32)
    col_pot = jnp.zeros((col_count,), jnp.float32)
    full_rows = row_count * lax.axis_size("row")
    full_cols = col_count * lax.axis_size("col")
    for iteration in range(ITERS):

        def local_peaks(running, block_index, row_pot=row_pot, col_pot=col_pot):
            row_side, col_side = scores(block_index, row_pot, col_pot)
            return (jnp.maximum(running, jnp.max(row_side, axis=1)), jnp.max(col_side, axis=0))

        row_local, col_local = lax.scan(
            local_peaks, jnp.full((row_count,), -jnp.inf, jnp.float32), block_ids
        )
        row_high = lax.pmax(row_local, "col")
        col_high = lax.pmax(col_local.reshape(col_count), "row")

        def local_totals(
            running,
            block_index,
            row_pot=row_pot,
            col_pot=col_pot,
            row_high=row_high,
            col_high=col_high,
        ):
            row_side, col_side = scores(block_index, row_pot, col_pot)
            block_high = lax.dynamic_slice_in_dim(col_high, block_index * block_cols, block_cols, 0)
            return (
                running + jnp.sum(jnp.exp(row_side - row_high[:, None]), axis=1),
                jnp.sum(jnp.exp(col_side - block_high[None, :]), axis=0),
            )

        row_part, col_part = lax.scan(local_totals, jnp.zeros((row_count,), jnp.float32), block_ids)
        row_sum = lax.psum(row_part, "col")
        col_sum = lax.psum(col_part.reshape(col_count), "row")
        row_new = entropy_scale * math.log(full_cols) - entropy_scale * (
            row_high + jnp.log(row_sum)
        )
        col_new = entropy_scale * math.log(full_rows) - entropy_scale * (
            col_high + jnp.log(col_sum)
        )
        row_pot = 0.5 * (row_pot + row_new)
        col_pot = 0.5 * (col_pot + col_new)
    potential_sum = lax.psum(jnp.sum(row_pot), "row")
    return (row_pot * full_rows - potential_sum) / (full_rows - 1)


def solution(mesh):
    placed = (
        P(("row", "col"), None),
        P(("row", "col"), None),
        P(("row", "col")),
        P(("row", "col")),
        P(),
        P(),
    )
    return jax.shard_map(shards, mesh=mesh, in_specs=placed, out_specs=P("row"), check_vma=False)
```

profile of v0, /device:TPU:1, one launch (start us, length us, event | category | flops | bytes accessed | tf_op | source)
XLA Modules:
  0.0 894.9 jit_solution(5116224132933514768)
XLA Ops:
  10.3 17.5 %all-reduce = s32[512]{0:T(512)S(1)} all-reduce(s32[512]{0:T(512)S(1)} %dynamic-update-slice), channel_id=1, replica_groups=mesh['row'=16,'col'=32] {'col'}, use_global_device_ids=true, to_apply=%add | all-reduce | flops 512 | bytes 4096
  27.7 28.0 %all-gather = s32[16,1,128]{2,1,0:T(1,128)S(1)} all-gather(s32[1,1,128]{2,1,0:T(1,128)} %bitcast.194), channel_id=1, replica_groups=mesh['row'=16,'col'=32] {'row'}, dimensions={0}, use_global_device_ids=true | all-gather | bytes 8704 | tf_op jit(solution)/shard_map/all_gather | solution.py:56
  55.7 34.7 %all_gather.12 = bf16[512,256]{1,0:T(8,128)(2,1)S(1)} all-gather(bf16[16,256]{1,0:T(8,128)(2,1)} %param.22), channel_id=1, replica_groups=mesh['row'=16,'col'=32] {'col'}, dimensions={0}, use_global_device_ids=true | all-gather | bytes 270336 | tf_op jit(solution)/shard_map/all_gather | solution.py:42
  97.4 13.7 %while.100 = (s32[]{:T(128)}, f32[512]{0:T(512)S(1)}, f32[4,512]{1,0:T(4,128)S(1)}, f32[512]{0:T(512)S(1)}, s32[4]{0:T(128)S(1)}, /*index=5*/f32[2048]{0:T(1024)...) while((s32[]{:T(128)}, f32[512]{0:T(512)S(1)}, ...), condition=%wide.region_6.7_spmd.clone, body=%wide.region_3.6_spmd.clone.sunk | while | flops 136577024 | bytes 1596617 | solution.py:94
  111.1 36.0 %pmax.50 = f32[2048]{0:T(1024)S(1)} all-reduce(f32[2048]{0:T(1024)S(1)} %bitcast.188), channel_id=1, replica_groups=mesh['row'=16,'col'=32] {'row'}, use_global_device_ids=true, to_apply=%region_8.9 | all-reduce | flops 2048 | bytes 16384 | tf_op jit(solution)/shard_map/pmax | solution.py:98
  147.1 58.1 %pmax.49 = f32[512]{0:T(512)S(1)} all-reduce(f32[512]{0:T(512)S(1)} %get-tuple-element.462), channel_id=1, replica_groups=mesh['row'=16,'col'=32] {'col'}, use_global_device_ids=true, to_apply=%region_7.8 | all-reduce | flops 512 | bytes 4096 | tf_op jit(solution)/shard_map/pmax | solution.py:97
  205.2 14.1 %while.101 = (s32[]{:T(128)}, f32[512]{0:T(512)S(1)}, f32[4,512]{1,0:T(4,128)S(1)}, f32[512]{0:T(512)S(1)}, s32[4]{0:T(128)S(1)}, /*index=5*/f32[2048]{0:T(1024)...) while((s32[]{:T(128)}, f32[512]{0:T(512)S(1)}, ...), condition=%wide.region_12.13_spmd.clone, body=%wide.region_9.12_spmd.clone.sunk | while | flops 137101312 | bytes 1604829 | solution.py:115
  219.3 56.1 %psum.56 = f32[512]{0:T(512)S(1)} all-reduce(f32[512]{0:T(512)S(1)} %get-tuple-element.464), channel_id=1, replica_groups=mesh['row'=16,'col'=32] {'col'}, use_global_device_ids=true, to_apply=%region_13.14 | all-reduce | flops 512 | bytes 4096 | tf_op jit(solution)/shard_map/psum | solution.py:116
  275.5 51.8 %psum.57 = f32[2048]{0:T(1024)S(1)} all-reduce(f32[2048]{0:T(1024)S(1)} %bitcast.189), channel_id=1, replica_groups=mesh['row'=16,'col'=32] {'row'}, use_global_device_ids=true, to_apply=%region_14.15 | all-reduce | flops 2048 | bytes 16384 | tf_op jit(solution)/shard_map/psum | solution.py:117
  327.3 13.7 %while.102 = (s32[]{:T(128)}, f32[512]{0:T(512)S(1)}, f32[4,512]{1,0:T(4,128)S(1)}, s32[4]{0:T(128)S(1)}, f32[2048]{0:T(1024)S(1)}, /*index=5*/f32[512]{0:T(512)...) while((s32[]{:T(128)}, f32[512]{0:T(512)S(1)}, ...), condition=%wide.region_18.19_spmd.clone, body=%wide.region_15.18_spmd.clone.sunk | while | flops 137101312 | bytes 1604829 | solution.py:94
  341.0 24.0 %pmax.52 = f32[2048]{0:T(1024)S(1)} all-reduce(f32[2048]{0:T(1024)S(1)} %bitcast.190), channel_id=1, replica_groups=mesh['row'=16,'col'=32] {'row'}, use_global_device_ids=true, to_apply=%region_20.21 | all-reduce | flops 2048 | bytes 16384 | tf_op jit(solution)/shard_map/pmax | solution.py:98
  365.1 57.4 %pmax.51 = f32[512]{0:T(512)S(1)} all-reduce(f32[512]{0:T(512)S(1)} %get-tuple-element.466), channel_id=1, replica_groups=mesh['row'=16,'col'=32] {'col'}, use_global_device_ids=true, to_apply=%region_19.20 | all-reduce | flops 512 | bytes 4096 | tf_op jit(solution)/shard_map/pmax | solution.py:97
  422.5 14.9 %while.103 = (s32[]{:T(128)}, f32[512]{0:T(512)S(1)}, f32[4,512]{1,0:T(4,128)S(1)}, s32[4]{0:T(128)S(1)}, f32[2048]{0:T(1024)S(1)}, /*index=5*/f32[512]{0:T(512)...) while((s32[]{:T(128)}, f32[512]{0:T(512)S(1)}, ...), condition=%wide.region_24.25_spmd.clone, body=%wide.region_21.24_spmd.clone.sunk | while | flops 137625600 | bytes 1613041 | solution.py:115
  437.4 56.1 %psum.58 = f32[512]{0:T(512)S(1)} all-reduce(f32[512]{0:T(512)S(1)} %get-tuple-element.468), channel_id=1, replica_groups=mesh['row'=16,'col'=32] {'col'}, use_global_device_ids=true, to_apply=%region_25.26 | all-reduce | flops 512 | bytes 4096 | tf_op jit(solution)/shard_map/psum | solution.py:116
  493.6 51.8 %psum.59 = f32[2048]{0:T(1024)S(1)} all-reduce(f32[2048]{0:T(1024)S(1)} %bitcast.191), channel_id=1, replica_groups=mesh['row'=16,'col'=32] {'row'}, use_global_device_ids=true, to_apply=%region_26.27 | all-reduce | flops 2048 | bytes 16384 | tf_op jit(solution)/shard_map/psum | solution.py:117
  545.4 13.5 %while.104 = (s32[]{:T(128)}, f32[512]{0:T(512)S(1)}, f32[4,512]{1,0:T(4,128)S(1)}, s32[4]{0:T(128)S(1)}, f32[2048]{0:T(1024)S(1)}, /*index=5*/f32[512]{0:T(512)...) while((s32[]{:T(128)}, f32[512]{0:T(512)S(1)}, ...), condition=%wide.region_30.31_spmd.clone, body=%wide.region_27.30_spmd.clone.sunk | while | flops 137101312 | bytes 1604829 | solution.py:94
  558.8 24.1 %pmax.54 = f32[2048]{0:T(1024)S(1)} all-reduce(f32[2048]{0:T(1024)S(1)} %bitcast.192), channel_id=1, replica_groups=mesh['row'=16,'col'=32] {'row'}, use_global_device_ids=true, to_apply=%region_32.33 | all-reduce | flops 2048 | bytes 16384 | tf_op jit(solution)/shard_map/pmax | solution.py:98
  582.9 57.4 %pmax.53 = f32[512]{0:T(512)S(1)} all-reduce(f32[512]{0:T(512)S(1)} %get-tuple-element.470), channel_id=1, replica_groups=mesh['row'=16,'col'=32] {'col'}, use_global_device_ids=true, to_apply=%region_31.32 | all-reduce | flops 512 | bytes 4096 | tf_op jit(solution)/shard_map/pmax | solution.py:97
  640.3 15.5 %while.105 = (s32[]{:T(128)}, f32[512]{0:T(512)S(1)}, f32[4,512]{1,0:T(4,128)S(1)}, s32[4]{0:T(128)S(1)}, f32[2048]{0:T(1024)S(1)}, /*index=5*/f32[512]{0:T(512)...) while((s32[]{:T(128)}, f32[512]{0:T(512)S(1)}, ...), condition=%wide.region_36.37_spmd.clone, body=%wide.region_33.36_spmd.clone.sunk | while | flops 137625600 | bytes 1613041 | solution.py:115
  655.8 38.2 %psum.61 = f32[2048]{0:T(1024)S(1)} all-reduce(f32[2048]{0:T(1024)S(1)} %bitcast.193), channel_id=1, replica_groups=mesh['row'=16,'col'=32] {'row'}, use_global_device_ids=true, to_apply=%region_38.39 | all-reduce | flops 2048 | bytes 16384 | tf_op jit(solution)/shard_map/psum | solution.py:117
  707.3 55.7 %pmax.55 = f32[512]{0:T(512)S(1)} all-reduce(f32[512]{0:T(512)S(1)} %get-tuple-element.474), channel_id=1, replica_groups=mesh['row'=16,'col'=32] {'col'}, use_global_device_ids=true, to_apply=%region_42.43 | all-reduce | flops 512 | bytes 4096 | tf_op jit(solution)/shard_map/pmax | solution.py:97
  763.0 13.4 %while.107 = (s32[]{:T(128)}, f32[512]{0:T(512)S(1)}, s32[4]{0:T(128)S(1)}, f32[2048]{0:T(1024)S(1)}, f32[512]{0:T(512)S(1)}, /*index=5*/f32[2048]{0:T(1024)S(1)...) while((s32[]{:T(128)}, f32[512]{0:T(512)S(1)}, ...), condition=%wide.region_45.46_spmd.clone, body=%wide.region_43.45_spmd.clone.sunk | while | flops 136577536 | bytes 1598673 | solution.py:115
  776.4 57.7 %all-reduce.1 = (f32[512]{0:T(512)S(1)}, f32[512]{0:T(512)S(1)}) all-reduce(f32[512]{0:T(512)S(1)} %get-tuple-element.475, f32[512]{0:T(512)S(1)} %get-tuple-element.472), channel_id=1, replica_groups=mesh['row'=16,'col'=32] {'col'}, use_global_device_ids=true, to_apply=%region_46.47 | all-reduce | flops 1024 | bytes 8192 | tf_op jit(solution)/shard_map/psum | solution.py:116
  834.7 52.1 %psum.63 = f32[]{:T(128)} all-reduce(f32[]{:T(128)} %get-tuple-element.1210), channel_id=1, replica_groups=mesh['row'=16,'col'=32] {'row'}, use_global_device_ids=true, to_apply=%region_48.49 | all-reduce | flops 1 | bytes 8 | tf_op jit(solution)/shard_map/psum | solution.py:126
  (235 shorter events, 115.6 us)
Async XLA Ops:
  6.5 89.3 %all-gather.3.cloned.1.call-start = ((), (), s32[]{:S(2)}) async-start(), calls=%async_computation | async-start | bytes 1114112 | tf_op jit(solution)/shard_map/all_gather | solution.py:55
Sparse Core Ops, SparseCore 0:
  9.5 48.0 all-gather.2
where the time goes:
time: 897 us; the launch traced here: 895 us
  blocking collectives  757 us (84%)
  matrix products  68.1 us (8%)
  local copies, waits for them, and re-layouts  28.5 us (3%)
  loops' own time  21.2 us (2%)
  between operations  14.4 us (2%)
    pmax x4, blocking collectives, shards(): row_high = lax.pmax(row_local, 'col')  229 us
    psum x3, blocking collectives, shards(): row_sum = lax.psum(row_part, 'col')  170 us
    psum x3, blocking collectives, shards(): col_sum = lax.psum(col_part.reshape(col_count), 'row')  142 us
    pmax x3, blocking collectives, shards(): col_high = lax.pmax(col_local.reshape(col_count), 'row')  84.1 us
    dot_general x32, matrix products, inner_products(): lax.dot_general(left_rows, right_rows, (((1,), (1,)), ((), ())), preferre...  64 us
    psum x1, blocking collectives, shards(): potential_sum = lax.psum(jnp.sum(row_pot), 'row')  52.1 us
    all_gather x1, blocking collectives, shards(): lax.all_gather(train_embed, 'col', axis=0, tiled=True)  34.7 us
    all_gather x1, blocking collectives, shards(): lax.all_gather(valid_labels, 'row', axis=0, tiled=True)  28 us
  transfers between devices with their start and end apart: 1, of which 0 were waited for; matrix products, arithmetic and copies ran while one was open for 1% of the time, Pallas kernels for 0%

commit v1 on v0

v1 whole, which is shorter than its diff:
```python
import math

import jax
import jax.numpy as jnp
from jax import lax
from jax.experimental import pallas as pl
from jax.experimental.pallas import tpu as pltpu
from jax.sharding import PartitionSpec as P

ITERS = 4
LANES = 128
SUB = 8

entropy_scale = 0.05
UNIT = entropy_scale * math.log(2.0)

VMEM = pl.BlockSpec(memory_space=pltpu.VMEM)


def lse_lead(parts):
    high = jnp.max(parts, axis=0)
    return high + jnp.log2(jnp.sum(jnp.exp2(parts - high[None]), axis=0))


def spread_rows(values, out_ref):
    for a in range(values.shape[0]):
        block = jnp.broadcast_to(values[a : a + 1, :], (LANES, LANES))
        out_ref[a * LANES : (a + 1) * LANES, :] = block.T


def lanes_of(ref, combine):
    rows = []
    for a in range(ref.shape[0] // LANES):
        block = ref[a * LANES : (a + 1) * LANES, :].T
        rows.append(combine(block, axis=0, keepdims=True))
    return jnp.concatenate(rows, axis=0)


def col_partial(cost_ref, row_ref):
    rows, cols = cost_ref.shape
    chunks = cols // LANES

    def tile(g, k, base):
        cell = cost_ref[pl.ds(g * SUB, SUB), k * LANES : (k + 1) * LANES]
        return -cell if base is None else base - cell

    def base_of(g):
        return None if row_ref is None else row_ref[pl.ds(pl.multiple_of(g * SUB, SUB), SUB), :]

    def peaks(g, high):
        g = pl.multiple_of(g, 1)
        base = base_of(g)
        return tuple(jnp.maximum(high[k], tile(g, k, base)) for k in range(chunks))

    start = tuple(jnp.full((SUB, LANES), -jnp.inf, jnp.float32) for _ in range(chunks))
    high = lax.fori_loop(0, rows // SUB, peaks, start, unroll=4)
    high = tuple(jnp.max(h, axis=0, keepdims=True) for h in high)

    def totals(g, total):
        base = base_of(g)
        return tuple(total[k] + jnp.exp2(tile(g, k, base) - high[k]) for k in range(chunks))

    zero = tuple(jnp.zeros((SUB, LANES), jnp.float32) for _ in range(chunks))
    total = lax.fori_loop(0, rows // SUB, totals, zero, unroll=4)
    return jnp.concatenate(
        [high[k] + jnp.log2(jnp.sum(total[k], axis=0, keepdims=True)) for k in range(chunks)], axis=0
    )


def row_partial(cost_ref, col, high_ref, total_ref):
    rows, cols = cost_ref.shape
    chunks = cols // LANES

    def tile(g, k):
        cell = cost_ref[pl.ds(g * SUB, SUB), k * LANES : (k + 1) * LANES]
        return -cell if col is None else col[k : k + 1, :] - cell

    def peaks(g, carry):
        high = tile(g, 0)
        for k in range(1, chunks):
            high = jnp.maximum(high, tile(g, k))
        high_ref[pl.ds(pl.multiple_of(g * SUB, SUB), SUB), :] = jnp.broadcast_to(
            jnp.max(high, axis=1, keepdims=True), (SUB, LANES)
        )
        return carry

    lax.fori_loop(0, rows // SUB, peaks, 0, unroll=4)

    def totals(g, carry):
        here = pl.ds(pl.multiple_of(g * SUB, SUB), SUB)
        high = high_ref[here, :]
        total = jnp.exp2(tile(g, 0) - high)
        for k in range(1, chunks):
            total = total + jnp.exp2(tile(g, k) - high)
        total_ref[here, :] = total
        return carry

    lax.fori_loop(0, rows // SUB, totals, 0, unroll=4)
    return lanes_of(high_ref, jnp.max) + jnp.log2(lanes_of(total_ref, jnp.sum))


def split3(values):
    high = values.astype(jnp.bfloat16)
    rest = values - high.astype(jnp.float32)
    mid = rest.astype(jnp.bfloat16)
    low = (rest - mid.astype(jnp.float32)).astype(jnp.bfloat16)
    return high, mid, low


def dot(left, right, dims):
    return lax.dot_general(left, right, (dims, ((), ())), preferred_element_type=jnp.float32)


def start_kernel(
    train_ref, valid_ref, levels_ref, level_cost_ref, cost_ref, row_out, col_out, row_a, row_b, *, num_levels
):
    shards, shard_rows, width = train_ref.shape
    embed = width - LANES
    rows = shards * shard_rows
    packed = train_ref[...].reshape(rows, width)
    train = packed[:, :embed]
    wide = train.astype(jnp.float32)
    train_sq = jnp.sum(wide * wide, axis=1, keepdims=True)
    levels = levels_ref[...]
    table = jnp.zeros(levels.shape, jnp.float32)
    for level in range(num_levels):
        table = table + jnp.where(levels == level, level_cost_ref[level], 0.0)
    labels = packed[:, embed:].astype(jnp.float32)
    lane_ids = lax.broadcasted_iota(jnp.int32, labels.shape, 1).astype(jnp.float32)
    train_hot = jnp.where(labels == lane_ids, 1.0, 0.0).astype(jnp.bfloat16)
    parts = [dot(train_hot, part, ((1,), (0,))).astype(jnp.bfloat16) for part in split3(table)]
    left = jnp.concatenate([train * jnp.bfloat16(-2.0 / embed), *parts], axis=1)
    ones = jnp.ones((SUB, embed), jnp.bfloat16)
    blocks, block_rows, _ = valid_ref.shape
    points = LANES
    for pair in range(blocks // 2):
        halves = (2 * pair, 2 * pair + 1)
        block = jnp.concatenate([valid_ref[h, :points, :] for h in halves], axis=0)
        hots = []
        for h in halves:
            label_row = valid_ref[h, points:, :LANES].astype(jnp.float32)[:1, :]
            class_ids = lax.broadcasted_iota(jnp.int32, (LANES, LANES), 0).astype(jnp.float32)
            hots.append(jnp.where(class_ids == label_row, 1.0, 0.0).astype(jnp.bfloat16))
        hot = jnp.concatenate(hots, axis=1)
        block_wide = block.astype(jnp.float32)
        squares = block_wide * block_wide
        sq_high = squares.astype(jnp.bfloat16)
        sq_low = (squares - sq_high.astype(jnp.float32)).astype(jnp.bfloat16)
        block_sq = (dot(ones, sq_high, ((1,), (1,))) + dot(ones, sq_low, ((1,), (1,))))[:1, :]
        products = dot(left[:, :embed], block, ((1,), (1,)))
        label_part = dot(left[:, embed:], jnp.concatenate([hot] * 3, axis=0), ((1,), (0,)))
        cost = products + (train_sq + block_sq) * (1.0 / embed) + label_part
        cost_ref[:, pair * 2 * points : (pair + 1) * 2 * points] = cost * (1.0 / UNIT)
    col_out[...] = jnp.broadcast_to(col_partial(cost_ref, None)[None], col_out.shape)
    row_out[...] = jnp.broadcast_to(row_partial(cost_ref, None, row_a, row_b)[None], row_out.shape)


def col_kernel(cost_ref, parts_ref, pot_ref, out_ref, new_ref, spread_ref, *, offset):
    pot = 0.5 * (pot_ref[...] + (offset - lse_lead(parts_ref[...])))
    new_ref[...] = pot
    spread_rows(pot, spread_ref)
    out_ref[...] = jnp.broadcast_to(col_partial(cost_ref, spread_ref)[None], out_ref.shape)


def row_kernel(cost_ref, parts_ref, pot_ref, out_ref, new_ref, row_a, row_b, *, offset):
    pot = 0.5 * (pot_ref[...] + (offset - lse_lead(parts_ref[...])))
    new_ref[...] = pot
    out_ref[...] = jnp.broadcast_to(row_partial(cost_ref, pot, row_a, row_b)[None], out_ref.shape)


def last_kernel(parts_ref, pot_ref, out_ref, *, offset):
    pot = 0.5 * (pot_ref[...] + (offset - lse_lead(parts_ref[...])))
    out_ref[...] = jnp.broadcast_to(pot[None], out_ref.shape)


def calibrate_kernel(parts_ref, pot_ref, out_ref, *, count):
    total = jnp.sum(jnp.sum(parts_ref[...], axis=0), keepdims=True)
    out_ref[...] = (pot_ref[...] * count - total) * (UNIT / (count - 1))


def exchange(copies, axis):
    return lax.all_to_all(copies, axis, 0, 0, tiled=True)


def call(kernel, out_shape, scratch, *args, smem=(), flops=0, **static):
    body = kernel if not static else (lambda *refs: kernel(*refs, **static))
    specs = [pl.BlockSpec(memory_space=pltpu.SMEM) if i in smem else VMEM for i in range(len(args))]
    return pl.pallas_call(
        body,
        out_shape=out_shape,
        in_specs=specs,
        out_specs=jax.tree.map(lambda _: VMEM, out_shape),
        scratch_shapes=scratch,
        compiler_params=pltpu.CompilerParams(vmem_limit_bytes=48 * 2**20),
        cost_estimate=pl.CostEstimate(flops=flops, bytes_accessed=4 * 2**20, transcendentals=2**20),
    )(*args)


def shards(train_embed, valid_embed, train_labels, valid_labels, pair_level, level_cost):
    row_size, col_size = lax.axis_size("row"), lax.axis_size("col")
    embed = train_embed.shape[1]
    train_pack = jnp.concatenate(
        [
            train_embed,
            jnp.broadcast_to(train_labels.astype(jnp.bfloat16)[:, None], (train_embed.shape[0], LANES)),
        ],
        axis=1,
    )
    label_row = jnp.tile(valid_labels.astype(jnp.bfloat16), embed // LANES)[None, :]
    valid_pack = jnp.concatenate([valid_embed, jnp.broadcast_to(label_row, (16, embed))], axis=0)
    train_all = exchange(jnp.broadcast_to(train_pack[None], (col_size,) + train_pack.shape), "col")
    valid_all = exchange(jnp.broadcast_to(valid_pack[None], (row_size,) + valid_pack.shape), "row")
    rows = train_embed.shape[0] * col_size
    cols = valid_embed.shape[0] * row_size
    row_chunks, col_chunks = rows // LANES, cols // LANES
    classes = pair_level.shape[0]
    levels = jnp.pad(pair_level, ((0, LANES - classes), (0, LANES - classes)), constant_values=-1)
    f32 = jnp.float32
    row_copies = jax.ShapeDtypeStruct((col_size, row_chunks, LANES), f32)
    col_copies = jax.ShapeDtypeStruct((row_size, col_chunks, LANES), f32)
    row_shape = jax.ShapeDtypeStruct((row_chunks, LANES), f32)
    col_shape = jax.ShapeDtypeStruct((col_chunks, LANES), f32)
    tall = pltpu.VMEM((rows, LANES), f32)
    cost, row_part, col_part = call(
        start_kernel,
        (jax.ShapeDtypeStruct((rows, cols), f32), row_copies, col_copies),
        [tall, tall],
        train_all,
        valid_all,
        levels,
        level_cost,
        smem=(3,),
        num_levels=level_cost.shape[0],
    )
    full_rows = rows * row_size
    full_cols = cols * col_size
    row_offset, col_offset = math.log2(full_cols), math.log2(full_rows)
    row_pot = jnp.zeros(row_shape.shape, f32)
    col_pot = jnp.zeros(col_shape.shape, f32)
    for iteration in range(ITERS - 1):
        row_got = exchange(row_part, "col")
        col_got = exchange(col_part, "row")
        row_before, col_before = row_pot, col_pot
        if iteration < ITERS - 2:
            col_part, row_pot = call(
                col_kernel, (col_copies, row_shape), [tall], cost, row_got, row_before, offset=row_offset
            )
        row_part, col_pot = call(
            row_kernel, (row_copies, col_shape), [tall, tall], cost, col_got, col_before, offset=col_offset
        )
        if iteration == ITERS - 2:
            row_pot = call(
                last_kernel, jax.ShapeDtypeStruct((1,) + row_shape.shape, f32), [], row_got, row_before, offset=row_offset
            )[0]
    row_got = exchange(row_part, "col")
    final = call(
        last_kernel,
        jax.ShapeDtypeStruct((row_size,) + row_shape.shape, f32),
        [],
        row_got,
        row_pot,
        offset=row_offset,
    )
    finals = exchange(final, "row")
    out = call(calibrate_kernel, row_shape, [], finals, final[0], count=full_rows)
    return out.reshape(rows)


def solution(mesh):
    placed = (
        P(("row", "col"), None),
        P(("row", "col"), None),
        P(("row", "col")),
        P(("row", "col")),
        P(),
        P(),
    )
    return jax.shard_map(shards, mesh=mesh, in_specs=placed, out_specs=P("row"), check_vma=False)
```

time: 897 us -> 190 us (0.21)
  blocking collectives: 757 us -> 12.6 us
  waiting for transfers between devices: 0.71 us -> 79.5 us
  matrix products: 68.1 us -> 0 us
  starting transfers between devices: 0.01 us -> 56.7 us
  Pallas kernels: 0 us -> 22.8 us
  loops' own time: 21.2 us -> 0 us
  between operations: 14.4 us -> 0.18 us
  local copies, waits for them, and re-layouts: 28.5 us -> 15.5 us
    psum x7 -> x0, blocking collectives: 364 us -> none  [the longest x3 170 us: shards(): row_sum = lax.psum(row_part, 'col')]
    pmax x7 -> x0, blocking collectives: 313 us -> none  [the longest x4 229 us: shards(): row_high = lax.pmax(row_local, 'col')]
    all_to_all x0 -> x9, waiting for transfers between devices: none -> 79.5 us  [exchange(): return lax.all_to_all(copies, axis, 0, 0, tiled=True)]
    dot_general x34 -> x0, matrix products: 68.1 us -> none  [the longest x32 64 us: inner_products(): lax.dot_general(left_rows, right_rows, (((1,), (1,)), ((), ())), preferre...]
    all_gather x2 -> x0, blocking collectives: 62.7 us -> none  [the longest x1 34.7 us: shards(): lax.all_gather(train_embed, 'col', axis=0, tiled=True)]
    all_to_all x0 -> x9, starting transfers between devices: none -> 56.7 us  [exchange(): return lax.all_to_all(copies, axis, 0, 0, tiled=True)]
    dynamic_slice x100 -> x0, local copies, waits for them, and re-layouts: 25.1 us -> none  [the longest x32 19.9 us: shards(): lax.scan(local_peaks, jnp.full((row_count,), -jnp.inf, jnp.float32), bloc...]
    pallas_call x0 -> x9, Pallas kernels: none -> 22.8 us  [call(): pl.pallas_call(body, out_shape=out_shape, in_specs=specs, out_specs=jax.t...]
  transfers between devices with their start and end apart: 1 -> 9, of which waited for: 0 -> 9; matrix products, arithmetic and copies ran while one was open for 1% -> 0% of each run, Pallas kernels for 0% -> 7%
where the time goes in v1:
time: 190 us; the launch traced here: 189 us
  waiting for transfers between devices  79.5 us (42%)
  starting transfers between devices  56.7 us (30%)
  Pallas kernels  22.8 us (12%)
  local copies, waits for them, and re-layouts  15.5 us (8%)
  blocking collectives  12.6 us (7%)
    all_to_all x9, waiting for transfers between devices, exchange(): return lax.all_to_all(copies, axis, 0, 0, tiled=True)  79.5 us
    all_to_all x9, starting transfers between devices, exchange(): return lax.all_to_all(copies, axis, 0, 0, tiled=True)  56.7 us
    pallas_call x9, Pallas kernels, call(): pl.pallas_call(body, out_shape=out_shape, in_specs=specs, out_specs=jax.t...  22.8 us
    unnamed x20, local copies, waits for them, and re-layouts  12.9 us
    all_to_all x1, blocking collectives, exchange(): return lax.all_to_all(copies, axis, 0, 0, tiled=True)  12.6 us
  transfers between devices with their start and end apart: 9, of which 9 were waited for; matrix products, arithmetic and copies ran while one was open for 0% of the time, Pallas kernels for 7%

profile of v1, /device:TPU:1, one launch (start us, length us, event | category | flops | bytes accessed | tf_op | source)
XLA Modules:
  0.0 188.8 jit_solution(2924724143925080821)
XLA Ops:
  2.3 10.5 %all-to-all-start = ((bf16[32,16,384]{2,1,0:T(8,128)(2,1)}), bf16[32,16,384]{2,1,0:T(8,128)(2,1)S(1)}, u32[]{:S(2)}, u32[]{:S(2)}) async-start(bf16[32,16,384]{2,1,0:T(8,128)(2,1)} %broadcast_in_dim.15), calls=%async_computation | async-start | bytes 786432 | tf_op jit(solution)/shard_map/all_to_all | solution.py:182
  12.8 13.7 %all-to-all-done.refs_0_ = bf16[32,16,384]{2,1,0:T(8,128)(2,1)S(1)} async-done(((bf16[32,16,384]{2,1,0:T(8,128)(2,1)}), bf16[32,16,384]{2,1,0:T(8,128)(2,1)S(1)}, u32[]{:S(2)}, u32[]{:S(2)}) %all-to-all-start) | async-done | bytes 393248 | tf_op jit(solution)/shard_map/all_to_all | solution.py:182
  27.7 13.0 %all-to-all-start.1 = ((bf16[16,144,256]{2,1,0:T(8,128)(2,1)}), bf16[16,144,256]{2,1,0:T(8,128)(2,1)S(1)}, u32[]{:S(2)}, u32[]{:S(2)}) async-start(bf16[16,144,256]{2,1,0:T(8,128)(2,1)} %broadcast_in_dim.35), calls=%async_computation.1 | async-start | bytes 2359296 | tf_op jit(solution)/shard_map/all_to_all | solution.py:182
  40.6 30.5 %all-to-all-done.1.refs_1_ = bf16[16,144,256]{2,1,0:T(8,128)(2,1)S(1)} async-done(((bf16[16,144,256]{2,1,0:T(8,128)(2,1)}), bf16[16,144,256]{2,1,0:T(8,128)(2,1)S(1)}, u32[]{:S(2)}, u32[]{:S(2)}) %all-to-all-start.1) | async-done | bytes 1179680 | tf_op jit(solution)/shard_map/all_to_all | solution.py:182
  71.2 7.4 %shard_map.64 = (f32[512,2048]{1,0:T(8,128)S(1)}, f32[32,4,128]{2,1,0:T(4,128)}, f32[16,16,128]{2,1,0:T(8,128)S(1)}) custom-call(bf16[32,16,384]{2,1,0:T(8,128)(2,1)S(1)} %all-to-all-done.refs_0_, bf16[16,144,256]{2,1,0:T(8,128)(2,1)S(1)} %all-to-all-done.1.refs_1_, s32[128,128]{1,0:T(8,128)S(1)} %pad.4.refs_2_, f32[4]{0:T(128)S(1)} %copy-done.6), custom_call_target="tpu_custom_call" | custom-call | bytes 4194304 | tf_op jit(solution)/shard_map/pallas_call | solution.py:188
  80.6 12.6 %all_to_all.50.refs_1_ = f32[16,16,128]{2,1,0:T(8,128)S(1)} all-to-all(f32[16,16,128]{2,1,0:T(8,128)S(1)} %get-tuple-element.18), channel_id=1, replica_groups=mesh['row'=16,'col'=32] {'row'}, dimensions={0} | all-to-all | bytes 262144 | tf_op jit(solution)/shard_map/all_to_all | solution.py:182
  93.2 4.0 %all-to-all-start.4 = ((f32[32,4,128]{2,1,0:T(4,128)}), f32[32,4,128]{2,1,0:T(4,128)S(1)}, u32[]{:S(2)}, u32[]{:S(2)}) async-start(f32[32,4,128]{2,1,0:T(4,128)} %get-tuple-element.20), calls=%async_computation.4 | async-start | bytes 131072 | tf_op jit(solution)/shard_map/all_to_all | solution.py:182
  99.4 3.3 %shard_map.65 = (f32[32,4,128]{2,1,0:T(4,128)}, f32[16,128]{1,0:T(8,128)S(1)}) custom-call(f32[512,2048]{1,0:T(8,128)S(1)} %copy-done.1, f32[16,16,128]{2,1,0:T(8,128)S(1)} %all_to_all.50.refs_1_, f32[16,128]{1,0:T(8,128)S(1)} %broadcast_in_dim.36.refs_2_), custom_call_target="tpu_custom_call" | custom-call | bytes 4194304 | tf_op jit(solution)/shard_map/pallas_call | solution.py:188
  102.7 3.7 %all-to-all-done.4.refs_1_ = f32[32,4,128]{2,1,0:T(4,128)S(1)} async-done(((f32[32,4,128]{2,1,0:T(4,128)}), f32[32,4,128]{2,1,0:T(4,128)S(1)}, u32[]{:S(2)}, u32[]{:S(2)}) %all-to-all-start.4) | async-done | bytes 65568 | tf_op jit(solution)/shard_map/all_to_all | solution.py:182
  106.4 5.5 %all-to-all-start.3 = ((f32[32,4,128]{2,1,0:T(4,128)}), f32[32,4,128]{2,1,0:T(4,128)S(1)}, u32[]{:S(2)}, u32[]{:S(2)}) async-start(f32[32,4,128]{2,1,0:T(4,128)} %get-tuple-element.19), calls=%async_computation.3 | async-start | bytes 131072 | tf_op jit(solution)/shard_map/all_to_all | solution.py:182
  116.2 4.6 %all-to-all-done.3.refs_1_ = f32[32,4,128]{2,1,0:T(4,128)S(1)} async-done(((f32[32,4,128]{2,1,0:T(4,128)}), f32[32,4,128]{2,1,0:T(4,128)S(1)}, u32[]{:S(2)}, u32[]{:S(2)}) %all-to-all-start.3) | async-done | bytes 65568 | tf_op jit(solution)/shard_map/all_to_all | solution.py:182
  120.7 5.0 %all-to-all-start.6 = ((f32[16,16,128]{2,1,0:T(8,128)}), f32[16,16,128]{2,1,0:T(8,128)S(1)}, u32[]{:S(2)}, u32[]{:S(2)}) async-start(f32[16,16,128]{2,1,0:T(8,128)} %get-tuple-element.23), calls=%async_computation.6 | async-start | bytes 262144 | tf_op jit(solution)/shard_map/all_to_all | solution.py:182
  125.7 2.2 %copy-done.3 = f32[512,2048]{1,0:T(8,128)S(1)} copy-done((f32[512,2048]{1,0:T(8,128)S(1)}, f32[512,2048]{1,0:T(8,128)}, u32[]{:S(2)}) %copy-start.3) | copy-done | bytes 4194328
  129.9 5.0 %all-to-all-done.6.refs_1_ = f32[16,16,128]{2,1,0:T(8,128)S(1)} async-done(((f32[16,16,128]{2,1,0:T(8,128)}), f32[16,16,128]{2,1,0:T(8,128)S(1)}, u32[]{:S(2)}, u32[]{:S(2)}) %all-to-all-start.6) | async-done | bytes 131104 | tf_op jit(solution)/shard_map/all_to_all | solution.py:182
  134.9 3.4 %all-to-all-start.5 = ((f32[16,16,128]{2,1,0:T(8,128)}), f32[16,16,128]{2,1,0:T(8,128)S(1)}, u32[]{:S(2)}, u32[]{:S(2)}) async-start(f32[16,16,128]{2,1,0:T(8,128)} %get-tuple-element.22), calls=%async_computation.5 | async-start | bytes 262144 | tf_op jit(solution)/shard_map/all_to_all | solution.py:182
  140.5 3.3 %shard_map.68 = (f32[32,4,128]{2,1,0:T(4,128)}, f32[16,128]{1,0:T(8,128)S(1)}) custom-call(f32[512,2048]{1,0:T(8,128)S(1)} %copy-done.4, f32[16,16,128]{2,1,0:T(8,128)S(1)} %all-to-all-done.6.refs_1_, f32[16,128]{1,0:T(8,128)S(1)} %get-tuple-element.24.refs_2_), custom_call_target="tpu_custom_call" | custom-call | bytes 4194304 | tf_op jit(solution)/shard_map/pallas_call | solution.py:188
  143.8 3.0 %all-to-all-done.5.refs_1_ = f32[16,16,128]{2,1,0:T(8,128)S(1)} async-done(((f32[16,16,128]{2,1,0:T(8,128)}), f32[16,16,128]{2,1,0:T(8,128)S(1)}, u32[]{:S(2)}, u32[]{:S(2)}) %all-to-all-start.5) | async-done | bytes 131104 | tf_op jit(solution)/shard_map/all_to_all | solution.py:182
  146.8 3.8 %all-to-all-start.8 = ((f32[32,4,128]{2,1,0:T(4,128)}), f32[32,4,128]{2,1,0:T(4,128)S(1)}, u32[]{:S(2)}, u32[]{:S(2)}) async-start(f32[32,4,128]{2,1,0:T(4,128)} %get-tuple-element.27), calls=%async_computation.8 | async-start | bytes 131072 | tf_op jit(solution)/shard_map/all_to_all | solution.py:182
  152.9 3.3 %shard_map.69 = (f32[32,4,128]{2,1,0:T(4,128)}, f32[16,128]{1,0:T(8,128)}) custom-call(f32[512,2048]{1,0:T(8,128)S(1)} %copy-done.5, f32[16,16,128]{2,1,0:T(8,128)S(1)} %all-to-all-done.5.refs_1_, f32[16,128]{1,0:T(8,128)S(1)} %get-tuple-element.25.refs_2_), custom_call_target="tpu_custom_call" | custom-call | bytes 4194304 | tf_op jit(solution)/shard_map/pallas_call | solution.py:188
  156.2 3.4 %all-to-all-done.8.refs_0_ = f32[32,4,128]{2,1,0:T(4,128)S(1)} async-done(((f32[32,4,128]{2,1,0:T(4,128)}), f32[32,4,128]{2,1,0:T(4,128)S(1)}, u32[]{:S(2)}, u32[]{:S(2)}) %all-to-all-start.8) | async-done | bytes 65568 | tf_op jit(solution)/shard_map/all_to_all | solution.py:182
  159.6 5.8 %all-to-all-start.7 = ((f32[32,4,128]{2,1,0:T(4,128)}), f32[32,4,128]{2,1,0:T(4,128)S(1)}, u32[]{:S(2)}, u32[]{:S(2)}) async-start(f32[32,4,128]{2,1,0:T(4,128)} %get-tuple-element.26), calls=%async_computation.7 | async-start | bytes 131072 | tf_op jit(solution)/shard_map/all_to_all | solution.py:182
  165.5 8.8 %all-to-all-done.7.refs_0_ = f32[32,4,128]{2,1,0:T(4,128)S(1)} async-done(((f32[32,4,128]{2,1,0:T(4,128)}), f32[32,4,128]{2,1,0:T(4,128)S(1)}, u32[]{:S(2)}, u32[]{:S(2)}) %all-to-all-start.7) | async-done | bytes 65568 | tf_op jit(solution)/shard_map/all_to_all | solution.py:182
  175.0 5.7 %all-to-all-start.9 = ((f32[16,4,128]{2,1,0:T(4,128)}), f32[16,4,128]{2,1,0:T(4,128)S(1)}, u32[]{:S(2)}, u32[]{:S(2)}) async-start(f32[16,4,128]{2,1,0:T(4,128)} %shard_map.71), calls=%async_computation.9 | async-start | bytes 65536 | tf_op jit(solution)/shard_map/all_to_all | solution.py:182
  181.3 6.7 %all-to-all-done.9.refs_0_ = f32[16,4,128]{2,1,0:T(4,128)S(1)} async-done(((f32[16,4,128]{2,1,0:T(4,128)}), f32[16,4,128]{2,1,0:T(4,128)S(1)}, u32[]{:S(2)}, u32[]{:S(2)}) %all-to-all-start.9) | async-done | bytes 32800 | tf_op jit(solution)/shard_map/all_to_all | solution.py:182
  (37 shorter events, 20.2 us)
Async XLA Ops:
  0.0 12.8 %copy-start.9 = (s32[128]{0:T(128)S(1)}, s32[128]{0:T(128)}, u32[]{:S(2)}) copy-start(s32[128]{0:T(128)} %param.9) | copy-start | bytes 1540
  0.0 12.8 %copy-start.7 = (bf16[128,256]{1,0:T(8,128)(2,1)S(1)}, bf16[128,256]{1,0:T(8,128)(2,1)}, u32[]{:S(2)}) copy-start(bf16[128,256]{1,0:T(8,128)(2,1)} %param.7) | copy-start | bytes 196612
  2.3 24.3 %all-to-all-start = ((bf16[32,16,384]{2,1,0:T(8,128)(2,1)}), bf16[32,16,384]{2,1,0:T(8,128)(2,1)S(1)}, u32[]{:S(2)}, u32[]{:S(2)}) async-start(bf16[32,16,384]{2,1,0:T(8,128)(2,1)} %broadcast_in_dim.15), calls=%async_computation | async-start | bytes 786432 | tf_op jit(solution)/shard_map/all_to_all | solution.py:182
  27.7 13.0 %copy-start.8 = (s32[100,100]{1,0:T(8,128)S(1)}, s32[100,100]{1,0:T(8,128)}, u32[]{:S(2)}) copy-start(s32[100,100]{1,0:T(8,128)} %param.10) | copy-start | bytes 120004
  27.7 43.5 %copy-start.6 = (f32[4]{0:T(128)S(1)}, f32[4]{0:T(128)}, u32[]{:S(2)}) copy-start(f32[4]{0:T(128)} %refs_3_.1) | copy-start | bytes 52
  27.7 43.5 %all-to-all-start.1 = ((bf16[16,144,256]{2,1,0:T(8,128)(2,1)}), bf16[16,144,256]{2,1,0:T(8,128)(2,1)S(1)}, u32[]{:S(2)}, u32[]{:S(2)}) async-start(bf16[16,144,256]{2,1,0:T(8,128)(2,1)} %broadcast_in_dim.35), calls=%async_computation.1 | async-start | bytes 2359296 | tf_op jit(solution)/shard_map/all_to_all | solution.py:182
  78.6 2.0 %copy-start = (f32[512,2048]{1,0:T(8,128)}, f32[512,2048]{1,0:T(8,128)S(1)}, u32[]{:S(2)}) copy-start(f32[512,2048]{1,0:T(8,128)S(1)} %get-tuple-element.17.refs_0_) | copy-start | bytes 12582916
  93.2 13.2 %all-to-all-start.4 = ((f32[32,4,128]{2,1,0:T(4,128)}), f32[32,4,128]{2,1,0:T(4,128)S(1)}, u32[]{:S(2)}, u32[]{:S(2)}) async-start(f32[32,4,128]{2,1,0:T(4,128)} %get-tuple-element.20), calls=%async_computation.4 | async-start | bytes 131072 | tf_op jit(solution)/shard_map/all_to_all | solution.py:182
  97.2 2.2 %copy-start.1 = (f32[512,2048]{1,0:T(8,128)S(1)}, f32[512,2048]{1,0:T(8,128)}, u32[]{:S(2)}) copy-start(f32[512,2048]{1,0:T(8,128)} %copy-done) | copy-start | bytes 12582916
  106.4 14.3 %all-to-all-start.3 = ((f32[32,4,128]{2,1,0:T(4,128)}), f32[32,4,128]{2,1,0:T(4,128)S(1)}, u32[]{:S(2)}, u32[]{:S(2)}) async-start(f32[32,4,128]{2,1,0:T(4,128)} %get-tuple-element.19), calls=%async_computation.3 | async-start | bytes 131072 | tf_op jit(solution)/shard_map/all_to_all | solution.py:182
  111.9 2.2 %copy-start.2 = (f32[512,2048]{1,0:T(8,128)S(1)}, f32[512,2048]{1,0:T(8,128)}, u32[]{:S(2)}) copy-start(f32[512,2048]{1,0:T(8,128)} %copy-done) | copy-start | bytes 12582916
  120.7 14.2 %all-to-all-start.6 = ((f32[16,16,128]{2,1,0:T(8,128)}), f32[16,16,128]{2,1,0:T(8,128)S(1)}, u32[]{:S(2)}, u32[]{:S(2)}) async-start(f32[16,16,128]{2,1,0:T(8,128)} %get-tuple-element.23), calls=%async_computation.6 | async-start | bytes 262144 | tf_op jit(solution)/shard_map/all_to_all | solution.py:182
  125.7 2.2 %copy-start.3 = (f32[512,2048]{1,0:T(8,128)S(1)}, f32[512,2048]{1,0:T(8,128)}, u32[]{:S(2)}) copy-start(f32[512,2048]{1,0:T(8,128)} %copy-done) | copy-start | bytes 12582916
  134.9 11.9 %all-to-all-start.5 = ((f32[16,16,128]{2,1,0:T(8,128)}), f32[16,16,128]{2,1,0:T(8,128)S(1)}, u32[]{:S(2)}, u32[]{:S(2)}) async-start(f32[16,16,128]{2,1,0:T(8,128)} %get-tuple-element.22), calls=%async_computation.5 | async-start | bytes 262144 | tf_op jit(solution)/shard_map/all_to_all | solution.py:182
  138.3 2.2 %copy-start.4 = (f32[512,2048]{1,0:T(8,128)S(1)}, f32[512,2048]{1,0:T(8,128)}, u32[]{:S(2)}) copy-start(f32[512,2048]{1,0:T(8,128)} %copy-done) | copy-start | bytes 12582916
  146.8 12.7 %all-to-all-start.8 = ((f32[32,4,128]{2,1,0:T(4,128)}), f32[32,4,128]{2,1,0:T(4,128)S(1)}, u32[]{:S(2)}, u32[]{:S(2)}) async-start(f32[32,4,128]{2,1,0:T(4,128)} %get-tuple-element.27), calls=%async_computation.8 | async-start | bytes 131072 | tf_op jit(solution)/shard_map/all_to_all | solution.py:182
  150.7 2.2 %copy-start.5 = (f32[512,2048]{1,0:T(8,128)S(1)}, f32[512,2048]{1,0:T(8,128)}, u32[]{:S(2)}) copy-start(f32[512,2048]{1,0:T(8,128)} %copy-done) | copy-start | bytes 12582916
  159.6 14.7 %all-to-all-start.7 = ((f32[32,4,128]{2,1,0:T(4,128)}), f32[32,4,128]{2,1,0:T(4,128)S(1)}, u32[]{:S(2)}, u32[]{:S(2)}) async-start(f32[32,4,128]{2,1,0:T(4,128)} %get-tuple-element.26), calls=%async_computation.7 | async-start | bytes 131072 | tf_op jit(solution)/shard_map/all_to_all | solution.py:182
  175.0 13.1 %all-to-all-start.9 = ((f32[16,4,128]{2,1,0:T(4,128)}), f32[16,4,128]{2,1,0:T(4,128)S(1)}, u32[]{:S(2)}, u32[]{:S(2)}) async-start(f32[16,4,128]{2,1,0:T(4,128)} %shard_map.71), calls=%async_computation.9 | async-start | bytes 65536 | tf_op jit(solution)/shard_map/all_to_all | solution.py:182

commit v2 on v1

--- a/solution.py
+++ b/solution.py
@@ -13,6 +13,8 @@
 
 entropy_scale = 0.05
 UNIT = entropy_scale * math.log(2.0)
+
+ROW = ("zh", "zl", "core")
 
 VMEM = pl.BlockSpec(memory_space=pltpu.VMEM)
 
@@ -112,7 +114,7 @@
 
 
 def start_kernel(
-    train_ref, valid_ref, levels_ref, level_cost_ref, cost_ref, row_out, col_out, row_a, row_b, *, num_levels
+    train_ref, valid_ref, levels_ref, level_cost_ref, cost_ref, col_out, *, num_levels
 ):
     shards, shard_rows, width = train_ref.shape
     embed = width - LANES
@@ -152,7 +154,10 @@
         cost = products + (train_sq + block_sq) * (1.0 / embed) + label_part
         cost_ref[:, pair * 2 * points : (pair + 1) * 2 * points] = cost * (1.0 / UNIT)
     col_out[...] = jnp.broadcast_to(col_partial(cost_ref, None)[None], col_out.shape)
-    row_out[...] = jnp.broadcast_to(row_partial(cost_ref, None, row_a, row_b)[None], row_out.shape)
+
+
+def first_row_kernel(cost_ref, out_ref, row_a, row_b):
+    out_ref[...] = jnp.broadcast_to(row_partial(cost_ref, None, row_a, row_b)[None], out_ref.shape)
 
 
 def col_kernel(cost_ref, parts_ref, pot_ref, out_ref, new_ref, spread_ref, *, offset):
@@ -182,7 +187,7 @@
     return lax.all_to_all(copies, axis, 0, 0, tiled=True)
 
 
-def call(kernel, out_shape, scratch, *args, smem=(), flops=0, **static):
+def call(kernel, out_shape, scratch, *args, smem=(), limit=8, **static):
     body = kernel if not static else (lambda *refs: kernel(*refs, **static))
     specs = [pl.BlockSpec(memory_space=pltpu.SMEM) if i in smem else VMEM for i in range(len(args))]
     return pl.pallas_call(
@@ -191,13 +196,13 @@
         in_specs=specs,
         out_specs=jax.tree.map(lambda _: VMEM, out_shape),
         scratch_shapes=scratch,
-        compiler_params=pltpu.CompilerParams(vmem_limit_bytes=48 * 2**20),
-        cost_estimate=pl.CostEstimate(flops=flops, bytes_accessed=4 * 2**20, transcendentals=2**20),
+        compiler_params=pltpu.CompilerParams(vmem_limit_bytes=limit * 2**20),
+        cost_estimate=pl.CostEstimate(flops=2**24, bytes_accessed=4 * 2**20, transcendentals=2**20),
     )(*args)
 
 
 def shards(train_embed, valid_embed, train_labels, valid_labels, pair_level, level_cost):
-    row_size, col_size = lax.axis_size("row"), lax.axis_size("col")
+    row_size, col_size = lax.axis_size(ROW), lax.axis_size("col")
     embed = train_embed.shape[1]
     train_pack = jnp.concatenate(
         [
@@ -209,7 +214,10 @@
     label_row = jnp.tile(valid_labels.astype(jnp.bfloat16), embed // LANES)[None, :]
     valid_pack = jnp.concatenate([valid_embed, jnp.broadcast_to(label_row, (16, embed))], axis=0)
     train_all = exchange(jnp.broadcast_to(train_pack[None], (col_size,) + train_pack.shape), "col")
-    valid_all = exchange(jnp.broadcast_to(valid_pack[None], (row_size,) + valid_pack.shape), "row")
+    valid_all = lax.all_gather(valid_pack[None], "zl", axis=0, tiled=True)
+    for axis in ("zh", "core"):
+        copies = jnp.broadcast_to(valid_all[None], (lax.axis_size(axis),) + valid_all.shape)
+        valid_all = exchange(copies, axis).reshape((-1,) + valid_pack.shape)
     rows = train_embed.shape[0] * col_size
     cols = valid_embed.shape[0] * row_size
     row_chunks, col_chunks = rows // LANES, cols // LANES
@@ -221,17 +229,19 @@
     row_shape = jax.ShapeDtypeStruct((row_chunks, LANES), f32)
     col_shape = jax.ShapeDtypeStruct((col_chunks, LANES), f32)
     tall = pltpu.VMEM((rows, LANES), f32)
-    cost, row_part, col_part = call(
+    cost, col_part = call(
         start_kernel,
-        (jax.ShapeDtypeStruct((rows, cols), f32), row_copies, col_copies),
-        [tall, tall],
+        (jax.ShapeDtypeStruct((rows, cols), f32), col_copies),
+        [],
         train_all,
         valid_all,
         levels,
         level_cost,
         smem=(3,),
         num_levels=level_cost.shape[0],
-    )
+        limit=24,
+    )
+    row_part = call(first_row_kernel, row_copies, [tall, tall], cost)
     full_rows = rows * row_size
     full_cols = cols * col_size
     row_offset, col_offset = math.log2(full_cols), math.log2(full_rows)
@@ -239,7 +249,7 @@
     col_pot = jnp.zeros(col_shape.shape, f32)
     for iteration in range(ITERS - 1):
         row_got = exchange(row_part, "col")
-        col_got = exchange(col_part, "row")
+        col_got = exchange(col_part, ROW)
         row_before, col_before = row_pot, col_pot
         if iteration < ITERS - 2:
             col_part, row_pot = call(
@@ -261,18 +271,14 @@
         row_pot,
         offset=row_offset,
     )
-    finals = exchange(final, "row")
+    finals = exchange(final, ROW)
     out = call(calibrate_kernel, row_shape, [], finals, final[0], count=full_rows)
     return out.reshape(rows)
 
 
 def solution(mesh):
-    placed = (
-        P(("row", "col"), None),
-        P(("row", "col"), None),
-        P(("row", "col")),
-        P(("row", "col")),
-        P(),
-        P(),
-    )
-    return jax.shard_map(shards, mesh=mesh, in_specs=placed, out_specs=P("row"), check_vma=False)
+    row_size, col_size = mesh.shape["row"], mesh.shape["col"]
+    finer = jax.sharding.Mesh(mesh.devices.reshape(row_size // 4, 2, 2, col_size), ROW + ("col",))
+    both = ROW + ("col",)
+    placed = (P(both, None), P(both, None), P(both), P(both), P(), P())
+    return jax.shard_map(shards, mesh=finer, in_specs=placed, out_specs=P(ROW), check_vma=False)

time: 190 us -> 178 us (0.937)
  waiting for transfers between devices: 79.5 us -> 57.6 us
  starting transfers between devices: 56.7 us -> 62.2 us
  local copies, waits for them, and re-layouts: 15.5 us -> 17.6 us
    all_to_all x9 -> x10, waiting for transfers between devices: 79.5 us -> 57.6 us  [exchange(): return lax.all_to_all(copies, axis, 0, 0, tiled=True)]
    all_to_all x9 -> x10, starting transfers between devices: 56.7 us -> 62.2 us  [exchange(): return lax.all_to_all(copies, axis, 0, 0, tiled=True)]
    all_gather x0 -> x1, blocking collectives: none -> 4.78 us  [shards(): valid_all = lax.all_gather(valid_pack[None], 'zl', axis=0, tiled=True)]
    all_to_all x1, blocking collectives: 12.6 us -> 9.65 us  [exchange(): return lax.all_to_all(copies, axis, 0, 0, tiled=True)]
    unnamed x20 -> x22, local copies, waits for them, and re-layouts: 12.9 us -> 15.1 us
    pallas_call x9 -> x10, Pallas kernels: 22.8 us -> 23.5 us  [call(): pl.pallas_call(body, out_shape=out_shape, in_specs=specs, out_specs=jax.t...]
  transfers between devices with their start and end apart: 9 -> 10, of which waited for: 9 -> 10; matrix products, arithmetic and copies ran while one was open for 0% -> 0% of each run, Pallas kernels for 7% -> 10%
where the time goes in v2:
time: 178 us; the launch traced here: 177 us
  starting transfers between devices  62.2 us (35%)
  waiting for transfers between devices  57.6 us (32%)
  Pallas kernels  23.5 us (13%)
  local copies, waits for them, and re-layouts  17.6 us (10%)
  blocking collectives  14.4 us (8%)
    all_to_all x10, starting transfers between devices, exchange(): return lax.all_to_all(copies, axis, 0, 0, tiled=True)  62.2 us
    all_to_all x10, waiting for transfers between devices, exchange(): return lax.all_to_all(copies, axis, 0, 0, tiled=True)  57.6 us
    pallas_call x10, Pallas kernels, call(): pl.pallas_call(body, out_shape=out_shape, in_specs=specs, out_specs=jax.t...  23.5 us
    unnamed x22, local copies, waits for them, and re-layouts  15.1 us
    all_to_all x1, blocking collectives, exchange(): return lax.all_to_all(copies, axis, 0, 0, tiled=True)  9.65 us
    all_gather x1, blocking collectives, shards(): valid_all = lax.all_gather(valid_pack[None], 'zl', axis=0, tiled=True)  4.78 us
  transfers between devices with their start and end apart: 10, of which 10 were waited for; matrix products, arithmetic and copies ran while one was open for 0% of the time, Pallas kernels for 10%

profile of v2, /device:TPU:1, one launch (start us, length us, event | category | flops | bytes accessed | tf_op | source)
XLA Modules:
  0.0 177.0 jit_solution(4192694656142351766)
XLA Ops:
  2.2 10.5 %all-to-all-start = ((bf16[32,16,384]{2,1,0:T(8,128)(2,1)}), bf16[32,16,384]{2,1,0:T(8,128)(2,1)S(1)}, u32[]{:S(2)}, u32[]{:S(2)}) async-start(bf16[32,16,384]{2,1,0:T(8,128)(2,1)} %broadcast_in_dim.42), calls=%async_computation | async-start | bytes 786432 | tf_op jit(solution)/shard_map/all_to_all | solution.py:187
  12.8 4.8 %all-gather = bf16[288,256]{1,0:T(8,128)(2,1)S(1)} all-gather(bf16[144,256]{1,0:T(8,128)(2,1)S(1)} %pad_maximum_fusion), channel_id=2, replica_groups=mesh['zh'=4,'zl'=2,'core'=2,'col'=32] {'zl'}, dimensions={0}, use_global_device_ids=true | all-gather | bytes 221184 | tf_op jit(solution)/shard_map/all_gather | solution.py:217
  17.6 8.9 %all-to-all-done.refs_0_ = bf16[32,16,384]{2,1,0:T(8,128)(2,1)S(1)} async-done(((bf16[32,16,384]{2,1,0:T(8,128)(2,1)}), bf16[32,16,384]{2,1,0:T(8,128)(2,1)S(1)}, u32[]{:S(2)}, u32[]{:S(2)}) %all-to-all-start) | async-done | bytes 393248 | tf_op jit(solution)/shard_map/all_to_all | solution.py:187
  27.4 10.0 %all-to-all-start.1 = ((bf16[4,2,144,256]{3,2,1,0:T(8,128)(2,1)}), bf16[4,2,144,256]{3,2,1,0:T(8,128)(2,1)S(1)}, u32[]{:S(2)}, u32[]{:S(2)}) async-start(bf16[4,2,144,256]{3,2,1,0:T(8,128)(2,1)} %broadcast_in_dim.46), calls=%async_computation.1 | async-start | bytes 1179648 | tf_op jit(solution)/shard_map/all_to_all | solution.py:187
  37.4 9.9 %all-to-all-done.1 = bf16[4,2,144,256]{3,2,1,0:T(8,128)(2,1)S(1)} async-done(((bf16[4,2,144,256]{3,2,1,0:T(8,128)(2,1)}), bf16[4,2,144,256]{3,2,1,0:T(8,128)(2,1)S(1)}, u32[]{:S(2)}, u32[]{:S(2)}) %all-to-all-start.1) | async-done | bytes 589856 | tf_op jit(solution)/shard_map/all_to_all | solution.py:187
  47.4 9.7 %all_to_all.55 = bf16[2,8,144,256]{3,2,1,0:T(8,128)(2,1)S(1)} all-to-all(bf16[2,8,144,256]{3,2,1,0:T(8,128)(2,1)S(1)} %broadcast_in_dim.48), channel_id=1, replica_groups=mesh['zh'=4,'zl'=2,'core'=2,'col'=32] {'core'}, dimensions={0} | all-to-all | bytes 2359296 | tf_op jit(solution)/shard_map/all_to_all | solution.py:187
  57.1 4.8 %shard_map.64 = (f32[512,2048]{1,0:T(8,128)S(1)}, f32[16,16,128]{2,1,0:T(8,128)}) custom-call(bf16[32,16,384]{2,1,0:T(8,128)(2,1)S(1)} %all-to-all-done.refs_0_, bf16[16,144,256]{2,1,0:T(8,128)(2,1)S(1)} %bitcast.9, s32[128,128]{1,0:T(8,128)S(1)} %pad.4.refs_2_, f32[4]{0:T(128)S(1)} %copy-done.7), custom_call_target="tpu_custom_call" | custom-call | flops 16777216 | bytes 4194304 | tf_op jit(solution)/shard_map/pallas_call | solution.py:193
  63.9 7.1 %all-to-all-start.3 = ((f32[16,16,128]{2,1,0:T(8,128)}), f32[16,16,128]{2,1,0:T(8,128)S(1)}, u32[]{:S(2)}, u32[]{:S(2)}) async-start(f32[16,16,128]{2,1,0:T(8,128)} %get-tuple-element.17), calls=%async_computation.3 | async-start | bytes 262144 | tf_op jit(solution)/shard_map/all_to_all | solution.py:187
  76.4 3.7 %all-to-all-done.3.refs_1_ = f32[16,16,128]{2,1,0:T(8,128)S(1)} async-done(((f32[16,16,128]{2,1,0:T(8,128)}), f32[16,16,128]{2,1,0:T(8,128)S(1)}, u32[]{:S(2)}, u32[]{:S(2)}) %all-to-all-start.3) | async-done | bytes 131104 | tf_op jit(solution)/shard_map/all_to_all | solution.py:187
  80.1 4.8 %all-to-all-start.5 = ((f32[32,4,128]{2,1,0:T(4,128)}), f32[32,4,128]{2,1,0:T(4,128)S(1)}, u32[]{:S(2)}, u32[]{:S(2)}) async-start(f32[32,4,128]{2,1,0:T(4,128)} %shard_map.66), calls=%async_computation.5 | async-start | bytes 131072 | tf_op jit(solution)/shard_map/all_to_all | solution.py:187
  90.4 3.7 %all-to-all-done.5.refs_1_ = f32[32,4,128]{2,1,0:T(4,128)S(1)} async-done(((f32[32,4,128]{2,1,0:T(4,128)}), f32[32,4,128]{2,1,0:T(4,128)S(1)}, u32[]{:S(2)}, u32[]{:S(2)}) %all-to-all-start.5) | async-done | bytes 65568 | tf_op jit(solution)/shard_map/all_to_all | solution.py:187
  94.1 5.5 %all-to-all-start.4 = ((f32[32,4,128]{2,1,0:T(4,128)}), f32[32,4,128]{2,1,0:T(4,128)S(1)}, u32[]{:S(2)}, u32[]{:S(2)}) async-start(f32[32,4,128]{2,1,0:T(4,128)} %get-tuple-element.18), calls=%async_computation.4 | async-start | bytes 131072 | tf_op jit(solution)/shard_map/all_to_all | solution.py:187
  103.8 4.6 %all-to-all-done.4.refs_1_ = f32[32,4,128]{2,1,0:T(4,128)S(1)} async-done(((f32[32,4,128]{2,1,0:T(4,128)}), f32[32,4,128]{2,1,0:T(4,128)S(1)}, u32[]{:S(2)}, u32[]{:S(2)}) %all-to-all-start.4) | async-done | bytes 65568 | tf_op jit(solution)/shard_map/all_to_all | solution.py:187
  108.5 5.5 %all-to-all-start.7 = ((f32[16,16,128]{2,1,0:T(8,128)}), f32[16,16,128]{2,1,0:T(8,128)S(1)}, u32[]{:S(2)}, u32[]{:S(2)}) async-start(f32[16,16,128]{2,1,0:T(8,128)} %get-tuple-element.21), calls=%async_computation.7 | async-start | bytes 262144 | tf_op jit(solution)/shard_map/all_to_all | solution.py:187
  118.2 4.9 %all-to-all-done.7.refs_1_ = f32[16,16,128]{2,1,0:T(8,128)S(1)} async-done(((f32[16,16,128]{2,1,0:T(8,128)}), f32[16,16,128]{2,1,0:T(8,128)S(1)}, u32[]{:S(2)}, u32[]{:S(2)}) %all-to-all-start.7) | async-done | bytes 131104 | tf_op jit(solution)/shard_map/all_to_all | solution.py:187
  123.1 3.4 %all-to-all-start.6 = ((f32[16,16,128]{2,1,0:T(8,128)}), f32[16,16,128]{2,1,0:T(8,128)S(1)}, u32[]{:S(2)}, u32[]{:S(2)}) async-start(f32[16,16,128]{2,1,0:T(8,128)} %get-tuple-element.20), calls=%async_computation.6 | async-start | bytes 262144 | tf_op jit(solution)/shard_map/all_to_all | solution.py:187
  128.7 3.3 %shard_map.69 = (f32[32,4,128]{2,1,0:T(4,128)}, f32[16,128]{1,0:T(8,128)S(1)}) custom-call(f32[512,2048]{1,0:T(8,128)S(1)} %copy-done.5, f32[16,16,128]{2,1,0:T(8,128)S(1)} %all-to-all-done.7.refs_1_, f32[16,128]{1,0:T(8,128)S(1)} %get-tuple-element.22.refs_2_), custom_call_target="tpu_custom_call" | custom-call | flops 16777216 | bytes 4194304 | tf_op jit(solution)/shard_map/pallas_call | solution.py:193
  135.0 3.8 %all-to-all-start.9 = ((f32[32,4,128]{2,1,0:T(4,128)}), f32[32,4,128]{2,1,0:T(4,128)S(1)}, u32[]{:S(2)}, u32[]{:S(2)}) async-start(f32[32,4,128]{2,1,0:T(4,128)} %get-tuple-element.25), calls=%async_computation.9 | async-start | bytes 131072 | tf_op jit(solution)/shard_map/all_to_all | solution.py:187
  141.0 3.3 %shard_map.70 = (f32[32,4,128]{2,1,0:T(4,128)}, f32[16,128]{1,0:T(8,128)}) custom-call(f32[512,2048]{1,0:T(8,128)S(1)} %copy-done.6, f32[16,16,128]{2,1,0:T(8,128)S(1)} %all-to-all-done.6.refs_1_, f32[16,128]{1,0:T(8,128)S(1)} %get-tuple-element.23.refs_2_), custom_call_target="tpu_custom_call" | custom-call | flops 16777216 | bytes 4194304 | tf_op jit(solution)/shard_map/pallas_call | solution.py:193
  144.4 3.4 %all-to-all-done.9.refs_0_ = f32[32,4,128]{2,1,0:T(4,128)S(1)} async-done(((f32[32,4,128]{2,1,0:T(4,128)}), f32[32,4,128]{2,1,0:T(4,128)S(1)}, u32[]{:S(2)}, u32[]{:S(2)}) %all-to-all-start.9) | async-done | bytes 65568 | tf_op jit(solution)/shard_map/all_to_all | solution.py:187
  147.7 5.9 %all-to-all-start.8 = ((f32[32,4,128]{2,1,0:T(4,128)}), f32[32,4,128]{2,1,0:T(4,128)S(1)}, u32[]{:S(2)}, u32[]{:S(2)}) async-start(f32[32,4,128]{2,1,0:T(4,128)} %get-tuple-element.24), calls=%async_computation.8 | async-start | bytes 131072 | tf_op jit(solution)/shard_map/all_to_all | solution.py:187
  153.6 8.8 %all-to-all-done.8.refs_0_ = f32[32,4,128]{2,1,0:T(4,128)S(1)} async-done(((f32[32,4,128]{2,1,0:T(4,128)}), f32[32,4,128]{2,1,0:T(4,128)S(1)}, u32[]{:S(2)}, u32[]{:S(2)}) %all-to-all-start.8) | async-done | bytes 65568 | tf_op jit(solution)/shard_map/all_to_all | solution.py:187
  163.1 5.7 %all-to-all-start.10 = ((f32[16,4,128]{2,1,0:T(4,128)}), f32[16,4,128]{2,1,0:T(4,128)S(1)}, u32[]{:S(2)}, u32[]{:S(2)}) async-start(f32[16,4,128]{2,1,0:T(4,128)} %shard_map.72), calls=%async_computation.10 | async-start | bytes 65536 | tf_op jit(solution)/shard_map/all_to_all | solution.py:187
  169.5 6.7 %all-to-all-done.10.refs_0_ = f32[16,4,128]{2,1,0:T(4,128)S(1)} async-done(((f32[16,4,128]{2,1,0:T(4,128)}), f32[16,4,128]{2,1,0:T(4,128)S(1)}, u32[]{:S(2)}, u32[]{:S(2)}) %all-to-all-start.10) | async-done | bytes 32800 | tf_op jit(solution)/shard_map/all_to_all | solution.py:187
  (44 shorter events, 34.0 us)
Async XLA Ops:
  0.0 12.8 %copy-start.10 = (s32[128]{0:T(128)S(1)}, s32[128]{0:T(128)}, u32[]{:S(2)}) copy-start(s32[128]{0:T(128)} %param.9) | copy-start | bytes 1540
  0.0 12.8 %copy-start.8 = (bf16[128,256]{1,0:T(8,128)(2,1)S(1)}, bf16[128,256]{1,0:T(8,128)(2,1)}, u32[]{:S(2)}) copy-start(bf16[128,256]{1,0:T(8,128)(2,1)} %param.7) | copy-start | bytes 196612
  2.2 24.3 %all-to-all-start = ((bf16[32,16,384]{2,1,0:T(8,128)(2,1)}), bf16[32,16,384]{2,1,0:T(8,128)(2,1)S(1)}, u32[]{:S(2)}, u32[]{:S(2)}) async-start(bf16[32,16,384]{2,1,0:T(8,128)(2,1)} %broadcast_in_dim.42), calls=%async_computation | async-start | bytes 786432 | tf_op jit(solution)/shard_map/all_to_all | solution.py:187
  12.8 24.7 %copy-start.9 = (s32[100,100]{1,0:T(8,128)S(1)}, s32[100,100]{1,0:T(8,128)}, u32[]{:S(2)}) copy-start(s32[100,100]{1,0:T(8,128)} %param.10) | copy-start | bytes 120004
  27.4 19.9 %all-to-all-start.1 = ((bf16[4,2,144,256]{3,2,1,0:T(8,128)(2,1)}), bf16[4,2,144,256]{3,2,1,0:T(8,128)(2,1)S(1)}, u32[]{:S(2)}, u32[]{:S(2)}) async-start(bf16[4,2,144,256]{3,2,1,0:T(8,128)(2,1)} %broadcast_in_dim.46), calls=%async_computation.1 | async-start | bytes 1179648 | tf_op jit(solution)/shard_map/all_to_all | solution.py:187
  47.4 9.7 %copy-start.7 = (f32[4]{0:T(128)S(1)}, f32[4]{0:T(128)}, u32[]{:S(2)}) copy-start(f32[4]{0:T(128)} %refs_3_.1) | copy-start | bytes 52
  61.9 2.0 %copy-start = (f32[512,2048]{1,0:T(8,128)}, f32[512,2048]{1,0:T(8,128)S(1)}, u32[]{:S(2)}) copy-start(f32[512,2048]{1,0:T(8,128)S(1)} %get-tuple-element.16.refs_0_.cost_ref) | copy-start | bytes 12582916
  63.9 16.2 %all-to-all-start.3 = ((f32[16,16,128]{2,1,0:T(8,128)}), f32[16,16,128]{2,1,0:T(8,128)S(1)}, u32[]{:S(2)}, u32[]{:S(2)}) async-start(f32[16,16,128]{2,1,0:T(8,128)} %get-tuple-element.17), calls=%async_computation.3 | async-start | bytes 262144 | tf_op jit(solution)/shard_map/all_to_all | solution.py:187
  70.9 2.2 %copy-start.1 = (f32[512,2048]{1,0:T(8,128)S(1)}, f32[512,2048]{1,0:T(8,128)}, u32[]{:S(2)}) copy-start(f32[512,2048]{1,0:T(8,128)} %copy-done) | copy-start | bytes 12582916
  80.1 14.0 %all-to-all-start.5 = ((f32[32,4,128]{2,1,0:T(4,128)}), f32[32,4,128]{2,1,0:T(4,128)S(1)}, u32[]{:S(2)}, u32[]{:S(2)}) async-start(f32[32,4,128]{2,1,0:T(4,128)} %shard_map.66), calls=%async_computation.5 | async-start | bytes 131072 | tf_op jit(solution)/shard_map/all_to_all | solution.py:187
  84.9 2.2 %copy-start.2 = (f32[512,2048]{1,0:T(8,128)S(1)}, f32[512,2048]{1,0:T(8,128)}, u32[]{:S(2)}) copy-start(f32[512,2048]{1,0:T(8,128)} %copy-done) | copy-start | bytes 12582916
  94.1 14.4 %all-to-all-start.4 = ((f32[32,4,128]{2,1,0:T(4,128)}), f32[32,4,128]{2,1,0:T(4,128)S(1)}, u32[]{:S(2)}, u32[]{:S(2)}) async-start(f32[32,4,128]{2,1,0:T(4,128)} %get-tuple-element.18), calls=%async_computation.4 | async-start | bytes 131072 | tf_op jit(solution)/shard_map/all_to_all | solution.py:187
  99.6 2.2 %copy-start.3 = (f32[512,2048]{1,0:T(8,128)S(1)}, f32[512,2048]{1,0:T(8,128)}, u32[]{:S(2)}) copy-start(f32[512,2048]{1,0:T(8,128)} %copy-done) | copy-start | bytes 12582916
  108.5 14.6 %all-to-all-start.7 = ((f32[16,16,128]{2,1,0:T(8,128)}), f32[16,16,128]{2,1,0:T(8,128)S(1)}, u32[]{:S(2)}, u32[]{:S(2)}) async-start(f32[16,16,128]{2,1,0:T(8,128)} %get-tuple-element.21), calls=%async_computation.7 | async-start | bytes 262144 | tf_op jit(solution)/shard_map/all_to_all | solution.py:187
  113.9 2.2 %copy-start.4 = (f32[512,2048]{1,0:T(8,128)S(1)}, f32[512,2048]{1,0:T(8,128)}, u32[]{:S(2)}) copy-start(f32[512,2048]{1,0:T(8,128)} %copy-done) | copy-start | bytes 12582916
  123.1 11.9 %all-to-all-start.6 = ((f32[16,16,128]{2,1,0:T(8,128)}), f32[16,16,128]{2,1,0:T(8,128)S(1)}, u32[]{:S(2)}, u32[]{:S(2)}) async-start(f32[16,16,128]{2,1,0:T(8,128)} %get-tuple-element.20), calls=%async_computation.6 | async-start | bytes 262144 | tf_op jit(solution)/shard_map/all_to_all | solution.py:187
  126.5 2.2 %copy-start.5 = (f32[512,2048]{1,0:T(8,128)S(1)}, f32[512,2048]{1,0:T(8,128)}, u32[]{:S(2)}) copy-start(f32[512,2048]{1,0:T(8,128)} %copy-done) | copy-start | bytes 12582916
  135.0 12.7 %all-to-all-start.9 = ((f32[32,4,128]{2,1,0:T(4,128)}), f32[32,4,128]{2,1,0:T(4,128)S(1)}, u32[]{:S(2)}, u32[]{:S(2)}) async-start(f32[32,4,128]{2,1,0:T(4,128)} %get-tuple-element.25), calls=%async_computation.9 | async-start | bytes 131072 | tf_op jit(solution)/shard_map/all_to_all | solution.py:187
  138.8 2.2 %copy-start.6 = (f32[512,2048]{1,0:T(8,128)S(1)}, f32[512,2048]{1,0:T(8,128)}, u32[]{:S(2)}) copy-start(f32[512,2048]{1,0:T(8,128)} %copy-done) | copy-start | bytes 12582916
  147.7 14.7 %all-to-all-start.8 = ((f32[32,4,128]{2,1,0:T(4,128)}), f32[32,4,128]{2,1,0:T(4,128)S(1)}, u32[]{:S(2)}, u32[]{:S(2)}) async-start(f32[32,4,128]{2,1,0:T(4,128)} %get-tuple-element.24), calls=%async_computation.8 | async-start | bytes 131072 | tf_op jit(solution)/shard_map/all_to_all | solution.py:187
  163.1 13.1 %all-to-all-start.10 = ((f32[16,4,128]{2,1,0:T(4,128)}), f32[16,4,128]{2,1,0:T(4,128)S(1)}, u32[]{:S(2)}, u32[]{:S(2)}) async-start(f32[16,4,128]{2,1,0:T(4,128)} %shard_map.72), calls=%async_computation.10 | async-start | bytes 65536 | tf_op jit(solution)/shard_map/all_to_all | solution.py:187

commit v3 on v2

v3 whole, which is shorter than its diff:
```python
import math

import jax
import jax.numpy as jnp
from jax import lax
from jax.experimental import pallas as pl
from jax.experimental.pallas import tpu as pltpu
from jax.sharding import PartitionSpec as P

ITERS = 4
LANES = 128
SUB = 8
CHUNKS = 4

entropy_scale = 0.05
UNIT = entropy_scale * math.log(2.0)

ORDER = ("zh", "zl", "core", "yh", "yl", "x")
NEAR = ("zl", "core", "yl")
FAR = ("zh", "yh", "x")

VMEM = pl.BlockSpec(memory_space=pltpu.VMEM)


def lse_lead(parts):
    high = jnp.max(parts, axis=0)
    return high + jnp.log2(jnp.sum(jnp.exp2(parts - high[None]), axis=0))


def spread_rows(values, out_ref):
    for a in range(values.shape[0]):
        block = jnp.broadcast_to(values[a : a + 1, :], (LANES, LANES))
        out_ref[a * LANES : (a + 1) * LANES, :] = block.T


def lanes_of(ref, combine):
    rows = []
    for a in range(ref.shape[0] // LANES):
        block = ref[a * LANES : (a + 1) * LANES, :].T
        rows.append(combine(block, axis=0, keepdims=True))
    return jnp.concatenate(rows, axis=0)


def bring(cost_hbm, cost_ref, sems):
    rows = cost_ref.shape[0] // CHUNKS
    copies = [
        pltpu.make_async_copy(
            cost_hbm.at[q * rows : (q + 1) * rows, :], cost_ref.at[q * rows : (q + 1) * rows, :], sems.at[q]
        )
        for q in range(CHUNKS)
    ]
    for copy in copies:
        copy.start()
    return lambda q: copies[q].wait()


def no_wait(q):
    return None


def group_loops(rows, wait, step, carry):
    groups = rows // SUB // CHUNKS
    for q in range(CHUNKS):
        wait(q)
        carry = lax.fori_loop(q * groups, (q + 1) * groups, step, carry, unroll=4)
    return carry


def group(g):
    return pl.ds(pl.multiple_of(g * SUB, SUB), SUB)


def col_partial(cost_ref, row_ref, wait):
    rows, cols = cost_ref.shape
    chunks = range(cols // LANES)

    def tiles(g):
        cells = [cost_ref[group(g), k * LANES : (k + 1) * LANES] for k in chunks]
        if row_ref is None:
            return [-cell for cell in cells]
        base = row_ref[group(g), :]
        return [base - cell for cell in cells]

    def peaks(g, high):
        return tuple(jnp.maximum(h, t) for h, t in zip(high, tiles(g)))

    start = tuple(jnp.full((SUB, LANES), -jnp.inf, jnp.float32) for _ in chunks)
    high = group_loops(rows, wait, peaks, start)
    high = tuple(jnp.max(h, axis=0, keepdims=True) for h in high)

    def totals(g, total):
        return tuple(s + jnp.exp2(t - h) for s, t, h in zip(total, tiles(g), high))

    zero = tuple(jnp.zeros((SUB, LANES), jnp.float32) for _ in chunks)
    total = group_loops(rows, no_wait, totals, zero)
    return jnp.concatenate(
        [h + jnp.log2(jnp.sum(s, axis=0, keepdims=True)) for h, s in zip(high, total)], axis=0
    )


def row_partial(cost_ref, col, high_ref, total_ref, wait):
    rows, cols = cost_ref.shape
    chunks = range(cols // LANES)

    def tile(g, k):
        cell = cost_ref[group(g), k * LANES : (k + 1) * LANES]
        return -cell if col is None else col[k : k + 1, :] - cell

    def peaks(g, carry):
        high = tile(g, 0)
        for k in chunks[1:]:
            high = jnp.maximum(high, tile(g, k))
        high_ref[group(g), :] = jnp.broadcast_to(jnp.max(high, axis=1, keepdims=True), (SUB, LANES))
        return carry

    group_loops(rows, wait, peaks, 0)

    def totals(g, carry):
        high = high_ref[group(g), :]
        total = jnp.exp2(tile(g, 0) - high)
        for k in chunks[1:]:
            total = total + jnp.exp2(tile(g, k) - high)
        total_ref[group(g), :] = total
        return carry

    group_loops(rows, no_wait, totals, 0)
    return lanes_of(high_ref, jnp.max) + jnp.log2(lanes_of(total_ref, jnp.sum))


def split3(values):
    high = values.astype(jnp.bfloat16)
    rest = values - high.astype(jnp.float32)
    mid = rest.astype(jnp.bfloat16)
    low = (rest - mid.astype(jnp.float32)).astype(jnp.bfloat16)
    return high, mid, low


def dot(left, right, dims):
    return lax.dot_general(left, right, (dims, ((), ())), preferred_element_type=jnp.float32)


def start_kernel(
    train_ref, valid_ref, levels_ref, level_cost_ref, cost_hbm, row_out, cost_ref, row_a, row_b, sems, *, num_levels
):
    shards, shard_rows, width = train_ref.shape
    embed = width - LANES
    rows = shards * shard_rows
    packed = train_ref[...].reshape(rows, width)
    train = packed[:, :embed]
    wide = train.astype(jnp.float32)
    train_sq = jnp.sum(wide * wide, axis=1, keepdims=True)
    levels = levels_ref[...]
    table = jnp.zeros(levels.shape, jnp.float32)
    for level in range(num_levels):
        table = table + jnp.where(levels == level, level_cost_ref[level], 0.0)
    labels = packed[:, embed:].astype(jnp.float32)
    lane_ids = lax.broadcasted_iota(jnp.int32, labels.shape, 1).astype(jnp.float32)
    train_hot = jnp.where(labels == lane_ids, 1.0, 0.0).astype(jnp.bfloat16)
    parts = [dot(train_hot, part, ((1,), (0,))).astype(jnp.bfloat16) for part in split3(table)]
    left = jnp.concatenate([train * jnp.bfloat16(-2.0 / embed), *parts], axis=1)
    ones = jnp.ones((SUB, embed), jnp.bfloat16)
    blocks, block_rows, _ = valid_ref.shape
    points = LANES
    copies = []
    for pair in range(blocks // 2):
        halves = (2 * pair, 2 * pair + 1)
        block = jnp.concatenate([valid_ref[h, :points, :] for h in halves], axis=0)
        hots = []
        for h in halves:
            label_row = valid_ref[h, points:, :LANES].astype(jnp.float32)[:1, :]
            class_ids = lax.broadcasted_iota(jnp.int32, (LANES, LANES), 0).astype(jnp.float32)
            hots.append(jnp.where(class_ids == label_row, 1.0, 0.0).astype(jnp.bfloat16))
        hot = jnp.concatenate(hots, axis=1)
        block_wide = block.astype(jnp.float32)
        squares = block_wide * block_wide
        sq_high = squares.astype(jnp.bfloat16)
        sq_low = (squares - sq_high.astype(jnp.float32)).astype(jnp.bfloat16)
        block_sq = (dot(ones, sq_high, ((1,), (1,))) + dot(ones, sq_low, ((1,), (1,))))[:1, :]
        products = dot(left[:, :embed], block, ((1,), (1,)))
        label_part = dot(left[:, embed:], jnp.concatenate([hot] * 3, axis=0), ((1,), (0,)))
        cost = products + (train_sq + block_sq) * (1.0 / embed) + label_part
        here = slice(pair * 2 * points, (pair + 1) * 2 * points)
        cost_ref[:, here] = cost * (1.0 / UNIT)
        copies.append(pltpu.make_async_copy(cost_ref.at[:, here], cost_hbm.at[:, here], sems.at[pair]))
        copies[-1].start()
    row_out[...] = jnp.broadcast_to(row_partial(cost_ref, None, row_a, row_b, no_wait)[None], row_out.shape)
    for copy in copies:
        copy.wait()


def first_col_kernel(cost_hbm, out_ref, cost_ref, sems):
    wait = bring(cost_hbm, cost_ref, sems)
    out_ref[...] = col_partial(cost_ref, None, wait)


def col_kernel(cost_hbm, parts_ref, pot_ref, out_ref, new_ref, cost_ref, sems, spread_ref, *, offset):
    wait = bring(cost_hbm, cost_ref, sems)
    pot = 0.5 * (pot_ref[...] + (offset - lse_lead(parts_ref[...])))
    new_ref[...] = pot
    spread_rows(pot, spread_ref)
    out_ref[...] = col_partial(cost_ref, spread_ref, wait)


def row_kernel(cost_hbm, parts_ref, pot_ref, out_ref, new_ref, cost_ref, sems, row_a, row_b, *, offset):
    wait = bring(cost_hbm, cost_ref, sems)
    pot = 0.5 * (pot_ref[...] + (offset - lse_lead(parts_ref[...])))
    new_ref[...] = pot
    out_ref[...] = jnp.broadcast_to(row_partial(cost_ref, pot, row_a, row_b, wait)[None], out_ref.shape)


def last_kernel(parts_ref, pot_ref, out_ref, *, offset):
    pot = 0.5 * (pot_ref[...] + (offset - lse_lead(parts_ref[...])))
    out_ref[...] = jnp.broadcast_to(pot[None], out_ref.shape)


def calibrate_kernel(where_ref, parts_ref, out_ref, *, count):
    total = jnp.sum(jnp.sum(parts_ref[...], axis=0), keepdims=True)
    blocks = [parts_ref[where_ref[0] * 2 + side] for side in range(2)]
    row_ids = lax.broadcasted_iota(jnp.int32, blocks[0].shape, 0)
    low_half = lax.broadcasted_iota(jnp.int32, (1, LANES), 1) < LANES // 2
    rows = []
    for q in range(out_ref.shape[0] // 2):
        mine = row_ids == where_ref[1] * (out_ref.shape[0] // 2) + q
        first, second = [jnp.sum(jnp.where(mine, block, 0.0), axis=0, keepdims=True) for block in blocks]
        rows.append(jnp.where(low_half, first, pltpu.roll(second, LANES // 2, 1)))
        rows.append(jnp.where(low_half, pltpu.roll(first, LANES // 2, 1), second))
    picked = jnp.concatenate(rows, axis=0)
    out_ref[...] = (picked * count - total) * (UNIT / (count - 1))


def exchange(copies, axis):
    return lax.all_to_all(copies, axis, 0, 0, tiled=True)


def near_gather(block):
    return lax.all_gather(lax.all_gather(block[None], NEAR[:2], axis=0, tiled=True), NEAR[2], axis=0, tiled=True)


def call(kernel, out_shape, scratch, *args, smem=(), hbm=(), limit=16, **static):
    body = kernel if not static else (lambda *refs: kernel(*refs, **static))
    smem_spec, hbm_spec = pl.BlockSpec(memory_space=pltpu.SMEM), pl.BlockSpec(memory_space=pltpu.HBM)
    specs = [smem_spec if i in smem else hbm_spec if i in hbm else VMEM for i in range(len(args))]
    out_specs = [hbm_spec if len(o.shape) == 2 and o.shape[0] > 4 * LANES else VMEM for o in out_shape]
    return pl.pallas_call(
        body,
        out_shape=out_shape,
        in_specs=specs,
        out_specs=out_specs,
        scratch_shapes=scratch,
        compiler_params=pltpu.CompilerParams(vmem_limit_bytes=limit * 2**20),
        cost_estimate=pl.CostEstimate(flops=2**24, bytes_accessed=4 * 2**20, transcendentals=2**20),
    )(*args)


def shards(train_embed, valid_embed, train_labels, valid_labels, pair_level, level_cost):
    row_size, col_size = lax.axis_size(NEAR), lax.axis_size(FAR)
    embed = train_embed.shape[1]
    f32 = jnp.float32
    train_pack = jnp.concatenate(
        [
            train_embed,
            jnp.broadcast_to(train_labels.astype(jnp.bfloat16)[:, None], (train_embed.shape[0], LANES)),
        ],
        axis=1,
    )
    label_row = jnp.tile(valid_labels.astype(jnp.bfloat16), embed // LANES)[None, :]
    valid_pack = jnp.concatenate([valid_embed, jnp.broadcast_to(label_row, (16, embed))], axis=0)
    train_all = exchange(jnp.broadcast_to(train_pack[None], (col_size,) + train_pack.shape), FAR)
    valid_all = near_gather(valid_pack)
    rows = train_embed.shape[0] * col_size
    cols = valid_embed.shape[0] * row_size
    row_chunks, col_chunks = rows // LANES, cols // LANES
    classes = pair_level.shape[0]
    levels = jnp.pad(pair_level, ((0, LANES - classes), (0, LANES - classes)), constant_values=-1)
    tile = jax.ShapeDtypeStruct((rows, cols), f32)
    row_copies = jax.ShapeDtypeStruct((col_size, row_chunks, LANES), f32)
    row_shape = jax.ShapeDtypeStruct((row_chunks, LANES), f32)
    col_shape = jax.ShapeDtypeStruct((col_chunks, LANES), f32)
    tall = pltpu.VMEM((rows, LANES), f32)
    held = [pltpu.VMEM((rows, cols), f32), pltpu.SemaphoreType.DMA((CHUNKS,))]
    cost, row_part = call(
        start_kernel,
        (tile, row_copies),
        [held[0], tall, tall, pltpu.SemaphoreType.DMA((row_size // 2,))],
        train_all,
        valid_all,
        levels,
        level_cost,
        smem=(3,),
        num_levels=level_cost.shape[0],
        limit=40,
    )
    full_rows, full_cols = rows * row_size, cols * col_size
    row_offset, col_offset = math.log2(full_cols), math.log2(full_rows)
    row_pot = jnp.zeros(row_shape.shape, f32)
    col_pot = jnp.zeros(col_shape.shape, f32)
    row_got = None
    for iteration in range(ITERS - 1):
        sent = exchange(row_part, FAR)
        if iteration == 0:
            (col_part,) = call(first_col_kernel, (col_shape,), held, cost, hbm=(0,))
        else:
            col_part, row_pot = call(
                col_kernel, (col_shape, row_shape), held + [tall], cost, row_got, row_pot, hbm=(0,), offset=row_offset
            )
        row_part, col_pot = call(
            row_kernel,
            (row_copies, col_shape),
            held + [tall, tall],
            cost,
            near_gather(col_part),
            col_pot,
            hbm=(0,),
            offset=col_offset,
        )
        row_got = sent
    (row_pot,) = call(
        last_kernel, (jax.ShapeDtypeStruct((1,) + row_shape.shape, f32),), [], row_got, row_pot, offset=row_offset
    )
    row_got = exchange(row_part, FAR)
    (final,) = call(
        last_kernel,
        (jax.ShapeDtypeStruct((row_size,) + row_shape.shape, f32),),
        [],
        row_got,
        row_pot[0],
        offset=row_offset,
    )
    finals = exchange(final, NEAR)
    where = jnp.stack([lax.axis_index(NEAR[:2]), lax.axis_index("zh")]).astype(jnp.int32)
    out_rows = full_rows // lax.axis_size(("zh",) + NEAR[:2]) // LANES
    (out,) = call(
        calibrate_kernel, (jax.ShapeDtypeStruct((out_rows, LANES), f32),), [], where, finals, smem=(0,), count=full_rows
    )
    return out.reshape(out_rows * LANES)


def solution(mesh):
    row_size, col_size = mesh.shape["row"], mesh.shape["col"]
    sizes = (row_size // 4, 2, 2, 4, 2, col_size // 8)
    finer = jax.sharding.Mesh(mesh.devices.reshape(sizes), ORDER)
    placed = (P(ORDER, None), P(ORDER, None), P(ORDER), P(ORDER), P(), P())
    return jax.shard_map(shards, mesh=finer, in_specs=placed, out_specs=P(ORDER[:3]), check_vma=False)
```

time: 178 us -> 209 us (1.17)
  blocking collectives: 14.4 us -> 58.1 us
  waiting for transfers between devices: 57.6 us -> 18.5 us
  starting transfers between devices: 62.2 us -> 83.5 us
  Pallas kernels: 23.5 us -> 34.1 us
  local copies, waits for them, and re-layouts: 17.6 us -> 11 us
    all_gather x1 -> x8, blocking collectives: 4.78 us -> 58.1 us  [the longest x4 30 us: near_gather(): lax.all_gather(block[None], NEAR[:2], axis=0, tiled=True)]
    all_to_all x10 -> x6, waiting for transfers between devices: 57.6 us -> 18.5 us  [exchange(): return lax.all_to_all(copies, axis, 0, 0, tiled=True)]
    all_to_all x10 -> x6, starting transfers between devices: 62.2 us -> 83.5 us  [exchange(): return lax.all_to_all(copies, axis, 0, 0, tiled=True)]
    pallas_call x10, Pallas kernels: 23.5 us -> 34.1 us  [call(): pl.pallas_call(body, out_shape=out_shape, in_specs=specs, out_specs=out_s...]
    all_to_all x1 -> x0, blocking collectives: 9.65 us -> none  [exchange(): return lax.all_to_all(copies, axis, 0, 0, tiled=True)]
    unnamed x22 -> x10, local copies, waits for them, and re-layouts: 15.1 us -> 9.13 us
  transfers between devices with their start and end apart: 10 -> 6, of which waited for: 10 -> 2; matrix products, arithmetic and copies ran while one was open for 0% -> 1% of each run, Pallas kernels for 10% -> 10%
where the time goes in v3:
time: 209 us; the launch traced here: 208 us
  starting transfers between devices  83.5 us (40%)
  blocking collectives  58.1 us (28%)
  Pallas kernels  34.1 us (16%)
  waiting for transfers between devices  18.5 us (9%)
  local copies, waits for them, and re-layouts  11 us (5%)
  other arithmetic  2.94 us (1%)
    all_to_all x6, starting transfers between devices, exchange(): return lax.all_to_all(copies, axis, 0, 0, tiled=True)  83.5 us
    pallas_call x10, Pallas kernels, call(): pl.pallas_call(body, out_shape=out_shape, in_specs=specs, out_specs=out_s...  34.1 us
    all_gather x4, blocking collectives, near_gather(): lax.all_gather(block[None], NEAR[:2], axis=0, tiled=True)  30 us
    all_gather x4, blocking collectives, near_gather(): lax.all_gather(lax.all_gather(block[None], NEAR[:2], axis=0, tiled=True),...  28 us
    all_to_all x6, waiting for transfers between devices, exchange(): return lax.all_to_all(copies, axis, 0, 0, tiled=True)  18.5 us
    unnamed x10, local copies, waits for them, and re-layouts  9.13 us
  transfers between devices with their start and end apart: 6, of which 2 were waited for; matrix products, arithmetic and copies ran while one was open for 1% of the time, Pallas kernels for 10%

profile of v3, /device:TPU:1, one launch (start us, length us, event | category | flops | bytes accessed | tf_op | source)
XLA Modules:
  0.0 208.2 jit_solution(6426229667204712499)
XLA Ops:
  2.4 19.6 %all-to-all-start = ((bf16[64,16,384]{2,1,0:T(8,128)(2,1)}), bf16[64,16,384]{2,1,0:T(8,128)(2,1)S(1)}, u32[]{:S(2)}, u32[]{:S(2)}) async-start(bf16[64,16,384]{2,1,0:T(8,128)(2,1)} %broadcast_in_dim.32), calls=%async_computation | async-start | bytes 1572864 | tf_op jit(solution)/shard_map/all_to_all | solution.py:232
  24.3 10.2 %all-gather = bf16[576,256]{1,0:T(8,128)(2,1)S(1)} all-gather(bf16[144,256]{1,0:T(8,128)(2,1)S(1)} %pad_maximum_fusion), channel_id=2, replica_groups=mesh['zh'=4,'zl'=2,'core'=2,'yh'=4,'yl'=2,'x'=4] {'zl','core'}, dimensions={0}, use_global_device_ids=true | all-gather | bytes 368640 | tf_op jit(solution)/shard_map/all_gather | solution.py:236
  34.5 17.4 %all_gather.25.refs_1_ = bf16[8,144,256]{2,1,0:T(8,128)(2,1)S(1)} all-gather(bf16[4,144,256]{2,1,0:T(8,128)(2,1)S(1)} %bitcast.11), channel_id=1, replica_groups=mesh['zh'=4,'zl'=2,'core'=2,'yh'=4,'yl'=2,'x'=4] {'yl'}, dimensions={0}, use_global_device_ids=true | all-gather | bytes 884736 | tf_op jit(solution)/shard_map/all_gather | solution.py:236
  52.5 10.6 %shard_map.64 = (f32[1024,1024]{1,0:T(8,128)S(1)}, f32[64,8,128]{2,1,0:T(8,128)}) custom-call(bf16[64,16,384]{2,1,0:T(8,128)(2,1)S(1)} %all-to-all-done.refs_0_, bf16[8,144,256]{2,1,0:T(8,128)(2,1)S(1)} %all_gather.25.refs_1_, s32[128,128]{1,0:T(8,128)S(1)} %pad.4.refs_2_, f32[4]{0:T(128)S(1)} %copy-done.4), custom_call_target="tpu_custom_call" | custom-call | flops 16777216 | bytes 4194304 | tf_op jit(solution)/shard_map/pallas_call | solution.py:244
  65.1 14.1 %all-to-all-start.2 = ((f32[64,8,128]{2,1,0:T(8,128)}), f32[64,8,128]{2,1,0:T(8,128)S(1)}, u32[]{:S(2)}, u32[]{:S(2)}) async-start(f32[64,8,128]{2,1,0:T(8,128)} %get-tuple-element.18), calls=%async_computation.2 | async-start | bytes 524288 | tf_op jit(solution)/shard_map/all_to_all | solution.py:232
  79.2 2.2 %copy-done.1 = f32[1024,1024]{1,0:T(8,128)S(1)} copy-done((f32[1024,1024]{1,0:T(8,128)S(1)}, f32[1024,1024]{1,0:T(8,128)}, u32[]{:S(2)}) %copy-start.1) | copy-done | bytes 4194328
  83.1 6.6 %all-gather.1 = f32[32,128]{1,0:T(8,128)S(1)} all-gather(f32[8,128]{1,0:T(8,128)S(1)} %shard_map.65), channel_id=3, replica_groups=mesh['zh'=4,'zl'=2,'core'=2,'yh'=4,'yl'=2,'x'=4] {'zl','core'}, dimensions={0}, use_global_device_ids=true | all-gather | bytes 20480 | tf_op jit(solution)/shard_map/all_gather | solution.py:236
  89.7 3.5 %all_gather.27.refs_1_ = f32[8,8,128]{2,1,0:T(8,128)S(1)} all-gather(f32[4,8,128]{2,1,0:T(8,128)S(1)} %bitcast.12), channel_id=1, replica_groups=mesh['zh'=4,'zl'=2,'core'=2,'yh'=4,'yl'=2,'x'=4] {'yl'}, dimensions={0}, use_global_device_ids=true | all-gather | bytes 49152 | tf_op jit(solution)/shard_map/all_gather | solution.py:236
  93.3 5.3 %shard_map.66 = (f32[64,8,128]{2,1,0:T(8,128)}, f32[8,128]{1,0:T(8,128)S(1)}) custom-call(f32[1024,1024]{1,0:T(8,128)S(1)} %copy-done.1, f32[8,8,128]{2,1,0:T(8,128)S(1)} %all_gather.27.refs_1_, f32[8,128]{1,0:T(8,128)S(1)} %broadcast_1_refs_2_.2.refs_2_), custom_call_target="tpu_custom_call" | custom-call | flops 16777216 | bytes 4194304 | tf_op jit(solution)/shard_map/pallas_call | solution.py:244
  98.5 14.1 %all-to-all-start.1 = ((f32[64,8,128]{2,1,0:T(8,128)}), f32[64,8,128]{2,1,0:T(8,128)S(1)}, u32[]{:S(2)}, u32[]{:S(2)}) async-start(f32[64,8,128]{2,1,0:T(8,128)} %get-tuple-element.17), calls=%async_computation.1 | async-start | bytes 524288 | tf_op jit(solution)/shard_map/all_to_all | solution.py:232
  112.6 2.2 %copy-done.2 = f32[1024,1024]{1,0:T(8,128)S(1)} copy-done((f32[1024,1024]{1,0:T(8,128)S(1)}, f32[1024,1024]{1,0:T(8,128)}, u32[]{:S(2)}) %copy-start.2) | copy-done | bytes 4194328
  116.8 6.6 %all-gather.3 = f32[32,128]{1,0:T(8,128)S(1)} all-gather(f32[8,128]{1,0:T(8,128)S(1)} %get-tuple-element.21), channel_id=5, replica_groups=mesh['zh'=4,'zl'=2,'core'=2,'yh'=4,'yl'=2,'x'=4] {'zl','core'}, dimensions={0}, use_global_device_ids=true | all-gather | bytes 20480 | tf_op jit(solution)/shard_map/all_gather | solution.py:236
  123.4 3.5 %all_gather.31.refs_1_ = f32[8,8,128]{2,1,0:T(8,128)S(1)} all-gather(f32[4,8,128]{2,1,0:T(8,128)S(1)} %bitcast.13), channel_id=1, replica_groups=mesh['zh'=4,'zl'=2,'core'=2,'yh'=4,'yl'=2,'x'=4] {'yl'}, dimensions={0}, use_global_device_ids=true | all-gather | bytes 49152 | tf_op jit(solution)/shard_map/all_gather | solution.py:236
  127.0 5.3 %shard_map.69 = (f32[64,8,128]{2,1,0:T(8,128)}, f32[8,128]{1,0:T(8,128)S(1)}) custom-call(f32[1024,1024]{1,0:T(8,128)S(1)} %copy-done.2, f32[8,8,128]{2,1,0:T(8,128)S(1)} %all_gather.31.refs_1_, f32[8,128]{1,0:T(8,128)S(1)} %get-tuple-element.22.refs_2_), custom_call_target="tpu_custom_call" | custom-call | flops 16777216 | bytes 4194304 | tf_op jit(solution)/shard_map/pallas_call | solution.py:244
  132.2 14.6 %all-to-all-start.4 = ((f32[64,8,128]{2,1,0:T(8,128)}), f32[64,8,128]{2,1,0:T(8,128)S(1)}, u32[]{:S(2)}, u32[]{:S(2)}) async-start(f32[64,8,128]{2,1,0:T(8,128)} %get-tuple-element.25), calls=%async_computation.4 | async-start | bytes 524288 | tf_op jit(solution)/shard_map/all_to_all | solution.py:232
  146.8 2.2 %copy-done.3 = f32[1024,1024]{1,0:T(8,128)S(1)} copy-done((f32[1024,1024]{1,0:T(8,128)S(1)}, f32[1024,1024]{1,0:T(8,128)}, u32[]{:S(2)}) %copy-start.3) | copy-done | bytes 4194328
  149.0 2.0 shard_map.68
  151.0 6.6 %all-gather.2 = f32[32,128]{1,0:T(8,128)S(1)} all-gather(f32[8,128]{1,0:T(8,128)S(1)} %get-tuple-element.20), channel_id=4, replica_groups=mesh['zh'=4,'zl'=2,'core'=2,'yh'=4,'yl'=2,'x'=4] {'zl','core'}, dimensions={0}, use_global_device_ids=true | all-gather | bytes 20480 | tf_op jit(solution)/shard_map/all_gather | solution.py:236
  157.6 3.5 %all_gather.29.refs_1_ = f32[8,8,128]{2,1,0:T(8,128)S(1)} all-gather(f32[4,8,128]{2,1,0:T(8,128)S(1)} %bitcast.14), channel_id=1, replica_groups=mesh['zh'=4,'zl'=2,'core'=2,'yh'=4,'yl'=2,'x'=4] {'yl'}, dimensions={0}, use_global_device_ids=true | all-gather | bytes 49152 | tf_op jit(solution)/shard_map/all_gather | solution.py:236
  161.2 5.2 %shard_map.70 = (f32[64,8,128]{2,1,0:T(8,128)}, f32[8,128]{1,0:T(8,128)}) custom-call(f32[1024,1024]{1,0:T(8,128)S(1)} %copy-done.3, f32[8,8,128]{2,1,0:T(8,128)S(1)} %all_gather.29.refs_1_, f32[8,128]{1,0:T(8,128)S(1)} %get-tuple-element.23.refs_2_), custom_call_target="tpu_custom_call" | custom-call | flops 16777216 | bytes 4194304 | tf_op jit(solution)/shard_map/pallas_call | solution.py:244
  166.4 14.6 %all-to-all-start.3 = ((f32[64,8,128]{2,1,0:T(8,128)}), f32[64,8,128]{2,1,0:T(8,128)S(1)}, u32[]{:S(2)}, u32[]{:S(2)}) async-start(f32[64,8,128]{2,1,0:T(8,128)} %get-tuple-element.24), calls=%async_computation.3 | async-start | bytes 524288 | tf_op jit(solution)/shard_map/all_to_all | solution.py:232
  181.1 14.2 %all-to-all-done.3.refs_0_ = f32[64,8,128]{2,1,0:T(8,128)S(1)} async-done(((f32[64,8,128]{2,1,0:T(8,128)}), f32[64,8,128]{2,1,0:T(8,128)S(1)}, u32[]{:S(2)}, u32[]{:S(2)}) %all-to-all-start.3) | async-done | bytes 262176 | tf_op jit(solution)/shard_map/all_to_all | solution.py:232
  196.0 6.7 %all-to-all-start.5 = ((f32[8,8,128]{2,1,0:T(8,128)}), f32[8,8,128]{2,1,0:T(8,128)S(1)}, u32[]{:S(2)}, u32[]{:S(2)}) async-start(f32[8,8,128]{2,1,0:T(8,128)} %shard_map.72), calls=%async_computation.5 | async-start | bytes 65536 | tf_op jit(solution)/shard_map/all_to_all | solution.py:232
  202.7 4.3 %all-to-all-done.5.refs_1_ = f32[8,8,128]{2,1,0:T(8,128)S(1)} async-done(((f32[8,8,128]{2,1,0:T(8,128)}), f32[8,8,128]{2,1,0:T(8,128)S(1)}, u32[]{:S(2)}, u32[]{:S(2)}) %all-to-all-start.5) | async-done | bytes 32800 | tf_op jit(solution)/shard_map/all_to_all | solution.py:232
  (27 shorter events, 13.1 us)
Async XLA Ops:
  2.4 49.5 %all-to-all-start = ((bf16[64,16,384]{2,1,0:T(8,128)(2,1)}), bf16[64,16,384]{2,1,0:T(8,128)(2,1)S(1)}, u32[]{:S(2)}, u32[]{:S(2)}) async-start(bf16[64,16,384]{2,1,0:T(8,128)(2,1)} %broadcast_in_dim.32), calls=%async_computation | async-start | bytes 1572864 | tf_op jit(solution)/shard_map/all_to_all | solution.py:232
  51.9 0.7 copy-start.4
  63.2 1.9 copy-start
  65.1 33.4 %all-to-all-start.2 = ((f32[64,8,128]{2,1,0:T(8,128)}), f32[64,8,128]{2,1,0:T(8,128)S(1)}, u32[]{:S(2)}, u32[]{:S(2)}) async-start(f32[64,8,128]{2,1,0:T(8,128)} %get-tuple-element.18), calls=%async_computation.2 | async-start | bytes 524288 | tf_op jit(solution)/shard_map/all_to_all | solution.py:232
  79.2 2.2 %copy-start.1 = (f32[1024,1024]{1,0:T(8,128)S(1)}, f32[1024,1024]{1,0:T(8,128)}, u32[]{:S(2)}) copy-start(f32[1024,1024]{1,0:T(8,128)} %copy-done) | copy-start | bytes 12582916
  98.5 33.7 %all-to-all-start.1 = ((f32[64,8,128]{2,1,0:T(8,128)}), f32[64,8,128]{2,1,0:T(8,128)S(1)}, u32[]{:S(2)}, u32[]{:S(2)}) async-start(f32[64,8,128]{2,1,0:T(8,128)} %get-tuple-element.17), calls=%async_computation.1 | async-start | bytes 524288 | tf_op jit(solution)/shard_map/all_to_all | solution.py:232
  112.6 2.2 %copy-start.2 = (f32[1024,1024]{1,0:T(8,128)S(1)}, f32[1024,1024]{1,0:T(8,128)}, u32[]{:S(2)}) copy-start(f32[1024,1024]{1,0:T(8,128)} %copy-done) | copy-start | bytes 12582916
  132.2 34.2 %all-to-all-start.4 = ((f32[64,8,128]{2,1,0:T(8,128)}), f32[64,8,128]{2,1,0:T(8,128)S(1)}, u32[]{:S(2)}, u32[]{:S(2)}) async-start(f32[64,8,128]{2,1,0:T(8,128)} %get-tuple-element.25), calls=%async_computation.4 | async-start | bytes 524288 | tf_op jit(solution)/shard_map/all_to_all | solution.py:232
  146.8 2.2 %copy-start.3 = (f32[1024,1024]{1,0:T(8,128)S(1)}, f32[1024,1024]{1,0:T(8,128)}, u32[]{:S(2)}) copy-start(f32[1024,1024]{1,0:T(8,128)} %copy-done) | copy-start | bytes 12582916
  166.4 28.8 %all-to-all-start.3 = ((f32[64,8,128]{2,1,0:T(8,128)}), f32[64,8,128]{2,1,0:T(8,128)S(1)}, u32[]{:S(2)}, u32[]{:S(2)}) async-start(f32[64,8,128]{2,1,0:T(8,128)} %get-tuple-element.24), calls=%async_computation.3 | async-start | bytes 524288 | tf_op jit(solution)/shard_map/all_to_all | solution.py:232
  196.0 11.0 %all-to-all-start.5 = ((f32[8,8,128]{2,1,0:T(8,128)}), f32[8,8,128]{2,1,0:T(8,128)S(1)}, u32[]{:S(2)}, u32[]{:S(2)}) async-start(f32[8,8,128]{2,1,0:T(8,128)} %shard_map.72), calls=%async_computation.5 | async-start | bytes 65536 | tf_op jit(solution)/shard_map/all_to_all | solution.py:232

commit v4 on v1

v4 whole, which is shorter than its diff:
```python
import math

import jax
import jax.numpy as jnp
from jax import lax
from jax.experimental import pallas as pl
from jax.experimental.pallas import tpu as pltpu
from jax.sharding import PartitionSpec as P

ITERS = 4
LANES = 128
SUB = 8

entropy_scale = 0.05
UNIT = entropy_scale * math.log(2.0)

VMEM = pl.BlockSpec(memory_space=pltpu.VMEM)


def lse_lead(parts):
    high = jnp.max(parts, axis=0)
    return high + jnp.log2(jnp.sum(jnp.exp2(parts - high[None]), axis=0))


def merge(high, total):
    top = jnp.max(high, axis=0, keepdims=True)
    return top + jnp.log2(jnp.sum(total * jnp.exp2(high - top), axis=0, keepdims=True))


def spread_rows(values, out_ref):
    for a in range(values.shape[0]):
        block = jnp.broadcast_to(values[a : a + 1, :], (LANES, LANES))
        out_ref[a * LANES : (a + 1) * LANES, :] = block.T


def peak_and_sum(tiles):
    high = tiles[0]
    for tile in tiles[1:]:
        high = jnp.maximum(high, tile)
    total = jnp.exp2(tiles[0] - high)
    for tile in tiles[1:]:
        total = total + jnp.exp2(tile - high)
    return high, total


def col_partial(cost_ref, row_ref, high_ref, total_ref):
    rows, cols = cost_ref.shape
    blocks, chunks = rows // LANES, cols // LANES
    groups = LANES // SUB

    def block_step(q, carry):
        start = pl.multiple_of(q * LANES, LANES)
        bases = None if row_ref is None else [row_ref[pl.ds(start + g * SUB, SUB), :] for g in range(groups)]
        for k in range(chunks):
            cells = [cost_ref[pl.ds(start + g * SUB, SUB), k * LANES : (k + 1) * LANES] for g in range(groups)]
            tiles = [-cell for cell in cells] if bases is None else [base - cell for base, cell in zip(bases, cells)]
            high, total = peak_and_sum(tiles)
            here = (pl.ds(pl.multiple_of(q * SUB, SUB), SUB), slice(k * LANES, (k + 1) * LANES))
            high_ref[here] = high
            total_ref[here] = total
        return carry

    lax.fori_loop(0, blocks, block_step, 0)
    out = [merge(high_ref[:, k * LANES : (k + 1) * LANES], total_ref[:, k * LANES : (k + 1) * LANES]) for k in range(chunks)]
    return jnp.concatenate(out, axis=0)


def row_partial(cost_ref, col, high_ref, total_ref):
    rows, cols = cost_ref.shape
    chunks = cols // LANES
    bases = None if col is None else [jnp.broadcast_to(col[k : k + 1, :], (SUB, LANES)) for k in range(chunks)]

    def group_step(g, carry):
        here = pl.ds(pl.multiple_of(g * SUB, SUB), SUB)
        cells = [cost_ref[here, k * LANES : (k + 1) * LANES] for k in range(chunks)]
        tiles = [-cell for cell in cells] if bases is None else [base - cell for base, cell in zip(bases, cells)]
        high_ref[here, :], total_ref[here, :] = peak_and_sum(tiles)
        return carry

    lax.fori_loop(0, rows // SUB, group_step, 0, unroll=4)
    out = []
    for a in range(rows // LANES):
        block = slice(a * LANES, (a + 1) * LANES)
        out.append(merge(high_ref[block, :].T, total_ref[block, :].T))
    return jnp.concatenate(out, axis=0)


def split3(values):
    high = values.astype(jnp.bfloat16)
    rest = values - high.astype(jnp.float32)
    mid = rest.astype(jnp.bfloat16)
    low = (rest - mid.astype(jnp.float32)).astype(jnp.bfloat16)
    return high, mid, low


def dot(left, right, dims):
    return lax.dot_general(left, right, (dims, ((), ())), preferred_element_type=jnp.float32)


def prepare_kernel(train_ref, label_ref, levels_ref, level_cost_ref, left_ref, sq_ref, hot_ref, *, num_levels):
    shards, shard_rows, width = train_ref.shape
    embed = width - LANES
    packed = train_ref[...].reshape(shards * shard_rows, width)
    train = packed[:, :embed]
    wide = train.astype(jnp.float32)
    train_sq = jnp.sum(wide * wide, axis=1, keepdims=True) * (1.0 / embed)
    sq_ref[...] = jnp.broadcast_to(train_sq, sq_ref.shape)
    left_ref[:, :embed] = train * jnp.bfloat16(-2.0 / embed)
    levels = levels_ref[...]
    table = jnp.zeros(levels.shape, jnp.float32)
    for level in range(num_levels):
        table = table + jnp.where(levels == level, level_cost_ref[level], 0.0)
    labels = packed[:, embed:].astype(jnp.float32)
    lane_ids = lax.broadcasted_iota(jnp.int32, labels.shape, 1).astype(jnp.float32)
    train_hot = jnp.where(labels == lane_ids, 1.0, 0.0).astype(jnp.bfloat16)
    parts = [dot(train_hot, part, ((1,), (0,))).astype(jnp.bfloat16) for part in split3(table)]
    left_ref[:, embed:] = jnp.concatenate(parts, axis=1)
    class_ids = lax.broadcasted_iota(jnp.int32, (LANES, LANES), 0).astype(jnp.float32)
    for k in range(label_ref.shape[0]):
        hot_ref[:, k * LANES : (k + 1) * LANES] = jnp.where(class_ids == label_ref[k], 1.0, 0.0).astype(jnp.bfloat16)


def start_kernel(left_ref, sq_ref, hot_ref, valid_ref, cost_ref, row_out, col_out, row_a, row_b, col_a, col_b):
    embed = valid_ref.shape[1]
    table_parts = (left_ref.shape[1] - embed) // LANES
    train_sq = jnp.concatenate([sq_ref[...]] * 2, axis=1)
    ones = jnp.ones((SUB, embed), jnp.bfloat16)
    step = 2 * LANES
    for pair in range(valid_ref.shape[0] // step):
        here = slice(pair * step, (pair + 1) * step)
        block = valid_ref[here, :]
        wide = block.astype(jnp.float32)
        squares = wide * wide
        sq_high = squares.astype(jnp.bfloat16)
        sq_low = (squares - sq_high.astype(jnp.float32)).astype(jnp.bfloat16)
        block_sq = (dot(ones, sq_high, ((1,), (1,))) + dot(ones, sq_low, ((1,), (1,))))[:1, :]
        cost = dot(left_ref[:, :embed], block, ((1,), (1,)))
        cost = cost + dot(left_ref[:, embed:], jnp.concatenate([hot_ref[:, here]] * table_parts, axis=0), ((1,), (0,)))
        cost_ref[:, here] = (cost + (train_sq + block_sq * (1.0 / embed))) * (1.0 / UNIT)
    row_out[...] = jnp.broadcast_to(row_partial(cost_ref, None, row_a, row_b)[None], row_out.shape)
    col_out[...] = jnp.broadcast_to(col_partial(cost_ref, None, col_a, col_b)[None], col_out.shape)


def updated(pot_ref, parts_ref, offset):
    return 0.5 * (pot_ref[...] + (offset - lse_lead(parts_ref[...])))


def both_kernel(
    cost_ref, row_parts, col_parts, row_pot, col_pot, row_out, col_out, row_new, col_new, row_a, row_b, col_a, col_b,
    spread_ref, *, row_offset, col_offset
):
    row, col = updated(row_pot, row_parts, row_offset), updated(col_pot, col_parts, col_offset)
    row_new[...] = row
    col_new[...] = col
    spread_rows(row, spread_ref)
    row_out[...] = jnp.broadcast_to(row_partial(cost_ref, col, row_a, row_b)[None], row_out.shape)
    col_out[...] = jnp.broadcast_to(col_partial(cost_ref, spread_ref, col_a, col_b)[None], col_out.shape)


def last_row_kernel(
    cost_ref, row_parts, col_parts, row_pot, col_pot, row_out, row_new, row_a, row_b, *, row_offset, col_offset
):
    row_new[...] = updated(row_pot, row_parts, row_offset)
    col = updated(col_pot, col_parts, col_offset)
    row_out[...] = jnp.broadcast_to(row_partial(cost_ref, col, row_a, row_b)[None], row_out.shape)


def last_kernel(parts_ref, pot_ref, out_ref, copies_ref, *, offset):
    pot = updated(pot_ref, parts_ref, offset)
    out_ref[...] = pot
    copies_ref[...] = jnp.broadcast_to(pot[None], copies_ref.shape)


def calibrate_kernel(parts_ref, pot_ref, out_ref, *, count):
    total = jnp.sum(jnp.sum(parts_ref[...], axis=0), keepdims=True)
    out_ref[...] = (pot_ref[...] * count - total) * (UNIT / (count - 1))


def exchange(block, axis):
    copies = block if block.ndim == 3 else jnp.broadcast_to(block[None], (lax.axis_size(axis),) + block.shape)
    return lax.all_to_all(copies, axis, 0, 0, tiled=True)


def call(kernel, out_shape, scratch, *args, smem=(), limit=8, **static):
    body = kernel if not static else (lambda *refs: kernel(*refs, **static))
    specs = [pl.BlockSpec(memory_space=pltpu.SMEM) if i in smem else VMEM for i in range(len(args))]
    return pl.pallas_call(
        body,
        out_shape=out_shape,
        in_specs=specs,
        out_specs=[VMEM] * len(out_shape),
        scratch_shapes=scratch,
        compiler_params=pltpu.CompilerParams(vmem_limit_bytes=limit * 2**20),
        cost_estimate=pl.CostEstimate(flops=2**24, bytes_accessed=4 * 2**20, transcendentals=2**20),
    )(*args)


def shards(train_embed, valid_embed, train_labels, valid_labels, pair_level, level_cost):
    row_size, col_size = lax.axis_size("row"), lax.axis_size("col")
    f32 = jnp.float32
    valid_all = lax.all_gather(valid_embed, "row", axis=0, tiled=True)
    shown = jnp.broadcast_to(train_labels.astype(jnp.bfloat16)[:, None], (train_embed.shape[0], LANES))
    train_all = exchange(jnp.concatenate([train_embed, shown], axis=1), "col")
    own_labels = valid_labels.astype(f32)[None, :]
    own_labels, train_all = lax.optimization_barrier((own_labels, train_all))
    label_all = exchange(own_labels, "row")
    rows, cols = train_embed.shape[0] * col_size, valid_all.shape[0]
    row_chunks, col_chunks = rows // LANES, cols // LANES
    classes = pair_level.shape[0]
    levels = jnp.pad(pair_level, ((0, LANES - classes), (0, LANES - classes)), constant_values=-1)
    tile = jax.ShapeDtypeStruct((rows, cols), f32)
    row_copies = jax.ShapeDtypeStruct((col_size, row_chunks, LANES), f32)
    col_copies = jax.ShapeDtypeStruct((row_size, col_chunks, LANES), f32)
    row_shape = jax.ShapeDtypeStruct((row_chunks, LANES), f32)
    col_shape = jax.ShapeDtypeStruct((col_chunks, LANES), f32)
    tall = [pltpu.VMEM((rows, LANES), f32)] * 2
    wide = [pltpu.VMEM((row_chunks * SUB, cols), f32)] * 2
    embed = train_embed.shape[1]
    prepared = call(
        prepare_kernel,
        (
            jax.ShapeDtypeStruct((rows, embed + 3 * LANES), jnp.bfloat16),
            jax.ShapeDtypeStruct((rows, LANES), f32),
            jax.ShapeDtypeStruct((LANES, cols), jnp.bfloat16),
        ),
        [],
        train_all,
        label_all,
        levels,
        level_cost,
        smem=(3,),
        num_levels=level_cost.shape[0],
        limit=16,
    )
    cost, row_part, col_part = call(
        start_kernel, (tile, row_copies, col_copies), tall + wide, *prepared, valid_all, limit=16
    )
    full_rows, full_cols = rows * row_size, cols * col_size
    offsets = {"row_offset": math.log2(full_cols), "col_offset": math.log2(full_rows)}
    row_pot = jnp.zeros(row_shape.shape, f32)
    col_pot = jnp.zeros(col_shape.shape, f32)
    for iteration in range(ITERS - 1):
        row_got = exchange(row_part, "col")
        col_got = exchange(col_part, "row")
        given = (cost, row_got, col_got, row_pot, col_pot)
        if iteration < ITERS - 2:
            row_part, col_part, row_pot, col_pot = call(
                both_kernel, (row_copies, col_copies, row_shape, col_shape), tall + wide + tall[:1], *given, **offsets
            )
        else:
            row_part, row_pot = call(last_row_kernel, (row_copies, row_shape), tall, *given, **offsets)
    row_got = exchange(row_part, "col")
    final_shape = jax.ShapeDtypeStruct((row_size, row_chunks, LANES), f32)
    final, copies = call(
        last_kernel, (row_shape, final_shape), [], row_got, row_pot, offset=offsets["row_offset"]
    )
    (out,) = call(calibrate_kernel, (row_shape,), [], exchange(copies, "row"), final, count=full_rows)
    return out.reshape(rows)


def solution(mesh):
    placed = (
        P(("row", "col"), None),
        P(("row", "col"), None),
        P(("row", "col")),
        P(("row", "col")),
        P(),
        P(),
    )
    return jax.shard_map(shards, mesh=mesh, in_specs=placed, out_specs=P("row"), check_vma=False)
```

time: 190 us -> 183 us (0.963)
  blocking collectives: 12.6 us -> 105 us
  waiting for transfers between devices: 79.5 us -> 21.6 us
  starting transfers between devices: 56.7 us -> 23.3 us
  between operations: 0.18 us -> 13.4 us
  local copies, waits for them, and re-layouts: 15.5 us -> 4.17 us
  Pallas kernels: 22.8 us -> 12.3 us
    all_to_all x1 -> x8, blocking collectives: 12.6 us -> 105 us  [exchange(): return lax.all_to_all(copies, axis, 0, 0, tiled=True)]
    all_to_all x9 -> x2, waiting for transfers between devices: 79.5 us -> 19.4 us  [exchange(): return lax.all_to_all(copies, axis, 0, 0, tiled=True)]
    all_to_all x9 -> x2, starting transfers between devices: 56.7 us -> 23.3 us  [exchange(): return lax.all_to_all(copies, axis, 0, 0, tiled=True)]
    unnamed x20 -> x4, local copies, waits for them, and re-layouts: 12.9 us -> 1.88 us
    pallas_call x9 -> x7, Pallas kernels: 22.8 us -> 12.3 us  [call(): pl.pallas_call(body, out_shape=out_shape, in_specs=specs, out_specs=[VMEM...]
  transfers between devices with their start and end apart: 9 -> 3, of which waited for: 9 -> 3; matrix products, arithmetic and copies ran while one was open for 0% -> 2% of each run, Pallas kernels for 7% -> 1%
where the time goes in v4:
time: 183 us; the launch traced here: 182 us
  blocking collectives  105 us (57%)
  starting transfers between devices  23.3 us (13%)
  waiting for transfers between devices  21.6 us (12%)
  between operations  13.4 us (7%)
  Pallas kernels  12.3 us (7%)
  local copies, waits for them, and re-layouts  4.17 us (2%)
  other arithmetic  2.02 us (1%)
    all_to_all x8, blocking collectives, exchange(): return lax.all_to_all(copies, axis, 0, 0, tiled=True)  105 us
    all_to_all x2, starting transfers between devices, exchange(): return lax.all_to_all(copies, axis, 0, 0, tiled=True)  23.3 us
    all_to_all x2, waiting for transfers between devices, exchange(): return lax.all_to_all(copies, axis, 0, 0, tiled=True)  19.4 us
    pallas_call x7, Pallas kernels, call(): pl.pallas_call(body, out_shape=out_shape, in_specs=specs, out_specs=[VMEM...  12.3 us
  transfers between devices with their start and end apart: 3, of which 3 were waited for; matrix products, arithmetic and copies ran while one was open for 2% of the time, Pallas kernels for 1%

profile of v4, /device:TPU:1, one launch (start us, length us, event | category | flops | bytes accessed | tf_op | source)
XLA Modules:
  0.0 182.3 jit_solution(3458111211624874406)
XLA Ops:
  6.5 0.7 all-gather.2.cloned.1.call-update
  8.0 0.7 pad_maximum_fusion
  8.7 0.8 broadcast_in_dim.31
  9.5 10.5 %all-to-all-start = ((bf16[32,16,384]{2,1,0:T(8,128)(2,1)}), bf16[32,16,384]{2,1,0:T(8,128)(2,1)S(1)}, u32[]{:S(2)}, u32[]{:S(2)}) async-start(bf16[32,16,384]{2,1,0:T(8,128)(2,1)} %broadcast_in_dim.31), calls=%async_computation | async-start | bytes 786432 | tf_op jit(solution)/shard_map/all_to_all | solution.py:181
  20.7 13.1 %all-to-all-done.refs_0_ = bf16[32,16,384]{2,1,0:T(8,128)(2,1)S(1)} async-done(((bf16[32,16,384]{2,1,0:T(8,128)(2,1)}), bf16[32,16,384]{2,1,0:T(8,128)(2,1)S(1)}, u32[]{:S(2)}, u32[]{:S(2)}) %all-to-all-start) | async-done | bytes 393248 | tf_op jit(solution)/shard_map/all_to_all | solution.py:181
  34.4 12.8 %all-to-all-start.1 = ((f32[16,1,128]{2,1,0:T(1,128)}), f32[16,1,128]{2,1,0:T(1,128)S(1)}, u32[]{:S(2)}, u32[]{:S(2)}) async-start(f32[16,1,128]{2,1,0:T(1,128)} %broadcast_in_dim.33), calls=%async_computation.1 | async-start | bytes 16384 | tf_op jit(solution)/shard_map/all_to_all | solution.py:181
  47.2 0.8 pad.4.refs_2_
  48.0 6.2 %all-to-all-done.1.refs_1_ = f32[16,1,128]{2,1,0:T(1,128)S(1)} async-done(((f32[16,1,128]{2,1,0:T(1,128)}), f32[16,1,128]{2,1,0:T(1,128)S(1)}, u32[]{:S(2)}, u32[]{:S(2)}) %all-to-all-start.1) | async-done | bytes 8224 | tf_op jit(solution)/shard_map/all_to_all | solution.py:181
  54.9 1.0 shard_map.64
  55.9 1.5 all-gather.2.cloned.1.call-done.valid_ref
  57.4 1.2 copy-done
  58.6 4.5 %shard_map.65 = (f32[512,2048]{1,0:T(8,128)S(1)}, f32[32,4,128]{2,1,0:T(4,128)S(1)}, f32[16,16,128]{2,1,0:T(8,128)S(1)}) custom-call(bf16[512,640]{1,0:T(8,128)(2,1)S(1)} %get-tuple-element.27.left_ref, f32[512,128]{1,0:T(8,128)S(1)} %get-tuple-element.28.sq_ref, bf16[128,2048]{1,0:T(8,128)(2,1)S(1)} %get-tuple-element.29.hot_ref, bf16[2048,256]{1,0:T(8,128)(2,1)S(1)} %copy-done), custom_call_target="tpu_custom_call" | custom-call | flops 16777216 | bytes 4194304 | tf_op jit(solution)/shard_map/pallas_call | solution.py:187
  63.2 18.0 %all_to_all.50.refs_1_ = f32[32,4,128]{2,1,0:T(4,128)S(1)} all-to-all(f32[32,4,128]{2,1,0:T(4,128)S(1)} %get-tuple-element.31), channel_id=1, replica_groups=mesh['row'=16,'col'=32] {'col'}, dimensions={0} | all-to-all | bytes 131072 | tf_op jit(solution)/shard_map/all_to_all | solution.py:181
  81.2 14.7 %all_to_all.51.refs_2_ = f32[16,16,128]{2,1,0:T(8,128)S(1)} all-to-all(f32[16,16,128]{2,1,0:T(8,128)S(1)} %get-tuple-element.32), channel_id=1, replica_groups=mesh['row'=16,'col'=32] {'row'}, dimensions={0} | all-to-all | bytes 262144 | tf_op jit(solution)/shard_map/all_to_all | solution.py:181
  95.9 2.3 %shard_map.66 = (f32[32,4,128]{2,1,0:T(4,128)S(1)}, f32[16,16,128]{2,1,0:T(8,128)S(1)}, f32[4,128]{1,0:T(4,128)S(1)}, f32[16,128]{1,0:T(8,128)S(1)}) custom-call(f32[512,2048]{1,0:T(8,128)S(1)} %get-tuple-element.30.refs_0_, f32[32,4,128]{2,1,0:T(4,128)S(1)} %all_to_all.50.refs_1_, f32[16,16,128]{2,1,0:T(8,128)S(1)} %all_to_all.51.refs_2_, ...), custom_call_target="tpu_custom_call" | custom-call | flops 16777216 | bytes 4194304 | tf_op jit(solution)/shard_map/pallas_call | solution.py:187
  98.2 12.3 %all_to_all.52.refs_1_ = f32[32,4,128]{2,1,0:T(4,128)S(1)} all-to-all(f32[32,4,128]{2,1,0:T(4,128)S(1)} %get-tuple-element.33), channel_id=1, replica_groups=mesh['row'=16,'col'=32] {'col'}, dimensions={0} | all-to-all | bytes 131072 | tf_op jit(solution)/shard_map/all_to_all | solution.py:181
  110.5 12.5 %all_to_all.53.refs_2_ = f32[16,16,128]{2,1,0:T(8,128)S(1)} all-to-all(f32[16,16,128]{2,1,0:T(8,128)S(1)} %get-tuple-element.34), channel_id=1, replica_groups=mesh['row'=16,'col'=32] {'row'}, dimensions={0} | all-to-all | bytes 262144 | tf_op jit(solution)/shard_map/all_to_all | solution.py:181
  123.0 2.3 %shard_map.67 = (f32[32,4,128]{2,1,0:T(4,128)S(1)}, f32[16,16,128]{2,1,0:T(8,128)S(1)}, f32[4,128]{1,0:T(4,128)S(1)}, f32[16,128]{1,0:T(8,128)S(1)}) custom-call(f32[512,2048]{1,0:T(8,128)S(1)} %get-tuple-element.30.refs_0_, f32[32,4,128]{2,1,0:T(4,128)S(1)} %all_to_all.52.refs_1_, f32[16,16,128]{2,1,0:T(8,128)S(1)} %all_to_all.53.refs_2_, ...), custom_call_target="tpu_custom_call" | custom-call | flops 16777216 | bytes 4194304 | tf_op jit(solution)/shard_map/pallas_call | solution.py:187
  125.4 12.3 %all_to_all.54.refs_1_ = f32[32,4,128]{2,1,0:T(4,128)S(1)} all-to-all(f32[32,4,128]{2,1,0:T(4,128)S(1)} %get-tuple-element.37), channel_id=1, replica_groups=mesh['row'=16,'col'=32] {'col'}, dimensions={0} | all-to-all | bytes 131072 | tf_op jit(solution)/shard_map/all_to_all | solution.py:181
  137.7 12.5 %all_to_all.55.refs_2_ = f32[16,16,128]{2,1,0:T(8,128)S(1)} all-to-all(f32[16,16,128]{2,1,0:T(8,128)S(1)} %get-tuple-element.38), channel_id=1, replica_groups=mesh['row'=16,'col'=32] {'row'}, dimensions={0} | all-to-all | bytes 262144 | tf_op jit(solution)/shard_map/all_to_all | solution.py:181
  150.2 1.4 shard_map.68
  151.6 12.3 %all_to_all.56.refs_0_ = f32[32,4,128]{2,1,0:T(4,128)S(1)} all-to-all(f32[32,4,128]{2,1,0:T(4,128)S(1)} %get-tuple-element.41), channel_id=1, replica_groups=mesh['row'=16,'col'=32] {'col'}, dimensions={0} | all-to-all | bytes 131072 | tf_op jit(solution)/shard_map/all_to_all | solution.py:181
  163.9 10.8 %all_to_all.57.refs_0_ = f32[16,4,128]{2,1,0:T(4,128)S(1)} all-to-all(f32[16,4,128]{2,1,0:T(4,128)S(1)} %get-tuple-element.43), channel_id=1, replica_groups=mesh['row'=16,'col'=32] {'row'}, dimensions={0} | all-to-all | bytes 65536 | tf_op jit(solution)/shard_map/all_to_all | solution.py:181
  174.7 0.7 shard_map.70
  (11 shorter events, 2.7 us)
Async XLA Ops:
  6.5 50.9 %all-gather.2.cloned.1.call-start = ((), (), s32[]{:S(2)}) async-start(), calls=%async_computation.10 | async-start | bytes 1114112 | tf_op jit(solution)/shard_map/all_gather | solution.py:201
  9.5 24.3 %all-to-all-start = ((bf16[32,16,384]{2,1,0:T(8,128)(2,1)}), bf16[32,16,384]{2,1,0:T(8,128)(2,1)S(1)}, u32[]{:S(2)}, u32[]{:S(2)}) async-start(bf16[32,16,384]{2,1,0:T(8,128)(2,1)} %broadcast_in_dim.31), calls=%async_computation | async-start | bytes 786432 | tf_op jit(solution)/shard_map/all_to_all | solution.py:181
  34.4 19.8 %all-to-all-start.1 = ((f32[16,1,128]{2,1,0:T(1,128)}), f32[16,1,128]{2,1,0:T(1,128)S(1)}, u32[]{:S(2)}, u32[]{:S(2)}) async-start(f32[16,1,128]{2,1,0:T(1,128)} %broadcast_in_dim.33), calls=%async_computation.1 | async-start | bytes 16384 | tf_op jit(solution)/shard_map/all_to_all | solution.py:181
  54.2 0.7 copy-start.1
  57.4 1.2 copy-start
Sparse Core Ops, SparseCore 0:
  9.5 47.8 all-gather.1

commit v5 on v4

--- a/solution.py
+++ b/solution.py
@@ -13,6 +13,8 @@
 
 entropy_scale = 0.05
 UNIT = entropy_scale * math.log(2.0)
+
+ROW = ("zh", "zl", "core")
 
 VMEM = pl.BlockSpec(memory_space=pltpu.VMEM)
 
@@ -97,7 +99,7 @@
     return lax.dot_general(left, right, (dims, ((), ())), preferred_element_type=jnp.float32)
 
 
-def prepare_kernel(train_ref, label_ref, levels_ref, level_cost_ref, left_ref, sq_ref, hot_ref, *, num_levels):
+def prepare_kernel(train_ref, levels_ref, level_cost_ref, left_ref, sq_ref, *, num_levels):
     shards, shard_rows, width = train_ref.shape
     embed = width - LANES
     packed = train_ref[...].reshape(shards * shard_rows, width)
@@ -115,27 +117,34 @@
     train_hot = jnp.where(labels == lane_ids, 1.0, 0.0).astype(jnp.bfloat16)
     parts = [dot(train_hot, part, ((1,), (0,))).astype(jnp.bfloat16) for part in split3(table)]
     left_ref[:, embed:] = jnp.concatenate(parts, axis=1)
+
+
+def start_kernel(
+    where_ref, left_ref, sq_ref, mine_ref, other_ref, cost_ref, row_out, col_out, row_a, row_b, col_a, col_b
+):
+    steps, sides, block_rows, embed = mine_ref.shape
+    table_parts = (left_ref.shape[1] - embed) // LANES
+    train_sq = jnp.concatenate([sq_ref[...]] * sides, axis=1)
+    ones = jnp.ones((SUB, embed), jnp.bfloat16)
     class_ids = lax.broadcasted_iota(jnp.int32, (LANES, LANES), 0).astype(jnp.float32)
-    for k in range(label_ref.shape[0]):
-        hot_ref[:, k * LANES : (k + 1) * LANES] = jnp.where(class_ids == label_ref[k], 1.0, 0.0).astype(jnp.bfloat16)
-
-
-def start_kernel(left_ref, sq_ref, hot_ref, valid_ref, cost_ref, row_out, col_out, row_a, row_b, col_a, col_b):
-    embed = valid_ref.shape[1]
-    table_parts = (left_ref.shape[1] - embed) // LANES
-    train_sq = jnp.concatenate([sq_ref[...]] * 2, axis=1)
-    ones = jnp.ones((SUB, embed), jnp.bfloat16)
-    step = 2 * LANES
-    for pair in range(valid_ref.shape[0] // step):
-        here = slice(pair * step, (pair + 1) * step)
-        block = valid_ref[here, :]
+    step = sides * LANES
+    for pair in range(2 * steps):
+        core, z_pair = divmod(pair, steps)
+        back = lax.rem(where_ref[0] - z_pair + steps, steps)
+        own = where_ref[1] == core
+        blocks = [jnp.where(own, mine_ref[back, side], other_ref[back, side]) for side in range(sides)]
+        block = jnp.concatenate([b[:LANES, :] for b in blocks], axis=0)
+        label_rows = [b[LANES:, :LANES].astype(jnp.float32)[:1, :] for b in blocks]
+        hots = [jnp.where(class_ids == label_row, 1.0, 0.0).astype(jnp.bfloat16) for label_row in label_rows]
+        hot = jnp.concatenate(hots, axis=1)
         wide = block.astype(jnp.float32)
         squares = wide * wide
         sq_high = squares.astype(jnp.bfloat16)
         sq_low = (squares - sq_high.astype(jnp.float32)).astype(jnp.bfloat16)
         block_sq = (dot(ones, sq_high, ((1,), (1,))) + dot(ones, sq_low, ((1,), (1,))))[:1, :]
         cost = dot(left_ref[:, :embed], block, ((1,), (1,)))
-        cost = cost + dot(left_ref[:, embed:], jnp.concatenate([hot_ref[:, here]] * table_parts, axis=0), ((1,), (0,)))
+        cost = cost + dot(left_ref[:, embed:], jnp.concatenate([hot] * table_parts, axis=0), ((1,), (0,)))
+        here = slice(pair * step, (pair + 1) * step)
         cost_ref[:, here] = (cost + (train_sq + block_sq * (1.0 / embed))) * (1.0 / UNIT)
     row_out[...] = jnp.broadcast_to(row_partial(cost_ref, None, row_a, row_b)[None], row_out.shape)
     col_out[...] = jnp.broadcast_to(col_partial(cost_ref, None, col_a, col_b)[None], col_out.shape)
@@ -196,15 +205,20 @@
 
 
 def shards(train_embed, valid_embed, train_labels, valid_labels, pair_level, level_cost):
-    row_size, col_size = lax.axis_size("row"), lax.axis_size("col")
+    row_size, col_size = lax.axis_size(ROW), lax.axis_size("col")
     f32 = jnp.float32
-    valid_all = lax.all_gather(valid_embed, "row", axis=0, tiled=True)
+    embed = train_embed.shape[1]
     shown = jnp.broadcast_to(train_labels.astype(jnp.bfloat16)[:, None], (train_embed.shape[0], LANES))
     train_all = exchange(jnp.concatenate([train_embed, shown], axis=1), "col")
-    own_labels = valid_labels.astype(f32)[None, :]
-    own_labels, train_all = lax.optimization_barrier((own_labels, train_all))
-    label_all = exchange(own_labels, "row")
-    rows, cols = train_embed.shape[0] * col_size, valid_all.shape[0]
+    label_row = jnp.tile(valid_labels.astype(jnp.bfloat16), embed // LANES)[None, :]
+    valid_pack = jnp.concatenate([valid_embed, jnp.broadcast_to(label_row, (16, embed))], axis=0)
+    pair = lax.all_gather(valid_pack, "zl", axis=0)
+    steps = lax.axis_size("zh")
+    turn = [[(i, (i + k) % steps) for i in range(steps)] for k in range(steps)]
+    mine = jnp.stack([pair] + [lax.ppermute(pair, "zh", turn[k]) for k in range(1, steps)])
+    other = lax.ppermute(mine, "core", [(0, 1), (1, 0)])
+    where = jnp.stack([lax.axis_index("zh"), lax.axis_index("core")]).astype(jnp.int32)
+    rows, cols = train_embed.shape[0] * col_size, valid_embed.shape[0] * row_size
     row_chunks, col_chunks = rows // LANES, cols // LANES
     classes = pair_level.shape[0]
     levels = jnp.pad(pair_level, ((0, LANES - classes), (0, LANES - classes)), constant_values=-1)
@@ -215,25 +229,27 @@
     col_shape = jax.ShapeDtypeStruct((col_chunks, LANES), f32)
     tall = [pltpu.VMEM((rows, LANES), f32)] * 2
     wide = [pltpu.VMEM((row_chunks * SUB, cols), f32)] * 2
-    embed = train_embed.shape[1]
     prepared = call(
         prepare_kernel,
-        (
-            jax.ShapeDtypeStruct((rows, embed + 3 * LANES), jnp.bfloat16),
-            jax.ShapeDtypeStruct((rows, LANES), f32),
-            jax.ShapeDtypeStruct((LANES, cols), jnp.bfloat16),
-        ),
+        (jax.ShapeDtypeStruct((rows, embed + 3 * LANES), jnp.bfloat16), jax.ShapeDtypeStruct((rows, LANES), f32)),
         [],
         train_all,
-        label_all,
         levels,
         level_cost,
-        smem=(3,),
+        smem=(2,),
         num_levels=level_cost.shape[0],
         limit=16,
     )
     cost, row_part, col_part = call(
-        start_kernel, (tile, row_copies, col_copies), tall + wide, *prepared, valid_all, limit=16
+        start_kernel,
+        (tile, row_copies, col_copies),
+        tall + wide,
+        where,
+        *prepared,
+        mine,
+        other,
+        smem=(0,),
+        limit=16,
     )
     full_rows, full_cols = rows * row_size, cols * col_size
     offsets = {"row_offset": math.log2(full_cols), "col_offset": math.log2(full_rows)}
@@ -241,7 +257,7 @@
     col_pot = jnp.zeros(col_shape.shape, f32)
     for iteration in range(ITERS - 1):
         row_got = exchange(row_part, "col")
-        col_got = exchange(col_part, "row")
+        col_got = exchange(col_part, ROW)
         given = (cost, row_got, col_got, row_pot, col_pot)
         if iteration < ITERS - 2:
             row_part, col_part, row_pot, col_pot = call(
@@ -254,17 +270,13 @@
     final, copies = call(
         last_kernel, (row_shape, final_shape), [], row_got, row_pot, offset=offsets["row_offset"]
     )
-    (out,) = call(calibrate_kernel, (row_shape,), [], exchange(copies, "row"), final, count=full_rows)
+    (out,) = call(calibrate_kernel, (row_shape,), [], exchange(copies, ROW), final, count=full_rows)
     return out.reshape(rows)
 
 
 def solution(mesh):
-    placed = (
-        P(("row", "col"), None),
-        P(("row", "col"), None),
-        P(("row", "col")),
-        P(("row", "col")),
-        P(),
-        P(),
-    )
-    return jax.shard_map(shards, mesh=mesh, in_specs=placed, out_specs=P("row"), check_vma=False)
+    row_size, col_size = mesh.shape["row"], mesh.shape["col"]
+    finer = jax.sharding.Mesh(mesh.devices.reshape(row_size // 4, 2, 2, col_size), ROW + ("col",))
+    both = ROW + ("col",)
+    placed = (P(both, None), P(both, None), P(both), P(both), P(), P())
+    return jax.shard_map(shards, mesh=finer, in_specs=placed, out_specs=P(ROW), check_vma=False)

time: 183 us -> 166 us (0.907)
  waiting for transfers between devices: 21.6 us -> 5.59 us
  between operations: 13.4 us -> 0.13 us
  starting transfers between devices: 23.3 us -> 31.9 us
  blocking collectives: 105 us -> 109 us
  local copies, waits for them, and re-layouts: 4.17 us -> 2.34 us
    ppermute x0 -> x4, starting transfers between devices: none -> 22.3 us  [the longest x3 17.4 us: shards(): lax.ppermute(pair, 'zh', turn[k])]
    all_to_all x2 -> x1, waiting for transfers between devices: 19.4 us -> 5.58 us  [exchange(): return lax.all_to_all(copies, axis, 0, 0, tiled=True)]
    all_to_all x2 -> x1, starting transfers between devices: 23.3 us -> 9.67 us  [exchange(): return lax.all_to_all(copies, axis, 0, 0, tiled=True)]
    all_gather x0 -> x1, blocking collectives: none -> 5.3 us  [shards(): pair = lax.all_gather(valid_pack, 'zl', axis=0)]
  transfers between devices with their start and end apart: 3 -> 5, of which waited for: 3 -> 1; matrix products, arithmetic and copies ran while one was open for 2% -> 2% of each run, Pallas kernels for 1% -> 0%
where the time goes in v5:
time: 166 us; the launch traced here: 165 us
  blocking collectives  109 us (66%)
  starting transfers between devices  31.9 us (19%)
  Pallas kernels  12.9 us (8%)
  waiting for transfers between devices  5.59 us (3%)
  other arithmetic  3.02 us (2%)
  local copies, waits for them, and re-layouts  2.34 us (1%)
    all_to_all x8, blocking collectives, exchange(): return lax.all_to_all(copies, axis, 0, 0, tiled=True)  104 us
    ppermute x3, starting transfers between devices, shards(): lax.ppermute(pair, 'zh', turn[k])  17.4 us
    pallas_call x7, Pallas kernels, call(): pl.pallas_call(body, out_shape=out_shape, in_specs=specs, out_specs=[VMEM...  12.9 us
    all_to_all x1, starting transfers between devices, exchange(): return lax.all_to_all(copies, axis, 0, 0, tiled=True)  9.67 us
    all_to_all x1, waiting for transfers between devices, exchange(): return lax.all_to_all(copies, axis, 0, 0, tiled=True)  5.58 us
    all_gather x1, blocking collectives, shards(): pair = lax.all_gather(valid_pack, 'zl', axis=0)  5.3 us
    ppermute x1, starting transfers between devices, shards(): other = lax.ppermute(mine, 'core', [(0, 1), (1, 0)])  4.85 us
  transfers between devices with their start and end apart: 5, of which 1 were waited for; matrix products, arithmetic and copies ran while one was open for 2% of the time, Pallas kernels for 0%

profile of v5, /device:TPU:1, one launch (start us, length us, event | category | flops | bytes accessed | tf_op | source)
XLA Modules:
  0.0 165.2 jit_solution(16915500616835361756)
XLA Ops:
  0.7 0.8 pad_maximum_fusion.1
  1.5 5.3 %all-gather = bf16[288,256]{1,0:T(8,128)(2,1)S(1)} all-gather(bf16[144,256]{1,0:T(8,128)(2,1)S(1)} %pad_maximum_fusion.1), channel_id=2, replica_groups=mesh['zh'=4,'zl'=2,'core'=2,'col'=32] {'zl'}, dimensions={0}, use_global_device_ids=true | all-gather | bytes 221184 | tf_op jit(solution)/shard_map/all_gather | solution.py:215
  6.8 5.8 %collective-permute-start = (bf16[2,144,256]{2,1,0:T(8,128)(2,1)S(1)}, bf16[2,144,256]{2,1,0:T(8,128)(2,1)S(1)}, u32[]{:S(2)}, u32[]{:S(2)}) collective-permute-start(bf16[2,144,256]{2,1,0:T(8,128)(2,1)S(1)} %bitcast.10), channel_id=1, source_target_pairs={{0,128},{128,256},{256,384},{384,0},{1,129},{129,257},{257,385},{3... | collective-permute-start | bytes 442376 | tf_op jit(solution)/shard_map/ppermute | solution.py:218
  12.6 8.2 %collective-permute-start.1 = (bf16[2,144,256]{2,1,0:T(8,128)(2,1)S(1)}, bf16[2,144,256]{2,1,0:T(8,128)(2,1)S(1)}, u32[]{:S(2)}, u32[]{:S(2)}) collective-permute-start(bf16[2,144,256]{2,1,0:T(8,128)(2,1)S(1)} %bitcast.11), channel_id=1, source_target_pairs={{0,256},{128,384},{256,0},{384,128},{1,257},{129,385},{257,1},{385... | collective-permute-start | bytes 442376 | tf_op jit(solution)/shard_map/ppermute | solution.py:218
  20.9 3.4 %collective-permute-start.2 = (bf16[2,144,256]{2,1,0:T(8,128)(2,1)S(1)}, bf16[2,144,256]{2,1,0:T(8,128)(2,1)S(1)}, u32[]{:S(2)}, u32[]{:S(2)}) collective-permute-start(bf16[2,144,256]{2,1,0:T(8,128)(2,1)S(1)} %bitcast.12), channel_id=1, source_target_pairs={{0,384},{128,0},{256,128},{384,256},{1,385},{129,1},{257,129},{385... | collective-permute-start | bytes 442376 | tf_op jit(solution)/shard_map/ppermute | solution.py:218
  25.7 0.8 broadcast_in_dim.26
  26.5 9.7 %all-to-all-start = ((bf16[32,16,384]{2,1,0:T(8,128)(2,1)}), bf16[32,16,384]{2,1,0:T(8,128)(2,1)S(1)}, u32[]{:S(2)}, u32[]{:S(2)}) async-start(bf16[32,16,384]{2,1,0:T(8,128)(2,1)} %broadcast_in_dim.26), calls=%async_computation | async-start | bytes 786432 | tf_op jit(solution)/shard_map/all_to_all | solution.py:190
  36.3 4.9 %collective-permute-start.3 = (bf16[4,2,144,256]{3,2,1,0:T(8,128)(2,1)S(1)}, bf16[4,2,144,256]{3,2,1,0:T(8,128)(2,1)S(1)}, u32[]{:S(2)}, u32[]{:S(2)}) collective-permute-start(bf16[4,2,144,256]{3,2,1,0:T(8,128)(2,1)S(1)} %pad_maximum_fusion.mine_ref), channel_id=1, source_target_pairs={{0,32},{32,0},{1,33},{33,1},{2,34},{34,2},{3,35},{35,3},{4,36},{36... | collective-permute-start | bytes 1769480 | tf_op jit(solution)/shard_map/ppermute | solution.py:219
  41.1 0.8 pad.4.refs_1_
  42.0 5.6 %all-to-all-done.refs_0_ = bf16[32,16,384]{2,1,0:T(8,128)(2,1)S(1)} async-done(((bf16[32,16,384]{2,1,0:T(8,128)(2,1)}), bf16[32,16,384]{2,1,0:T(8,128)(2,1)S(1)}, u32[]{:S(2)}, u32[]{:S(2)}) %all-to-all-start) | async-done | bytes 393248 | tf_op jit(solution)/shard_map/all_to_all | solution.py:190
  48.3 0.8 shard_map.64
  49.1 5.1 %shard_map.65 = (f32[512,2048]{1,0:T(8,128)S(1)}, f32[32,4,128]{2,1,0:T(4,128)S(1)}, f32[16,16,128]{2,1,0:T(8,128)S(1)}) custom-call(s32[2]{0:T(128)S(1)} %pad_add_fusion.where_ref, bf16[512,640]{1,0:T(8,128)(2,1)S(1)} %get-tuple-element.22.left_ref, f32[512,128]{1,0:T(8,128)S(1)} %get-tuple-element.23.sq_ref, ...), custom_call_target="tpu_custom_call" | custom-call | flops 16777216 | bytes 4194304 | tf_op jit(solution)/shard_map/pallas_call | solution.py:196
  54.3 14.4 %all_to_all.45.refs_1_ = f32[32,4,128]{2,1,0:T(4,128)S(1)} all-to-all(f32[32,4,128]{2,1,0:T(4,128)S(1)} %get-tuple-element.25), channel_id=1, replica_groups=mesh['zh'=4,'zl'=2,'core'=2,'col'=32] {'col'}, dimensions={0} | all-to-all | bytes 131072 | tf_op jit(solution)/shard_map/all_to_all | solution.py:190
  68.7 16.8 %all_to_all.46.refs_2_ = f32[16,16,128]{2,1,0:T(8,128)S(1)} all-to-all(f32[16,16,128]{2,1,0:T(8,128)S(1)} %get-tuple-element.26), channel_id=1, replica_groups=mesh['zh'=4,'zl'=2,'core'=2,'col'=32] {'zh','zl','core'}, dimensions={0} | all-to-all | bytes 262144 | tf_op jit(solution)/shard_map/all_to_all | solution.py:190
  85.5 2.4 %shard_map.66 = (f32[32,4,128]{2,1,0:T(4,128)S(1)}, f32[16,16,128]{2,1,0:T(8,128)S(1)}, f32[4,128]{1,0:T(4,128)S(1)}, f32[16,128]{1,0:T(8,128)S(1)}) custom-call(f32[512,2048]{1,0:T(8,128)S(1)} %get-tuple-element.24.refs_0_, f32[32,4,128]{2,1,0:T(4,128)S(1)} %all_to_all.45.refs_1_, f32[16,16,128]{2,1,0:T(8,128)S(1)} %all_to_all.46.refs_2_, ...), custom_call_target="tpu_custom_call" | custom-call | flops 16777216 | bytes 4194304 | tf_op jit(solution)/shard_map/pallas_call | solution.py:196
  87.8 12.3 %all_to_all.47.refs_1_ = f32[32,4,128]{2,1,0:T(4,128)S(1)} all-to-all(f32[32,4,128]{2,1,0:T(4,128)S(1)} %get-tuple-element.27), channel_id=1, replica_groups=mesh['zh'=4,'zl'=2,'core'=2,'col'=32] {'col'}, dimensions={0} | all-to-all | bytes 131072 | tf_op jit(solution)/shard_map/all_to_all | solution.py:190
  100.2 12.5 %all_to_all.48.refs_2_ = f32[16,16,128]{2,1,0:T(8,128)S(1)} all-to-all(f32[16,16,128]{2,1,0:T(8,128)S(1)} %get-tuple-element.28), channel_id=1, replica_groups=mesh['zh'=4,'zl'=2,'core'=2,'col'=32] {'zh','zl','core'}, dimensions={0} | all-to-all | bytes 262144 | tf_op jit(solution)/shard_map/all_to_all | solution.py:190
  112.7 2.4 %shard_map.67 = (f32[32,4,128]{2,1,0:T(4,128)S(1)}, f32[16,16,128]{2,1,0:T(8,128)S(1)}, f32[4,128]{1,0:T(4,128)S(1)}, f32[16,128]{1,0:T(8,128)S(1)}) custom-call(f32[512,2048]{1,0:T(8,128)S(1)} %get-tuple-element.24.refs_0_, f32[32,4,128]{2,1,0:T(4,128)S(1)} %all_to_all.47.refs_1_, f32[16,16,128]{2,1,0:T(8,128)S(1)} %all_to_all.48.refs_2_, ...), custom_call_target="tpu_custom_call" | custom-call | flops 16777216 | bytes 4194304 | tf_op jit(solution)/shard_map/pallas_call | solution.py:196
  115.1 12.3 %all_to_all.49.refs_1_ = f32[32,4,128]{2,1,0:T(4,128)S(1)} all-to-all(f32[32,4,128]{2,1,0:T(4,128)S(1)} %get-tuple-element.31), channel_id=1, replica_groups=mesh['zh'=4,'zl'=2,'core'=2,'col'=32] {'col'}, dimensions={0} | all-to-all | bytes 131072 | tf_op jit(solution)/shard_map/all_to_all | solution.py:190
  127.4 12.5 %all_to_all.50.refs_2_ = f32[16,16,128]{2,1,0:T(8,128)S(1)} all-to-all(f32[16,16,128]{2,1,0:T(8,128)S(1)} %get-tuple-element.32), channel_id=1, replica_groups=mesh['zh'=4,'zl'=2,'core'=2,'col'=32] {'zh','zl','core'}, dimensions={0} | all-to-all | bytes 262144 | tf_op jit(solution)/shard_map/all_to_all | solution.py:190
  139.9 1.4 shard_map.68
  141.3 12.3 %all_to_all.51.refs_0_ = f32[32,4,128]{2,1,0:T(4,128)S(1)} all-to-all(f32[32,4,128]{2,1,0:T(4,128)S(1)} %get-tuple-element.35), channel_id=1, replica_groups=mesh['zh'=4,'zl'=2,'core'=2,'col'=32] {'col'}, dimensions={0} | all-to-all | bytes 131072 | tf_op jit(solution)/shard_map/all_to_all | solution.py:190
  153.6 10.8 %all_to_all.52.refs_0_ = f32[16,4,128]{2,1,0:T(4,128)S(1)} all-to-all(f32[16,4,128]{2,1,0:T(4,128)S(1)} %get-tuple-element.37), channel_id=1, replica_groups=mesh['zh'=4,'zl'=2,'core'=2,'col'=32] {'zh','zl','core'}, dimensions={0} | all-to-all | bytes 65536 | tf_op jit(solution)/shard_map/all_to_all | solution.py:190
  164.4 0.7 shard_map.70
  (17 shorter events, 3.0 us)
Async XLA Ops:
  6.8 29.3 %collective-permute-start = (bf16[2,144,256]{2,1,0:T(8,128)(2,1)S(1)}, bf16[2,144,256]{2,1,0:T(8,128)(2,1)S(1)}, u32[]{:S(2)}, u32[]{:S(2)}) collective-permute-start(bf16[2,144,256]{2,1,0:T(8,128)(2,1)S(1)} %bitcast.10), channel_id=1, source_target_pairs={{0,128},{128,256},{256,384},{384,0},{1,129},{129,257},{257,385},{3... | collective-permute-start | bytes 442376 | tf_op jit(solution)/shard_map/ppermute | solution.py:218
  12.6 23.5 %collective-permute-start.1 = (bf16[2,144,256]{2,1,0:T(8,128)(2,1)S(1)}, bf16[2,144,256]{2,1,0:T(8,128)(2,1)S(1)}, u32[]{:S(2)}, u32[]{:S(2)}) collective-permute-start(bf16[2,144,256]{2,1,0:T(8,128)(2,1)S(1)} %bitcast.11), channel_id=1, source_target_pairs={{0,256},{128,384},{256,0},{384,128},{1,257},{129,385},{257,1},{385... | collective-permute-start | bytes 442376 | tf_op jit(solution)/shard_map/ppermute | solution.py:218
  20.9 15.3 %collective-permute-start.2 = (bf16[2,144,256]{2,1,0:T(8,128)(2,1)S(1)}, bf16[2,144,256]{2,1,0:T(8,128)(2,1)S(1)}, u32[]{:S(2)}, u32[]{:S(2)}) collective-permute-start(bf16[2,144,256]{2,1,0:T(8,128)(2,1)S(1)} %bitcast.12), channel_id=1, source_target_pairs={{0,384},{128,0},{256,128},{384,256},{1,385},{129,1},{257,129},{385... | collective-permute-start | bytes 442376 | tf_op jit(solution)/shard_map/ppermute | solution.py:218
  26.5 21.1 %all-to-all-start = ((bf16[32,16,384]{2,1,0:T(8,128)(2,1)}), bf16[32,16,384]{2,1,0:T(8,128)(2,1)S(1)}, u32[]{:S(2)}, u32[]{:S(2)}) async-start(bf16[32,16,384]{2,1,0:T(8,128)(2,1)} %broadcast_in_dim.26), calls=%async_computation | async-start | bytes 786432 | tf_op jit(solution)/shard_map/all_to_all | solution.py:190
  36.3 12.8 %collective-permute-start.3 = (bf16[4,2,144,256]{3,2,1,0:T(8,128)(2,1)S(1)}, bf16[4,2,144,256]{3,2,1,0:T(8,128)(2,1)S(1)}, u32[]{:S(2)}, u32[]{:S(2)}) collective-permute-start(bf16[4,2,144,256]{3,2,1,0:T(8,128)(2,1)S(1)} %pad_maximum_fusion.mine_ref), channel_id=1, source_target_pairs={{0,32},{32,0},{1,33},{33,1},{2,34},{34,2},{3,35},{35,3},{4,36},{36... | collective-permute-start | bytes 1769480 | tf_op jit(solution)/shard_map/ppermute | solution.py:219
  47.6 0.7 copy-start

commit v6 on v5

--- a/solution.py
+++ b/solution.py
@@ -216,6 +216,7 @@
     steps = lax.axis_size("zh")
     turn = [[(i, (i + k) % steps) for i in range(steps)] for k in range(steps)]
     mine = jnp.stack([pair] + [lax.ppermute(pair, "zh", turn[k]) for k in range(1, steps)])
+    mine, train_all = lax.optimization_barrier((mine, train_all))
     other = lax.ppermute(mine, "core", [(0, 1), (1, 0)])
     where = jnp.stack([lax.axis_index("zh"), lax.axis_index("core")]).astype(jnp.int32)
     rows, cols = train_embed.shape[0] * col_size, valid_embed.shape[0] * row_size

time: 166 us -> 172 us (1.036)
  waiting for transfers between devices: 5.59 us -> 11.3 us
  blocking collectives: 109 us -> 111 us
    ppermute x3, waiting for transfers between devices: 0.01 us -> 11.3 us  [shards(): lax.ppermute(pair, 'zh', turn[k])]
    all_to_all x1, waiting for transfers between devices: 5.58 us -> 0.01 us  [exchange(): return lax.all_to_all(copies, axis, 0, 0, tiled=True)]
    ppermute x1, starting transfers between devices: 4.85 us -> 2.51 us  [shards(): other = lax.ppermute(mine, 'core', [(0, 1), (1, 0)])]
    all_to_all x8, blocking collectives: 104 us -> 106 us  [exchange(): return lax.all_to_all(copies, axis, 0, 0, tiled=True)]
  transfers between devices with their start and end apart: 5 -> 5, of which waited for: 1 -> 2; matrix products, arithmetic and copies ran while one was open for 2% -> 1% of each run, Pallas kernels for 0% -> 0%
where the time goes in v6:
time: 172 us; the launch traced here: 171 us
  blocking collectives  111 us (65%)
  starting transfers between devices  30.4 us (18%)
  Pallas kernels  12.9 us (8%)
  waiting for transfers between devices  11.3 us (7%)
  other arithmetic  3.01 us (2%)
  local copies, waits for them, and re-layouts  2.34 us (1%)
    all_to_all x8, blocking collectives, exchange(): return lax.all_to_all(copies, axis, 0, 0, tiled=True)  106 us
    ppermute x3, starting transfers between devices, shards(): lax.ppermute(pair, 'zh', turn[k])  17.4 us
    pallas_call x7, Pallas kernels, call(): pl.pallas_call(body, out_shape=out_shape, in_specs=specs, out_specs=[VMEM...  12.9 us
    ppermute x3, waiting for transfers between devices, shards(): lax.ppermute(pair, 'zh', turn[k])  11.3 us
    all_to_all x1, starting transfers between devices, exchange(): return lax.all_to_all(copies, axis, 0, 0, tiled=True)  10.5 us
    all_gather x1, blocking collectives, shards(): pair = lax.all_gather(valid_pack, 'zl', axis=0)  4.77 us
  transfers between devices with their start and end apart: 5, of which 2 were waited for; matrix products, arithmetic and copies ran while one was open for 1% of the time, Pallas kernels for 0%

profile of v6, /device:TPU:1, one launch (start us, length us, event | category | flops | bytes accessed | tf_op | source)
XLA Modules:
  0.0 170.9 jit_solution(15293918467315797472)
XLA Ops:
  1.4 0.8 broadcast_in_dim.28
  2.2 10.5 %all-to-all-start = ((bf16[32,16,384]{2,1,0:T(8,128)(2,1)}), bf16[32,16,384]{2,1,0:T(8,128)(2,1)S(1)}, u32[]{:S(2)}, u32[]{:S(2)}) async-start(bf16[32,16,384]{2,1,0:T(8,128)(2,1)} %broadcast_in_dim.28), calls=%async_computation | async-start | bytes 786432 | tf_op jit(solution)/shard_map/all_to_all | solution.py:190
  13.4 0.8 pad_maximum_fusion.1
  14.2 4.8 %all-gather = bf16[288,256]{1,0:T(8,128)(2,1)S(1)} all-gather(bf16[144,256]{1,0:T(8,128)(2,1)S(1)} %pad_maximum_fusion.1), channel_id=2, replica_groups=mesh['zh'=4,'zl'=2,'core'=2,'col'=32] {'zl'}, dimensions={0}, use_global_device_ids=true | all-gather | bytes 221184 | tf_op jit(solution)/shard_map/all_gather | solution.py:215
  19.0 5.8 %collective-permute-start = (bf16[2,144,256]{2,1,0:T(8,128)(2,1)S(1)}, bf16[2,144,256]{2,1,0:T(8,128)(2,1)S(1)}, u32[]{:S(2)}, u32[]{:S(2)}) collective-permute-start(bf16[2,144,256]{2,1,0:T(8,128)(2,1)S(1)} %bitcast.10), channel_id=1, source_target_pairs={{0,128},{128,256},{256,384},{384,0},{1,129},{129,257},{257,385},{3... | collective-permute-start | bytes 442376 | tf_op jit(solution)/shard_map/ppermute | solution.py:218
  24.8 8.2 %collective-permute-start.1 = (bf16[2,144,256]{2,1,0:T(8,128)(2,1)S(1)}, bf16[2,144,256]{2,1,0:T(8,128)(2,1)S(1)}, u32[]{:S(2)}, u32[]{:S(2)}) collective-permute-start(bf16[2,144,256]{2,1,0:T(8,128)(2,1)S(1)} %bitcast.11), channel_id=1, source_target_pairs={{0,256},{128,384},{256,0},{384,128},{1,257},{129,385},{257,1},{385... | collective-permute-start | bytes 442376 | tf_op jit(solution)/shard_map/ppermute | solution.py:218
  33.1 3.4 %collective-permute-start.2 = (bf16[2,144,256]{2,1,0:T(8,128)(2,1)S(1)}, bf16[2,144,256]{2,1,0:T(8,128)(2,1)S(1)}, u32[]{:S(2)}, u32[]{:S(2)}) collective-permute-start(bf16[2,144,256]{2,1,0:T(8,128)(2,1)S(1)} %bitcast.12), channel_id=1, source_target_pairs={{0,384},{128,0},{256,128},{384,256},{1,385},{129,1},{257,129},{385... | collective-permute-start | bytes 442376 | tf_op jit(solution)/shard_map/ppermute | solution.py:218
  36.5 5.4 %collective-permute-done.1 = bf16[2,144,256]{2,1,0:T(8,128)(2,1)S(1)} collective-permute-done((bf16[2,144,256]{2,1,0:T(8,128)(2,1)S(1)}, bf16[2,144,256]{2,1,0:T(8,128)(2,1)S(1)}, u32[]{:S(2)}, u32[]{:S(2)}) %collective-permute-start.1) | collective-permute-done | bytes 147488 | tf_op jit(solution)/shard_map/ppermute | solution.py:218
  41.8 5.9 %collective-permute-done.2 = bf16[2,144,256]{2,1,0:T(8,128)(2,1)S(1)} collective-permute-done((bf16[2,144,256]{2,1,0:T(8,128)(2,1)S(1)}, bf16[2,144,256]{2,1,0:T(8,128)(2,1)S(1)}, u32[]{:S(2)}, u32[]{:S(2)}) %collective-permute-start.2) | collective-permute-done | bytes 147488 | tf_op jit(solution)/shard_map/ppermute | solution.py:218
  47.9 2.5 %collective-permute-start.3 = (bf16[4,2,144,256]{3,2,1,0:T(8,128)(2,1)S(1)}, bf16[4,2,144,256]{3,2,1,0:T(8,128)(2,1)S(1)}, u32[]{:S(2)}, u32[]{:S(2)}) collective-permute-start(bf16[4,2,144,256]{3,2,1,0:T(8,128)(2,1)S(1)} %pad_maximum_fusion.mine_ref), channel_id=1, source_target_pairs={{0,32},{32,0},{1,33},{33,1},{2,34},{34,2},{3,35},{35,3},{4,36},{36... | collective-permute-start | bytes 1769480 | tf_op jit(solution)/shard_map/ppermute | solution.py:220
  50.4 0.8 pad.4.refs_1_
  51.9 0.8 shard_map.64
  52.8 5.1 %shard_map.65 = (f32[512,2048]{1,0:T(8,128)S(1)}, f32[32,4,128]{2,1,0:T(4,128)S(1)}, f32[16,16,128]{2,1,0:T(8,128)S(1)}) custom-call(s32[2]{0:T(128)S(1)} %pad_add_fusion.where_ref, bf16[512,640]{1,0:T(8,128)(2,1)S(1)} %get-tuple-element.25.left_ref, f32[512,128]{1,0:T(8,128)S(1)} %get-tuple-element.26.sq_ref, ...), custom_call_target="tpu_custom_call" | custom-call | flops 16777216 | bytes 4194304 | tf_op jit(solution)/shard_map/pallas_call | solution.py:196
  57.9 18.0 %all_to_all.45.refs_1_ = f32[32,4,128]{2,1,0:T(4,128)S(1)} all-to-all(f32[32,4,128]{2,1,0:T(4,128)S(1)} %get-tuple-element.29), channel_id=1, replica_groups=mesh['zh'=4,'zl'=2,'core'=2,'col'=32] {'col'}, dimensions={0} | all-to-all | bytes 131072 | tf_op jit(solution)/shard_map/all_to_all | solution.py:190
  75.9 15.3 %all_to_all.46.refs_2_ = f32[16,16,128]{2,1,0:T(8,128)S(1)} all-to-all(f32[16,16,128]{2,1,0:T(8,128)S(1)} %get-tuple-element.30), channel_id=1, replica_groups=mesh['zh'=4,'zl'=2,'core'=2,'col'=32] {'zh','zl','core'}, dimensions={0} | all-to-all | bytes 262144 | tf_op jit(solution)/shard_map/all_to_all | solution.py:190
  91.2 2.4 %shard_map.66 = (f32[32,4,128]{2,1,0:T(4,128)S(1)}, f32[16,16,128]{2,1,0:T(8,128)S(1)}, f32[4,128]{1,0:T(4,128)S(1)}, f32[16,128]{1,0:T(8,128)S(1)}) custom-call(f32[512,2048]{1,0:T(8,128)S(1)} %get-tuple-element.28.refs_0_, f32[32,4,128]{2,1,0:T(4,128)S(1)} %all_to_all.45.refs_1_, f32[16,16,128]{2,1,0:T(8,128)S(1)} %all_to_all.46.refs_2_, ...), custom_call_target="tpu_custom_call" | custom-call | flops 16777216 | bytes 4194304 | tf_op jit(solution)/shard_map/pallas_call | solution.py:196
  93.5 12.3 %all_to_all.47.refs_1_ = f32[32,4,128]{2,1,0:T(4,128)S(1)} all-to-all(f32[32,4,128]{2,1,0:T(4,128)S(1)} %get-tuple-element.31), channel_id=1, replica_groups=mesh['zh'=4,'zl'=2,'core'=2,'col'=32] {'col'}, dimensions={0} | all-to-all | bytes 131072 | tf_op jit(solution)/shard_map/all_to_all | solution.py:190
  105.9 12.5 %all_to_all.48.refs_2_ = f32[16,16,128]{2,1,0:T(8,128)S(1)} all-to-all(f32[16,16,128]{2,1,0:T(8,128)S(1)} %get-tuple-element.32), channel_id=1, replica_groups=mesh['zh'=4,'zl'=2,'core'=2,'col'=32] {'zh','zl','core'}, dimensions={0} | all-to-all | bytes 262144 | tf_op jit(solution)/shard_map/all_to_all | solution.py:190
  118.4 2.4 %shard_map.67 = (f32[32,4,128]{2,1,0:T(4,128)S(1)}, f32[16,16,128]{2,1,0:T(8,128)S(1)}, f32[4,128]{1,0:T(4,128)S(1)}, f32[16,128]{1,0:T(8,128)S(1)}) custom-call(f32[512,2048]{1,0:T(8,128)S(1)} %get-tuple-element.28.refs_0_, f32[32,4,128]{2,1,0:T(4,128)S(1)} %all_to_all.47.refs_1_, f32[16,16,128]{2,1,0:T(8,128)S(1)} %all_to_all.48.refs_2_, ...), custom_call_target="tpu_custom_call" | custom-call | flops 16777216 | bytes 4194304 | tf_op jit(solution)/shard_map/pallas_call | solution.py:196
  120.8 12.3 %all_to_all.49.refs_1_ = f32[32,4,128]{2,1,0:T(4,128)S(1)} all-to-all(f32[32,4,128]{2,1,0:T(4,128)S(1)} %get-tuple-element.35), channel_id=1, replica_groups=mesh['zh'=4,'zl'=2,'core'=2,'col'=32] {'col'}, dimensions={0} | all-to-all | bytes 131072 | tf_op jit(solution)/shard_map/all_to_all | solution.py:190
  133.1 12.5 %all_to_all.50.refs_2_ = f32[16,16,128]{2,1,0:T(8,128)S(1)} all-to-all(f32[16,16,128]{2,1,0:T(8,128)S(1)} %get-tuple-element.36), channel_id=1, replica_groups=mesh['zh'=4,'zl'=2,'core'=2,'col'=32] {'zh','zl','core'}, dimensions={0} | all-to-all | bytes 262144 | tf_op jit(solution)/shard_map/all_to_all | solution.py:190
  145.6 1.4 shard_map.68
  147.0 12.3 %all_to_all.51.refs_0_ = f32[32,4,128]{2,1,0:T(4,128)S(1)} all-to-all(f32[32,4,128]{2,1,0:T(4,128)S(1)} %get-tuple-element.39), channel_id=1, replica_groups=mesh['zh'=4,'zl'=2,'core'=2,'col'=32] {'col'}, dimensions={0} | all-to-all | bytes 131072 | tf_op jit(solution)/shard_map/all_to_all | solution.py:190
  159.3 10.8 %all_to_all.52.refs_0_ = f32[16,4,128]{2,1,0:T(4,128)S(1)} all-to-all(f32[16,4,128]{2,1,0:T(4,128)S(1)} %get-tuple-element.41), channel_id=1, replica_groups=mesh['zh'=4,'zl'=2,'core'=2,'col'=32] {'zh','zl','core'}, dimensions={0} | all-to-all | bytes 65536 | tf_op jit(solution)/shard_map/all_to_all | solution.py:190
  (17 shorter events, 3.7 us)
Async XLA Ops:
  2.2 45.7 %all-to-all-start = ((bf16[32,16,384]{2,1,0:T(8,128)(2,1)}), bf16[32,16,384]{2,1,0:T(8,128)(2,1)S(1)}, u32[]{:S(2)}, u32[]{:S(2)}) async-start(bf16[32,16,384]{2,1,0:T(8,128)(2,1)} %broadcast_in_dim.28), calls=%async_computation | async-start | bytes 786432 | tf_op jit(solution)/shard_map/all_to_all | solution.py:190
  19.0 17.4 %collective-permute-start = (bf16[2,144,256]{2,1,0:T(8,128)(2,1)S(1)}, bf16[2,144,256]{2,1,0:T(8,128)(2,1)S(1)}, u32[]{:S(2)}, u32[]{:S(2)}) collective-permute-start(bf16[2,144,256]{2,1,0:T(8,128)(2,1)S(1)} %bitcast.10), channel_id=1, source_target_pairs={{0,128},{128,256},{256,384},{384,0},{1,129},{129,257},{257,385},{3... | collective-permute-start | bytes 442376 | tf_op jit(solution)/shard_map/ppermute | solution.py:218
  24.8 17.0 %collective-permute-start.1 = (bf16[2,144,256]{2,1,0:T(8,128)(2,1)S(1)}, bf16[2,144,256]{2,1,0:T(8,128)(2,1)S(1)}, u32[]{:S(2)}, u32[]{:S(2)}) collective-permute-start(bf16[2,144,256]{2,1,0:T(8,128)(2,1)S(1)} %bitcast.11), channel_id=1, source_target_pairs={{0,256},{128,384},{256,0},{384,128},{1,257},{129,385},{257,1},{385... | collective-permute-start | bytes 442376 | tf_op jit(solution)/shard_map/ppermute | solution.py:218
  33.1 14.7 %collective-permute-start.2 = (bf16[2,144,256]{2,1,0:T(8,128)(2,1)S(1)}, bf16[2,144,256]{2,1,0:T(8,128)(2,1)S(1)}, u32[]{:S(2)}, u32[]{:S(2)}) collective-permute-start(bf16[2,144,256]{2,1,0:T(8,128)(2,1)S(1)} %bitcast.12), channel_id=1, source_target_pairs={{0,384},{128,0},{256,128},{384,256},{1,385},{129,1},{257,129},{385... | collective-permute-start | bytes 442376 | tf_op jit(solution)/shard_map/ppermute | solution.py:218
  47.9 4.9 %collective-permute-start.3 = (bf16[4,2,144,256]{3,2,1,0:T(8,128)(2,1)S(1)}, bf16[4,2,144,256]{3,2,1,0:T(8,128)(2,1)S(1)}, u32[]{:S(2)}, u32[]{:S(2)}) collective-permute-start(bf16[4,2,144,256]{3,2,1,0:T(8,128)(2,1)S(1)} %pad_maximum_fusion.mine_ref), channel_id=1, source_target_pairs={{0,32},{32,0},{1,33},{33,1},{2,34},{34,2},{3,35},{35,3},{4,36},{36... | collective-permute-start | bytes 1769480 | tf_op jit(solution)/shard_map/ppermute | solution.py:220
  51.3 0.7 copy-start

commit v7 on v6

--- a/solution.py
+++ b/solution.py
@@ -214,8 +214,10 @@
     valid_pack = jnp.concatenate([valid_embed, jnp.broadcast_to(label_row, (16, embed))], axis=0)
     pair = lax.all_gather(valid_pack, "zl", axis=0)
     steps = lax.axis_size("zh")
-    turn = [[(i, (i + k) % steps) for i in range(steps)] for k in range(steps)]
-    mine = jnp.stack([pair] + [lax.ppermute(pair, "zh", turn[k]) for k in range(1, steps)])
+    ahead, behind = [[(i, (i + k) % steps) for i in range(steps)] for k in (1, -1)]
+    from_low, from_high = lax.ppermute(pair, "zh", ahead), lax.ppermute(pair, "zh", behind)
+    opposite = [lax.ppermute(from_high[:1], "zh", behind), lax.ppermute(from_low[1:], "zh", ahead)]
+    mine = jnp.stack([pair, from_low, jnp.concatenate(opposite), from_high])
     mine, train_all = lax.optimization_barrier((mine, train_all))
     other = lax.ppermute(mine, "core", [(0, 1), (1, 0)])
     where = jnp.stack([lax.axis_index("zh"), lax.axis_index("core")]).astype(jnp.int32)

time: 172 us -> 173 us (level)
  starting transfers between devices: 30.4 us -> 38.1 us
  waiting for transfers between devices: 11.3 us -> 6.5 us
  blocking collectives: 111 us -> 109 us
    ppermute x3 -> x4, starting transfers between devices: 17.4 us -> 22.9 us  [the longest x1 10 us: shards(): lax.ppermute(pair, 'zh', behind)]
    ppermute x3 -> x4, waiting for transfers between devices: 11.3 us -> 6.49 us  [the longest x1 5.61 us: shards(): lax.ppermute(from_low[1:], 'zh', ahead)]
    ppermute x1, starting transfers between devices: 2.51 us -> 4.65 us  [shards(): other = lax.ppermute(mine, 'core', [(0, 1), (1, 0)])]
  transfers between devices with their start and end apart: 5 -> 6, of which waited for: 2 -> 3; matrix products, arithmetic and copies ran while one was open for 1% -> 1% of each run, Pallas kernels for 0% -> 0%
where the time goes in v7:
time: 173 us; the launch traced here: 172 us
  blocking collectives  109 us (63%)
  starting transfers between devices  38.1 us (22%)
  Pallas kernels  12.9 us (7%)
  waiting for transfers between devices  6.5 us (4%)
  other arithmetic  3.03 us (2%)
  local copies, waits for them, and re-layouts  2.35 us (1%)
    all_to_all x8, blocking collectives, exchange(): return lax.all_to_all(copies, axis, 0, 0, tiled=True)  104 us
    pallas_call x7, Pallas kernels, call(): pl.pallas_call(body, out_shape=out_shape, in_specs=specs, out_specs=[VMEM...  12.9 us
    all_to_all x1, starting transfers between devices, exchange(): return lax.all_to_all(copies, axis, 0, 0, tiled=True)  10.5 us
    ppermute x1, starting transfers between devices, shards(): lax.ppermute(pair, 'zh', behind)  10 us
    ppermute x1, starting transfers between devices, shards(): lax.ppermute(from_high[:1], 'zh', behind)  9.07 us
    ppermute x1, waiting for transfers between devices, shards(): lax.ppermute(from_low[1:], 'zh', ahead)  5.61 us
    all_gather x1, blocking collectives, shards(): pair = lax.all_gather(valid_pack, 'zl', axis=0)  4.77 us
    ppermute x1, starting transfers between devices, shards(): other = lax.ppermute(mine, 'core', [(0, 1), (1, 0)])  4.65 us
  transfers between devices with their start and end apart: 6, of which 3 were waited for; matrix products, arithmetic and copies ran while one was open for 1% of the time, Pallas kernels for 0%

profile of v7, /device:TPU:1, one launch (start us, length us, event | category | flops | bytes accessed | tf_op | source)
XLA Modules:
  0.0 172.2 jit_solution(9415728168092706339)
XLA Ops:
  1.4 0.8 broadcast_in_dim.28
  2.2 10.5 %all-to-all-start = ((bf16[32,16,384]{2,1,0:T(8,128)(2,1)}), bf16[32,16,384]{2,1,0:T(8,128)(2,1)S(1)}, u32[]{:S(2)}, u32[]{:S(2)}) async-start(bf16[32,16,384]{2,1,0:T(8,128)(2,1)} %broadcast_in_dim.28), calls=%async_computation | async-start | bytes 786432 | tf_op jit(solution)/shard_map/all_to_all | solution.py:190
  13.4 0.8 pad_maximum_fusion.1
  14.2 4.8 %all-gather = bf16[288,256]{1,0:T(8,128)(2,1)S(1)} all-gather(bf16[144,256]{1,0:T(8,128)(2,1)S(1)} %pad_maximum_fusion.1), channel_id=2, replica_groups=mesh['zh'=4,'zl'=2,'core'=2,'col'=32] {'zl'}, dimensions={0}, use_global_device_ids=true | all-gather | bytes 221184 | tf_op jit(solution)/shard_map/all_gather | solution.py:215
  19.0 10.0 %collective-permute-start.1 = (bf16[2,144,256]{2,1,0:T(8,128)(2,1)S(1)}, bf16[2,144,256]{2,1,0:T(8,128)(2,1)S(1)}, u32[]{:S(2)}, u32[]{:S(2)}) collective-permute-start(bf16[2,144,256]{2,1,0:T(8,128)(2,1)S(1)} %bitcast.11), channel_id=1, source_target_pairs={{0,384},{128,0},{256,128},{384,256},{1,385},{129,1},{257,129},{385... | collective-permute-start | bytes 442376 | tf_op jit(solution)/shard_map/ppermute | solution.py:218
  29.1 1.9 %collective-permute-start = (bf16[2,144,256]{2,1,0:T(8,128)(2,1)S(1)}, bf16[2,144,256]{2,1,0:T(8,128)(2,1)S(1)}, u32[]{:S(2)}, u32[]{:S(2)}) collective-permute-start(bf16[2,144,256]{2,1,0:T(8,128)(2,1)S(1)} %bitcast.12), channel_id=1, source_target_pairs={{0,128},{128,256},{256,384},{384,0},{1,129},{129,257},{257,385},{3... | collective-permute-start | bytes 442376 | tf_op jit(solution)/shard_map/ppermute | solution.py:218
  31.6 9.1 %collective-permute-start.2 = (bf16[1,144,256]{2,1,0:T(8,128)(2,1)S(1)}, bf16[1,144,256]{2,1,0:T(8,128)(2,1)S(1)}, u32[]{:S(2)}, u32[]{:S(2)}) collective-permute-start(bf16[1,144,256]{2,1,0:T(8,128)(2,1)S(1)} %slice.8), channel_id=1, source_target_pairs={{0,384},{128,0},{256,128},{384,256},{1,385},{129,1},{257,129},{385... | collective-permute-start | bytes 221192 | tf_op jit(solution)/shard_map/ppermute | solution.py:219
  41.0 1.9 %collective-permute-start.3 = (bf16[1,144,256]{2,1,0:T(8,128)(2,1)S(1)}, bf16[1,144,256]{2,1,0:T(8,128)(2,1)S(1)}, u32[]{:S(2)}, u32[]{:S(2)}) collective-permute-start(bf16[1,144,256]{2,1,0:T(8,128)(2,1)S(1)} %slice.9), channel_id=1, source_target_pairs={{0,128},{128,256},{256,384},{384,0},{1,129},{129,257},{257,385},{3... | collective-permute-start | bytes 221192 | tf_op jit(solution)/shard_map/ppermute | solution.py:219
  42.9 5.6 %collective-permute-done.3 = bf16[1,144,256]{2,1,0:T(8,128)(2,1)S(1)} collective-permute-done((bf16[1,144,256]{2,1,0:T(8,128)(2,1)S(1)}, bf16[1,144,256]{2,1,0:T(8,128)(2,1)S(1)}, u32[]{:S(2)}, u32[]{:S(2)}) %collective-permute-start.3) | collective-permute-done | bytes 73760 | tf_op jit(solution)/shard_map/ppermute | solution.py:219
  48.6 4.7 %collective-permute-start.4 = (bf16[4,2,144,256]{3,2,1,0:T(8,128)(2,1)S(1)}, bf16[4,2,144,256]{3,2,1,0:T(8,128)(2,1)S(1)}, u32[]{:S(2)}, u32[]{:S(2)}) collective-permute-start(bf16[4,2,144,256]{3,2,1,0:T(8,128)(2,1)S(1)} %pad_maximum_fusion.mine_ref), channel_id=1, source_target_pairs={{0,32},{32,0},{1,33},{33,1},{2,34},{34,2},{3,35},{35,3},{4,36},{36... | collective-permute-start | bytes 1769480 | tf_op jit(solution)/shard_map/ppermute | solution.py:222
  53.3 0.8 pad.4.refs_1_
  54.8 0.8 shard_map.64
  55.7 5.1 %shard_map.65 = (f32[512,2048]{1,0:T(8,128)S(1)}, f32[32,4,128]{2,1,0:T(4,128)S(1)}, f32[16,16,128]{2,1,0:T(8,128)S(1)}) custom-call(s32[2]{0:T(128)S(1)} %pad_add_fusion.where_ref, bf16[512,640]{1,0:T(8,128)(2,1)S(1)} %get-tuple-element.25.left_ref, f32[512,128]{1,0:T(8,128)S(1)} %get-tuple-element.26.sq_ref, ...), custom_call_target="tpu_custom_call" | custom-call | flops 16777216 | bytes 4194304 | tf_op jit(solution)/shard_map/pallas_call | solution.py:196
  60.8 18.0 %all_to_all.45.refs_1_ = f32[32,4,128]{2,1,0:T(4,128)S(1)} all-to-all(f32[32,4,128]{2,1,0:T(4,128)S(1)} %get-tuple-element.29), channel_id=1, replica_groups=mesh['zh'=4,'zl'=2,'core'=2,'col'=32] {'col'}, dimensions={0} | all-to-all | bytes 131072 | tf_op jit(solution)/shard_map/all_to_all | solution.py:190
  78.8 13.6 %all_to_all.46.refs_2_ = f32[16,16,128]{2,1,0:T(8,128)S(1)} all-to-all(f32[16,16,128]{2,1,0:T(8,128)S(1)} %get-tuple-element.30), channel_id=1, replica_groups=mesh['zh'=4,'zl'=2,'core'=2,'col'=32] {'zh','zl','core'}, dimensions={0} | all-to-all | bytes 262144 | tf_op jit(solution)/shard_map/all_to_all | solution.py:190
  92.5 2.4 %shard_map.66 = (f32[32,4,128]{2,1,0:T(4,128)S(1)}, f32[16,16,128]{2,1,0:T(8,128)S(1)}, f32[4,128]{1,0:T(4,128)S(1)}, f32[16,128]{1,0:T(8,128)S(1)}) custom-call(f32[512,2048]{1,0:T(8,128)S(1)} %get-tuple-element.28.refs_0_, f32[32,4,128]{2,1,0:T(4,128)S(1)} %all_to_all.45.refs_1_, f32[16,16,128]{2,1,0:T(8,128)S(1)} %all_to_all.46.refs_2_, ...), custom_call_target="tpu_custom_call" | custom-call | flops 16777216 | bytes 4194304 | tf_op jit(solution)/shard_map/pallas_call | solution.py:196
  94.8 12.3 %all_to_all.47.refs_1_ = f32[32,4,128]{2,1,0:T(4,128)S(1)} all-to-all(f32[32,4,128]{2,1,0:T(4,128)S(1)} %get-tuple-element.31), channel_id=1, replica_groups=mesh['zh'=4,'zl'=2,'core'=2,'col'=32] {'col'}, dimensions={0} | all-to-all | bytes 131072 | tf_op jit(solution)/shard_map/all_to_all | solution.py:190
  107.2 12.5 %all_to_all.48.refs_2_ = f32[16,16,128]{2,1,0:T(8,128)S(1)} all-to-all(f32[16,16,128]{2,1,0:T(8,128)S(1)} %get-tuple-element.32), channel_id=1, replica_groups=mesh['zh'=4,'zl'=2,'core'=2,'col'=32] {'zh','zl','core'}, dimensions={0} | all-to-all | bytes 262144 | tf_op jit(solution)/shard_map/all_to_all | solution.py:190
  119.7 2.4 %shard_map.67 = (f32[32,4,128]{2,1,0:T(4,128)S(1)}, f32[16,16,128]{2,1,0:T(8,128)S(1)}, f32[4,128]{1,0:T(4,128)S(1)}, f32[16,128]{1,0:T(8,128)S(1)}) custom-call(f32[512,2048]{1,0:T(8,128)S(1)} %get-tuple-element.28.refs_0_, f32[32,4,128]{2,1,0:T(4,128)S(1)} %all_to_all.47.refs_1_, f32[16,16,128]{2,1,0:T(8,128)S(1)} %all_to_all.48.refs_2_, ...), custom_call_target="tpu_custom_call" | custom-call | flops 16777216 | bytes 4194304 | tf_op jit(solution)/shard_map/pallas_call | solution.py:196
  122.1 12.3 %all_to_all.49.refs_1_ = f32[32,4,128]{2,1,0:T(4,128)S(1)} all-to-all(f32[32,4,128]{2,1,0:T(4,128)S(1)} %get-tuple-element.35), channel_id=1, replica_groups=mesh['zh'=4,'zl'=2,'core'=2,'col'=32] {'col'}, dimensions={0} | all-to-all | bytes 131072 | tf_op jit(solution)/shard_map/all_to_all | solution.py:190
  134.4 12.5 %all_to_all.50.refs_2_ = f32[16,16,128]{2,1,0:T(8,128)S(1)} all-to-all(f32[16,16,128]{2,1,0:T(8,128)S(1)} %get-tuple-element.36), channel_id=1, replica_groups=mesh['zh'=4,'zl'=2,'core'=2,'col'=32] {'zh','zl','core'}, dimensions={0} | all-to-all | bytes 262144 | tf_op jit(solution)/shard_map/all_to_all | solution.py:190
  146.9 1.4 shard_map.68
  148.3 12.3 %all_to_all.51.refs_0_ = f32[32,4,128]{2,1,0:T(4,128)S(1)} all-to-all(f32[32,4,128]{2,1,0:T(4,128)S(1)} %get-tuple-element.39), channel_id=1, replica_groups=mesh['zh'=4,'zl'=2,'core'=2,'col'=32] {'col'}, dimensions={0} | all-to-all | bytes 131072 | tf_op jit(solution)/shard_map/all_to_all | solution.py:190
  160.6 10.8 %all_to_all.52.refs_0_ = f32[16,4,128]{2,1,0:T(4,128)S(1)} all-to-all(f32[16,4,128]{2,1,0:T(4,128)S(1)} %get-tuple-element.41), channel_id=1, replica_groups=mesh['zh'=4,'zl'=2,'core'=2,'col'=32] {'zh','zl','core'}, dimensions={0} | all-to-all | bytes 65536 | tf_op jit(solution)/shard_map/all_to_all | solution.py:190
  (22 shorter events, 4.6 us)
Async XLA Ops:
  2.2 46.4 %all-to-all-start = ((bf16[32,16,384]{2,1,0:T(8,128)(2,1)}), bf16[32,16,384]{2,1,0:T(8,128)(2,1)S(1)}, u32[]{:S(2)}, u32[]{:S(2)}) async-start(bf16[32,16,384]{2,1,0:T(8,128)(2,1)} %broadcast_in_dim.28), calls=%async_computation | async-start | bytes 786432 | tf_op jit(solution)/shard_map/all_to_all | solution.py:190
  19.0 12.6 %collective-permute-start.1 = (bf16[2,144,256]{2,1,0:T(8,128)(2,1)S(1)}, bf16[2,144,256]{2,1,0:T(8,128)(2,1)S(1)}, u32[]{:S(2)}, u32[]{:S(2)}) collective-permute-start(bf16[2,144,256]{2,1,0:T(8,128)(2,1)S(1)} %bitcast.11), channel_id=1, source_target_pairs={{0,384},{128,0},{256,128},{384,256},{1,385},{129,1},{257,129},{385... | collective-permute-start | bytes 442376 | tf_op jit(solution)/shard_map/ppermute | solution.py:218
  29.1 11.9 %collective-permute-start = (bf16[2,144,256]{2,1,0:T(8,128)(2,1)S(1)}, bf16[2,144,256]{2,1,0:T(8,128)(2,1)S(1)}, u32[]{:S(2)}, u32[]{:S(2)}) collective-permute-start(bf16[2,144,256]{2,1,0:T(8,128)(2,1)S(1)} %bitcast.12), channel_id=1, source_target_pairs={{0,128},{128,256},{256,384},{384,0},{1,129},{129,257},{257,385},{3... | collective-permute-start | bytes 442376 | tf_op jit(solution)/shard_map/ppermute | solution.py:218
  31.6 11.3 %collective-permute-start.2 = (bf16[1,144,256]{2,1,0:T(8,128)(2,1)S(1)}, bf16[1,144,256]{2,1,0:T(8,128)(2,1)S(1)}, u32[]{:S(2)}, u32[]{:S(2)}) collective-permute-start(bf16[1,144,256]{2,1,0:T(8,128)(2,1)S(1)} %slice.8), channel_id=1, source_target_pairs={{0,384},{128,0},{256,128},{384,256},{1,385},{129,1},{257,129},{385... | collective-permute-start | bytes 221192 | tf_op jit(solution)/shard_map/ppermute | solution.py:219
  41.0 7.5 %collective-permute-start.3 = (bf16[1,144,256]{2,1,0:T(8,128)(2,1)S(1)}, bf16[1,144,256]{2,1,0:T(8,128)(2,1)S(1)}, u32[]{:S(2)}, u32[]{:S(2)}) collective-permute-start(bf16[1,144,256]{2,1,0:T(8,128)(2,1)S(1)} %slice.9), channel_id=1, source_target_pairs={{0,128},{128,256},{256,384},{384,0},{1,129},{129,257},{257,385},{3... | collective-permute-start | bytes 221192 | tf_op jit(solution)/shard_map/ppermute | solution.py:219
  48.6 7.0 %collective-permute-start.4 = (bf16[4,2,144,256]{3,2,1,0:T(8,128)(2,1)S(1)}, bf16[4,2,144,256]{3,2,1,0:T(8,128)(2,1)S(1)}, u32[]{:S(2)}, u32[]{:S(2)}) collective-permute-start(bf16[4,2,144,256]{3,2,1,0:T(8,128)(2,1)S(1)} %pad_maximum_fusion.mine_ref), channel_id=1, source_target_pairs={{0,32},{32,0},{1,33},{33,1},{2,34},{34,2},{3,35},{35,3},{4,36},{36... | collective-permute-start | bytes 1769480 | tf_op jit(solution)/shard_map/ppermute | solution.py:222
  54.2 0.7 copy-start

commit v8 on v5

--- a/solution.py
+++ b/solution.py
@@ -99,32 +99,47 @@
     return lax.dot_general(left, right, (dims, ((), ())), preferred_element_type=jnp.float32)
 
 
-def prepare_kernel(train_ref, levels_ref, level_cost_ref, left_ref, sq_ref, *, num_levels):
-    shards, shard_rows, width = train_ref.shape
-    embed = width - LANES
-    packed = train_ref[...].reshape(shards * shard_rows, width)
+def pack_kernel(
+    train_label_hbm, train_hbm, valid_hbm, valid_label_hbm, train_out, valid_out,
+    train_label_ref, train_ref, valid_label_ref, sems
+):
+    count, embed = train_hbm.shape
+    points = valid_hbm.shape[0]
+    pairs = (
+        (train_label_hbm, train_label_ref),
+        (train_hbm, train_ref),
+        (valid_label_hbm, valid_label_ref),
+        (valid_hbm, valid_out.at[:points, :]),
+    )
+    copies = [pltpu.make_async_copy(source, target, sems.at[i]) for i, (source, target) in enumerate(pairs)]
+    for copy in copies:
+        copy.start()
+    for copy in copies:
+        copy.wait()
+    row_ids = lax.broadcasted_iota(jnp.int32, (count, LANES), 0)
+    shown = jnp.zeros((count, LANES), jnp.int32)
+    for i in range(count):
+        shown = jnp.where(row_ids == i, train_label_ref[i], shown)
+    packed = jnp.concatenate([train_ref[...], shown.astype(jnp.float32).astype(jnp.bfloat16)], axis=1)
+    train_out[...] = jnp.broadcast_to(packed[None], train_out.shape)
+    row = jnp.broadcast_to(valid_label_ref[...].astype(jnp.float32), (valid_out.shape[0] - points, LANES))
+    valid_out[points:, :] = jnp.concatenate([row] * (embed // LANES), axis=1).astype(jnp.bfloat16)
+
+
+def start_kernel(
+    where_ref, train_ref, table_ref, mine_ref, other_ref, cost_ref, row_out, col_out, left_ref, row_a, row_b, col_a, col_b
+):
+    steps, sides, block_rows, embed = mine_ref.shape
+    packed = train_ref[...].reshape(cost_ref.shape[0], embed + LANES)
     train = packed[:, :embed]
     wide = train.astype(jnp.float32)
     train_sq = jnp.sum(wide * wide, axis=1, keepdims=True) * (1.0 / embed)
-    sq_ref[...] = jnp.broadcast_to(train_sq, sq_ref.shape)
-    left_ref[:, :embed] = train * jnp.bfloat16(-2.0 / embed)
-    levels = levels_ref[...]
-    table = jnp.zeros(levels.shape, jnp.float32)
-    for level in range(num_levels):
-        table = table + jnp.where(levels == level, level_cost_ref[level], 0.0)
     labels = packed[:, embed:].astype(jnp.float32)
     lane_ids = lax.broadcasted_iota(jnp.int32, labels.shape, 1).astype(jnp.float32)
     train_hot = jnp.where(labels == lane_ids, 1.0, 0.0).astype(jnp.bfloat16)
-    parts = [dot(train_hot, part, ((1,), (0,))).astype(jnp.bfloat16) for part in split3(table)]
-    left_ref[:, embed:] = jnp.concatenate(parts, axis=1)
-
-
-def start_kernel(
-    where_ref, left_ref, sq_ref, mine_ref, other_ref, cost_ref, row_out, col_out, row_a, row_b, col_a, col_b
-):
-    steps, sides, block_rows, embed = mine_ref.shape
-    table_parts = (left_ref.shape[1] - embed) // LANES
-    train_sq = jnp.concatenate([sq_ref[...]] * sides, axis=1)
+    parts = [dot(train_hot, part, ((1,), (0,))).astype(jnp.bfloat16) for part in split3(table_ref[...])]
+    table_parts = len(parts)
+    left_ref[...] = jnp.concatenate([train * jnp.bfloat16(-2.0 / embed), *parts], axis=1)
     ones = jnp.ones((SUB, embed), jnp.bfloat16)
     class_ids = lax.broadcasted_iota(jnp.int32, (LANES, LANES), 0).astype(jnp.float32)
     step = sides * LANES
@@ -190,9 +205,10 @@
     return lax.all_to_all(copies, axis, 0, 0, tiled=True)
 
 
-def call(kernel, out_shape, scratch, *args, smem=(), limit=8, **static):
+def call(kernel, out_shape, scratch, *args, smem=(), hbm=(), limit=8, **static):
     body = kernel if not static else (lambda *refs: kernel(*refs, **static))
-    specs = [pl.BlockSpec(memory_space=pltpu.SMEM) if i in smem else VMEM for i in range(len(args))]
+    smem_spec, hbm_spec = pl.BlockSpec(memory_space=pltpu.SMEM), pl.BlockSpec(memory_space=pl.ANY)
+    specs = [smem_spec if i in smem else hbm_spec if i in hbm else VMEM for i in range(len(args))]
     return pl.pallas_call(
         body,
         out_shape=out_shape,
@@ -208,10 +224,26 @@
     row_size, col_size = lax.axis_size(ROW), lax.axis_size("col")
     f32 = jnp.float32
     embed = train_embed.shape[1]
-    shown = jnp.broadcast_to(train_labels.astype(jnp.bfloat16)[:, None], (train_embed.shape[0], LANES))
-    train_all = exchange(jnp.concatenate([train_embed, shown], axis=1), "col")
-    label_row = jnp.tile(valid_labels.astype(jnp.bfloat16), embed // LANES)[None, :]
-    valid_pack = jnp.concatenate([valid_embed, jnp.broadcast_to(label_row, (16, embed))], axis=0)
+    train_copies, valid_pack = call(
+        pack_kernel,
+        (
+            jax.ShapeDtypeStruct((col_size, train_embed.shape[0], embed + LANES), jnp.bfloat16),
+            jax.ShapeDtypeStruct((valid_embed.shape[0] + 16, embed), jnp.bfloat16),
+        ),
+        [
+            pltpu.SMEM(train_labels.shape, jnp.int32),
+            pltpu.VMEM(train_embed.shape, train_embed.dtype),
+            pltpu.VMEM((1,) + valid_labels.shape, jnp.int32),
+            pltpu.SemaphoreType.DMA((4,)),
+        ],
+        train_labels,
+        train_embed,
+        valid_embed,
+        valid_labels[None, :],
+        hbm=(0, 1, 2, 3),
+        limit=60,
+    )
+    train_all = exchange(train_copies, "col")
     pair = lax.all_gather(valid_pack, "zl", axis=0)
     steps = lax.axis_size("zh")
     turn = [[(i, (i + k) % steps) for i in range(steps)] for k in range(steps)]
@@ -221,7 +253,9 @@
     rows, cols = train_embed.shape[0] * col_size, valid_embed.shape[0] * row_size
     row_chunks, col_chunks = rows // LANES, cols // LANES
     classes = pair_level.shape[0]
-    levels = jnp.pad(pair_level, ((0, LANES - classes), (0, LANES - classes)), constant_values=-1)
+    level_ids = jnp.arange(level_cost.shape[0], dtype=jnp.int32)
+    chosen = (pair_level[:, :, None] == level_ids).astype(f32)
+    table = jnp.pad(jnp.sum(chosen * level_cost, axis=2), ((0, LANES - classes), (0, LANES - classes)))
     tile = jax.ShapeDtypeStruct((rows, cols), f32)
     row_copies = jax.ShapeDtypeStruct((col_size, row_chunks, LANES), f32)
     col_copies = jax.ShapeDtypeStruct((row_size, col_chunks, LANES), f32)
@@ -229,23 +263,13 @@
     col_shape = jax.ShapeDtypeStruct((col_chunks, LANES), f32)
     tall = [pltpu.VMEM((rows, LANES), f32)] * 2
     wide = [pltpu.VMEM((row_chunks * SUB, cols), f32)] * 2
-    prepared = call(
-        prepare_kernel,
-        (jax.ShapeDtypeStruct((rows, embed + 3 * LANES), jnp.bfloat16), jax.ShapeDtypeStruct((rows, LANES), f32)),
-        [],
-        train_all,
-        levels,
-        level_cost,
-        smem=(2,),
-        num_levels=level_cost.shape[0],
-        limit=16,
-    )
     cost, row_part, col_part = call(
         start_kernel,
         (tile, row_copies, col_copies),
-        tall + wide,
+        [pltpu.VMEM((rows, embed + 3 * LANES), jnp.bfloat16)] + tall + wide,
         where,
-        *prepared,
+        train_all,
+        table,
         mine,
         other,
         smem=(0,),

time: 166 us -> 163 us (0.982)
  other arithmetic: 3.02 us -> 0.37 us
  local copies, waits for them, and re-layouts: 2.34 us -> 0.02 us
  waiting for transfers between devices: 5.59 us -> 7.77 us
  transfers between devices with their start and end apart: 5 -> 5, of which waited for: 1 -> 3; matrix products, arithmetic and copies ran while one was open for 2% -> 0% of each run, Pallas kernels for 0% -> 0%
where the time goes in v8:
time: 163 us; the launch traced here: 162 us
  blocking collectives  110 us (67%)
  starting transfers between devices  30.3 us (19%)
  Pallas kernels  13.8 us (8%)
  waiting for transfers between devices  7.77 us (5%)
    all_to_all x8, blocking collectives, exchange(): return lax.all_to_all(copies, axis, 0, 0, tiled=True)  104 us
    ppermute x3, starting transfers between devices, shards(): lax.ppermute(pair, 'zh', turn[k])  17.3 us
    pallas_call x7, Pallas kernels, call(): pl.pallas_call(body, out_shape=out_shape, in_specs=specs, out_specs=[VMEM...  13.8 us
    all_to_all x1, starting transfers between devices, exchange(): return lax.all_to_all(copies, axis, 0, 0, tiled=True)  9.68 us
    all_gather x1, blocking collectives, shards(): pair = lax.all_gather(valid_pack, 'zl', axis=0)  5.59 us
    all_to_all x1, waiting for transfers between devices, exchange(): return lax.all_to_all(copies, axis, 0, 0, tiled=True)  4.87 us
  transfers between devices with their start and end apart: 5, of which 3 were waited for; matrix products, arithmetic and copies ran while one was open for 0% of the time, Pallas kernels for 0%

profile of v8, /device:TPU:1, one launch (start us, length us, event | category | flops | bytes accessed | tf_op | source)
XLA Modules:
  0.0 161.9 jit_solution(3854544721395934456)
XLA Ops:
  0.0 1.7 %shard_map.64 = (bf16[32,16,384]{2,1,0:T(8,128)(2,1)}, bf16[144,256]{1,0:T(8,128)(2,1)}) custom-call(s32[16]{0:T(128)} %train_label_hbm.1, bf16[16,256]{1,0:T(8,128)(2,1)} %train_hbm.1, bf16[128,256]{1,0:T(8,128)(2,1)} %valid_hbm.1, s32[1,128]{1,0:T(1,128)} %bitcast.16), custom_call_target="tpu_custom_call" | custom-call | flops 16777216 | bytes 4194304 | tf_op jit(solution)/shard_map/pallas_call | solution.py:212
  1.7 5.6 %all-gather = bf16[288,256]{1,0:T(8,128)(2,1)S(1)} all-gather(bf16[144,256]{1,0:T(8,128)(2,1)} %get-tuple-element.23), channel_id=2, replica_groups=mesh['zh'=4,'zl'=2,'core'=2,'col'=32] {'zl'}, dimensions={0}, use_global_device_ids=true | all-gather | bytes 221184 | tf_op jit(solution)/shard_map/all_gather | solution.py:247
  7.3 5.8 %collective-permute-start = (bf16[2,144,256]{2,1,0:T(8,128)(2,1)S(1)}, bf16[2,144,256]{2,1,0:T(8,128)(2,1)S(1)}, u32[]{:S(2)}, u32[]{:S(2)}) collective-permute-start(bf16[2,144,256]{2,1,0:T(8,128)(2,1)S(1)} %bitcast.9), channel_id=1, source_target_pairs={{0,128},{128,256},{256,384},{384,0},{1,129},{129,257},{257,385},{3... | collective-permute-start | bytes 442376 | tf_op jit(solution)/shard_map/ppermute | solution.py:250
  13.1 8.2 %collective-permute-start.1 = (bf16[2,144,256]{2,1,0:T(8,128)(2,1)S(1)}, bf16[2,144,256]{2,1,0:T(8,128)(2,1)S(1)}, u32[]{:S(2)}, u32[]{:S(2)}) collective-permute-start(bf16[2,144,256]{2,1,0:T(8,128)(2,1)S(1)} %bitcast.10), channel_id=1, source_target_pairs={{0,256},{128,384},{256,0},{384,128},{1,257},{129,385},{257,1},{385... | collective-permute-start | bytes 442376 | tf_op jit(solution)/shard_map/ppermute | solution.py:250
  21.3 3.4 %collective-permute-start.2 = (bf16[2,144,256]{2,1,0:T(8,128)(2,1)S(1)}, bf16[2,144,256]{2,1,0:T(8,128)(2,1)S(1)}, u32[]{:S(2)}, u32[]{:S(2)}) collective-permute-start(bf16[2,144,256]{2,1,0:T(8,128)(2,1)S(1)} %bitcast.11), channel_id=1, source_target_pairs={{0,384},{128,0},{256,128},{384,256},{1,385},{129,1},{257,129},{385... | collective-permute-start | bytes 442376 | tf_op jit(solution)/shard_map/ppermute | solution.py:250
  24.7 9.7 %all-to-all-start = ((bf16[32,16,384]{2,1,0:T(8,128)(2,1)}), bf16[32,16,384]{2,1,0:T(8,128)(2,1)S(1)}, u32[]{:S(2)}, u32[]{:S(2)}) async-start(bf16[32,16,384]{2,1,0:T(8,128)(2,1)} %get-tuple-element.22), calls=%async_computation | async-start | bytes 786432 | tf_op jit(solution)/shard_map/all_to_all | solution.py:205
  34.4 1.6 %collective-permute-done.2 = bf16[2,144,256]{2,1,0:T(8,128)(2,1)S(1)} collective-permute-done((bf16[2,144,256]{2,1,0:T(8,128)(2,1)S(1)}, bf16[2,144,256]{2,1,0:T(8,128)(2,1)S(1)}, u32[]{:S(2)}, u32[]{:S(2)}) %collective-permute-start.2) | collective-permute-done | bytes 147488 | tf_op jit(solution)/shard_map/ppermute | solution.py:250
  36.1 3.2 %collective-permute-start.3 = (bf16[4,2,144,256]{3,2,1,0:T(8,128)(2,1)S(1)}, bf16[4,2,144,256]{3,2,1,0:T(8,128)(2,1)S(1)}, u32[]{:S(2)}, u32[]{:S(2)}) collective-permute-start(bf16[4,2,144,256]{3,2,1,0:T(8,128)(2,1)S(1)} %pad_maximum_fusion.mine_ref), channel_id=1, source_target_pairs={{0,32},{32,0},{1,33},{33,1},{2,34},{34,2},{3,35},{35,3},{4,36},{36... | collective-permute-start | bytes 1769480 | tf_op jit(solution)/shard_map/ppermute | solution.py:251
  39.4 0.2 select_reduce_fusion
  39.7 1.3 collective-permute-done.3.other_ref
  41.0 4.9 %all-to-all-done.train_ref = bf16[32,16,384]{2,1,0:T(8,128)(2,1)S(1)} async-done(((bf16[32,16,384]{2,1,0:T(8,128)(2,1)}), bf16[32,16,384]{2,1,0:T(8,128)(2,1)S(1)}, u32[]{:S(2)}, u32[]{:S(2)}) %all-to-all-start) | async-done | bytes 393248 | tf_op jit(solution)/shard_map/all_to_all | solution.py:205
  45.8 5.3 %shard_map.65 = (f32[512,2048]{1,0:T(8,128)S(1)}, f32[32,4,128]{2,1,0:T(4,128)S(1)}, f32[16,16,128]{2,1,0:T(8,128)S(1)}) custom-call(s32[2]{0:T(128)S(1)} %pad_add_fusion.where_ref, bf16[32,16,384]{2,1,0:T(8,128)(2,1)S(1)} %all-to-all-done.train_ref, f32[128,128]{1,0:T(8,128)S(1)} %pad.4.table_ref, bf16[4,2,144,256]{3,2,1,0:T(8,128)(2,1)S(1)} %pad_maximum_fusion.mine_ref, ...), custom_call_target="tpu_custom_call" | custom-call | flops 16777216 | bytes 4194304 | tf_op jit(solution)/shard_map/pallas_call | solution.py:212
  51.1 14.4 %all_to_all.45.refs_1_ = f32[32,4,128]{2,1,0:T(4,128)S(1)} all-to-all(f32[32,4,128]{2,1,0:T(4,128)S(1)} %get-tuple-element.25), channel_id=1, replica_groups=mesh['zh'=4,'zl'=2,'core'=2,'col'=32] {'col'}, dimensions={0} | all-to-all | bytes 131072 | tf_op jit(solution)/shard_map/all_to_all | solution.py:205
  65.5 16.8 %all_to_all.46.refs_2_ = f32[16,16,128]{2,1,0:T(8,128)S(1)} all-to-all(f32[16,16,128]{2,1,0:T(8,128)S(1)} %get-tuple-element.26), channel_id=1, replica_groups=mesh['zh'=4,'zl'=2,'core'=2,'col'=32] {'zh','zl','core'}, dimensions={0} | all-to-all | bytes 262144 | tf_op jit(solution)/shard_map/all_to_all | solution.py:205
  82.3 2.3 %shard_map.66 = (f32[32,4,128]{2,1,0:T(4,128)S(1)}, f32[16,16,128]{2,1,0:T(8,128)S(1)}, f32[4,128]{1,0:T(4,128)S(1)}, f32[16,128]{1,0:T(8,128)S(1)}) custom-call(f32[512,2048]{1,0:T(8,128)S(1)} %get-tuple-element.24.refs_0_, f32[32,4,128]{2,1,0:T(4,128)S(1)} %all_to_all.45.refs_1_, f32[16,16,128]{2,1,0:T(8,128)S(1)} %all_to_all.46.refs_2_, ...), custom_call_target="tpu_custom_call" | custom-call | flops 16777216 | bytes 4194304 | tf_op jit(solution)/shard_map/pallas_call | solution.py:212
  84.6 12.3 %all_to_all.47.refs_1_ = f32[32,4,128]{2,1,0:T(4,128)S(1)} all-to-all(f32[32,4,128]{2,1,0:T(4,128)S(1)} %get-tuple-element.27), channel_id=1, replica_groups=mesh['zh'=4,'zl'=2,'core'=2,'col'=32] {'col'}, dimensions={0} | all-to-all | bytes 131072 | tf_op jit(solution)/shard_map/all_to_all | solution.py:205
  97.0 12.5 %all_to_all.48.refs_2_ = f32[16,16,128]{2,1,0:T(8,128)S(1)} all-to-all(f32[16,16,128]{2,1,0:T(8,128)S(1)} %get-tuple-element.28), channel_id=1, replica_groups=mesh['zh'=4,'zl'=2,'core'=2,'col'=32] {'zh','zl','core'}, dimensions={0} | all-to-all | bytes 262144 | tf_op jit(solution)/shard_map/all_to_all | solution.py:205
  109.5 2.3 %shard_map.67 = (f32[32,4,128]{2,1,0:T(4,128)S(1)}, f32[16,16,128]{2,1,0:T(8,128)S(1)}, f32[4,128]{1,0:T(4,128)S(1)}, f32[16,128]{1,0:T(8,128)S(1)}) custom-call(f32[512,2048]{1,0:T(8,128)S(1)} %get-tuple-element.24.refs_0_, f32[32,4,128]{2,1,0:T(4,128)S(1)} %all_to_all.47.refs_1_, f32[16,16,128]{2,1,0:T(8,128)S(1)} %all_to_all.48.refs_2_, ...), custom_call_target="tpu_custom_call" | custom-call | flops 16777216 | bytes 4194304 | tf_op jit(solution)/shard_map/pallas_call | solution.py:212
  111.8 12.3 %all_to_all.49.refs_1_ = f32[32,4,128]{2,1,0:T(4,128)S(1)} all-to-all(f32[32,4,128]{2,1,0:T(4,128)S(1)} %get-tuple-element.31), channel_id=1, replica_groups=mesh['zh'=4,'zl'=2,'core'=2,'col'=32] {'col'}, dimensions={0} | all-to-all | bytes 131072 | tf_op jit(solution)/shard_map/all_to_all | solution.py:205
  124.1 12.5 %all_to_all.50.refs_2_ = f32[16,16,128]{2,1,0:T(8,128)S(1)} all-to-all(f32[16,16,128]{2,1,0:T(8,128)S(1)} %get-tuple-element.32), channel_id=1, replica_groups=mesh['zh'=4,'zl'=2,'core'=2,'col'=32] {'zh','zl','core'}, dimensions={0} | all-to-all | bytes 262144 | tf_op jit(solution)/shard_map/all_to_all | solution.py:205
  136.7 1.4 shard_map.68
  138.0 12.3 %all_to_all.51.refs_0_ = f32[32,4,128]{2,1,0:T(4,128)S(1)} all-to-all(f32[32,4,128]{2,1,0:T(4,128)S(1)} %get-tuple-element.35), channel_id=1, replica_groups=mesh['zh'=4,'zl'=2,'core'=2,'col'=32] {'col'}, dimensions={0} | all-to-all | bytes 131072 | tf_op jit(solution)/shard_map/all_to_all | solution.py:205
  150.4 10.8 %all_to_all.52.refs_0_ = f32[16,4,128]{2,1,0:T(4,128)S(1)} all-to-all(f32[16,4,128]{2,1,0:T(4,128)S(1)} %get-tuple-element.37), channel_id=1, replica_groups=mesh['zh'=4,'zl'=2,'core'=2,'col'=32] {'zh','zl','core'}, dimensions={0} | all-to-all | bytes 65536 | tf_op jit(solution)/shard_map/all_to_all | solution.py:205
  161.2 0.7 shard_map.70
  (12 shorter events, 0.2 us)
Async XLA Ops:
  0.0 39.4 %copy-start = (s32[100,100]{1,0:T(8,128)S(1)}, s32[100,100]{1,0:T(8,128)}, u32[]{:S(2)}) copy-start(s32[100,100]{1,0:T(8,128)} %param.10) | copy-start | bytes 120004
  0.0 39.4 %copy-start.1 = (f32[4]{0:T(128)S(1)}, f32[4]{0:T(128)}, u32[]{:S(2)}) copy-start(f32[4]{0:T(128)} %param.11) | copy-start | bytes 52
  7.3 27.1 %collective-permute-start = (bf16[2,144,256]{2,1,0:T(8,128)(2,1)S(1)}, bf16[2,144,256]{2,1,0:T(8,128)(2,1)S(1)}, u32[]{:S(2)}, u32[]{:S(2)}) collective-permute-start(bf16[2,144,256]{2,1,0:T(8,128)(2,1)S(1)} %bitcast.9), channel_id=1, source_target_pairs={{0,128},{128,256},{256,384},{384,0},{1,129},{129,257},{257,385},{3... | collective-permute-start | bytes 442376 | tf_op jit(solution)/shard_map/ppermute | solution.py:250
  13.1 21.3 %collective-permute-start.1 = (bf16[2,144,256]{2,1,0:T(8,128)(2,1)S(1)}, bf16[2,144,256]{2,1,0:T(8,128)(2,1)S(1)}, u32[]{:S(2)}, u32[]{:S(2)}) collective-permute-start(bf16[2,144,256]{2,1,0:T(8,128)(2,1)S(1)} %bitcast.10), channel_id=1, source_target_pairs={{0,256},{128,384},{256,0},{384,128},{1,257},{129,385},{257,1},{385... | collective-permute-start | bytes 442376 | tf_op jit(solution)/shard_map/ppermute | solution.py:250
  21.3 14.7 %collective-permute-start.2 = (bf16[2,144,256]{2,1,0:T(8,128)(2,1)S(1)}, bf16[2,144,256]{2,1,0:T(8,128)(2,1)S(1)}, u32[]{:S(2)}, u32[]{:S(2)}) collective-permute-start(bf16[2,144,256]{2,1,0:T(8,128)(2,1)S(1)} %bitcast.11), channel_id=1, source_target_pairs={{0,384},{128,0},{256,128},{384,256},{1,385},{129,1},{257,129},{385... | collective-permute-start | bytes 442376 | tf_op jit(solution)/shard_map/ppermute | solution.py:250
  24.7 21.2 %all-to-all-start = ((bf16[32,16,384]{2,1,0:T(8,128)(2,1)}), bf16[32,16,384]{2,1,0:T(8,128)(2,1)S(1)}, u32[]{:S(2)}, u32[]{:S(2)}) async-start(bf16[32,16,384]{2,1,0:T(8,128)(2,1)} %get-tuple-element.22), calls=%async_computation | async-start | bytes 786432 | tf_op jit(solution)/shard_map/all_to_all | solution.py:205
  36.1 4.9 %collective-permute-start.3 = (bf16[4,2,144,256]{3,2,1,0:T(8,128)(2,1)S(1)}, bf16[4,2,144,256]{3,2,1,0:T(8,128)(2,1)S(1)}, u32[]{:S(2)}, u32[]{:S(2)}) collective-permute-start(bf16[4,2,144,256]{3,2,1,0:T(8,128)(2,1)S(1)} %pad_maximum_fusion.mine_ref), channel_id=1, source_target_pairs={{0,32},{32,0},{1,33},{33,1},{2,34},{34,2},{3,35},{35,3},{4,36},{36... | collective-permute-start | bytes 1769480 | tf_op jit(solution)/shard_map/ppermute | solution.py:251

commit v9 on v8

--- a/solution.py
+++ b/solution.py
@@ -127,9 +127,10 @@
 
 
 def start_kernel(
-    where_ref, train_ref, table_ref, mine_ref, other_ref, cost_ref, row_out, col_out, left_ref, row_a, row_b, col_a, col_b
+    where_ref, train_ref, table_ref, own_ref, core_ref, beside_ref, both_ref, cost_ref, row_out, col_out, left_ref, row_a, row_b, col_a, col_b
 ):
-    steps, sides, block_rows, embed = mine_ref.shape
+    steps, _, embed = own_ref.shape
+    sides = 2
     packed = train_ref[...].reshape(cost_ref.shape[0], embed + LANES)
     train = packed[:, :embed]
     wide = train.astype(jnp.float32)
@@ -146,8 +147,11 @@
     for pair in range(2 * steps):
         core, z_pair = divmod(pair, steps)
         back = lax.rem(where_ref[0] - z_pair + steps, steps)
-        own = where_ref[1] == core
-        blocks = [jnp.where(own, mine_ref[back, side], other_ref[back, side]) for side in range(sides)]
+        same_core = where_ref[2] == core
+        near = jnp.where(same_core, own_ref[back], core_ref[back])
+        far = jnp.where(same_core, beside_ref[back], both_ref[back])
+        even = where_ref[1] == 0
+        blocks = [jnp.where(even, near, far), jnp.where(even, far, near)]
         block = jnp.concatenate([b[:LANES, :] for b in blocks], axis=0)
         label_rows = [b[LANES:, :LANES].astype(jnp.float32)[:1, :] for b in blocks]
         hots = [jnp.where(class_ids == label_row, 1.0, 0.0).astype(jnp.bfloat16) for label_row in label_rows]
@@ -244,12 +248,13 @@
         limit=60,
     )
     train_all = exchange(train_copies, "col")
-    pair = lax.all_gather(valid_pack, "zl", axis=0)
     steps = lax.axis_size("zh")
     turn = [[(i, (i + k) % steps) for i in range(steps)] for k in range(steps)]
-    mine = jnp.stack([pair] + [lax.ppermute(pair, "zh", turn[k]) for k in range(1, steps)])
-    other = lax.ppermute(mine, "core", [(0, 1), (1, 0)])
-    where = jnp.stack([lax.axis_index("zh"), lax.axis_index("core")]).astype(jnp.int32)
+    swap = [(0, 1), (1, 0)]
+    own = jnp.stack([valid_pack] + [lax.ppermute(valid_pack, "zh", turn[k]) for k in range(1, steps)])
+    beside = lax.ppermute(own, "zl", swap)
+    valid_all = (own, lax.ppermute(own, "core", swap), beside, lax.ppermute(beside, "core", swap))
+    where = jnp.stack([lax.axis_index(axis) for axis in ROW]).astype(jnp.int32)
     rows, cols = train_embed.shape[0] * col_size, valid_embed.shape[0] * row_size
     row_chunks, col_chunks = rows // LANES, cols // LANES
     classes = pair_level.shape[0]
@@ -270,8 +275,7 @@
         where,
         train_all,
         table,
-        mine,
-        other,
+        *valid_all,
         smem=(0,),
         limit=16,
     )

time: 163 us -> 163 us (level)
  starting transfers between devices: 30.3 us -> 40.2 us
  waiting for transfers between devices: 7.77 us -> 1.54 us
  blocking collectives: 110 us -> 105 us
  other arithmetic: 0.37 us -> 2.06 us
    ppermute x4 -> x6, starting transfers between devices: 20.6 us -> 30.6 us  [the longest x3 18.9 us: shards(): lax.ppermute(valid_pack, 'zh', turn[k])]
    all_gather x1 -> x0, blocking collectives: 5.59 us -> none  [shards(): pair = lax.all_gather(valid_pack, 'zl', axis=0)]
    all_to_all x1, waiting for transfers between devices: 4.87 us -> 0.01 us  [exchange(): return lax.all_to_all(copies, axis, 0, 0, tiled=True)]
  transfers between devices with their start and end apart: 5 -> 7, of which waited for: 3 -> 1; matrix products, arithmetic and copies ran while one was open for 0% -> 1% of each run, Pallas kernels for 0% -> 0%
where the time goes in v9:
time: 163 us
  blocking collectives  105 us (64%)
  starting transfers between devices  40.2 us (25%)
  Pallas kernels  13.8 us (8%)
  other arithmetic  2.06 us (1%)
    all_to_all x8, blocking collectives, exchange(): return lax.all_to_all(copies, axis, 0, 0, tiled=True)  105 us
    ppermute x3, starting transfers between devices, shards(): lax.ppermute(valid_pack, 'zh', turn[k])  18.9 us
    pallas_call x7, Pallas kernels, call(): pl.pallas_call(body, out_shape=out_shape, in_specs=specs, out_specs=[VMEM...  13.8 us
    all_to_all x1, starting transfers between devices, exchange(): return lax.all_to_all(copies, axis, 0, 0, tiled=True)  9.68 us
    ppermute x1, starting transfers between devices, shards(): lax.ppermute(beside, 'core', swap)  4.62 us
    ppermute x1, starting transfers between devices, shards(): lax.ppermute(own, 'core', swap)  3.98 us
  transfers between devices with their start and end apart: 7, of which 1 were waited for; matrix products, arithmetic and copies ran while one was open for 1% of the time, Pallas kernels for 0%

profile of v9, /device:TPU:1, one launch (start us, length us, event | category | flops | bytes accessed | tf_op | source)
XLA Modules:
  0.0 162.5 jit_solution(520375769709978282)
XLA Ops:
  0.0 1.7 %shard_map.64 = (bf16[32,16,384]{2,1,0:T(8,128)(2,1)}, bf16[144,256]{1,0:T(8,128)(2,1)}) custom-call(s32[16]{0:T(128)} %train_label_hbm.1, bf16[16,256]{1,0:T(8,128)(2,1)} %train_hbm.1, bf16[128,256]{1,0:T(8,128)(2,1)} %valid_hbm.1, s32[1,128]{1,0:T(1,128)} %bitcast.13), custom_call_target="tpu_custom_call" | custom-call | flops 16777216 | bytes 4194304 | tf_op jit(solution)/shard_map/pallas_call | solution.py:216
  1.7 6.6 %collective-permute-start = (bf16[144,256]{1,0:T(8,128)(2,1)}, bf16[144,256]{1,0:T(8,128)(2,1)S(1)}, u32[]{:S(2)}, u32[]{:S(2)}) collective-permute-start(bf16[144,256]{1,0:T(8,128)(2,1)} %get-tuple-element.23), channel_id=1, source_target_pairs={{0,128},{128,256},{256,384},{384,0},{1,129},{129,257},{257,385},{3... | collective-permute-start | bytes 221192 | tf_op jit(solution)/shard_map/ppermute | solution.py:254
  8.4 8.8 %collective-permute-start.1 = (bf16[144,256]{1,0:T(8,128)(2,1)}, bf16[144,256]{1,0:T(8,128)(2,1)S(1)}, u32[]{:S(2)}, u32[]{:S(2)}) collective-permute-start(bf16[144,256]{1,0:T(8,128)(2,1)} %get-tuple-element.23), channel_id=1, source_target_pairs={{0,256},{128,384},{256,0},{384,128},{1,257},{129,385},{257,1},{385... | collective-permute-start | bytes 221192 | tf_op jit(solution)/shard_map/ppermute | solution.py:254
  17.2 3.4 %collective-permute-start.2 = (bf16[144,256]{1,0:T(8,128)(2,1)}, bf16[144,256]{1,0:T(8,128)(2,1)S(1)}, u32[]{:S(2)}, u32[]{:S(2)}) collective-permute-start(bf16[144,256]{1,0:T(8,128)(2,1)} %get-tuple-element.23), channel_id=1, source_target_pairs={{0,384},{128,0},{256,128},{384,256},{1,385},{129,1},{257,129},{385... | collective-permute-start | bytes 221192 | tf_op jit(solution)/shard_map/ppermute | solution.py:254
  20.6 9.7 %all-to-all-start = ((bf16[32,16,384]{2,1,0:T(8,128)(2,1)}), bf16[32,16,384]{2,1,0:T(8,128)(2,1)S(1)}, u32[]{:S(2)}, u32[]{:S(2)}) async-start(bf16[32,16,384]{2,1,0:T(8,128)(2,1)} %get-tuple-element.22), calls=%async_computation | async-start | bytes 786432 | tf_op jit(solution)/shard_map/all_to_all | solution.py:209
  30.3 0.9 pad_maximum_fusion.own_ref
  31.2 3.1 %collective-permute-start.4 = (bf16[4,144,256]{2,1,0:T(8,128)(2,1)S(1)}, bf16[4,144,256]{2,1,0:T(8,128)(2,1)S(1)}, u32[]{:S(2)}, u32[]{:S(2)}) collective-permute-start(bf16[4,144,256]{2,1,0:T(8,128)(2,1)S(1)} %pad_maximum_fusion.own_ref), channel_id=1, source_target_pairs={{0,64},{64,0},{1,65},{65,1},{2,66},{66,2},{3,67},{67,3},{4,68},{68... | collective-permute-start | bytes 884744 | tf_op jit(solution)/shard_map/ppermute | solution.py:255
  34.4 4.0 %collective-permute-start.3 = (bf16[4,144,256]{2,1,0:T(8,128)(2,1)S(1)}, bf16[4,144,256]{2,1,0:T(8,128)(2,1)S(1)}, u32[]{:S(2)}, u32[]{:S(2)}) collective-permute-start(bf16[4,144,256]{2,1,0:T(8,128)(2,1)S(1)} %pad_maximum_fusion.own_ref), channel_id=1, source_target_pairs={{0,32},{32,0},{1,33},{33,1},{2,34},{34,2},{3,35},{35,3},{4,36},{36... | collective-permute-start | bytes 884744 | tf_op jit(solution)/shard_map/ppermute | solution.py:256
  38.3 1.5 collective-permute-done.4.beside_ref
  39.8 4.6 %collective-permute-start.5 = (bf16[4,144,256]{2,1,0:T(8,128)(2,1)S(1)}, bf16[4,144,256]{2,1,0:T(8,128)(2,1)S(1)}, u32[]{:S(2)}, u32[]{:S(2)}) collective-permute-start(bf16[4,144,256]{2,1,0:T(8,128)(2,1)S(1)} %collective-permute-done.4.beside_ref), channel_id=1, source_target_pairs={{0,32},{32,0},{1,33},{33,1},{2,34},{34,2},{3,35},{35,3},{4,36},{36... | collective-permute-start | bytes 884744 | tf_op jit(solution)/shard_map/ppermute | solution.py:256
  44.5 1.1 select_reduce_fusion
  45.7 5.3 %shard_map.65 = (f32[512,2048]{1,0:T(8,128)S(1)}, f32[32,4,128]{2,1,0:T(4,128)S(1)}, f32[16,16,128]{2,1,0:T(8,128)S(1)}) custom-call(s32[3]{0:T(128)S(1)} %pad_add_fusion.where_ref, bf16[32,16,384]{2,1,0:T(8,128)(2,1)S(1)} %all-to-all-done.train_ref, f32[128,128]{1,0:T(8,128)S(1)} %pad.4.table_ref, bf16[4,144,256]{2,1,0:T(8,128)(2,1)S(1)} %pad_maximum_fusion.own_ref, ...), custom_call_target="tpu_custom_call" | custom-call | flops 16777216 | bytes 4194304 | tf_op jit(solution)/shard_map/pallas_call | solution.py:216
  50.9 17.8 %all_to_all.45.refs_1_ = f32[32,4,128]{2,1,0:T(4,128)S(1)} all-to-all(f32[32,4,128]{2,1,0:T(4,128)S(1)} %get-tuple-element.25), channel_id=1, replica_groups=mesh['zh'=4,'zl'=2,'core'=2,'col'=32] {'col'}, dimensions={0} | all-to-all | bytes 131072 | tf_op jit(solution)/shard_map/all_to_all | solution.py:209
  68.8 14.2 %all_to_all.46.refs_2_ = f32[16,16,128]{2,1,0:T(8,128)S(1)} all-to-all(f32[16,16,128]{2,1,0:T(8,128)S(1)} %get-tuple-element.26), channel_id=1, replica_groups=mesh['zh'=4,'zl'=2,'core'=2,'col'=32] {'zh','zl','core'}, dimensions={0} | all-to-all | bytes 262144 | tf_op jit(solution)/shard_map/all_to_all | solution.py:209
  83.0 2.3 %shard_map.66 = (f32[32,4,128]{2,1,0:T(4,128)S(1)}, f32[16,16,128]{2,1,0:T(8,128)S(1)}, f32[4,128]{1,0:T(4,128)S(1)}, f32[16,128]{1,0:T(8,128)S(1)}) custom-call(f32[512,2048]{1,0:T(8,128)S(1)} %get-tuple-element.24.refs_0_, f32[32,4,128]{2,1,0:T(4,128)S(1)} %all_to_all.45.refs_1_, f32[16,16,128]{2,1,0:T(8,128)S(1)} %all_to_all.46.refs_2_, ...), custom_call_target="tpu_custom_call" | custom-call | flops 16777216 | bytes 4194304 | tf_op jit(solution)/shard_map/pallas_call | solution.py:216
  85.3 12.3 %all_to_all.47.refs_1_ = f32[32,4,128]{2,1,0:T(4,128)S(1)} all-to-all(f32[32,4,128]{2,1,0:T(4,128)S(1)} %get-tuple-element.27), channel_id=1, replica_groups=mesh['zh'=4,'zl'=2,'core'=2,'col'=32] {'col'}, dimensions={0} | all-to-all | bytes 131072 | tf_op jit(solution)/shard_map/all_to_all | solution.py:209
  97.6 12.5 %all_to_all.48.refs_2_ = f32[16,16,128]{2,1,0:T(8,128)S(1)} all-to-all(f32[16,16,128]{2,1,0:T(8,128)S(1)} %get-tuple-element.28), channel_id=1, replica_groups=mesh['zh'=4,'zl'=2,'core'=2,'col'=32] {'zh','zl','core'}, dimensions={0} | all-to-all | bytes 262144 | tf_op jit(solution)/shard_map/all_to_all | solution.py:209
  110.1 2.3 %shard_map.67 = (f32[32,4,128]{2,1,0:T(4,128)S(1)}, f32[16,16,128]{2,1,0:T(8,128)S(1)}, f32[4,128]{1,0:T(4,128)S(1)}, f32[16,128]{1,0:T(8,128)S(1)}) custom-call(f32[512,2048]{1,0:T(8,128)S(1)} %get-tuple-element.24.refs_0_, f32[32,4,128]{2,1,0:T(4,128)S(1)} %all_to_all.47.refs_1_, f32[16,16,128]{2,1,0:T(8,128)S(1)} %all_to_all.48.refs_2_, ...), custom_call_target="tpu_custom_call" | custom-call | flops 16777216 | bytes 4194304 | tf_op jit(solution)/shard_map/pallas_call | solution.py:216
  112.4 12.3 %all_to_all.49.refs_1_ = f32[32,4,128]{2,1,0:T(4,128)S(1)} all-to-all(f32[32,4,128]{2,1,0:T(4,128)S(1)} %get-tuple-element.31), channel_id=1, replica_groups=mesh['zh'=4,'zl'=2,'core'=2,'col'=32] {'col'}, dimensions={0} | all-to-all | bytes 131072 | tf_op jit(solution)/shard_map/all_to_all | solution.py:209
  124.7 12.5 %all_to_all.50.refs_2_ = f32[16,16,128]{2,1,0:T(8,128)S(1)} all-to-all(f32[16,16,128]{2,1,0:T(8,128)S(1)} %get-tuple-element.32), channel_id=1, replica_groups=mesh['zh'=4,'zl'=2,'core'=2,'col'=32] {'zh','zl','core'}, dimensions={0} | all-to-all | bytes 262144 | tf_op jit(solution)/shard_map/all_to_all | solution.py:209
  137.3 1.4 shard_map.68
  138.7 12.3 %all_to_all.51.refs_0_ = f32[32,4,128]{2,1,0:T(4,128)S(1)} all-to-all(f32[32,4,128]{2,1,0:T(4,128)S(1)} %get-tuple-element.35), channel_id=1, replica_groups=mesh['zh'=4,'zl'=2,'core'=2,'col'=32] {'col'}, dimensions={0} | all-to-all | bytes 131072 | tf_op jit(solution)/shard_map/all_to_all | solution.py:209
  151.0 10.8 %all_to_all.52.refs_0_ = f32[16,4,128]{2,1,0:T(4,128)S(1)} all-to-all(f32[16,4,128]{2,1,0:T(4,128)S(1)} %get-tuple-element.37), channel_id=1, replica_groups=mesh['zh'=4,'zl'=2,'core'=2,'col'=32] {'zh','zl','core'}, dimensions={0} | all-to-all | bytes 65536 | tf_op jit(solution)/shard_map/all_to_all | solution.py:209
  161.8 0.7 shard_map.70
  (11 shorter events, 0.2 us)
Async XLA Ops:
  1.7 28.6 %collective-permute-start = (bf16[144,256]{1,0:T(8,128)(2,1)}, bf16[144,256]{1,0:T(8,128)(2,1)S(1)}, u32[]{:S(2)}, u32[]{:S(2)}) collective-permute-start(bf16[144,256]{1,0:T(8,128)(2,1)} %get-tuple-element.23), channel_id=1, source_target_pairs={{0,128},{128,256},{256,384},{384,0},{1,129},{129,257},{257,385},{3... | collective-permute-start | bytes 221192 | tf_op jit(solution)/shard_map/ppermute | solution.py:254
  8.4 21.9 %collective-permute-start.1 = (bf16[144,256]{1,0:T(8,128)(2,1)}, bf16[144,256]{1,0:T(8,128)(2,1)S(1)}, u32[]{:S(2)}, u32[]{:S(2)}) collective-permute-start(bf16[144,256]{1,0:T(8,128)(2,1)} %get-tuple-element.23), channel_id=1, source_target_pairs={{0,256},{128,384},{256,0},{384,128},{1,257},{129,385},{257,1},{385... | collective-permute-start | bytes 221192 | tf_op jit(solution)/shard_map/ppermute | solution.py:254
  17.2 13.1 %collective-permute-start.2 = (bf16[144,256]{1,0:T(8,128)(2,1)}, bf16[144,256]{1,0:T(8,128)(2,1)S(1)}, u32[]{:S(2)}, u32[]{:S(2)}) collective-permute-start(bf16[144,256]{1,0:T(8,128)(2,1)} %get-tuple-element.23), channel_id=1, source_target_pairs={{0,384},{128,0},{256,128},{384,256},{1,385},{129,1},{257,129},{385... | collective-permute-start | bytes 221192 | tf_op jit(solution)/shard_map/ppermute | solution.py:254
  20.6 25.1 %all-to-all-start = ((bf16[32,16,384]{2,1,0:T(8,128)(2,1)}), bf16[32,16,384]{2,1,0:T(8,128)(2,1)S(1)}, u32[]{:S(2)}, u32[]{:S(2)}) async-start(bf16[32,16,384]{2,1,0:T(8,128)(2,1)} %get-tuple-element.22), calls=%async_computation | async-start | bytes 786432 | tf_op jit(solution)/shard_map/all_to_all | solution.py:209
  31.2 8.6 %collective-permute-start.4 = (bf16[4,144,256]{2,1,0:T(8,128)(2,1)S(1)}, bf16[4,144,256]{2,1,0:T(8,128)(2,1)S(1)}, u32[]{:S(2)}, u32[]{:S(2)}) collective-permute-start(bf16[4,144,256]{2,1,0:T(8,128)(2,1)S(1)} %pad_maximum_fusion.own_ref), channel_id=1, source_target_pairs={{0,64},{64,0},{1,65},{65,1},{2,66},{66,2},{3,67},{67,3},{4,68},{68... | collective-permute-start | bytes 884744 | tf_op jit(solution)/shard_map/ppermute | solution.py:255
  34.4 11.3 %collective-permute-start.3 = (bf16[4,144,256]{2,1,0:T(8,128)(2,1)S(1)}, bf16[4,144,256]{2,1,0:T(8,128)(2,1)S(1)}, u32[]{:S(2)}, u32[]{:S(2)}) collective-permute-start(bf16[4,144,256]{2,1,0:T(8,128)(2,1)S(1)} %pad_maximum_fusion.own_ref), channel_id=1, source_target_pairs={{0,32},{32,0},{1,33},{33,1},{2,34},{34,2},{3,35},{35,3},{4,36},{36... | collective-permute-start | bytes 884744 | tf_op jit(solution)/shard_map/ppermute | solution.py:256
  39.8 5.8 %collective-permute-start.5 = (bf16[4,144,256]{2,1,0:T(8,128)(2,1)S(1)}, bf16[4,144,256]{2,1,0:T(8,128)(2,1)S(1)}, u32[]{:S(2)}, u32[]{:S(2)}) collective-permute-start(bf16[4,144,256]{2,1,0:T(8,128)(2,1)S(1)} %collective-permute-done.4.beside_ref), channel_id=1, source_target_pairs={{0,32},{32,0},{1,33},{33,1},{2,34},{34,2},{3,35},{35,3},{4,36},{36... | collective-permute-start | bytes 884744 | tf_op jit(solution)/shard_map/ppermute | solution.py:256

commit v10 on v8

--- a/solution.py
+++ b/solution.py
@@ -15,6 +15,7 @@
 UNIT = entropy_scale * math.log(2.0)
 
 ROW = ("zh", "zl", "core")
+COL = ("y", "x")
 
 VMEM = pl.BlockSpec(memory_space=pltpu.VMEM)
 
@@ -127,7 +128,7 @@
 
 
 def start_kernel(
-    where_ref, train_ref, table_ref, mine_ref, other_ref, cost_ref, row_out, col_out, left_ref, row_a, row_b, col_a, col_b
+    where_ref, train_ref, table_ref, mine_ref, other_ref, cost_ref, partial_ref, left_ref, row_a, row_b, col_a, col_b
 ):
     steps, sides, block_rows, embed = mine_ref.shape
     packed = train_ref[...].reshape(cost_ref.shape[0], embed + LANES)
@@ -146,7 +147,7 @@
     for pair in range(2 * steps):
         core, z_pair = divmod(pair, steps)
         back = lax.rem(where_ref[0] - z_pair + steps, steps)
-        own = where_ref[1] == core
+        own = where_ref[2] == core
         blocks = [jnp.where(own, mine_ref[back, side], other_ref[back, side]) for side in range(sides)]
         block = jnp.concatenate([b[:LANES, :] for b in blocks], axis=0)
         label_rows = [b[LANES:, :LANES].astype(jnp.float32)[:1, :] for b in blocks]
@@ -161,36 +162,70 @@
         cost = cost + dot(left_ref[:, embed:], jnp.concatenate([hot] * table_parts, axis=0), ((1,), (0,)))
         here = slice(pair * step, (pair + 1) * step)
         cost_ref[:, here] = (cost + (train_sq + block_sq * (1.0 / embed))) * (1.0 / UNIT)
-    row_out[...] = jnp.broadcast_to(row_partial(cost_ref, None, row_a, row_b)[None], row_out.shape)
-    col_out[...] = jnp.broadcast_to(col_partial(cost_ref, None, col_a, col_b)[None], col_out.shape)
-
-
-def updated(pot_ref, parts_ref, offset):
-    return 0.5 * (pot_ref[...] + (offset - lse_lead(parts_ref[...])))
+    put_partials(partial_ref, row_partial(cost_ref, None, row_a, row_b), col_partial(cost_ref, None, col_a, col_b))
+
+
+def put_partials(out_ref, row, col):
+    unused = jnp.zeros((out_ref.shape[0] - col.shape[0] - row.shape[0], LANES), jnp.float32)
+    out_ref[...] = jnp.concatenate([col, row, unused], axis=0)
+
+
+def share_kernel(where_ref, partials_ref, out_ref, *, row_chunks):
+    _, chunks, _ = out_ref.shape
+    rows = [partials_ref[core, chunks : chunks + row_chunks, :] for core in range(2)]
+    unused = jnp.zeros((chunks - 2 * row_chunks, LANES), jnp.float32)
+    row_side = jnp.concatenate(rows + [unused], axis=0)
+    col_side = lse_lead(partials_ref[:, :chunks, :])
+    out_ref[...] = jnp.broadcast_to(jnp.where(where_ref[2] == 0, row_side, col_side)[None], out_ref.shape)
+
+
+def settle_kernel(where_ref, parts_ref, out_ref, *, lines):
+    parts = []
+    for k in range(parts_ref.shape[0]):
+        wanted = jnp.logical_or(where_ref[2] == 0, where_ref[3] == k % lines)
+        parts.append(jnp.where(wanted, parts_ref[k], -jnp.inf))
+    high = parts[0]
+    for part in parts[1:]:
+        high = jnp.maximum(high, part)
+    total = jnp.exp2(parts[0] - high)
+    for part in parts[1:]:
+        total = total + jnp.exp2(part - high)
+    out_ref[...] = high + jnp.log2(total)
+
+
+def updated(pot_ref, lse, offset):
+    return 0.5 * (pot_ref[...] + (offset - lse))
+
+
+def both_updated(where_ref, lse_ref, row_pot, col_pot, row_offset, col_offset):
+    chunks = row_pot.shape[0]
+    rows = jnp.where(where_ref[2] == 0, lse_ref[0, :chunks, :], lse_ref[0, chunks : 2 * chunks, :])
+    return updated(row_pot, rows, row_offset), updated(col_pot, lse_ref[1], col_offset)
 
 
 def both_kernel(
-    cost_ref, row_parts, col_parts, row_pot, col_pot, row_out, col_out, row_new, col_new, row_a, row_b, col_a, col_b,
-    spread_ref, *, row_offset, col_offset
+    where_ref, cost_ref, lse_ref, row_pot, col_pot, partial_ref, row_new, col_new, row_a, row_b, col_a, col_b, spread_ref,
+    *, row_offset, col_offset
 ):
-    row, col = updated(row_pot, row_parts, row_offset), updated(col_pot, col_parts, col_offset)
+    row, col = both_updated(where_ref, lse_ref, row_pot, col_pot, row_offset, col_offset)
     row_new[...] = row
     col_new[...] = col
     spread_rows(row, spread_ref)
+    put_partials(
+        partial_ref, row_partial(cost_ref, col, row_a, row_b), col_partial(cost_ref, spread_ref, col_a, col_b)
+    )
+
+
+def last_row_kernel(
+    where_ref, cost_ref, lse_ref, row_pot, col_pot, row_out, row_new, row_a, row_b, *, row_offset, col_offset
+):
+    row, col = both_updated(where_ref, lse_ref, row_pot, col_pot, row_offset, col_offset)
+    row_new[...] = row
     row_out[...] = jnp.broadcast_to(row_partial(cost_ref, col, row_a, row_b)[None], row_out.shape)
-    col_out[...] = jnp.broadcast_to(col_partial(cost_ref, spread_ref, col_a, col_b)[None], col_out.shape)
-
-
-def last_row_kernel(
-    cost_ref, row_parts, col_parts, row_pot, col_pot, row_out, row_new, row_a, row_b, *, row_offset, col_offset
-):
-    row_new[...] = updated(row_pot, row_parts, row_offset)
-    col = updated(col_pot, col_parts, col_offset)
-    row_out[...] = jnp.broadcast_to(row_partial(cost_ref, col, row_a, row_b)[None], row_out.shape)
 
 
 def last_kernel(parts_ref, pot_ref, out_ref, copies_ref, *, offset):
-    pot = updated(pot_ref, parts_ref, offset)
+    pot = updated(pot_ref, lse_lead(parts_ref[...]), offset)
     out_ref[...] = pot
     copies_ref[...] = jnp.broadcast_to(pot[None], copies_ref.shape)
 
@@ -203,6 +238,18 @@
 def exchange(block, axis):
     copies = block if block.ndim == 3 else jnp.broadcast_to(block[None], (lax.axis_size(axis),) + block.shape)
     return lax.all_to_all(copies, axis, 0, 0, tiled=True)
+
+
+def core_groups():
+    z_size, y_size, x_size = lax.axis_size(ROW[:2]), lax.axis_size("y"), lax.axis_size("x")
+
+    def index(z, core, y, x):
+        return ((z * 2 + core) * y_size + y) * x_size + x
+
+    ys, xs, zs = range(y_size), range(x_size), range(z_size)
+    over_yx = [[index(z, 0, y, x) for y in ys for x in xs] for z in zs]
+    over_zx = [[index(z, 1, y, x) for z in zs for x in xs] for y in ys]
+    return over_yx + over_zx
 
 
 def call(kernel, out_shape, scratch, *args, smem=(), hbm=(), limit=8, **static):
@@ -221,7 +268,7 @@
 
 
 def shards(train_embed, valid_embed, train_labels, valid_labels, pair_level, level_cost):
-    row_size, col_size = lax.axis_size(ROW), lax.axis_size("col")
+    row_size, col_size = lax.axis_size(ROW), lax.axis_size(COL)
     f32 = jnp.float32
     embed = train_embed.shape[1]
     train_copies, valid_pack = call(
@@ -243,13 +290,13 @@
         hbm=(0, 1, 2, 3),
         limit=60,
     )
-    train_all = exchange(train_copies, "col")
+    train_all = exchange(train_copies, COL)
     pair = lax.all_gather(valid_pack, "zl", axis=0)
     steps = lax.axis_size("zh")
     turn = [[(i, (i + k) % steps) for i in range(steps)] for k in range(steps)]
     mine = jnp.stack([pair] + [lax.ppermute(pair, "zh", turn[k]) for k in range(1, steps)])
     other = lax.ppermute(mine, "core", [(0, 1), (1, 0)])
-    where = jnp.stack([lax.axis_index("zh"), lax.axis_index("core")]).astype(jnp.int32)
+    where = jnp.stack([lax.axis_index(axis) for axis in ROW + ("x",)]).astype(jnp.int32)
     rows, cols = train_embed.shape[0] * col_size, valid_embed.shape[0] * row_size
     row_chunks, col_chunks = rows // LANES, cols // LANES
     classes = pair_level.shape[0]
@@ -258,14 +305,15 @@
     table = jnp.pad(jnp.sum(chosen * level_cost, axis=2), ((0, LANES - classes), (0, LANES - classes)))
     tile = jax.ShapeDtypeStruct((rows, cols), f32)
     row_copies = jax.ShapeDtypeStruct((col_size, row_chunks, LANES), f32)
-    col_copies = jax.ShapeDtypeStruct((row_size, col_chunks, LANES), f32)
+    part_shape = jax.ShapeDtypeStruct((-(-(row_chunks + col_chunks) // SUB) * SUB, LANES), f32)
+    sent_shape = jax.ShapeDtypeStruct((col_size, col_chunks, LANES), f32)
     row_shape = jax.ShapeDtypeStruct((row_chunks, LANES), f32)
     col_shape = jax.ShapeDtypeStruct((col_chunks, LANES), f32)
     tall = [pltpu.VMEM((rows, LANES), f32)] * 2
     wide = [pltpu.VMEM((row_chunks * SUB, cols), f32)] * 2
-    cost, row_part, col_part = call(
+    cost, partials = call(
         start_kernel,
-        (tile, row_copies, col_copies),
+        (tile, part_shape),
         [pltpu.VMEM((rows, embed + 3 * LANES), jnp.bfloat16)] + tall + wide,
         where,
         train_all,
@@ -279,17 +327,20 @@
     offsets = {"row_offset": math.log2(full_cols), "col_offset": math.log2(full_rows)}
     row_pot = jnp.zeros(row_shape.shape, f32)
     col_pot = jnp.zeros(col_shape.shape, f32)
+    groups = core_groups()
     for iteration in range(ITERS - 1):
-        row_got = exchange(row_part, "col")
-        col_got = exchange(col_part, ROW)
-        given = (cost, row_got, col_got, row_pot, col_pot)
+        both_cores = lax.all_gather(partials, "core")
+        (sent,) = call(share_kernel, (sent_shape,), [], where, both_cores, smem=(0,), row_chunks=row_chunks)
+        got = lax.all_to_all(sent, ROW + COL, 0, 0, tiled=True, axis_index_groups=groups)
+        (lse,) = call(settle_kernel, (col_shape,), [], where, got, smem=(0,), lines=lax.axis_size("x"))
+        given = (where, cost, lax.all_gather(lse, "core"), row_pot, col_pot)
         if iteration < ITERS - 2:
-            row_part, col_part, row_pot, col_pot = call(
-                both_kernel, (row_copies, col_copies, row_shape, col_shape), tall + wide + tall[:1], *given, **offsets
+            partials, row_pot, col_pot = call(
+                both_kernel, (part_shape, row_shape, col_shape), tall + wide + tall[:1], *given, smem=(0,), **offsets
             )
         else:
-            row_part, row_pot = call(last_row_kernel, (row_copies, row_shape), tall, *given, **offsets)
-    row_got = exchange(row_part, "col")
+            row_part, row_pot = call(last_row_kernel, (row_copies, row_shape), tall, *given, smem=(0,), **offsets)
+    row_got = exchange(row_part, COL)
     final_shape = jax.ShapeDtypeStruct((row_size, row_chunks, LANES), f32)
     final, copies = call(
         last_kernel, (row_shape, final_shape), [], row_got, row_pot, offset=offsets["row_offset"]
@@ -300,7 +351,7 @@
 
 def solution(mesh):
     row_size, col_size = mesh.shape["row"], mesh.shape["col"]
-    finer = jax.sharding.Mesh(mesh.devices.reshape(row_size // 4, 2, 2, col_size), ROW + ("col",))
-    both = ROW + ("col",)
+    finer = jax.sharding.Mesh(mesh.devices.reshape(row_size // 4, 2, 2, col_size // 4, 4), ROW + COL)
+    both = ROW + COL
     placed = (P(both, None), P(both, None), P(both), P(both), P(), P())
     return jax.shard_map(shards, mesh=finer, in_specs=placed, out_specs=P(ROW), check_vma=False)

time: 163 us -> 150 us (0.920)
  blocking collectives: 110 us -> 91.5 us
  Pallas kernels: 13.8 us -> 18.8 us
    all_to_all x8 -> x2, blocking collectives: 104 us -> 24.5 us  [exchange(): return lax.all_to_all(copies, axis, 0, 0, tiled=True)]
    all_to_all x0 -> x3, blocking collectives: none -> 44.1 us  [shards(): lax.all_to_all(sent, ROW + COL, 0, 0, tiled=True, axis_index_groups=groups)]
    all_gather x0 -> x6, blocking collectives: none -> 17.3 us  [the longest x3 10.4 us: shards(): both_cores = lax.all_gather(partials, 'core')]
    pallas_call x7 -> x13, Pallas kernels: 13.8 us -> 18.8 us  [call(): pl.pallas_call(body, out_shape=out_shape, in_specs=specs, out_specs=[VMEM...]
where the time goes in v10:
time: 150 us; the launch traced here: 149 us
  blocking collectives  91.5 us (61%)
  starting transfers between devices  30.3 us (20%)
  Pallas kernels  18.8 us (13%)
  waiting for transfers between devices  7.77 us (5%)
    all_to_all x3, blocking collectives, shards(): lax.all_to_all(sent, ROW + COL, 0, 0, tiled=True, axis_index_groups=groups)  44.1 us
    all_to_all x2, blocking collectives, exchange(): return lax.all_to_all(copies, axis, 0, 0, tiled=True)  24.5 us
    pallas_call x13, Pallas kernels, call(): pl.pallas_call(body, out_shape=out_shape, in_specs=specs, out_specs=[VMEM...  18.8 us
    ppermute x3, starting transfers between devices, shards(): lax.ppermute(pair, 'zh', turn[k])  17.3 us
    all_gather x3, blocking collectives, shards(): both_cores = lax.all_gather(partials, 'core')  10.4 us
    all_to_all x1, starting transfers between devices, exchange(): return lax.all_to_all(copies, axis, 0, 0, tiled=True)  9.68 us
    all_gather x3, blocking collectives, shards(): given = (where, cost, lax.all_gather(lse, 'core'), row_pot, col_pot)  6.88 us
    all_gather x1, blocking collectives, shards(): pair = lax.all_gather(valid_pack, 'zl', axis=0)  5.59 us
  transfers between devices with their start and end apart: 5, of which 3 were waited for; matrix products, arithmetic and copies ran while one was open for 0% of the time, Pallas kernels for 0%

profile of v10, /device:TPU:1, one launch (start us, length us, event | category | flops | bytes accessed | tf_op | source)
XLA Modules:
  0.0 148.9 jit_solution(13880234147066629564)
XLA Ops:
  0.0 1.7 %shard_map.64 = (bf16[32,16,384]{2,1,0:T(8,128)(2,1)}, bf16[144,256]{1,0:T(8,128)(2,1)}) custom-call(s32[16]{0:T(128)} %train_label_hbm.1, bf16[16,256]{1,0:T(8,128)(2,1)} %train_hbm.1, bf16[128,256]{1,0:T(8,128)(2,1)} %valid_hbm.1, s32[1,128]{1,0:T(1,128)} %bitcast.30), custom_call_target="tpu_custom_call" | custom-call | flops 16777216 | bytes 4194304 | tf_op jit(solution)/shard_map/pallas_call | solution.py:259
  1.7 5.6 %all-gather = bf16[288,256]{1,0:T(8,128)(2,1)S(1)} all-gather(bf16[144,256]{1,0:T(8,128)(2,1)} %get-tuple-element.20), channel_id=2, replica_groups=mesh['zh'=4,'zl'=2,'core'=2,'y'=8,'x'=4] {'zl'}, dimensions={0}, use_global_device_ids=true | all-gather | bytes 221184 | tf_op jit(solution)/shard_map/all_gather | solution.py:294
  7.3 5.8 %collective-permute-start = (bf16[2,144,256]{2,1,0:T(8,128)(2,1)S(1)}, bf16[2,144,256]{2,1,0:T(8,128)(2,1)S(1)}, u32[]{:S(2)}, u32[]{:S(2)}) collective-permute-start(bf16[2,144,256]{2,1,0:T(8,128)(2,1)S(1)} %bitcast.23), channel_id=1, source_target_pairs={{0,128},{128,256},{256,384},{384,0},{1,129},{129,257},{257,385},{3... | collective-permute-start | bytes 442376 | tf_op jit(solution)/shard_map/ppermute | solution.py:297
  13.1 8.2 %collective-permute-start.1 = (bf16[2,144,256]{2,1,0:T(8,128)(2,1)S(1)}, bf16[2,144,256]{2,1,0:T(8,128)(2,1)S(1)}, u32[]{:S(2)}, u32[]{:S(2)}) collective-permute-start(bf16[2,144,256]{2,1,0:T(8,128)(2,1)S(1)} %bitcast.24), channel_id=1, source_target_pairs={{0,256},{128,384},{256,0},{384,128},{1,257},{129,385},{257,1},{385... | collective-permute-start | bytes 442376 | tf_op jit(solution)/shard_map/ppermute | solution.py:297
  21.3 3.4 %collective-permute-start.2 = (bf16[2,144,256]{2,1,0:T(8,128)(2,1)S(1)}, bf16[2,144,256]{2,1,0:T(8,128)(2,1)S(1)}, u32[]{:S(2)}, u32[]{:S(2)}) collective-permute-start(bf16[2,144,256]{2,1,0:T(8,128)(2,1)S(1)} %bitcast.25), channel_id=1, source_target_pairs={{0,384},{128,0},{256,128},{384,256},{1,385},{129,1},{257,129},{385... | collective-permute-start | bytes 442376 | tf_op jit(solution)/shard_map/ppermute | solution.py:297
  24.7 9.7 %all-to-all-start = ((bf16[32,16,384]{2,1,0:T(8,128)(2,1)}), bf16[32,16,384]{2,1,0:T(8,128)(2,1)S(1)}, u32[]{:S(2)}, u32[]{:S(2)}) async-start(bf16[32,16,384]{2,1,0:T(8,128)(2,1)} %get-tuple-element.19), calls=%async_computation | async-start | bytes 786432 | tf_op jit(solution)/shard_map/all_to_all | solution.py:240
  34.4 1.6 %collective-permute-done.2 = bf16[2,144,256]{2,1,0:T(8,128)(2,1)S(1)} collective-permute-done((bf16[2,144,256]{2,1,0:T(8,128)(2,1)S(1)}, bf16[2,144,256]{2,1,0:T(8,128)(2,1)S(1)}, u32[]{:S(2)}, u32[]{:S(2)}) %collective-permute-start.2) | collective-permute-done | bytes 147488 | tf_op jit(solution)/shard_map/ppermute | solution.py:297
  36.1 3.2 %collective-permute-start.3 = (bf16[4,2,144,256]{3,2,1,0:T(8,128)(2,1)S(1)}, bf16[4,2,144,256]{3,2,1,0:T(8,128)(2,1)S(1)}, u32[]{:S(2)}, u32[]{:S(2)}) collective-permute-start(bf16[4,2,144,256]{3,2,1,0:T(8,128)(2,1)S(1)} %pad_maximum_fusion.mine_ref), channel_id=1, source_target_pairs={{0,32},{32,0},{1,33},{33,1},{2,34},{34,2},{3,35},{35,3},{4,36},{36... | collective-permute-start | bytes 1769480 | tf_op jit(solution)/shard_map/ppermute | solution.py:298
  41.0 4.9 %all-to-all-done.train_ref = bf16[32,16,384]{2,1,0:T(8,128)(2,1)S(1)} async-done(((bf16[32,16,384]{2,1,0:T(8,128)(2,1)}), bf16[32,16,384]{2,1,0:T(8,128)(2,1)S(1)}, u32[]{:S(2)}, u32[]{:S(2)}) %all-to-all-start) | async-done | bytes 393248 | tf_op jit(solution)/shard_map/all_to_all | solution.py:240
  45.8 5.3 %shard_map.65 = (f32[512,2048]{1,0:T(8,128)S(1)}, f32[24,128]{1,0:T(8,128)S(1)}) custom-call(s32[4]{0:T(128)S(1)} %pad_add_fusion.where_ref.refs_0_, bf16[32,16,384]{2,1,0:T(8,128)(2,1)S(1)} %all-to-all-done.train_ref, f32[128,128]{1,0:T(8,128)S(1)} %pad.4.table_ref, bf16[4,2,144,256]{3,2,1,0:T(8,128)(2,1)S(1)} %pad_maximum_fusion.mine_ref, ...), custom_call_target="tpu_custom_call" | custom-call | flops 16777216 | bytes 4194304 | tf_op jit(solution)/shard_map/pallas_call | solution.py:259
  51.1 6.8 %all-gather.1 = f32[48,128]{1,0:T(8,128)S(1)} all-gather(f32[24,128]{1,0:T(8,128)S(1)} %get-tuple-element.22), channel_id=3, replica_groups=mesh['zh'=4,'zl'=2,'core'=2,'y'=8,'x'=4] {'core'}, dimensions={0}, use_global_device_ids=true | all-gather | bytes 36864 | tf_op jit(solution)/shard_map/all_gather | solution.py:332
  58.5 14.7 %all_to_all.30.refs_1_ = f32[32,16,128]{2,1,0:T(8,128)S(1)} all-to-all(f32[32,16,128]{2,1,0:T(8,128)S(1)} %shard_map.66), channel_id=1, replica_groups={{0,1,2,3,4,5,6,7,8,9,10,11,12,13,14,15,16,17,18,19,20,21,22,23,24,25,26..., dimensions={0} | all-to-all | bytes 524288 | tf_op jit(solution)/shard_map/all_to_all | solution.py:334
  73.8 2.3 %all-gather.2 = f32[32,128]{1,0:T(8,128)S(1)} all-gather(f32[16,128]{1,0:T(8,128)S(1)} %shard_map.67), channel_id=4, replica_groups=mesh['zh'=4,'zl'=2,'core'=2,'y'=8,'x'=4] {'core'}, dimensions={0}, use_global_device_ids=true | all-gather | bytes 24576 | tf_op jit(solution)/shard_map/all_gather | solution.py:336
  76.1 2.8 %shard_map.68 = (f32[24,128]{1,0:T(8,128)S(1)}, f32[4,128]{1,0:T(4,128)S(1)}, f32[16,128]{1,0:T(8,128)S(1)}) custom-call(s32[4]{0:T(128)S(1)} %pad_add_fusion.where_ref.refs_0_, f32[512,2048]{1,0:T(8,128)S(1)} %get-tuple-element.21.refs_1_, f32[2,16,128]{2,1,0:T(8,128)S(1)} %bitcast.17, f32[4,128]{1,0:T(4,128)S(1)} %broadcast_in_dim.13.refs_3_, ...), custom_call_target="tpu_custom_call" | custom-call | flops 16777216 | bytes 4194304 | tf_op jit(solution)/shard_map/pallas_call | solution.py:259
  78.9 1.8 %all-gather.3 = f32[48,128]{1,0:T(8,128)S(1)} all-gather(f32[24,128]{1,0:T(8,128)S(1)} %get-tuple-element.23), channel_id=5, replica_groups=mesh['zh'=4,'zl'=2,'core'=2,'y'=8,'x'=4] {'core'}, dimensions={0}, use_global_device_ids=true | all-gather | bytes 36864 | tf_op jit(solution)/shard_map/all_gather | solution.py:332
  81.3 14.7 %all_to_all.31.refs_1_ = f32[32,16,128]{2,1,0:T(8,128)S(1)} all-to-all(f32[32,16,128]{2,1,0:T(8,128)S(1)} %shard_map.69), channel_id=1, replica_groups={{0,1,2,3,4,5,6,7,8,9,10,11,12,13,14,15,16,17,18,19,20,21,22,23,24,25,26..., dimensions={0} | all-to-all | bytes 524288 | tf_op jit(solution)/shard_map/all_to_all | solution.py:334
  96.7 2.3 %all-gather.4 = f32[32,128]{1,0:T(8,128)S(1)} all-gather(f32[16,128]{1,0:T(8,128)S(1)} %shard_map.70), channel_id=6, replica_groups=mesh['zh'=4,'zl'=2,'core'=2,'y'=8,'x'=4] {'core'}, dimensions={0}, use_global_device_ids=true | all-gather | bytes 24576 | tf_op jit(solution)/shard_map/all_gather | solution.py:336
  98.9 2.8 %shard_map.71 = (f32[24,128]{1,0:T(8,128)S(1)}, f32[4,128]{1,0:T(4,128)S(1)}, f32[16,128]{1,0:T(8,128)S(1)}) custom-call(s32[4]{0:T(128)S(1)} %pad_add_fusion.where_ref.refs_0_, f32[512,2048]{1,0:T(8,128)S(1)} %get-tuple-element.21.refs_1_, f32[2,16,128]{2,1,0:T(8,128)S(1)} %bitcast.19, f32[4,128]{1,0:T(4,128)S(1)} %get-tuple-element.24.refs_3_, ...), custom_call_target="tpu_custom_call" | custom-call | flops 16777216 | bytes 4194304 | tf_op jit(solution)/shard_map/pallas_call | solution.py:259
  101.7 1.8 %all-gather.5 = f32[48,128]{1,0:T(8,128)S(1)} all-gather(f32[24,128]{1,0:T(8,128)S(1)} %get-tuple-element.26), channel_id=7, replica_groups=mesh['zh'=4,'zl'=2,'core'=2,'y'=8,'x'=4] {'core'}, dimensions={0}, use_global_device_ids=true | all-gather | bytes 36864 | tf_op jit(solution)/shard_map/all_gather | solution.py:332
  104.2 14.7 %all_to_all.32.refs_1_ = f32[32,16,128]{2,1,0:T(8,128)S(1)} all-to-all(f32[32,16,128]{2,1,0:T(8,128)S(1)} %shard_map.72), channel_id=1, replica_groups={{0,1,2,3,4,5,6,7,8,9,10,11,12,13,14,15,16,17,18,19,20,21,22,23,24,25,26..., dimensions={0} | all-to-all | bytes 524288 | tf_op jit(solution)/shard_map/all_to_all | solution.py:334
  119.5 2.3 %all-gather.6 = f32[32,128]{1,0:T(8,128)S(1)} all-gather(f32[16,128]{1,0:T(8,128)S(1)} %shard_map.73), channel_id=8, replica_groups=mesh['zh'=4,'zl'=2,'core'=2,'y'=8,'x'=4] {'core'}, dimensions={0}, use_global_device_ids=true | all-gather | bytes 24576 | tf_op jit(solution)/shard_map/all_gather | solution.py:336
  121.8 1.8 %shard_map.74 = (f32[32,4,128]{2,1,0:T(4,128)S(1)}, f32[4,128]{1,0:T(4,128)S(1)}) custom-call(s32[4]{0:T(128)S(1)} %pad_add_fusion.where_ref.refs_0_, f32[512,2048]{1,0:T(8,128)S(1)} %get-tuple-element.21.refs_1_, f32[2,16,128]{2,1,0:T(8,128)S(1)} %bitcast.18, f32[4,128]{1,0:T(4,128)S(1)} %get-tuple-element.27.refs_3_, f32[16,128]{1,0:T(8,128)S(1)} %get-tuple-element.28.refs_4_), custom_call_target="tpu_custom_call" | custom-call | flops 16777216 | bytes 4194304 | tf_op jit(solution)/shard_map/pallas_call | solution.py:259
  123.6 12.2 %all_to_all.33.refs_0_ = f32[32,4,128]{2,1,0:T(4,128)S(1)} all-to-all(f32[32,4,128]{2,1,0:T(4,128)S(1)} %get-tuple-element.29), channel_id=1, replica_groups=mesh['zh'=4,'zl'=2,'core'=2,'y'=8,'x'=4] {'y','x'}, dimensions={0} | all-to-all | bytes 131072 | tf_op jit(solution)/shard_map/all_to_all | solution.py:240
  135.9 12.3 %all_to_all.34.refs_0_ = f32[16,4,128]{2,1,0:T(4,128)S(1)} all-to-all(f32[16,4,128]{2,1,0:T(4,128)S(1)} %get-tuple-element.31), channel_id=1, replica_groups=mesh['zh'=4,'zl'=2,'core'=2,'y'=8,'x'=4] {'zh','zl','core'}, dimensions={0} | all-to-all | bytes 65536 | tf_op jit(solution)/shard_map/all_to_all | solution.py:240
  (21 shorter events, 6.1 us)
Async XLA Ops:
  0.0 39.4 %copy-start = (s32[100,100]{1,0:T(8,128)S(1)}, s32[100,100]{1,0:T(8,128)}, u32[]{:S(2)}) copy-start(s32[100,100]{1,0:T(8,128)} %param.10) | copy-start | bytes 120004
  0.0 39.4 %copy-start.1 = (f32[4]{0:T(128)S(1)}, f32[4]{0:T(128)}, u32[]{:S(2)}) copy-start(f32[4]{0:T(128)} %param.11) | copy-start | bytes 52
  7.3 27.1 %collective-permute-start = (bf16[2,144,256]{2,1,0:T(8,128)(2,1)S(1)}, bf16[2,144,256]{2,1,0:T(8,128)(2,1)S(1)}, u32[]{:S(2)}, u32[]{:S(2)}) collective-permute-start(bf16[2,144,256]{2,1,0:T(8,128)(2,1)S(1)} %bitcast.23), channel_id=1, source_target_pairs={{0,128},{128,256},{256,384},{384,0},{1,129},{129,257},{257,385},{3... | collective-permute-start | bytes 442376 | tf_op jit(solution)/shard_map/ppermute | solution.py:297
  13.1 21.3 %collective-permute-start.1 = (bf16[2,144,256]{2,1,0:T(8,128)(2,1)S(1)}, bf16[2,144,256]{2,1,0:T(8,128)(2,1)S(1)}, u32[]{:S(2)}, u32[]{:S(2)}) collective-permute-start(bf16[2,144,256]{2,1,0:T(8,128)(2,1)S(1)} %bitcast.24), channel_id=1, source_target_pairs={{0,256},{128,384},{256,0},{384,128},{1,257},{129,385},{257,1},{385... | collective-permute-start | bytes 442376 | tf_op jit(solution)/shard_map/ppermute | solution.py:297
  21.3 14.7 %collective-permute-start.2 = (bf16[2,144,256]{2,1,0:T(8,128)(2,1)S(1)}, bf16[2,144,256]{2,1,0:T(8,128)(2,1)S(1)}, u32[]{:S(2)}, u32[]{:S(2)}) collective-permute-start(bf16[2,144,256]{2,1,0:T(8,128)(2,1)S(1)} %bitcast.25), channel_id=1, source_target_pairs={{0,384},{128,0},{256,128},{384,256},{1,385},{129,1},{257,129},{385... | collective-permute-start | bytes 442376 | tf_op jit(solution)/shard_map/ppermute | solution.py:297
  24.7 21.2 %all-to-all-start = ((bf16[32,16,384]{2,1,0:T(8,128)(2,1)}), bf16[32,16,384]{2,1,0:T(8,128)(2,1)S(1)}, u32[]{:S(2)}, u32[]{:S(2)}) async-start(bf16[32,16,384]{2,1,0:T(8,128)(2,1)} %get-tuple-element.19), calls=%async_computation | async-start | bytes 786432 | tf_op jit(solution)/shard_map/all_to_all | solution.py:240
  36.1 4.9 %collective-permute-start.3 = (bf16[4,2,144,256]{3,2,1,0:T(8,128)(2,1)S(1)}, bf16[4,2,144,256]{3,2,1,0:T(8,128)(2,1)S(1)}, u32[]{:S(2)}, u32[]{:S(2)}) collective-permute-start(bf16[4,2,144,256]{3,2,1,0:T(8,128)(2,1)S(1)} %pad_maximum_fusion.mine_ref), channel_id=1, source_target_pairs={{0,32},{32,0},{1,33},{33,1},{2,34},{34,2},{3,35},{35,3},{4,36},{36... | collective-permute-start | bytes 1769480 | tf_op jit(solution)/shard_map/ppermute | solution.py:298

commit v11 on v10

--- a/solution.py
+++ b/solution.py
@@ -63,7 +63,7 @@
             total_ref[here] = total
         return carry
 
-    lax.fori_loop(0, blocks, block_step, 0)
+    lax.fori_loop(0, blocks, block_step, 0, unroll=True)
     out = [merge(high_ref[:, k * LANES : (k + 1) * LANES], total_ref[:, k * LANES : (k + 1) * LANES]) for k in range(chunks)]
     return jnp.concatenate(out, axis=0)
 
@@ -170,20 +170,21 @@
     out_ref[...] = jnp.concatenate([col, row, unused], axis=0)
 
 
-def share_kernel(where_ref, partials_ref, out_ref, *, row_chunks):
+def share_kernel(flags_ref, partials_ref, out_ref, *, row_chunks):
     _, chunks, _ = out_ref.shape
     rows = [partials_ref[core, chunks : chunks + row_chunks, :] for core in range(2)]
     unused = jnp.zeros((chunks - 2 * row_chunks, LANES), jnp.float32)
     row_side = jnp.concatenate(rows + [unused], axis=0)
     col_side = lse_lead(partials_ref[:, :chunks, :])
-    out_ref[...] = jnp.broadcast_to(jnp.where(where_ref[2] == 0, row_side, col_side)[None], out_ref.shape)
-
-
-def settle_kernel(where_ref, parts_ref, out_ref, *, lines):
-    parts = []
-    for k in range(parts_ref.shape[0]):
-        wanted = jnp.logical_or(where_ref[2] == 0, where_ref[3] == k % lines)
-        parts.append(jnp.where(wanted, parts_ref[k], -jnp.inf))
+    first_core = jnp.concatenate([flags_ref[0]] * (chunks // SUB), axis=0) > 0.5
+    out_ref[...] = jnp.broadcast_to(jnp.where(first_core, row_side, col_side)[None], out_ref.shape)
+
+
+def settle_kernel(flags_ref, parts_ref, out_ref):
+    repeats = parts_ref.shape[1] // SUB
+    lines = flags_ref.shape[0] - 1
+    wanted = [jnp.concatenate([flags_ref[1 + line]] * repeats, axis=0) > 0.5 for line in range(lines)]
+    parts = [jnp.where(wanted[k % lines], parts_ref[k], -jnp.inf) for k in range(parts_ref.shape[0])]
     high = parts[0]
     for part in parts[1:]:
         high = jnp.maximum(high, part)
@@ -197,17 +198,18 @@
     return 0.5 * (pot_ref[...] + (offset - lse))
 
 
-def both_updated(where_ref, lse_ref, row_pot, col_pot, row_offset, col_offset):
+def both_updated(flags_ref, lse_ref, row_pot, col_pot, row_offset, col_offset):
     chunks = row_pot.shape[0]
-    rows = jnp.where(where_ref[2] == 0, lse_ref[0, :chunks, :], lse_ref[0, chunks : 2 * chunks, :])
+    first_core = flags_ref[0, :chunks, :] > 0.5
+    rows = jnp.where(first_core, lse_ref[0, :chunks, :], lse_ref[0, chunks : 2 * chunks, :])
     return updated(row_pot, rows, row_offset), updated(col_pot, lse_ref[1], col_offset)
 
 
 def both_kernel(
-    where_ref, cost_ref, lse_ref, row_pot, col_pot, partial_ref, row_new, col_new, row_a, row_b, col_a, col_b, spread_ref,
+    flags_ref, cost_ref, lse_ref, row_pot, col_pot, partial_ref, row_new, col_new, row_a, row_b, col_a, col_b, spread_ref,
     *, row_offset, col_offset
 ):
-    row, col = both_updated(where_ref, lse_ref, row_pot, col_pot, row_offset, col_offset)
+    row, col = both_updated(flags_ref, lse_ref, row_pot, col_pot, row_offset, col_offset)
     row_new[...] = row
     col_new[...] = col
     spread_rows(row, spread_ref)
@@ -217,9 +219,9 @@
 
 
 def last_row_kernel(
-    where_ref, cost_ref, lse_ref, row_pot, col_pot, row_out, row_new, row_a, row_b, *, row_offset, col_offset
+    flags_ref, cost_ref, lse_ref, row_pot, col_pot, row_out, row_new, row_a, row_b, *, row_offset, col_offset
 ):
-    row, col = both_updated(where_ref, lse_ref, row_pot, col_pot, row_offset, col_offset)
+    row, col = both_updated(flags_ref, lse_ref, row_pot, col_pot, row_offset, col_offset)
     row_new[...] = row
     row_out[...] = jnp.broadcast_to(row_partial(cost_ref, col, row_a, row_b)[None], row_out.shape)
 
@@ -328,18 +330,22 @@
     row_pot = jnp.zeros(row_shape.shape, f32)
     col_pot = jnp.zeros(col_shape.shape, f32)
     groups = core_groups()
+    lines = jnp.arange(lax.axis_size("x"), dtype=jnp.int32)
+    counts = jnp.logical_or(where[2] == 0, lines == where[3])
+    flags = jnp.concatenate([where[2:3] == 0, counts]).astype(f32)
+    flags = jnp.broadcast_to(flags[:, None, None], (lines.shape[0] + 1, SUB, LANES))
     for iteration in range(ITERS - 1):
         both_cores = lax.all_gather(partials, "core")
-        (sent,) = call(share_kernel, (sent_shape,), [], where, both_cores, smem=(0,), row_chunks=row_chunks)
+        (sent,) = call(share_kernel, (sent_shape,), [], flags, both_cores, row_chunks=row_chunks)
         got = lax.all_to_all(sent, ROW + COL, 0, 0, tiled=True, axis_index_groups=groups)
-        (lse,) = call(settle_kernel, (col_shape,), [], where, got, smem=(0,), lines=lax.axis_size("x"))
-        given = (where, cost, lax.all_gather(lse, "core"), row_pot, col_pot)
+        (lse,) = call(settle_kernel, (col_shape,), [], flags, got)
+        given = (flags, cost, lax.all_gather(lse, "core"), row_pot, col_pot)
         if iteration < ITERS - 2:
             partials, row_pot, col_pot = call(
-                both_kernel, (part_shape, row_shape, col_shape), tall + wide + tall[:1], *given, smem=(0,), **offsets
+                both_kernel, (part_shape, row_shape, col_shape), tall + wide + tall[:1], *given, **offsets
             )
         else:
-            row_part, row_pot = call(last_row_kernel, (row_copies, row_shape), tall, *given, smem=(0,), **offsets)
+            row_part, row_pot = call(last_row_kernel, (row_copies, row_shape), tall, *given, **offsets)
     row_got = exchange(row_part, COL)
     final_shape = jax.ShapeDtypeStruct((row_size, row_chunks, LANES), f32)
     final, copies = call(

time: 150 us -> 144 us (0.960)
  Pallas kernels: 18.8 us -> 13.5 us
    pallas_call x13, Pallas kernels: 18.8 us -> 13.5 us  [call(): pl.pallas_call(body, out_shape=out_shape, in_specs=specs, out_specs=[VMEM...]
where the time goes in v11:
time: 144 us
  blocking collectives  91.5 us (64%)
  starting transfers between devices  30.3 us (21%)
  Pallas kernels  13.5 us (9%)
  waiting for transfers between devices  7.67 us (5%)
    all_to_all x3, blocking collectives, shards(): lax.all_to_all(sent, ROW + COL, 0, 0, tiled=True, axis_index_groups=groups)  44.1 us
    all_to_all x2, blocking collectives, exchange(): return lax.all_to_all(copies, axis, 0, 0, tiled=True)  24.5 us
    ppermute x3, starting transfers between devices, shards(): lax.ppermute(pair, 'zh', turn[k])  17.3 us
    pallas_call x13, Pallas kernels, call(): pl.pallas_call(body, out_shape=out_shape, in_specs=specs, out_specs=[VMEM...  13.5 us
    all_gather x3, blocking collectives, shards(): both_cores = lax.all_gather(partials, 'core')  10.4 us
    all_to_all x1, starting transfers between devices, exchange(): return lax.all_to_all(copies, axis, 0, 0, tiled=True)  9.68 us
    all_gather x3, blocking collectives, shards(): given = (flags, cost, lax.all_gather(lse, 'core'), row_pot, col_pot)  6.89 us
    all_gather x1, blocking collectives, shards(): pair = lax.all_gather(valid_pack, 'zl', axis=0)  5.59 us
  transfers between devices with their start and end apart: 5, of which 3 were waited for; matrix products, arithmetic and copies ran while one was open for 0% of the time, Pallas kernels for 0%

profile of v11, /device:TPU:1, one launch (start us, length us, event | category | flops | bytes accessed | tf_op | source)
XLA Modules:
  0.0 143.7 jit_solution(12617399371485643138)
XLA Ops:
  0.0 1.7 %shard_map.64 = (bf16[32,16,384]{2,1,0:T(8,128)(2,1)}, bf16[144,256]{1,0:T(8,128)(2,1)}) custom-call(s32[16]{0:T(128)} %train_label_hbm.1, bf16[16,256]{1,0:T(8,128)(2,1)} %train_hbm.1, bf16[128,256]{1,0:T(8,128)(2,1)} %valid_hbm.1, s32[1,128]{1,0:T(1,128)} %bitcast.30), custom_call_target="tpu_custom_call" | custom-call | flops 16777216 | bytes 4194304 | tf_op jit(solution)/shard_map/pallas_call | solution.py:261
  1.7 5.6 %all-gather = bf16[288,256]{1,0:T(8,128)(2,1)S(1)} all-gather(bf16[144,256]{1,0:T(8,128)(2,1)} %get-tuple-element.20), channel_id=2, replica_groups=mesh['zh'=4,'zl'=2,'core'=2,'y'=8,'x'=4] {'zl'}, dimensions={0}, use_global_device_ids=true | all-gather | bytes 221184 | tf_op jit(solution)/shard_map/all_gather | solution.py:296
  7.3 5.8 %collective-permute-start = (bf16[2,144,256]{2,1,0:T(8,128)(2,1)S(1)}, bf16[2,144,256]{2,1,0:T(8,128)(2,1)S(1)}, u32[]{:S(2)}, u32[]{:S(2)}) collective-permute-start(bf16[2,144,256]{2,1,0:T(8,128)(2,1)S(1)} %bitcast.23), channel_id=1, source_target_pairs={{0,128},{128,256},{256,384},{384,0},{1,129},{129,257},{257,385},{3... | collective-permute-start | bytes 442376 | tf_op jit(solution)/shard_map/ppermute | solution.py:299
  13.1 8.2 %collective-permute-start.1 = (bf16[2,144,256]{2,1,0:T(8,128)(2,1)S(1)}, bf16[2,144,256]{2,1,0:T(8,128)(2,1)S(1)}, u32[]{:S(2)}, u32[]{:S(2)}) collective-permute-start(bf16[2,144,256]{2,1,0:T(8,128)(2,1)S(1)} %bitcast.24), channel_id=1, source_target_pairs={{0,256},{128,384},{256,0},{384,128},{1,257},{129,385},{257,1},{385... | collective-permute-start | bytes 442376 | tf_op jit(solution)/shard_map/ppermute | solution.py:299
  21.3 3.4 %collective-permute-start.2 = (bf16[2,144,256]{2,1,0:T(8,128)(2,1)S(1)}, bf16[2,144,256]{2,1,0:T(8,128)(2,1)S(1)}, u32[]{:S(2)}, u32[]{:S(2)}) collective-permute-start(bf16[2,144,256]{2,1,0:T(8,128)(2,1)S(1)} %bitcast.25), channel_id=1, source_target_pairs={{0,384},{128,0},{256,128},{384,256},{1,385},{129,1},{257,129},{385... | collective-permute-start | bytes 442376 | tf_op jit(solution)/shard_map/ppermute | solution.py:299
  24.7 9.7 %all-to-all-start = ((bf16[32,16,384]{2,1,0:T(8,128)(2,1)}), bf16[32,16,384]{2,1,0:T(8,128)(2,1)S(1)}, u32[]{:S(2)}, u32[]{:S(2)}) async-start(bf16[32,16,384]{2,1,0:T(8,128)(2,1)} %get-tuple-element.19), calls=%async_computation | async-start | bytes 786432 | tf_op jit(solution)/shard_map/all_to_all | solution.py:242
  34.4 1.6 %collective-permute-done.2 = bf16[2,144,256]{2,1,0:T(8,128)(2,1)S(1)} collective-permute-done((bf16[2,144,256]{2,1,0:T(8,128)(2,1)S(1)}, bf16[2,144,256]{2,1,0:T(8,128)(2,1)S(1)}, u32[]{:S(2)}, u32[]{:S(2)}) %collective-permute-start.2) | collective-permute-done | bytes 147488 | tf_op jit(solution)/shard_map/ppermute | solution.py:299
  36.1 3.2 %collective-permute-start.3 = (bf16[4,2,144,256]{3,2,1,0:T(8,128)(2,1)S(1)}, bf16[4,2,144,256]{3,2,1,0:T(8,128)(2,1)S(1)}, u32[]{:S(2)}, u32[]{:S(2)}) collective-permute-start(bf16[4,2,144,256]{3,2,1,0:T(8,128)(2,1)S(1)} %pad_maximum_fusion.mine_ref), channel_id=1, source_target_pairs={{0,32},{32,0},{1,33},{33,1},{2,34},{34,2},{3,35},{35,3},{4,36},{36... | collective-permute-start | bytes 1769480 | tf_op jit(solution)/shard_map/ppermute | solution.py:300
  41.0 4.9 %all-to-all-done.train_ref = bf16[32,16,384]{2,1,0:T(8,128)(2,1)S(1)} async-done(((bf16[32,16,384]{2,1,0:T(8,128)(2,1)}), bf16[32,16,384]{2,1,0:T(8,128)(2,1)S(1)}, u32[]{:S(2)}, u32[]{:S(2)}) %all-to-all-start) | async-done | bytes 393248 | tf_op jit(solution)/shard_map/all_to_all | solution.py:242
  45.8 5.1 %shard_map.65 = (f32[512,2048]{1,0:T(8,128)S(1)}, f32[24,128]{1,0:T(8,128)S(1)}) custom-call(s32[4]{0:T(128)S(1)} %pad_add_fusion.where_ref, bf16[32,16,384]{2,1,0:T(8,128)(2,1)S(1)} %all-to-all-done.train_ref, f32[128,128]{1,0:T(8,128)S(1)} %pad.4.table_ref, bf16[4,2,144,256]{3,2,1,0:T(8,128)(2,1)S(1)} %pad_maximum_fusion.mine_ref, ...), custom_call_target="tpu_custom_call" | custom-call | flops 16777216 | bytes 4194304 | tf_op jit(solution)/shard_map/pallas_call | solution.py:261
  51.0 6.8 %all-gather.1 = f32[48,128]{1,0:T(8,128)S(1)} all-gather(f32[24,128]{1,0:T(8,128)S(1)} %get-tuple-element.22), channel_id=3, replica_groups=mesh['zh'=4,'zl'=2,'core'=2,'y'=8,'x'=4] {'core'}, dimensions={0}, use_global_device_ids=true | all-gather | bytes 36864 | tf_op jit(solution)/shard_map/all_gather | solution.py:338
  57.9 14.7 %all_to_all.30.parts_ref = f32[32,16,128]{2,1,0:T(8,128)S(1)} all-to-all(f32[32,16,128]{2,1,0:T(8,128)S(1)} %shard_map.66), channel_id=1, replica_groups={{0,1,2,3,4,5,6,7,8,9,10,11,12,13,14,15,16,17,18,19,20,21,22,23,24,25,26..., dimensions={0} | all-to-all | bytes 524288 | tf_op jit(solution)/shard_map/all_to_all | solution.py:340
  72.6 2.3 %all-gather.2 = f32[32,128]{1,0:T(8,128)S(1)} all-gather(f32[16,128]{1,0:T(8,128)S(1)} %shard_map.67), channel_id=4, replica_groups=mesh['zh'=4,'zl'=2,'core'=2,'y'=8,'x'=4] {'core'}, dimensions={0}, use_global_device_ids=true | all-gather | bytes 24576 | tf_op jit(solution)/shard_map/all_gather | solution.py:342
  74.9 2.1 %shard_map.68 = (f32[24,128]{1,0:T(8,128)S(1)}, f32[4,128]{1,0:T(4,128)S(1)}, f32[16,128]{1,0:T(8,128)S(1)}) custom-call(f32[5,8,128]{2,1,0:T(8,128)S(1)} %broadcast_in_dim.8.refs_0_.flags_ref, f32[512,2048]{1,0:T(8,128)S(1)} %get-tuple-element.21.refs_1_, f32[2,16,128]{2,1,0:T(8,128)S(1)} %bitcast.17, f32[4,128]{1,0:T(4,128)S(1)} %broadcast_in_dim.20.refs_3_, ...), custom_call_target="tpu_custom_call" | custom-call | flops 16777216 | bytes 4194304 | tf_op jit(solution)/shard_map/pallas_call | solution.py:261
  77.1 1.8 %all-gather.3 = f32[48,128]{1,0:T(8,128)S(1)} all-gather(f32[24,128]{1,0:T(8,128)S(1)} %get-tuple-element.23), channel_id=5, replica_groups=mesh['zh'=4,'zl'=2,'core'=2,'y'=8,'x'=4] {'core'}, dimensions={0}, use_global_device_ids=true | all-gather | bytes 36864 | tf_op jit(solution)/shard_map/all_gather | solution.py:338
  78.9 14.7 %all_to_all.31.parts_ref = f32[32,16,128]{2,1,0:T(8,128)S(1)} all-to-all(f32[32,16,128]{2,1,0:T(8,128)S(1)} %shard_map.69), channel_id=1, replica_groups={{0,1,2,3,4,5,6,7,8,9,10,11,12,13,14,15,16,17,18,19,20,21,22,23,24,25,26..., dimensions={0} | all-to-all | bytes 524288 | tf_op jit(solution)/shard_map/all_to_all | solution.py:340
  93.7 2.3 %all-gather.4 = f32[32,128]{1,0:T(8,128)S(1)} all-gather(f32[16,128]{1,0:T(8,128)S(1)} %shard_map.70), channel_id=6, replica_groups=mesh['zh'=4,'zl'=2,'core'=2,'y'=8,'x'=4] {'core'}, dimensions={0}, use_global_device_ids=true | all-gather | bytes 24576 | tf_op jit(solution)/shard_map/all_gather | solution.py:342
  96.0 2.1 %shard_map.71 = (f32[24,128]{1,0:T(8,128)S(1)}, f32[4,128]{1,0:T(4,128)S(1)}, f32[16,128]{1,0:T(8,128)S(1)}) custom-call(f32[5,8,128]{2,1,0:T(8,128)S(1)} %broadcast_in_dim.8.refs_0_.flags_ref, f32[512,2048]{1,0:T(8,128)S(1)} %get-tuple-element.21.refs_1_, f32[2,16,128]{2,1,0:T(8,128)S(1)} %bitcast.19, f32[4,128]{1,0:T(4,128)S(1)} %get-tuple-element.24.refs_3_, ...), custom_call_target="tpu_custom_call" | custom-call | flops 16777216 | bytes 4194304 | tf_op jit(solution)/shard_map/pallas_call | solution.py:261
  98.1 1.8 %all-gather.5 = f32[48,128]{1,0:T(8,128)S(1)} all-gather(f32[24,128]{1,0:T(8,128)S(1)} %get-tuple-element.26), channel_id=7, replica_groups=mesh['zh'=4,'zl'=2,'core'=2,'y'=8,'x'=4] {'core'}, dimensions={0}, use_global_device_ids=true | all-gather | bytes 36864 | tf_op jit(solution)/shard_map/all_gather | solution.py:338
  100.0 14.7 %all_to_all.32.parts_ref = f32[32,16,128]{2,1,0:T(8,128)S(1)} all-to-all(f32[32,16,128]{2,1,0:T(8,128)S(1)} %shard_map.72), channel_id=1, replica_groups={{0,1,2,3,4,5,6,7,8,9,10,11,12,13,14,15,16,17,18,19,20,21,22,23,24,25,26..., dimensions={0} | all-to-all | bytes 524288 | tf_op jit(solution)/shard_map/all_to_all | solution.py:340
  114.8 2.3 %all-gather.6 = f32[32,128]{1,0:T(8,128)S(1)} all-gather(f32[16,128]{1,0:T(8,128)S(1)} %shard_map.73), channel_id=8, replica_groups=mesh['zh'=4,'zl'=2,'core'=2,'y'=8,'x'=4] {'core'}, dimensions={0}, use_global_device_ids=true | all-gather | bytes 24576 | tf_op jit(solution)/shard_map/all_gather | solution.py:342
  117.1 1.3 shard_map.74
  118.4 12.2 %all_to_all.33.refs_0_ = f32[32,4,128]{2,1,0:T(4,128)S(1)} all-to-all(f32[32,4,128]{2,1,0:T(4,128)S(1)} %get-tuple-element.29), channel_id=1, replica_groups=mesh['zh'=4,'zl'=2,'core'=2,'y'=8,'x'=4] {'y','x'}, dimensions={0} | all-to-all | bytes 131072 | tf_op jit(solution)/shard_map/all_to_all | solution.py:242
  130.7 12.3 %all_to_all.34.refs_0_ = f32[16,4,128]{2,1,0:T(4,128)S(1)} all-to-all(f32[16,4,128]{2,1,0:T(4,128)S(1)} %get-tuple-element.31), channel_id=1, replica_groups=mesh['zh'=4,'zl'=2,'core'=2,'y'=8,'x'=4] {'zh','zl','core'}, dimensions={0} | all-to-all | bytes 65536 | tf_op jit(solution)/shard_map/all_to_all | solution.py:242
  (24 shorter events, 2.9 us)
Async XLA Ops:
  0.0 39.4 %copy-start = (s32[100,100]{1,0:T(8,128)S(1)}, s32[100,100]{1,0:T(8,128)}, u32[]{:S(2)}) copy-start(s32[100,100]{1,0:T(8,128)} %param.10) | copy-start | bytes 120004
  0.0 39.4 %copy-start.1 = (f32[4]{0:T(128)S(1)}, f32[4]{0:T(128)}, u32[]{:S(2)}) copy-start(f32[4]{0:T(128)} %param.11) | copy-start | bytes 52
  7.3 27.1 %collective-permute-start = (bf16[2,144,256]{2,1,0:T(8,128)(2,1)S(1)}, bf16[2,144,256]{2,1,0:T(8,128)(2,1)S(1)}, u32[]{:S(2)}, u32[]{:S(2)}) collective-permute-start(bf16[2,144,256]{2,1,0:T(8,128)(2,1)S(1)} %bitcast.23), channel_id=1, source_target_pairs={{0,128},{128,256},{256,384},{384,0},{1,129},{129,257},{257,385},{3... | collective-permute-start | bytes 442376 | tf_op jit(solution)/shard_map/ppermute | solution.py:299
  13.1 21.3 %collective-permute-start.1 = (bf16[2,144,256]{2,1,0:T(8,128)(2,1)S(1)}, bf16[2,144,256]{2,1,0:T(8,128)(2,1)S(1)}, u32[]{:S(2)}, u32[]{:S(2)}) collective-permute-start(bf16[2,144,256]{2,1,0:T(8,128)(2,1)S(1)} %bitcast.24), channel_id=1, source_target_pairs={{0,256},{128,384},{256,0},{384,128},{1,257},{129,385},{257,1},{385... | collective-permute-start | bytes 442376 | tf_op jit(solution)/shard_map/ppermute | solution.py:299
  21.3 14.7 %collective-permute-start.2 = (bf16[2,144,256]{2,1,0:T(8,128)(2,1)S(1)}, bf16[2,144,256]{2,1,0:T(8,128)(2,1)S(1)}, u32[]{:S(2)}, u32[]{:S(2)}) collective-permute-start(bf16[2,144,256]{2,1,0:T(8,128)(2,1)S(1)} %bitcast.25), channel_id=1, source_target_pairs={{0,384},{128,0},{256,128},{384,256},{1,385},{129,1},{257,129},{385... | collective-permute-start | bytes 442376 | tf_op jit(solution)/shard_map/ppermute | solution.py:299
  24.7 21.2 %all-to-all-start = ((bf16[32,16,384]{2,1,0:T(8,128)(2,1)}), bf16[32,16,384]{2,1,0:T(8,128)(2,1)S(1)}, u32[]{:S(2)}, u32[]{:S(2)}) async-start(bf16[32,16,384]{2,1,0:T(8,128)(2,1)} %get-tuple-element.19), calls=%async_computation | async-start | bytes 786432 | tf_op jit(solution)/shard_map/all_to_all | solution.py:242
  36.1 4.9 %collective-permute-start.3 = (bf16[4,2,144,256]{3,2,1,0:T(8,128)(2,1)S(1)}, bf16[4,2,144,256]{3,2,1,0:T(8,128)(2,1)S(1)}, u32[]{:S(2)}, u32[]{:S(2)}) collective-permute-start(bf16[4,2,144,256]{3,2,1,0:T(8,128)(2,1)S(1)} %pad_maximum_fusion.mine_ref), channel_id=1, source_target_pairs={{0,32},{32,0},{1,33},{33,1},{2,34},{34,2},{3,35},{35,3},{4,36},{36... | collective-permute-start | bytes 1769480 | tf_op jit(solution)/shard_map/ppermute | solution.py:300

commit v12 on v11

--- a/solution.py
+++ b/solution.py
@@ -127,41 +127,53 @@
     valid_out[points:, :] = jnp.concatenate([row] * (embed // LANES), axis=1).astype(jnp.bfloat16)
 
 
+def squared_sums(rows, ones, swap):
+    wide = rows.astype(jnp.float32)
+    squares = wide * wide
+    high = squares.astype(jnp.bfloat16)
+    low = (squares - high.astype(jnp.float32)).astype(jnp.bfloat16)
+    if swap:
+        return dot(ones, high, ((1,), (1,))) + dot(ones, low, ((1,), (1,)))
+    return dot(high, ones, ((1,), (1,))) + dot(low, ones, ((1,), (1,)))
+
+
+def valid_kernel(where_ref, mine_ref, other_ref, valid_ref, hot_ref, sq_ref):
+    steps, sides, _, embed = mine_ref.shape
+    ones = jnp.ones((SUB, embed), jnp.bfloat16)
+    class_ids = lax.broadcasted_iota(jnp.int32, (LANES, LANES), 0).astype(jnp.float32)
+    for k in range(2 * steps * sides):
+        core, z_pair, side = k // (steps * sides), k // sides % steps, k % sides
+        back = lax.rem(where_ref[0] - z_pair + steps, steps)
+        block = jnp.where(where_ref[2] == core, mine_ref[back, side], other_ref[back, side])
+        here = slice(k * LANES, (k + 1) * LANES)
+        points = block[:LANES, :]
+        label_row = block[LANES:, :LANES].astype(jnp.float32)[:1, :]
+        valid_ref[here, :] = points
+        hot_ref[:, here] = jnp.where(class_ids == label_row, 1.0, 0.0).astype(jnp.bfloat16)
+        sq_ref[:, here] = squared_sums(points, ones, True) * (1.0 / embed)
+
+
 def start_kernel(
-    where_ref, train_ref, table_ref, mine_ref, other_ref, cost_ref, partial_ref, left_ref, row_a, row_b, col_a, col_b
+    train_ref, table_ref, valid_ref, hot_ref, sq_ref, cost_ref, partial_ref, left_ref, row_a, row_b, col_a, col_b
 ):
-    steps, sides, block_rows, embed = mine_ref.shape
+    embed = valid_ref.shape[1]
     packed = train_ref[...].reshape(cost_ref.shape[0], embed + LANES)
     train = packed[:, :embed]
-    wide = train.astype(jnp.float32)
-    train_sq = jnp.sum(wide * wide, axis=1, keepdims=True) * (1.0 / embed)
+    train_sq = squared_sums(train, jnp.ones((LANES, embed), jnp.bfloat16), False) * (1.0 / embed)
     labels = packed[:, embed:].astype(jnp.float32)
     lane_ids = lax.broadcasted_iota(jnp.int32, labels.shape, 1).astype(jnp.float32)
     train_hot = jnp.where(labels == lane_ids, 1.0, 0.0).astype(jnp.bfloat16)
-    parts = [dot(train_hot, part, ((1,), (0,))).astype(jnp.bfloat16) for part in split3(table_ref[...])]
-    table_parts = len(parts)
-    left_ref[...] = jnp.concatenate([train * jnp.bfloat16(-2.0 / embed), *parts], axis=1)
-    ones = jnp.ones((SUB, embed), jnp.bfloat16)
-    class_ids = lax.broadcasted_iota(jnp.int32, (LANES, LANES), 0).astype(jnp.float32)
-    step = sides * LANES
-    for pair in range(2 * steps):
-        core, z_pair = divmod(pair, steps)
-        back = lax.rem(where_ref[0] - z_pair + steps, steps)
-        own = where_ref[2] == core
-        blocks = [jnp.where(own, mine_ref[back, side], other_ref[back, side]) for side in range(sides)]
-        block = jnp.concatenate([b[:LANES, :] for b in blocks], axis=0)
-        label_rows = [b[LANES:, :LANES].astype(jnp.float32)[:1, :] for b in blocks]
-        hots = [jnp.where(class_ids == label_row, 1.0, 0.0).astype(jnp.bfloat16) for label_row in label_rows]
-        hot = jnp.concatenate(hots, axis=1)
-        wide = block.astype(jnp.float32)
-        squares = wide * wide
-        sq_high = squares.astype(jnp.bfloat16)
-        sq_low = (squares - sq_high.astype(jnp.float32)).astype(jnp.bfloat16)
-        block_sq = (dot(ones, sq_high, ((1,), (1,))) + dot(ones, sq_low, ((1,), (1,))))[:1, :]
-        cost = dot(left_ref[:, :embed], block, ((1,), (1,)))
-        cost = cost + dot(left_ref[:, embed:], jnp.concatenate([hot] * table_parts, axis=0), ((1,), (0,)))
+    table_parts = split3(table_ref[...])
+    table_rows = dot(train_hot, jnp.concatenate(table_parts, axis=1), ((1,), (0,))).astype(jnp.bfloat16)
+    left_ref[...] = jnp.concatenate([train * jnp.bfloat16(-2.0 / embed), table_rows], axis=1)
+    step = 2 * LANES
+    train_sq = jnp.concatenate([train_sq] * 2, axis=1)
+    for pair in range(valid_ref.shape[0] // step):
         here = slice(pair * step, (pair + 1) * step)
-        cost_ref[:, here] = (cost + (train_sq + block_sq * (1.0 / embed))) * (1.0 / UNIT)
+        cost = dot(left_ref[:, :embed], valid_ref[here, :], ((1,), (1,)))
+        hot = jnp.concatenate([hot_ref[:, here]] * len(table_parts), axis=0)
+        cost = cost + dot(left_ref[:, embed:], hot, ((1,), (0,)))
+        cost_ref[:, here] = (cost + (train_sq + sq_ref[:1, here])) * (1.0 / UNIT)
     put_partials(partial_ref, row_partial(cost_ref, None, row_a, row_b), col_partial(cost_ref, None, col_a, col_b))
 
 
@@ -313,16 +325,26 @@
     col_shape = jax.ShapeDtypeStruct((col_chunks, LANES), f32)
     tall = [pltpu.VMEM((rows, LANES), f32)] * 2
     wide = [pltpu.VMEM((row_chunks * SUB, cols), f32)] * 2
+    valid_side = call(
+        valid_kernel,
+        (
+            jax.ShapeDtypeStruct((cols, embed), jnp.bfloat16),
+            jax.ShapeDtypeStruct((LANES, cols), jnp.bfloat16),
+            jax.ShapeDtypeStruct((SUB, cols), f32),
+        ),
+        [],
+        where,
+        mine,
+        other,
+        smem=(0,),
+    )
     cost, partials = call(
         start_kernel,
         (tile, part_shape),
         [pltpu.VMEM((rows, embed + 3 * LANES), jnp.bfloat16)] + tall + wide,
-        where,
         train_all,
         table,
-        mine,
-        other,
-        smem=(0,),
+        *valid_side,
         limit=16,
     )
     full_rows, full_cols = rows * row_size, cols * col_size

time: 144 us -> 143 us (level)
    pallas_call x13 -> x14, Pallas kernels: 13.5 us -> 13.9 us  [call(): pl.pallas_call(body, out_shape=out_shape, in_specs=specs, out_specs=[VMEM...]
  transfers between devices with their start and end apart: 5 -> 5, of which waited for: 3 -> 3; matrix products, arithmetic and copies ran while one was open for 0% -> 0% of each run, Pallas kernels for 0% -> 1%
where the time goes in v12:
time: 143 us
  blocking collectives  91.5 us (64%)
  starting transfers between devices  30.3 us (21%)
  Pallas kernels  13.9 us (10%)
  waiting for transfers between devices  6.4 us (4%)
    all_to_all x3, blocking collectives, shards(): lax.all_to_all(sent, ROW + COL, 0, 0, tiled=True, axis_index_groups=groups)  44.1 us
    all_to_all x2, blocking collectives, exchange(): return lax.all_to_all(copies, axis, 0, 0, tiled=True)  24.5 us
    ppermute x3, starting transfers between devices, shards(): lax.ppermute(pair, 'zh', turn[k])  17.3 us
    pallas_call x14, Pallas kernels, call(): pl.pallas_call(body, out_shape=out_shape, in_specs=specs, out_specs=[VMEM...  13.9 us
    all_gather x3, blocking collectives, shards(): both_cores = lax.all_gather(partials, 'core')  10.4 us
    all_to_all x1, starting transfers between devices, exchange(): return lax.all_to_all(copies, axis, 0, 0, tiled=True)  9.68 us
    all_gather x3, blocking collectives, shards(): given = (flags, cost, lax.all_gather(lse, 'core'), row_pot, col_pot)  6.88 us
    all_gather x1, blocking collectives, shards(): pair = lax.all_gather(valid_pack, 'zl', axis=0)  5.59 us
  transfers between devices with their start and end apart: 5, of which 3 were waited for; matrix products, arithmetic and copies ran while one was open for 0% of the time, Pallas kernels for 1%

profile of v12, /device:TPU:1, one launch (start us, length us, event | category | flops | bytes accessed | tf_op | source)
XLA Modules:
  0.0 142.8 jit_solution(3690317242435215687)
XLA Ops:
  0.0 1.7 %shard_map.64 = (bf16[32,16,384]{2,1,0:T(8,128)(2,1)}, bf16[144,256]{1,0:T(8,128)(2,1)}) custom-call(s32[16]{0:T(128)} %train_label_hbm.1, bf16[16,256]{1,0:T(8,128)(2,1)} %train_hbm.1, bf16[128,256]{1,0:T(8,128)(2,1)} %valid_hbm.1, s32[1,128]{1,0:T(1,128)} %bitcast.30), custom_call_target="tpu_custom_call" | custom-call | flops 16777216 | bytes 4194304 | tf_op jit(solution)/shard_map/pallas_call | solution.py:273
  1.7 5.6 %all-gather = bf16[288,256]{1,0:T(8,128)(2,1)S(1)} all-gather(bf16[144,256]{1,0:T(8,128)(2,1)} %get-tuple-element.23), channel_id=2, replica_groups=mesh['zh'=4,'zl'=2,'core'=2,'y'=8,'x'=4] {'zl'}, dimensions={0}, use_global_device_ids=true | all-gather | bytes 221184 | tf_op jit(solution)/shard_map/all_gather | solution.py:308
  7.3 5.8 %collective-permute-start = (bf16[2,144,256]{2,1,0:T(8,128)(2,1)S(1)}, bf16[2,144,256]{2,1,0:T(8,128)(2,1)S(1)}, u32[]{:S(2)}, u32[]{:S(2)}) collective-permute-start(bf16[2,144,256]{2,1,0:T(8,128)(2,1)S(1)} %bitcast.23), channel_id=1, source_target_pairs={{0,128},{128,256},{256,384},{384,0},{1,129},{129,257},{257,385},{3... | collective-permute-start | bytes 442376 | tf_op jit(solution)/shard_map/ppermute | solution.py:311
  13.1 8.2 %collective-permute-start.1 = (bf16[2,144,256]{2,1,0:T(8,128)(2,1)S(1)}, bf16[2,144,256]{2,1,0:T(8,128)(2,1)S(1)}, u32[]{:S(2)}, u32[]{:S(2)}) collective-permute-start(bf16[2,144,256]{2,1,0:T(8,128)(2,1)S(1)} %bitcast.24), channel_id=1, source_target_pairs={{0,256},{128,384},{256,0},{384,128},{1,257},{129,385},{257,1},{385... | collective-permute-start | bytes 442376 | tf_op jit(solution)/shard_map/ppermute | solution.py:311
  21.3 3.4 %collective-permute-start.2 = (bf16[2,144,256]{2,1,0:T(8,128)(2,1)S(1)}, bf16[2,144,256]{2,1,0:T(8,128)(2,1)S(1)}, u32[]{:S(2)}, u32[]{:S(2)}) collective-permute-start(bf16[2,144,256]{2,1,0:T(8,128)(2,1)S(1)} %bitcast.25), channel_id=1, source_target_pairs={{0,384},{128,0},{256,128},{384,256},{1,385},{129,1},{257,129},{385... | collective-permute-start | bytes 442376 | tf_op jit(solution)/shard_map/ppermute | solution.py:311
  24.7 9.7 %all-to-all-start = ((bf16[32,16,384]{2,1,0:T(8,128)(2,1)}), bf16[32,16,384]{2,1,0:T(8,128)(2,1)S(1)}, u32[]{:S(2)}, u32[]{:S(2)}) async-start(bf16[32,16,384]{2,1,0:T(8,128)(2,1)} %get-tuple-element.22), calls=%async_computation | async-start | bytes 786432 | tf_op jit(solution)/shard_map/all_to_all | solution.py:254
  34.4 1.6 %collective-permute-done.2 = bf16[2,144,256]{2,1,0:T(8,128)(2,1)S(1)} collective-permute-done((bf16[2,144,256]{2,1,0:T(8,128)(2,1)S(1)}, bf16[2,144,256]{2,1,0:T(8,128)(2,1)S(1)}, u32[]{:S(2)}, u32[]{:S(2)}) %collective-permute-start.2) | collective-permute-done | bytes 147488 | tf_op jit(solution)/shard_map/ppermute | solution.py:311
  36.1 3.2 %collective-permute-start.3 = (bf16[4,2,144,256]{3,2,1,0:T(8,128)(2,1)S(1)}, bf16[4,2,144,256]{3,2,1,0:T(8,128)(2,1)S(1)}, u32[]{:S(2)}, u32[]{:S(2)}) collective-permute-start(bf16[4,2,144,256]{3,2,1,0:T(8,128)(2,1)S(1)} %pad_maximum_fusion.mine_ref), channel_id=1, source_target_pairs={{0,32},{32,0},{1,33},{33,1},{2,34},{34,2},{3,35},{35,3},{4,36},{36... | collective-permute-start | bytes 1769480 | tf_op jit(solution)/shard_map/ppermute | solution.py:312
  42.2 3.6 %all-to-all-done.train_ref = bf16[32,16,384]{2,1,0:T(8,128)(2,1)S(1)} async-done(((bf16[32,16,384]{2,1,0:T(8,128)(2,1)}), bf16[32,16,384]{2,1,0:T(8,128)(2,1)S(1)}, u32[]{:S(2)}, u32[]{:S(2)}) %all-to-all-start) | async-done | bytes 393248 | tf_op jit(solution)/shard_map/all_to_all | solution.py:254
  45.8 4.2 %shard_map.66 = (f32[512,2048]{1,0:T(8,128)S(1)}, f32[24,128]{1,0:T(8,128)S(1)}) custom-call(bf16[32,16,384]{2,1,0:T(8,128)(2,1)S(1)} %all-to-all-done.train_ref, f32[128,128]{1,0:T(8,128)S(1)} %pad.4.table_ref, bf16[2048,256]{1,0:T(8,128)(2,1)S(1)} %get-tuple-element.24.valid_ref, bf16[128,2048]{1,0:T(8,128)(2,1)S(1)} %get-tuple-element.25.hot_ref, ...), custom_call_target="tpu_custom_call" | custom-call | flops 16777216 | bytes 4194304 | tf_op jit(solution)/shard_map/pallas_call | solution.py:273
  50.0 6.8 %all-gather.1 = f32[48,128]{1,0:T(8,128)S(1)} all-gather(f32[24,128]{1,0:T(8,128)S(1)} %get-tuple-element.28), channel_id=3, replica_groups=mesh['zh'=4,'zl'=2,'core'=2,'y'=8,'x'=4] {'core'}, dimensions={0}, use_global_device_ids=true | all-gather | bytes 36864 | tf_op jit(solution)/shard_map/all_gather | solution.py:360
  56.9 14.7 %all_to_all.30.parts_ref = f32[32,16,128]{2,1,0:T(8,128)S(1)} all-to-all(f32[32,16,128]{2,1,0:T(8,128)S(1)} %shard_map.67), channel_id=1, replica_groups={{0,1,2,3,4,5,6,7,8,9,10,11,12,13,14,15,16,17,18,19,20,21,22,23,24,25,26..., dimensions={0} | all-to-all | bytes 524288 | tf_op jit(solution)/shard_map/all_to_all | solution.py:362
  71.7 2.3 %all-gather.2 = f32[32,128]{1,0:T(8,128)S(1)} all-gather(f32[16,128]{1,0:T(8,128)S(1)} %shard_map.68), channel_id=4, replica_groups=mesh['zh'=4,'zl'=2,'core'=2,'y'=8,'x'=4] {'core'}, dimensions={0}, use_global_device_ids=true | all-gather | bytes 24576 | tf_op jit(solution)/shard_map/all_gather | solution.py:364
  74.0 2.1 %shard_map.69 = (f32[24,128]{1,0:T(8,128)S(1)}, f32[4,128]{1,0:T(4,128)S(1)}, f32[16,128]{1,0:T(8,128)S(1)}) custom-call(f32[5,8,128]{2,1,0:T(8,128)S(1)} %broadcast_in_dim.8.refs_0_.flags_ref, f32[512,2048]{1,0:T(8,128)S(1)} %get-tuple-element.27.refs_1_, f32[2,16,128]{2,1,0:T(8,128)S(1)} %bitcast.17, f32[4,128]{1,0:T(4,128)S(1)} %broadcast_in_dim.20.refs_3_, ...), custom_call_target="tpu_custom_call" | custom-call | flops 16777216 | bytes 4194304 | tf_op jit(solution)/shard_map/pallas_call | solution.py:273
  76.1 1.8 %all-gather.3 = f32[48,128]{1,0:T(8,128)S(1)} all-gather(f32[24,128]{1,0:T(8,128)S(1)} %get-tuple-element.29), channel_id=5, replica_groups=mesh['zh'=4,'zl'=2,'core'=2,'y'=8,'x'=4] {'core'}, dimensions={0}, use_global_device_ids=true | all-gather | bytes 36864 | tf_op jit(solution)/shard_map/all_gather | solution.py:360
  78.0 14.7 %all_to_all.31.parts_ref = f32[32,16,128]{2,1,0:T(8,128)S(1)} all-to-all(f32[32,16,128]{2,1,0:T(8,128)S(1)} %shard_map.70), channel_id=1, replica_groups={{0,1,2,3,4,5,6,7,8,9,10,11,12,13,14,15,16,17,18,19,20,21,22,23,24,25,26..., dimensions={0} | all-to-all | bytes 524288 | tf_op jit(solution)/shard_map/all_to_all | solution.py:362
  92.8 2.3 %all-gather.4 = f32[32,128]{1,0:T(8,128)S(1)} all-gather(f32[16,128]{1,0:T(8,128)S(1)} %shard_map.71), channel_id=6, replica_groups=mesh['zh'=4,'zl'=2,'core'=2,'y'=8,'x'=4] {'core'}, dimensions={0}, use_global_device_ids=true | all-gather | bytes 24576 | tf_op jit(solution)/shard_map/all_gather | solution.py:364
  95.1 2.1 %shard_map.72 = (f32[24,128]{1,0:T(8,128)S(1)}, f32[4,128]{1,0:T(4,128)S(1)}, f32[16,128]{1,0:T(8,128)S(1)}) custom-call(f32[5,8,128]{2,1,0:T(8,128)S(1)} %broadcast_in_dim.8.refs_0_.flags_ref, f32[512,2048]{1,0:T(8,128)S(1)} %get-tuple-element.27.refs_1_, f32[2,16,128]{2,1,0:T(8,128)S(1)} %bitcast.19, f32[4,128]{1,0:T(4,128)S(1)} %get-tuple-element.30.refs_3_, ...), custom_call_target="tpu_custom_call" | custom-call | flops 16777216 | bytes 4194304 | tf_op jit(solution)/shard_map/pallas_call | solution.py:273
  97.2 1.8 %all-gather.5 = f32[48,128]{1,0:T(8,128)S(1)} all-gather(f32[24,128]{1,0:T(8,128)S(1)} %get-tuple-element.32), channel_id=7, replica_groups=mesh['zh'=4,'zl'=2,'core'=2,'y'=8,'x'=4] {'core'}, dimensions={0}, use_global_device_ids=true | all-gather | bytes 36864 | tf_op jit(solution)/shard_map/all_gather | solution.py:360
  99.1 14.7 %all_to_all.32.parts_ref = f32[32,16,128]{2,1,0:T(8,128)S(1)} all-to-all(f32[32,16,128]{2,1,0:T(8,128)S(1)} %shard_map.73), channel_id=1, replica_groups={{0,1,2,3,4,5,6,7,8,9,10,11,12,13,14,15,16,17,18,19,20,21,22,23,24,25,26..., dimensions={0} | all-to-all | bytes 524288 | tf_op jit(solution)/shard_map/all_to_all | solution.py:362
  113.9 2.3 %all-gather.6 = f32[32,128]{1,0:T(8,128)S(1)} all-gather(f32[16,128]{1,0:T(8,128)S(1)} %shard_map.74), channel_id=8, replica_groups=mesh['zh'=4,'zl'=2,'core'=2,'y'=8,'x'=4] {'core'}, dimensions={0}, use_global_device_ids=true | all-gather | bytes 24576 | tf_op jit(solution)/shard_map/all_gather | solution.py:364
  116.2 1.3 shard_map.75
  117.5 12.2 %all_to_all.33.refs_0_ = f32[32,4,128]{2,1,0:T(4,128)S(1)} all-to-all(f32[32,4,128]{2,1,0:T(4,128)S(1)} %get-tuple-element.35), channel_id=1, replica_groups=mesh['zh'=4,'zl'=2,'core'=2,'y'=8,'x'=4] {'y','x'}, dimensions={0} | all-to-all | bytes 131072 | tf_op jit(solution)/shard_map/all_to_all | solution.py:254
  129.7 12.3 %all_to_all.34.refs_0_ = f32[16,4,128]{2,1,0:T(4,128)S(1)} all-to-all(f32[16,4,128]{2,1,0:T(4,128)S(1)} %get-tuple-element.37), channel_id=1, replica_groups=mesh['zh'=4,'zl'=2,'core'=2,'y'=8,'x'=4] {'zh','zl','core'}, dimensions={0} | all-to-all | bytes 65536 | tf_op jit(solution)/shard_map/all_to_all | solution.py:254
  (25 shorter events, 4.1 us)
Async XLA Ops:
  0.0 39.4 %copy-start = (s32[100,100]{1,0:T(8,128)S(1)}, s32[100,100]{1,0:T(8,128)}, u32[]{:S(2)}) copy-start(s32[100,100]{1,0:T(8,128)} %param.10) | copy-start | bytes 120004
  0.0 39.4 %copy-start.1 = (f32[4]{0:T(128)S(1)}, f32[4]{0:T(128)}, u32[]{:S(2)}) copy-start(f32[4]{0:T(128)} %param.11) | copy-start | bytes 52
  7.3 27.1 %collective-permute-start = (bf16[2,144,256]{2,1,0:T(8,128)(2,1)S(1)}, bf16[2,144,256]{2,1,0:T(8,128)(2,1)S(1)}, u32[]{:S(2)}, u32[]{:S(2)}) collective-permute-start(bf16[2,144,256]{2,1,0:T(8,128)(2,1)S(1)} %bitcast.23), channel_id=1, source_target_pairs={{0,128},{128,256},{256,384},{384,0},{1,129},{129,257},{257,385},{3... | collective-permute-start | bytes 442376 | tf_op jit(solution)/shard_map/ppermute | solution.py:311
  13.1 21.3 %collective-permute-start.1 = (bf16[2,144,256]{2,1,0:T(8,128)(2,1)S(1)}, bf16[2,144,256]{2,1,0:T(8,128)(2,1)S(1)}, u32[]{:S(2)}, u32[]{:S(2)}) collective-permute-start(bf16[2,144,256]{2,1,0:T(8,128)(2,1)S(1)} %bitcast.24), channel_id=1, source_target_pairs={{0,256},{128,384},{256,0},{384,128},{1,257},{129,385},{257,1},{385... | collective-permute-start | bytes 442376 | tf_op jit(solution)/shard_map/ppermute | solution.py:311
  21.3 14.7 %collective-permute-start.2 = (bf16[2,144,256]{2,1,0:T(8,128)(2,1)S(1)}, bf16[2,144,256]{2,1,0:T(8,128)(2,1)S(1)}, u32[]{:S(2)}, u32[]{:S(2)}) collective-permute-start(bf16[2,144,256]{2,1,0:T(8,128)(2,1)S(1)} %bitcast.25), channel_id=1, source_target_pairs={{0,384},{128,0},{256,128},{384,256},{1,385},{129,1},{257,129},{385... | collective-permute-start | bytes 442376 | tf_op jit(solution)/shard_map/ppermute | solution.py:311
  24.7 21.2 %all-to-all-start = ((bf16[32,16,384]{2,1,0:T(8,128)(2,1)}), bf16[32,16,384]{2,1,0:T(8,128)(2,1)S(1)}, u32[]{:S(2)}, u32[]{:S(2)}) async-start(bf16[32,16,384]{2,1,0:T(8,128)(2,1)} %get-tuple-element.22), calls=%async_computation | async-start | bytes 786432 | tf_op jit(solution)/shard_map/all_to_all | solution.py:254
  36.1 4.9 %collective-permute-start.3 = (bf16[4,2,144,256]{3,2,1,0:T(8,128)(2,1)S(1)}, bf16[4,2,144,256]{3,2,1,0:T(8,128)(2,1)S(1)}, u32[]{:S(2)}, u32[]{:S(2)}) collective-permute-start(bf16[4,2,144,256]{3,2,1,0:T(8,128)(2,1)S(1)} %pad_maximum_fusion.mine_ref), channel_id=1, source_target_pairs={{0,32},{32,0},{1,33},{33,1},{2,34},{34,2},{3,35},{35,3},{4,36},{36... | collective-permute-start | bytes 1769480 | tf_op jit(solution)/shard_map/ppermute | solution.py:312

commit v13 on v12

--- a/solution.py
+++ b/solution.py
@@ -14,7 +14,7 @@
 entropy_scale = 0.05
 UNIT = entropy_scale * math.log(2.0)
 
-ROW = ("zh", "zl", "core")
+ROW = ("half", "place", "core")
 COL = ("y", "x")
 
 VMEM = pl.BlockSpec(memory_space=pltpu.VMEM)
@@ -143,7 +143,7 @@
     class_ids = lax.broadcasted_iota(jnp.int32, (LANES, LANES), 0).astype(jnp.float32)
     for k in range(2 * steps * sides):
         core, z_pair, side = k // (steps * sides), k // sides % steps, k % sides
-        back = lax.rem(where_ref[0] - z_pair + steps, steps)
+        back = lax.rem(where_ref[1] - z_pair + steps, steps)
         block = jnp.where(where_ref[2] == core, mine_ref[back, side], other_ref[back, side])
         here = slice(k * LANES, (k + 1) * LANES)
         points = block[:LANES, :]
@@ -305,10 +305,10 @@
         limit=60,
     )
     train_all = exchange(train_copies, COL)
-    pair = lax.all_gather(valid_pack, "zl", axis=0)
-    steps = lax.axis_size("zh")
-    turn = [[(i, (i + k) % steps) for i in range(steps)] for k in range(steps)]
-    mine = jnp.stack([pair] + [lax.ppermute(pair, "zh", turn[k]) for k in range(1, steps)])
+    pair = lax.all_gather(valid_pack, "half", axis=0)
+    steps, ring = lax.axis_size("place"), lax.axis_size(ROW[:2])
+    turn = [[(i, (i + k) % ring) for i in range(ring)] for k in (1, 2, -1)]
+    mine = jnp.stack([pair] + [lax.ppermute(pair, ROW[:2], there) for there in turn])
     other = lax.ppermute(mine, "core", [(0, 1), (1, 0)])
     where = jnp.stack([lax.axis_index(axis) for axis in ROW + ("x",)]).astype(jnp.int32)
     rows, cols = train_embed.shape[0] * col_size, valid_embed.shape[0] * row_size
@@ -379,7 +379,7 @@
 
 def solution(mesh):
     row_size, col_size = mesh.shape["row"], mesh.shape["col"]
-    finer = jax.sharding.Mesh(mesh.devices.reshape(row_size // 4, 2, 2, col_size // 4, 4), ROW + COL)
+    finer = jax.sharding.Mesh(mesh.devices.reshape(2, row_size // 4, 2, col_size // 4, 4), ROW + COL)
     both = ROW + COL
     placed = (P(both, None), P(both, None), P(both), P(both), P(), P())
     return jax.shard_map(shards, mesh=finer, in_specs=placed, out_specs=P(ROW), check_vma=False)

time: 143 us -> 149 us (1.042)
  blocking collectives: 91.5 us -> 99.7 us
  starting transfers between devices: 30.3 us -> 26.3 us
    all_gather x1, blocking collectives: 5.59 us -> 12.3 us  [shards(): pair = lax.all_gather(valid_pack, 'half', axis=0)]
    ppermute x3, starting transfers between devices: 17.3 us -> 12.2 us  [shards(): lax.ppermute(pair, ROW[:2], there)]
    all_to_all x3, blocking collectives: 44.1 us -> 48.4 us  [shards(): lax.all_to_all(sent, ROW + COL, 0, 0, tiled=True, axis_index_groups=groups)]
    all_to_all x1, waiting for transfers between devices: 3.6 us -> 6.25 us  [exchange(): return lax.all_to_all(copies, axis, 0, 0, tiled=True)]
    all_gather x3, blocking collectives: 10.4 us -> 8.54 us  [shards(): both_cores = lax.all_gather(partials, 'core')]
    ppermute x3, waiting for transfers between devices: 1.63 us -> 0.01 us  [shards(): lax.ppermute(pair, ROW[:2], there)]
  transfers between devices with their start and end apart: 5 -> 5, of which waited for: 3 -> 2; matrix products, arithmetic and copies ran while one was open for 0% -> 0% of each run, Pallas kernels for 1% -> 1%
where the time goes in v13:
time: 149 us; the launch traced here: 148 us
  blocking collectives  99.7 us (67%)
  starting transfers between devices  26.3 us (18%)
  Pallas kernels  13.9 us (9%)
  waiting for transfers between devices  7.42 us (5%)
    all_to_all x3, blocking collectives, shards(): lax.all_to_all(sent, ROW + COL, 0, 0, tiled=True, axis_index_groups=groups)  48.4 us
    all_to_all x2, blocking collectives, exchange(): return lax.all_to_all(copies, axis, 0, 0, tiled=True)  25 us
    pallas_call x14, Pallas kernels, call(): pl.pallas_call(body, out_shape=out_shape, in_specs=specs, out_specs=[VMEM...  13.9 us
    all_gather x1, blocking collectives, shards(): pair = lax.all_gather(valid_pack, 'half', axis=0)  12.3 us
    ppermute x3, starting transfers between devices, shards(): lax.ppermute(pair, ROW[:2], there)  12.2 us
    all_to_all x1, starting transfers between devices, exchange(): return lax.all_to_all(copies, axis, 0, 0, tiled=True)  10.5 us
    all_gather x3, blocking collectives, shards(): both_cores = lax.all_gather(partials, 'core')  8.54 us
    all_to_all x1, waiting for transfers between devices, exchange(): return lax.all_to_all(copies, axis, 0, 0, tiled=True)  6.25 us
  transfers between devices with their start and end apart: 5, of which 2 were waited for; matrix products, arithmetic and copies ran while one was open for 0% of the time, Pallas kernels for 1%

profile of v13, /device:TPU:1, one launch (start us, length us, event | category | flops | bytes accessed | tf_op | source)
XLA Modules:
  0.0 148.0 jit_solution(11111803925579030695)
XLA Ops:
  0.0 1.7 %shard_map.64 = (bf16[32,16,384]{2,1,0:T(8,128)(2,1)}, bf16[144,256]{1,0:T(8,128)(2,1)}) custom-call(s32[16]{0:T(128)} %train_label_hbm.1, bf16[16,256]{1,0:T(8,128)(2,1)} %train_hbm.1, bf16[128,256]{1,0:T(8,128)(2,1)} %valid_hbm.1, s32[1,128]{1,0:T(1,128)} %bitcast.30), custom_call_target="tpu_custom_call" | custom-call | flops 16777216 | bytes 4194304 | tf_op jit(solution)/shard_map/pallas_call | solution.py:273
  1.7 12.3 %all-gather = bf16[288,256]{1,0:T(8,128)(2,1)S(1)} all-gather(bf16[144,256]{1,0:T(8,128)(2,1)} %get-tuple-element.23), channel_id=2, replica_groups=mesh['half'=2,'place'=4,'core'=2,'y'=8,'x'=4] {'half'}, dimensions={0}, use_global_device_ids=true | all-gather | bytes 221184 | tf_op jit(solution)/shard_map/all_gather | solution.py:308
  14.0 3.0 %collective-permute-start = (bf16[2,144,256]{2,1,0:T(8,128)(2,1)S(1)}, bf16[2,144,256]{2,1,0:T(8,128)(2,1)S(1)}, u32[]{:S(2)}, u32[]{:S(2)}) collective-permute-start(bf16[2,144,256]{2,1,0:T(8,128)(2,1)S(1)} %bitcast.23), channel_id=1, source_target_pairs={{0,64},{64,128},{128,192},{192,256},{256,320},{320,384},{384,448},... | collective-permute-start | bytes 442376 | tf_op jit(solution)/shard_map/ppermute | solution.py:311
  17.1 4.6 %collective-permute-start.1 = (bf16[2,144,256]{2,1,0:T(8,128)(2,1)S(1)}, bf16[2,144,256]{2,1,0:T(8,128)(2,1)S(1)}, u32[]{:S(2)}, u32[]{:S(2)}) collective-permute-start(bf16[2,144,256]{2,1,0:T(8,128)(2,1)S(1)} %bitcast.24), channel_id=1, source_target_pairs={{0,128},{64,192},{128,256},{192,320},{256,384},{320,448},{384,0},{... | collective-permute-start | bytes 442376 | tf_op jit(solution)/shard_map/ppermute | solution.py:311
  21.7 4.6 %collective-permute-start.2 = (bf16[2,144,256]{2,1,0:T(8,128)(2,1)S(1)}, bf16[2,144,256]{2,1,0:T(8,128)(2,1)S(1)}, u32[]{:S(2)}, u32[]{:S(2)}) collective-permute-start(bf16[2,144,256]{2,1,0:T(8,128)(2,1)S(1)} %bitcast.25), channel_id=1, source_target_pairs={{0,448},{64,0},{128,64},{192,128},{256,192},{320,256},{384,320},{4... | collective-permute-start | bytes 442376 | tf_op jit(solution)/shard_map/ppermute | solution.py:311
  26.2 10.5 %all-to-all-start = ((bf16[32,16,384]{2,1,0:T(8,128)(2,1)}), bf16[32,16,384]{2,1,0:T(8,128)(2,1)S(1)}, u32[]{:S(2)}, u32[]{:S(2)}) async-start(bf16[32,16,384]{2,1,0:T(8,128)(2,1)} %get-tuple-element.22), calls=%async_computation | async-start | bytes 786432 | tf_op jit(solution)/shard_map/all_to_all | solution.py:254
  36.8 3.6 %collective-permute-start.3 = (bf16[4,2,144,256]{3,2,1,0:T(8,128)(2,1)S(1)}, bf16[4,2,144,256]{3,2,1,0:T(8,128)(2,1)S(1)}, u32[]{:S(2)}, u32[]{:S(2)}) collective-permute-start(bf16[4,2,144,256]{3,2,1,0:T(8,128)(2,1)S(1)} %pad_maximum_fusion.mine_ref), channel_id=1, source_target_pairs={{0,32},{32,0},{1,33},{33,1},{2,34},{34,2},{3,35},{35,3},{4,36},{36... | collective-permute-start | bytes 1769480 | tf_op jit(solution)/shard_map/ppermute | solution.py:312
  42.1 1.3 shard_map.65
  43.3 6.2 %all-to-all-done.train_ref = bf16[32,16,384]{2,1,0:T(8,128)(2,1)S(1)} async-done(((bf16[32,16,384]{2,1,0:T(8,128)(2,1)}), bf16[32,16,384]{2,1,0:T(8,128)(2,1)S(1)}, u32[]{:S(2)}, u32[]{:S(2)}) %all-to-all-start) | async-done | bytes 393248 | tf_op jit(solution)/shard_map/all_to_all | solution.py:254
  49.6 4.2 %shard_map.66 = (f32[512,2048]{1,0:T(8,128)S(1)}, f32[24,128]{1,0:T(8,128)S(1)}) custom-call(bf16[32,16,384]{2,1,0:T(8,128)(2,1)S(1)} %all-to-all-done.train_ref, f32[128,128]{1,0:T(8,128)S(1)} %pad.4.table_ref, bf16[2048,256]{1,0:T(8,128)(2,1)S(1)} %get-tuple-element.24.valid_ref, bf16[128,2048]{1,0:T(8,128)(2,1)S(1)} %get-tuple-element.25.hot_ref, ...), custom_call_target="tpu_custom_call" | custom-call | flops 16777216 | bytes 4194304 | tf_op jit(solution)/shard_map/pallas_call | solution.py:273
  53.8 4.9 %all-gather.1 = f32[48,128]{1,0:T(8,128)S(1)} all-gather(f32[24,128]{1,0:T(8,128)S(1)} %get-tuple-element.28), channel_id=3, replica_groups=mesh['half'=2,'place'=4,'core'=2,'y'=8,'x'=4] {'core'}, dimensions={0}, use_global_device_ids=true | all-gather | bytes 36864 | tf_op jit(solution)/shard_map/all_gather | solution.py:360
  58.8 18.0 %all_to_all.30.parts_ref = f32[32,16,128]{2,1,0:T(8,128)S(1)} all-to-all(f32[32,16,128]{2,1,0:T(8,128)S(1)} %shard_map.67), channel_id=1, replica_groups={{0,1,2,3,4,5,6,7,8,9,10,11,12,13,14,15,16,17,18,19,20,21,22,23,24,25,26..., dimensions={0} | all-to-all | bytes 524288 | tf_op jit(solution)/shard_map/all_to_all | solution.py:362
  76.9 1.8 %all-gather.2 = f32[32,128]{1,0:T(8,128)S(1)} all-gather(f32[16,128]{1,0:T(8,128)S(1)} %shard_map.68), channel_id=4, replica_groups=mesh['half'=2,'place'=4,'core'=2,'y'=8,'x'=4] {'core'}, dimensions={0}, use_global_device_ids=true | all-gather | bytes 24576 | tf_op jit(solution)/shard_map/all_gather | solution.py:364
  78.7 2.1 %shard_map.69 = (f32[24,128]{1,0:T(8,128)S(1)}, f32[4,128]{1,0:T(4,128)S(1)}, f32[16,128]{1,0:T(8,128)S(1)}) custom-call(f32[5,8,128]{2,1,0:T(8,128)S(1)} %broadcast_in_dim.8.refs_0_.flags_ref, f32[512,2048]{1,0:T(8,128)S(1)} %get-tuple-element.27.refs_1_, f32[2,16,128]{2,1,0:T(8,128)S(1)} %bitcast.17, f32[4,128]{1,0:T(4,128)S(1)} %broadcast_in_dim.20.refs_3_, ...), custom_call_target="tpu_custom_call" | custom-call | flops 16777216 | bytes 4194304 | tf_op jit(solution)/shard_map/pallas_call | solution.py:273
  80.8 1.8 %all-gather.3 = f32[48,128]{1,0:T(8,128)S(1)} all-gather(f32[24,128]{1,0:T(8,128)S(1)} %get-tuple-element.29), channel_id=5, replica_groups=mesh['half'=2,'place'=4,'core'=2,'y'=8,'x'=4] {'core'}, dimensions={0}, use_global_device_ids=true | all-gather | bytes 36864 | tf_op jit(solution)/shard_map/all_gather | solution.py:360
  82.7 15.2 %all_to_all.31.parts_ref = f32[32,16,128]{2,1,0:T(8,128)S(1)} all-to-all(f32[32,16,128]{2,1,0:T(8,128)S(1)} %shard_map.70), channel_id=1, replica_groups={{0,1,2,3,4,5,6,7,8,9,10,11,12,13,14,15,16,17,18,19,20,21,22,23,24,25,26..., dimensions={0} | all-to-all | bytes 524288 | tf_op jit(solution)/shard_map/all_to_all | solution.py:362
  98.0 1.8 %all-gather.4 = f32[32,128]{1,0:T(8,128)S(1)} all-gather(f32[16,128]{1,0:T(8,128)S(1)} %shard_map.71), channel_id=6, replica_groups=mesh['half'=2,'place'=4,'core'=2,'y'=8,'x'=4] {'core'}, dimensions={0}, use_global_device_ids=true | all-gather | bytes 24576 | tf_op jit(solution)/shard_map/all_gather | solution.py:364
  99.8 2.1 %shard_map.72 = (f32[24,128]{1,0:T(8,128)S(1)}, f32[4,128]{1,0:T(4,128)S(1)}, f32[16,128]{1,0:T(8,128)S(1)}) custom-call(f32[5,8,128]{2,1,0:T(8,128)S(1)} %broadcast_in_dim.8.refs_0_.flags_ref, f32[512,2048]{1,0:T(8,128)S(1)} %get-tuple-element.27.refs_1_, f32[2,16,128]{2,1,0:T(8,128)S(1)} %bitcast.19, f32[4,128]{1,0:T(4,128)S(1)} %get-tuple-element.30.refs_3_, ...), custom_call_target="tpu_custom_call" | custom-call | flops 16777216 | bytes 4194304 | tf_op jit(solution)/shard_map/pallas_call | solution.py:273
  101.9 1.8 %all-gather.5 = f32[48,128]{1,0:T(8,128)S(1)} all-gather(f32[24,128]{1,0:T(8,128)S(1)} %get-tuple-element.32), channel_id=7, replica_groups=mesh['half'=2,'place'=4,'core'=2,'y'=8,'x'=4] {'core'}, dimensions={0}, use_global_device_ids=true | all-gather | bytes 36864 | tf_op jit(solution)/shard_map/all_gather | solution.py:360
  103.8 15.2 %all_to_all.32.parts_ref = f32[32,16,128]{2,1,0:T(8,128)S(1)} all-to-all(f32[32,16,128]{2,1,0:T(8,128)S(1)} %shard_map.73), channel_id=1, replica_groups={{0,1,2,3,4,5,6,7,8,9,10,11,12,13,14,15,16,17,18,19,20,21,22,23,24,25,26..., dimensions={0} | all-to-all | bytes 524288 | tf_op jit(solution)/shard_map/all_to_all | solution.py:362
  119.1 1.8 %all-gather.6 = f32[32,128]{1,0:T(8,128)S(1)} all-gather(f32[16,128]{1,0:T(8,128)S(1)} %shard_map.74), channel_id=8, replica_groups=mesh['half'=2,'place'=4,'core'=2,'y'=8,'x'=4] {'core'}, dimensions={0}, use_global_device_ids=true | all-gather | bytes 24576 | tf_op jit(solution)/shard_map/all_gather | solution.py:364
  120.9 1.3 shard_map.75
  122.2 12.2 %all_to_all.33.refs_0_ = f32[32,4,128]{2,1,0:T(4,128)S(1)} all-to-all(f32[32,4,128]{2,1,0:T(4,128)S(1)} %get-tuple-element.35), channel_id=1, replica_groups=mesh['half'=2,'place'=4,'core'=2,'y'=8,'x'=4] {'y','x'}, dimensions={0} | all-to-all | bytes 131072 | tf_op jit(solution)/shard_map/all_to_all | solution.py:254
  134.5 12.8 %all_to_all.34.refs_0_ = f32[16,4,128]{2,1,0:T(4,128)S(1)} all-to-all(f32[16,4,128]{2,1,0:T(4,128)S(1)} %get-tuple-element.37), channel_id=1, replica_groups=mesh['half'=2,'place'=4,'core'=2,'y'=8,'x'=4] {'half','place','core'}, dimensions={0} | all-to-all | bytes 65536 | tf_op jit(solution)/shard_map/all_to_all | solution.py:254
  (25 shorter events, 2.9 us)
Async XLA Ops:
  0.0 40.5 %copy-start = (s32[100,100]{1,0:T(8,128)S(1)}, s32[100,100]{1,0:T(8,128)}, u32[]{:S(2)}) copy-start(s32[100,100]{1,0:T(8,128)} %param.10) | copy-start | bytes 120004
  0.0 40.5 %copy-start.1 = (f32[4]{0:T(128)S(1)}, f32[4]{0:T(128)}, u32[]{:S(2)}) copy-start(f32[4]{0:T(128)} %param.11) | copy-start | bytes 52
  14.0 22.7 %collective-permute-start = (bf16[2,144,256]{2,1,0:T(8,128)(2,1)S(1)}, bf16[2,144,256]{2,1,0:T(8,128)(2,1)S(1)}, u32[]{:S(2)}, u32[]{:S(2)}) collective-permute-start(bf16[2,144,256]{2,1,0:T(8,128)(2,1)S(1)} %bitcast.23), channel_id=1, source_target_pairs={{0,64},{64,128},{128,192},{192,256},{256,320},{320,384},{384,448},... | collective-permute-start | bytes 442376 | tf_op jit(solution)/shard_map/ppermute | solution.py:311
  17.1 19.7 %collective-permute-start.1 = (bf16[2,144,256]{2,1,0:T(8,128)(2,1)S(1)}, bf16[2,144,256]{2,1,0:T(8,128)(2,1)S(1)}, u32[]{:S(2)}, u32[]{:S(2)}) collective-permute-start(bf16[2,144,256]{2,1,0:T(8,128)(2,1)S(1)} %bitcast.24), channel_id=1, source_target_pairs={{0,128},{64,192},{128,256},{192,320},{256,384},{320,448},{384,0},{... | collective-permute-start | bytes 442376 | tf_op jit(solution)/shard_map/ppermute | solution.py:311
  21.7 15.1 %collective-permute-start.2 = (bf16[2,144,256]{2,1,0:T(8,128)(2,1)S(1)}, bf16[2,144,256]{2,1,0:T(8,128)(2,1)S(1)}, u32[]{:S(2)}, u32[]{:S(2)}) collective-permute-start(bf16[2,144,256]{2,1,0:T(8,128)(2,1)S(1)} %bitcast.25), channel_id=1, source_target_pairs={{0,448},{64,0},{128,64},{192,128},{256,192},{320,256},{384,320},{4... | collective-permute-start | bytes 442376 | tf_op jit(solution)/shard_map/ppermute | solution.py:311
  26.2 23.4 %all-to-all-start = ((bf16[32,16,384]{2,1,0:T(8,128)(2,1)}), bf16[32,16,384]{2,1,0:T(8,128)(2,1)S(1)}, u32[]{:S(2)}, u32[]{:S(2)}) async-start(bf16[32,16,384]{2,1,0:T(8,128)(2,1)} %get-tuple-element.22), calls=%async_computation | async-start | bytes 786432 | tf_op jit(solution)/shard_map/all_to_all | solution.py:254
  36.8 5.2 %collective-permute-start.3 = (bf16[4,2,144,256]{3,2,1,0:T(8,128)(2,1)S(1)}, bf16[4,2,144,256]{3,2,1,0:T(8,128)(2,1)S(1)}, u32[]{:S(2)}, u32[]{:S(2)}) collective-permute-start(bf16[4,2,144,256]{3,2,1,0:T(8,128)(2,1)S(1)} %pad_maximum_fusion.mine_ref), channel_id=1, source_target_pairs={{0,32},{32,0},{1,33},{33,1},{2,34},{34,2},{3,35},{35,3},{4,36},{36... | collective-permute-start | bytes 1769480 | tf_op jit(solution)/shard_map/ppermute | solution.py:312

commit v14 on v12

--- a/solution.py
+++ b/solution.py
@@ -144,7 +144,8 @@
     for k in range(2 * steps * sides):
         core, z_pair, side = k // (steps * sides), k // sides % steps, k % sides
         back = lax.rem(where_ref[0] - z_pair + steps, steps)
-        block = jnp.where(where_ref[2] == core, mine_ref[back, side], other_ref[back, side])
+        slot = jnp.where(back < 2, back, 5 - back)
+        block = jnp.where(where_ref[2] == core, mine_ref[slot, side], other_ref[slot, side])
         here = slice(k * LANES, (k + 1) * LANES)
         points = block[:LANES, :]
         label_row = block[LANES:, :LANES].astype(jnp.float32)[:1, :]
@@ -308,7 +309,7 @@
     pair = lax.all_gather(valid_pack, "zl", axis=0)
     steps = lax.axis_size("zh")
     turn = [[(i, (i + k) % steps) for i in range(steps)] for k in range(steps)]
-    mine = jnp.stack([pair] + [lax.ppermute(pair, "zh", turn[k]) for k in range(1, steps)])
+    mine = jnp.stack([pair] + [lax.ppermute(pair, "zh", turn[k]) for k in (1, 3, 2)])
     other = lax.ppermute(mine, "core", [(0, 1), (1, 0)])
     where = jnp.stack([lax.axis_index(axis) for axis in ROW + ("x",)]).astype(jnp.int32)
     rows, cols = train_embed.shape[0] * col_size, valid_embed.shape[0] * row_size

time: 143 us -> 143 us (level)
  waiting for transfers between devices: 6.4 us -> 4.76 us
  starting transfers between devices: 30.3 us -> 31.9 us
    ppermute x3, waiting for transfers between devices: 1.63 us -> 0.01 us  [shards(): lax.ppermute(pair, 'zh', turn[k])]
    ppermute x1, starting transfers between devices: 3.24 us -> 4.85 us  [shards(): other = lax.ppermute(mine, 'core', [(0, 1), (1, 0)])]
  transfers between devices with their start and end apart: 5 -> 5, of which waited for: 3 -> 2; matrix products, arithmetic and copies ran while one was open for 0% -> 0% of each run, Pallas kernels for 1% -> 1%
where the time goes in v14:
time: 143 us
  blocking collectives  91.5 us (64%)
  starting transfers between devices  31.9 us (22%)
  Pallas kernels  13.9 us (10%)
  waiting for transfers between devices  4.76 us (3%)
    all_to_all x3, blocking collectives, shards(): lax.all_to_all(sent, ROW + COL, 0, 0, tiled=True, axis_index_groups=groups)  44.1 us
    all_to_all x2, blocking collectives, exchange(): return lax.all_to_all(copies, axis, 0, 0, tiled=True)  24.5 us
    ppermute x3, starting transfers between devices, shards(): lax.ppermute(pair, 'zh', turn[k])  17.3 us
    pallas_call x14, Pallas kernels, call(): pl.pallas_call(body, out_shape=out_shape, in_specs=specs, out_specs=[VMEM...  13.9 us
    all_gather x3, blocking collectives, shards(): both_cores = lax.all_gather(partials, 'core')  10.4 us
    all_to_all x1, starting transfers between devices, exchange(): return lax.all_to_all(copies, axis, 0, 0, tiled=True)  9.68 us
    all_gather x3, blocking collectives, shards(): given = (flags, cost, lax.all_gather(lse, 'core'), row_pot, col_pot)  6.88 us
    all_gather x1, blocking collectives, shards(): pair = lax.all_gather(valid_pack, 'zl', axis=0)  5.59 us
  transfers between devices with their start and end apart: 5, of which 2 were waited for; matrix products, arithmetic and copies ran while one was open for 0% of the time, Pallas kernels for 1%

profile of v14, /device:TPU:1, one launch (start us, length us, event | category | flops | bytes accessed | tf_op | source)
XLA Modules:
  0.0 142.8 jit_solution(15322223469275209818)
XLA Ops:
  0.0 1.7 %shard_map.64 = (bf16[32,16,384]{2,1,0:T(8,128)(2,1)}, bf16[144,256]{1,0:T(8,128)(2,1)}) custom-call(s32[16]{0:T(128)} %train_label_hbm.1, bf16[16,256]{1,0:T(8,128)(2,1)} %train_hbm.1, bf16[128,256]{1,0:T(8,128)(2,1)} %valid_hbm.1, s32[1,128]{1,0:T(1,128)} %bitcast.30), custom_call_target="tpu_custom_call" | custom-call | flops 16777216 | bytes 4194304 | tf_op jit(solution)/shard_map/pallas_call | solution.py:274
  1.7 5.6 %all-gather = bf16[288,256]{1,0:T(8,128)(2,1)S(1)} all-gather(bf16[144,256]{1,0:T(8,128)(2,1)} %get-tuple-element.23), channel_id=2, replica_groups=mesh['zh'=4,'zl'=2,'core'=2,'y'=8,'x'=4] {'zl'}, dimensions={0}, use_global_device_ids=true | all-gather | bytes 221184 | tf_op jit(solution)/shard_map/all_gather | solution.py:309
  7.3 5.8 %collective-permute-start = (bf16[2,144,256]{2,1,0:T(8,128)(2,1)S(1)}, bf16[2,144,256]{2,1,0:T(8,128)(2,1)S(1)}, u32[]{:S(2)}, u32[]{:S(2)}) collective-permute-start(bf16[2,144,256]{2,1,0:T(8,128)(2,1)S(1)} %bitcast.23), channel_id=1, source_target_pairs={{0,128},{128,256},{256,384},{384,0},{1,129},{129,257},{257,385},{3... | collective-permute-start | bytes 442376 | tf_op jit(solution)/shard_map/ppermute | solution.py:312
  13.1 6.1 %collective-permute-start.1 = (bf16[2,144,256]{2,1,0:T(8,128)(2,1)S(1)}, bf16[2,144,256]{2,1,0:T(8,128)(2,1)S(1)}, u32[]{:S(2)}, u32[]{:S(2)}) collective-permute-start(bf16[2,144,256]{2,1,0:T(8,128)(2,1)S(1)} %bitcast.24), channel_id=1, source_target_pairs={{0,384},{128,0},{256,128},{384,256},{1,385},{129,1},{257,129},{385... | collective-permute-start | bytes 442376 | tf_op jit(solution)/shard_map/ppermute | solution.py:312
  19.2 5.5 %collective-permute-start.2 = (bf16[2,144,256]{2,1,0:T(8,128)(2,1)S(1)}, bf16[2,144,256]{2,1,0:T(8,128)(2,1)S(1)}, u32[]{:S(2)}, u32[]{:S(2)}) collective-permute-start(bf16[2,144,256]{2,1,0:T(8,128)(2,1)S(1)} %bitcast.25), channel_id=1, source_target_pairs={{0,256},{128,384},{256,0},{384,128},{1,257},{129,385},{257,1},{385... | collective-permute-start | bytes 442376 | tf_op jit(solution)/shard_map/ppermute | solution.py:312
  24.7 9.7 %all-to-all-start = ((bf16[32,16,384]{2,1,0:T(8,128)(2,1)}), bf16[32,16,384]{2,1,0:T(8,128)(2,1)S(1)}, u32[]{:S(2)}, u32[]{:S(2)}) async-start(bf16[32,16,384]{2,1,0:T(8,128)(2,1)} %get-tuple-element.22), calls=%async_computation | async-start | bytes 786432 | tf_op jit(solution)/shard_map/all_to_all | solution.py:255
  34.5 4.9 %collective-permute-start.3 = (bf16[4,2,144,256]{3,2,1,0:T(8,128)(2,1)S(1)}, bf16[4,2,144,256]{3,2,1,0:T(8,128)(2,1)S(1)}, u32[]{:S(2)}, u32[]{:S(2)}) collective-permute-start(bf16[4,2,144,256]{3,2,1,0:T(8,128)(2,1)S(1)} %pad_maximum_fusion.mine_ref), channel_id=1, source_target_pairs={{0,32},{32,0},{1,33},{33,1},{2,34},{34,2},{3,35},{35,3},{4,36},{36... | collective-permute-start | bytes 1769480 | tf_op jit(solution)/shard_map/ppermute | solution.py:313
  41.0 1.3 shard_map.65
  42.3 3.6 %all-to-all-done.train_ref = bf16[32,16,384]{2,1,0:T(8,128)(2,1)S(1)} async-done(((bf16[32,16,384]{2,1,0:T(8,128)(2,1)}), bf16[32,16,384]{2,1,0:T(8,128)(2,1)S(1)}, u32[]{:S(2)}, u32[]{:S(2)}) %all-to-all-start) | async-done | bytes 393248 | tf_op jit(solution)/shard_map/all_to_all | solution.py:255
  45.8 4.2 %shard_map.66 = (f32[512,2048]{1,0:T(8,128)S(1)}, f32[24,128]{1,0:T(8,128)S(1)}) custom-call(bf16[32,16,384]{2,1,0:T(8,128)(2,1)S(1)} %all-to-all-done.train_ref, f32[128,128]{1,0:T(8,128)S(1)} %pad.4.table_ref, bf16[2048,256]{1,0:T(8,128)(2,1)S(1)} %get-tuple-element.24.valid_ref, bf16[128,2048]{1,0:T(8,128)(2,1)S(1)} %get-tuple-element.25.hot_ref, ...), custom_call_target="tpu_custom_call" | custom-call | flops 16777216 | bytes 4194304 | tf_op jit(solution)/shard_map/pallas_call | solution.py:274
  50.0 6.8 %all-gather.1 = f32[48,128]{1,0:T(8,128)S(1)} all-gather(f32[24,128]{1,0:T(8,128)S(1)} %get-tuple-element.28), channel_id=3, replica_groups=mesh['zh'=4,'zl'=2,'core'=2,'y'=8,'x'=4] {'core'}, dimensions={0}, use_global_device_ids=true | all-gather | bytes 36864 | tf_op jit(solution)/shard_map/all_gather | solution.py:361
  56.9 14.7 %all_to_all.30.parts_ref = f32[32,16,128]{2,1,0:T(8,128)S(1)} all-to-all(f32[32,16,128]{2,1,0:T(8,128)S(1)} %shard_map.67), channel_id=1, replica_groups={{0,1,2,3,4,5,6,7,8,9,10,11,12,13,14,15,16,17,18,19,20,21,22,23,24,25,26..., dimensions={0} | all-to-all | bytes 524288 | tf_op jit(solution)/shard_map/all_to_all | solution.py:363
  71.7 2.3 %all-gather.2 = f32[32,128]{1,0:T(8,128)S(1)} all-gather(f32[16,128]{1,0:T(8,128)S(1)} %shard_map.68), channel_id=4, replica_groups=mesh['zh'=4,'zl'=2,'core'=2,'y'=8,'x'=4] {'core'}, dimensions={0}, use_global_device_ids=true | all-gather | bytes 24576 | tf_op jit(solution)/shard_map/all_gather | solution.py:365
  74.0 2.1 %shard_map.69 = (f32[24,128]{1,0:T(8,128)S(1)}, f32[4,128]{1,0:T(4,128)S(1)}, f32[16,128]{1,0:T(8,128)S(1)}) custom-call(f32[5,8,128]{2,1,0:T(8,128)S(1)} %broadcast_in_dim.8.refs_0_.flags_ref, f32[512,2048]{1,0:T(8,128)S(1)} %get-tuple-element.27.refs_1_, f32[2,16,128]{2,1,0:T(8,128)S(1)} %bitcast.17, f32[4,128]{1,0:T(4,128)S(1)} %broadcast_in_dim.20.refs_3_, ...), custom_call_target="tpu_custom_call" | custom-call | flops 16777216 | bytes 4194304 | tf_op jit(solution)/shard_map/pallas_call | solution.py:274
  76.1 1.8 %all-gather.3 = f32[48,128]{1,0:T(8,128)S(1)} all-gather(f32[24,128]{1,0:T(8,128)S(1)} %get-tuple-element.29), channel_id=5, replica_groups=mesh['zh'=4,'zl'=2,'core'=2,'y'=8,'x'=4] {'core'}, dimensions={0}, use_global_device_ids=true | all-gather | bytes 36864 | tf_op jit(solution)/shard_map/all_gather | solution.py:361
  78.0 14.7 %all_to_all.31.parts_ref = f32[32,16,128]{2,1,0:T(8,128)S(1)} all-to-all(f32[32,16,128]{2,1,0:T(8,128)S(1)} %shard_map.70), channel_id=1, replica_groups={{0,1,2,3,4,5,6,7,8,9,10,11,12,13,14,15,16,17,18,19,20,21,22,23,24,25,26..., dimensions={0} | all-to-all | bytes 524288 | tf_op jit(solution)/shard_map/all_to_all | solution.py:363
  92.8 2.3 %all-gather.4 = f32[32,128]{1,0:T(8,128)S(1)} all-gather(f32[16,128]{1,0:T(8,128)S(1)} %shard_map.71), channel_id=6, replica_groups=mesh['zh'=4,'zl'=2,'core'=2,'y'=8,'x'=4] {'core'}, dimensions={0}, use_global_device_ids=true | all-gather | bytes 24576 | tf_op jit(solution)/shard_map/all_gather | solution.py:365
  95.1 2.1 %shard_map.72 = (f32[24,128]{1,0:T(8,128)S(1)}, f32[4,128]{1,0:T(4,128)S(1)}, f32[16,128]{1,0:T(8,128)S(1)}) custom-call(f32[5,8,128]{2,1,0:T(8,128)S(1)} %broadcast_in_dim.8.refs_0_.flags_ref, f32[512,2048]{1,0:T(8,128)S(1)} %get-tuple-element.27.refs_1_, f32[2,16,128]{2,1,0:T(8,128)S(1)} %bitcast.19, f32[4,128]{1,0:T(4,128)S(1)} %get-tuple-element.30.refs_3_, ...), custom_call_target="tpu_custom_call" | custom-call | flops 16777216 | bytes 4194304 | tf_op jit(solution)/shard_map/pallas_call | solution.py:274
  97.2 1.8 %all-gather.5 = f32[48,128]{1,0:T(8,128)S(1)} all-gather(f32[24,128]{1,0:T(8,128)S(1)} %get-tuple-element.32), channel_id=7, replica_groups=mesh['zh'=4,'zl'=2,'core'=2,'y'=8,'x'=4] {'core'}, dimensions={0}, use_global_device_ids=true | all-gather | bytes 36864 | tf_op jit(solution)/shard_map/all_gather | solution.py:361
  99.1 14.7 %all_to_all.32.parts_ref = f32[32,16,128]{2,1,0:T(8,128)S(1)} all-to-all(f32[32,16,128]{2,1,0:T(8,128)S(1)} %shard_map.73), channel_id=1, replica_groups={{0,1,2,3,4,5,6,7,8,9,10,11,12,13,14,15,16,17,18,19,20,21,22,23,24,25,26..., dimensions={0} | all-to-all | bytes 524288 | tf_op jit(solution)/shard_map/all_to_all | solution.py:363
  113.9 2.3 %all-gather.6 = f32[32,128]{1,0:T(8,128)S(1)} all-gather(f32[16,128]{1,0:T(8,128)S(1)} %shard_map.74), channel_id=8, replica_groups=mesh['zh'=4,'zl'=2,'core'=2,'y'=8,'x'=4] {'core'}, dimensions={0}, use_global_device_ids=true | all-gather | bytes 24576 | tf_op jit(solution)/shard_map/all_gather | solution.py:365
  116.2 1.3 shard_map.75
  117.5 12.2 %all_to_all.33.refs_0_ = f32[32,4,128]{2,1,0:T(4,128)S(1)} all-to-all(f32[32,4,128]{2,1,0:T(4,128)S(1)} %get-tuple-element.35), channel_id=1, replica_groups=mesh['zh'=4,'zl'=2,'core'=2,'y'=8,'x'=4] {'y','x'}, dimensions={0} | all-to-all | bytes 131072 | tf_op jit(solution)/shard_map/all_to_all | solution.py:255
  129.7 12.3 %all_to_all.34.refs_0_ = f32[16,4,128]{2,1,0:T(4,128)S(1)} all-to-all(f32[16,4,128]{2,1,0:T(4,128)S(1)} %get-tuple-element.37), channel_id=1, replica_groups=mesh['zh'=4,'zl'=2,'core'=2,'y'=8,'x'=4] {'zh','zl','core'}, dimensions={0} | all-to-all | bytes 65536 | tf_op jit(solution)/shard_map/all_to_all | solution.py:255
  (25 shorter events, 2.9 us)
Async XLA Ops:
  0.0 39.4 %copy-start = (s32[100,100]{1,0:T(8,128)S(1)}, s32[100,100]{1,0:T(8,128)}, u32[]{:S(2)}) copy-start(s32[100,100]{1,0:T(8,128)} %param.10) | copy-start | bytes 120004
  0.0 39.4 %copy-start.1 = (f32[4]{0:T(128)S(1)}, f32[4]{0:T(128)}, u32[]{:S(2)}) copy-start(f32[4]{0:T(128)} %param.11) | copy-start | bytes 52
  7.3 27.1 %collective-permute-start = (bf16[2,144,256]{2,1,0:T(8,128)(2,1)S(1)}, bf16[2,144,256]{2,1,0:T(8,128)(2,1)S(1)}, u32[]{:S(2)}, u32[]{:S(2)}) collective-permute-start(bf16[2,144,256]{2,1,0:T(8,128)(2,1)S(1)} %bitcast.23), channel_id=1, source_target_pairs={{0,128},{128,256},{256,384},{384,0},{1,129},{129,257},{257,385},{3... | collective-permute-start | bytes 442376 | tf_op jit(solution)/shard_map/ppermute | solution.py:312
  13.1 21.3 %collective-permute-start.1 = (bf16[2,144,256]{2,1,0:T(8,128)(2,1)S(1)}, bf16[2,144,256]{2,1,0:T(8,128)(2,1)S(1)}, u32[]{:S(2)}, u32[]{:S(2)}) collective-permute-start(bf16[2,144,256]{2,1,0:T(8,128)(2,1)S(1)} %bitcast.24), channel_id=1, source_target_pairs={{0,384},{128,0},{256,128},{384,256},{1,385},{129,1},{257,129},{385... | collective-permute-start | bytes 442376 | tf_op jit(solution)/shard_map/ppermute | solution.py:312
  19.2 15.2 %collective-permute-start.2 = (bf16[2,144,256]{2,1,0:T(8,128)(2,1)S(1)}, bf16[2,144,256]{2,1,0:T(8,128)(2,1)S(1)}, u32[]{:S(2)}, u32[]{:S(2)}) collective-permute-start(bf16[2,144,256]{2,1,0:T(8,128)(2,1)S(1)} %bitcast.25), channel_id=1, source_target_pairs={{0,256},{128,384},{256,0},{384,128},{1,257},{129,385},{257,1},{385... | collective-permute-start | bytes 442376 | tf_op jit(solution)/shard_map/ppermute | solution.py:312
  24.7 21.2 %all-to-all-start = ((bf16[32,16,384]{2,1,0:T(8,128)(2,1)}), bf16[32,16,384]{2,1,0:T(8,128)(2,1)S(1)}, u32[]{:S(2)}, u32[]{:S(2)}) async-start(bf16[32,16,384]{2,1,0:T(8,128)(2,1)} %get-tuple-element.22), calls=%async_computation | async-start | bytes 786432 | tf_op jit(solution)/shard_map/all_to_all | solution.py:255
  34.5 6.5 %collective-permute-start.3 = (bf16[4,2,144,256]{3,2,1,0:T(8,128)(2,1)S(1)}, bf16[4,2,144,256]{3,2,1,0:T(8,128)(2,1)S(1)}, u32[]{:S(2)}, u32[]{:S(2)}) collective-permute-start(bf16[4,2,144,256]{3,2,1,0:T(8,128)(2,1)S(1)} %pad_maximum_fusion.mine_ref), channel_id=1, source_target_pairs={{0,32},{32,0},{1,33},{33,1},{2,34},{34,2},{3,35},{35,3},{4,36},{36... | collective-permute-start | bytes 1769480 | tf_op jit(solution)/shard_map/ppermute | solution.py:313

commit v15 on v12

--- a/solution.py
+++ b/solution.py
@@ -36,14 +36,16 @@
         out_ref[a * LANES : (a + 1) * LANES, :] = block.T
 
 
+def tree(combine, tiles):
+    while len(tiles) > 1:
+        odd = tiles[len(tiles) // 2 * 2 :]
+        tiles = [combine(left, right) for left, right in zip(tiles[::2], tiles[1::2])] + odd
+    return tiles[0]
+
+
 def peak_and_sum(tiles):
-    high = tiles[0]
-    for tile in tiles[1:]:
-        high = jnp.maximum(high, tile)
-    total = jnp.exp2(tiles[0] - high)
-    for tile in tiles[1:]:
-        total = total + jnp.exp2(tile - high)
-    return high, total
+    high = tree(jnp.maximum, tiles)
+    return high, tree(jnp.add, [jnp.exp2(tile - high) for tile in tiles])
 
 
 def col_partial(cost_ref, row_ref, high_ref, total_ref):

time: 143 us -> 143 us (level)
  no operation moved by 1% of the time
where the time goes in v15:
time: 143 us
  blocking collectives  91.5 us (64%)
  starting transfers between devices  30.3 us (21%)
  Pallas kernels  13.8 us (10%)
  waiting for transfers between devices  6.4 us (4%)
    all_to_all x3, blocking collectives, shards(): lax.all_to_all(sent, ROW + COL, 0, 0, tiled=True, axis_index_groups=groups)  44.1 us
    all_to_all x2, blocking collectives, exchange(): return lax.all_to_all(copies, axis, 0, 0, tiled=True)  24.5 us
    ppermute x3, starting transfers between devices, shards(): lax.ppermute(pair, 'zh', turn[k])  17.3 us
    pallas_call x14, Pallas kernels, call(): pl.pallas_call(body, out_shape=out_shape, in_specs=specs, out_specs=[VMEM...  13.8 us
    all_gather x3, blocking collectives, shards(): both_cores = lax.all_gather(partials, 'core')  10.4 us
    all_to_all x1, starting transfers between devices, exchange(): return lax.all_to_all(copies, axis, 0, 0, tiled=True)  9.68 us
    all_gather x3, blocking collectives, shards(): given = (flags, cost, lax.all_gather(lse, 'core'), row_pot, col_pot)  6.88 us
    all_gather x1, blocking collectives, shards(): pair = lax.all_gather(valid_pack, 'zl', axis=0)  5.59 us
  transfers between devices with their start and end apart: 5, of which 3 were waited for; matrix products, arithmetic and copies ran while one was open for 0% of the time, Pallas kernels for 1%

profile of v15, /device:TPU:1, one launch (start us, length us, event | category | flops | bytes accessed | tf_op | source)
XLA Modules:
  0.0 142.7 jit_solution(383630862282983753)
XLA Ops:
  0.0 1.7 %shard_map.64 = (bf16[32,16,384]{2,1,0:T(8,128)(2,1)}, bf16[144,256]{1,0:T(8,128)(2,1)}) custom-call(s32[16]{0:T(128)} %train_label_hbm.1, bf16[16,256]{1,0:T(8,128)(2,1)} %train_hbm.1, bf16[128,256]{1,0:T(8,128)(2,1)} %valid_hbm.1, s32[1,128]{1,0:T(1,128)} %bitcast.30), custom_call_target="tpu_custom_call" | custom-call | flops 16777216 | bytes 4194304 | tf_op jit(solution)/shard_map/pallas_call | solution.py:275
  1.7 5.6 %all-gather = bf16[288,256]{1,0:T(8,128)(2,1)S(1)} all-gather(bf16[144,256]{1,0:T(8,128)(2,1)} %get-tuple-element.23), channel_id=2, replica_groups=mesh['zh'=4,'zl'=2,'core'=2,'y'=8,'x'=4] {'zl'}, dimensions={0}, use_global_device_ids=true | all-gather | bytes 221184 | tf_op jit(solution)/shard_map/all_gather | solution.py:310
  7.3 5.8 %collective-permute-start = (bf16[2,144,256]{2,1,0:T(8,128)(2,1)S(1)}, bf16[2,144,256]{2,1,0:T(8,128)(2,1)S(1)}, u32[]{:S(2)}, u32[]{:S(2)}) collective-permute-start(bf16[2,144,256]{2,1,0:T(8,128)(2,1)S(1)} %bitcast.23), channel_id=1, source_target_pairs={{0,128},{128,256},{256,384},{384,0},{1,129},{129,257},{257,385},{3... | collective-permute-start | bytes 442376 | tf_op jit(solution)/shard_map/ppermute | solution.py:313
  13.1 8.2 %collective-permute-start.1 = (bf16[2,144,256]{2,1,0:T(8,128)(2,1)S(1)}, bf16[2,144,256]{2,1,0:T(8,128)(2,1)S(1)}, u32[]{:S(2)}, u32[]{:S(2)}) collective-permute-start(bf16[2,144,256]{2,1,0:T(8,128)(2,1)S(1)} %bitcast.24), channel_id=1, source_target_pairs={{0,256},{128,384},{256,0},{384,128},{1,257},{129,385},{257,1},{385... | collective-permute-start | bytes 442376 | tf_op jit(solution)/shard_map/ppermute | solution.py:313
  21.3 3.4 %collective-permute-start.2 = (bf16[2,144,256]{2,1,0:T(8,128)(2,1)S(1)}, bf16[2,144,256]{2,1,0:T(8,128)(2,1)S(1)}, u32[]{:S(2)}, u32[]{:S(2)}) collective-permute-start(bf16[2,144,256]{2,1,0:T(8,128)(2,1)S(1)} %bitcast.25), channel_id=1, source_target_pairs={{0,384},{128,0},{256,128},{384,256},{1,385},{129,1},{257,129},{385... | collective-permute-start | bytes 442376 | tf_op jit(solution)/shard_map/ppermute | solution.py:313
  24.7 9.7 %all-to-all-start = ((bf16[32,16,384]{2,1,0:T(8,128)(2,1)}), bf16[32,16,384]{2,1,0:T(8,128)(2,1)S(1)}, u32[]{:S(2)}, u32[]{:S(2)}) async-start(bf16[32,16,384]{2,1,0:T(8,128)(2,1)} %get-tuple-element.22), calls=%async_computation | async-start | bytes 786432 | tf_op jit(solution)/shard_map/all_to_all | solution.py:256
  34.4 1.6 %collective-permute-done.2 = bf16[2,144,256]{2,1,0:T(8,128)(2,1)S(1)} collective-permute-done((bf16[2,144,256]{2,1,0:T(8,128)(2,1)S(1)}, bf16[2,144,256]{2,1,0:T(8,128)(2,1)S(1)}, u32[]{:S(2)}, u32[]{:S(2)}) %collective-permute-start.2) | collective-permute-done | bytes 147488 | tf_op jit(solution)/shard_map/ppermute | solution.py:313
  36.1 3.2 %collective-permute-start.3 = (bf16[4,2,144,256]{3,2,1,0:T(8,128)(2,1)S(1)}, bf16[4,2,144,256]{3,2,1,0:T(8,128)(2,1)S(1)}, u32[]{:S(2)}, u32[]{:S(2)}) collective-permute-start(bf16[4,2,144,256]{3,2,1,0:T(8,128)(2,1)S(1)} %pad_maximum_fusion.mine_ref), channel_id=1, source_target_pairs={{0,32},{32,0},{1,33},{33,1},{2,34},{34,2},{3,35},{35,3},{4,36},{36... | collective-permute-start | bytes 1769480 | tf_op jit(solution)/shard_map/ppermute | solution.py:314
  41.0 1.3 shard_map.65
  42.2 3.6 %all-to-all-done.train_ref = bf16[32,16,384]{2,1,0:T(8,128)(2,1)S(1)} async-done(((bf16[32,16,384]{2,1,0:T(8,128)(2,1)}), bf16[32,16,384]{2,1,0:T(8,128)(2,1)S(1)}, u32[]{:S(2)}, u32[]{:S(2)}) %all-to-all-start) | async-done | bytes 393248 | tf_op jit(solution)/shard_map/all_to_all | solution.py:256
  45.8 4.1 %shard_map.66 = (f32[512,2048]{1,0:T(8,128)S(1)}, f32[24,128]{1,0:T(8,128)S(1)}) custom-call(bf16[32,16,384]{2,1,0:T(8,128)(2,1)S(1)} %all-to-all-done.train_ref, f32[128,128]{1,0:T(8,128)S(1)} %pad.4.table_ref, bf16[2048,256]{1,0:T(8,128)(2,1)S(1)} %get-tuple-element.24.valid_ref, bf16[128,2048]{1,0:T(8,128)(2,1)S(1)} %get-tuple-element.25.hot_ref, ...), custom_call_target="tpu_custom_call" | custom-call | flops 16777216 | bytes 4194304 | tf_op jit(solution)/shard_map/pallas_call | solution.py:275
  50.0 6.8 %all-gather.1 = f32[48,128]{1,0:T(8,128)S(1)} all-gather(f32[24,128]{1,0:T(8,128)S(1)} %get-tuple-element.28), channel_id=3, replica_groups=mesh['zh'=4,'zl'=2,'core'=2,'y'=8,'x'=4] {'core'}, dimensions={0}, use_global_device_ids=true | all-gather | bytes 36864 | tf_op jit(solution)/shard_map/all_gather | solution.py:362
  56.9 14.7 %all_to_all.30.parts_ref = f32[32,16,128]{2,1,0:T(8,128)S(1)} all-to-all(f32[32,16,128]{2,1,0:T(8,128)S(1)} %shard_map.67), channel_id=1, replica_groups={{0,1,2,3,4,5,6,7,8,9,10,11,12,13,14,15,16,17,18,19,20,21,22,23,24,25,26..., dimensions={0} | all-to-all | bytes 524288 | tf_op jit(solution)/shard_map/all_to_all | solution.py:364
  71.6 2.3 %all-gather.2 = f32[32,128]{1,0:T(8,128)S(1)} all-gather(f32[16,128]{1,0:T(8,128)S(1)} %shard_map.68), channel_id=4, replica_groups=mesh['zh'=4,'zl'=2,'core'=2,'y'=8,'x'=4] {'core'}, dimensions={0}, use_global_device_ids=true | all-gather | bytes 24576 | tf_op jit(solution)/shard_map/all_gather | solution.py:366
  73.9 2.1 %shard_map.69 = (f32[24,128]{1,0:T(8,128)S(1)}, f32[4,128]{1,0:T(4,128)S(1)}, f32[16,128]{1,0:T(8,128)S(1)}) custom-call(f32[5,8,128]{2,1,0:T(8,128)S(1)} %broadcast_in_dim.8.refs_0_.flags_ref, f32[512,2048]{1,0:T(8,128)S(1)} %get-tuple-element.27.refs_1_, f32[2,16,128]{2,1,0:T(8,128)S(1)} %bitcast.17, f32[4,128]{1,0:T(4,128)S(1)} %broadcast_in_dim.20.refs_3_, ...), custom_call_target="tpu_custom_call" | custom-call | flops 16777216 | bytes 4194304 | tf_op jit(solution)/shard_map/pallas_call | solution.py:275
  76.1 1.8 %all-gather.3 = f32[48,128]{1,0:T(8,128)S(1)} all-gather(f32[24,128]{1,0:T(8,128)S(1)} %get-tuple-element.29), channel_id=5, replica_groups=mesh['zh'=4,'zl'=2,'core'=2,'y'=8,'x'=4] {'core'}, dimensions={0}, use_global_device_ids=true | all-gather | bytes 36864 | tf_op jit(solution)/shard_map/all_gather | solution.py:362
  77.9 14.7 %all_to_all.31.parts_ref = f32[32,16,128]{2,1,0:T(8,128)S(1)} all-to-all(f32[32,16,128]{2,1,0:T(8,128)S(1)} %shard_map.70), channel_id=1, replica_groups={{0,1,2,3,4,5,6,7,8,9,10,11,12,13,14,15,16,17,18,19,20,21,22,23,24,25,26..., dimensions={0} | all-to-all | bytes 524288 | tf_op jit(solution)/shard_map/all_to_all | solution.py:364
  92.7 2.3 %all-gather.4 = f32[32,128]{1,0:T(8,128)S(1)} all-gather(f32[16,128]{1,0:T(8,128)S(1)} %shard_map.71), channel_id=6, replica_groups=mesh['zh'=4,'zl'=2,'core'=2,'y'=8,'x'=4] {'core'}, dimensions={0}, use_global_device_ids=true | all-gather | bytes 24576 | tf_op jit(solution)/shard_map/all_gather | solution.py:366
  95.0 2.1 %shard_map.72 = (f32[24,128]{1,0:T(8,128)S(1)}, f32[4,128]{1,0:T(4,128)S(1)}, f32[16,128]{1,0:T(8,128)S(1)}) custom-call(f32[5,8,128]{2,1,0:T(8,128)S(1)} %broadcast_in_dim.8.refs_0_.flags_ref, f32[512,2048]{1,0:T(8,128)S(1)} %get-tuple-element.27.refs_1_, f32[2,16,128]{2,1,0:T(8,128)S(1)} %bitcast.19, f32[4,128]{1,0:T(4,128)S(1)} %get-tuple-element.30.refs_3_, ...), custom_call_target="tpu_custom_call" | custom-call | flops 16777216 | bytes 4194304 | tf_op jit(solution)/shard_map/pallas_call | solution.py:275
  97.1 1.8 %all-gather.5 = f32[48,128]{1,0:T(8,128)S(1)} all-gather(f32[24,128]{1,0:T(8,128)S(1)} %get-tuple-element.32), channel_id=7, replica_groups=mesh['zh'=4,'zl'=2,'core'=2,'y'=8,'x'=4] {'core'}, dimensions={0}, use_global_device_ids=true | all-gather | bytes 36864 | tf_op jit(solution)/shard_map/all_gather | solution.py:362
  99.0 14.7 %all_to_all.32.parts_ref = f32[32,16,128]{2,1,0:T(8,128)S(1)} all-to-all(f32[32,16,128]{2,1,0:T(8,128)S(1)} %shard_map.73), channel_id=1, replica_groups={{0,1,2,3,4,5,6,7,8,9,10,11,12,13,14,15,16,17,18,19,20,21,22,23,24,25,26..., dimensions={0} | all-to-all | bytes 524288 | tf_op jit(solution)/shard_map/all_to_all | solution.py:364
  113.8 2.3 %all-gather.6 = f32[32,128]{1,0:T(8,128)S(1)} all-gather(f32[16,128]{1,0:T(8,128)S(1)} %shard_map.74), channel_id=8, replica_groups=mesh['zh'=4,'zl'=2,'core'=2,'y'=8,'x'=4] {'core'}, dimensions={0}, use_global_device_ids=true | all-gather | bytes 24576 | tf_op jit(solution)/shard_map/all_gather | solution.py:366
  117.4 12.2 %all_to_all.33.refs_0_ = f32[32,4,128]{2,1,0:T(4,128)S(1)} all-to-all(f32[32,4,128]{2,1,0:T(4,128)S(1)} %get-tuple-element.35), channel_id=1, replica_groups=mesh['zh'=4,'zl'=2,'core'=2,'y'=8,'x'=4] {'y','x'}, dimensions={0} | all-to-all | bytes 131072 | tf_op jit(solution)/shard_map/all_to_all | solution.py:256
  129.6 12.3 %all_to_all.34.refs_0_ = f32[16,4,128]{2,1,0:T(4,128)S(1)} all-to-all(f32[16,4,128]{2,1,0:T(4,128)S(1)} %get-tuple-element.37), channel_id=1, replica_groups=mesh['zh'=4,'zl'=2,'core'=2,'y'=8,'x'=4] {'zh','zl','core'}, dimensions={0} | all-to-all | bytes 65536 | tf_op jit(solution)/shard_map/all_to_all | solution.py:256
  (25 shorter events, 4.1 us)
Async XLA Ops:
  0.0 39.4 %copy-start = (s32[100,100]{1,0:T(8,128)S(1)}, s32[100,100]{1,0:T(8,128)}, u32[]{:S(2)}) copy-start(s32[100,100]{1,0:T(8,128)} %param.10) | copy-start | bytes 120004
  0.0 39.4 %copy-start.1 = (f32[4]{0:T(128)S(1)}, f32[4]{0:T(128)}, u32[]{:S(2)}) copy-start(f32[4]{0:T(128)} %param.11) | copy-start | bytes 52
  7.3 27.1 %collective-permute-start = (bf16[2,144,256]{2,1,0:T(8,128)(2,1)S(1)}, bf16[2,144,256]{2,1,0:T(8,128)(2,1)S(1)}, u32[]{:S(2)}, u32[]{:S(2)}) collective-permute-start(bf16[2,144,256]{2,1,0:T(8,128)(2,1)S(1)} %bitcast.23), channel_id=1, source_target_pairs={{0,128},{128,256},{256,384},{384,0},{1,129},{129,257},{257,385},{3... | collective-permute-start | bytes 442376 | tf_op jit(solution)/shard_map/ppermute | solution.py:313
  13.1 21.3 %collective-permute-start.1 = (bf16[2,144,256]{2,1,0:T(8,128)(2,1)S(1)}, bf16[2,144,256]{2,1,0:T(8,128)(2,1)S(1)}, u32[]{:S(2)}, u32[]{:S(2)}) collective-permute-start(bf16[2,144,256]{2,1,0:T(8,128)(2,1)S(1)} %bitcast.24), channel_id=1, source_target_pairs={{0,256},{128,384},{256,0},{384,128},{1,257},{129,385},{257,1},{385... | collective-permute-start | bytes 442376 | tf_op jit(solution)/shard_map/ppermute | solution.py:313
  21.3 14.7 %collective-permute-start.2 = (bf16[2,144,256]{2,1,0:T(8,128)(2,1)S(1)}, bf16[2,144,256]{2,1,0:T(8,128)(2,1)S(1)}, u32[]{:S(2)}, u32[]{:S(2)}) collective-permute-start(bf16[2,144,256]{2,1,0:T(8,128)(2,1)S(1)} %bitcast.25), channel_id=1, source_target_pairs={{0,384},{128,0},{256,128},{384,256},{1,385},{129,1},{257,129},{385... | collective-permute-start | bytes 442376 | tf_op jit(solution)/shard_map/ppermute | solution.py:313
  24.7 21.2 %all-to-all-start = ((bf16[32,16,384]{2,1,0:T(8,128)(2,1)}), bf16[32,16,384]{2,1,0:T(8,128)(2,1)S(1)}, u32[]{:S(2)}, u32[]{:S(2)}) async-start(bf16[32,16,384]{2,1,0:T(8,128)(2,1)} %get-tuple-element.22), calls=%async_computation | async-start | bytes 786432 | tf_op jit(solution)/shard_map/all_to_all | solution.py:256
  36.1 4.9 %collective-permute-start.3 = (bf16[4,2,144,256]{3,2,1,0:T(8,128)(2,1)S(1)}, bf16[4,2,144,256]{3,2,1,0:T(8,128)(2,1)S(1)}, u32[]{:S(2)}, u32[]{:S(2)}) collective-permute-start(bf16[4,2,144,256]{3,2,1,0:T(8,128)(2,1)S(1)} %pad_maximum_fusion.mine_ref), channel_id=1, source_target_pairs={{0,32},{32,0},{1,33},{33,1},{2,34},{34,2},{3,35},{35,3},{4,36},{36... | collective-permute-start | bytes 1769480 | tf_op jit(solution)/shard_map/ppermute | solution.py:314

commit v16 on v12

--- a/solution.py
+++ b/solution.py
@@ -80,7 +80,7 @@
         high_ref[here, :], total_ref[here, :] = peak_and_sum(tiles)
         return carry
 
-    lax.fori_loop(0, rows // SUB, group_step, 0, unroll=4)
+    lax.fori_loop(0, rows // SUB, group_step, 0, unroll=8)
     out = []
     for a in range(rows // LANES):
         block = slice(a * LANES, (a + 1) * LANES)

time: 143 us -> 143 us (level)
  no operation moved by 1% of the time
where the time goes in v16:
time: 143 us
  blocking collectives  91.5 us (64%)
  starting transfers between devices  30.3 us (21%)
  Pallas kernels  13.6 us (10%)
  waiting for transfers between devices  6.4 us (4%)
    all_to_all x3, blocking collectives, shards(): lax.all_to_all(sent, ROW + COL, 0, 0, tiled=True, axis_index_groups=groups)  44.1 us
    all_to_all x2, blocking collectives, exchange(): return lax.all_to_all(copies, axis, 0, 0, tiled=True)  24.5 us
    ppermute x3, starting transfers between devices, shards(): lax.ppermute(pair, 'zh', turn[k])  17.3 us
    pallas_call x14, Pallas kernels, call(): pl.pallas_call(body, out_shape=out_shape, in_specs=specs, out_specs=[VMEM...  13.6 us
    all_gather x3, blocking collectives, shards(): both_cores = lax.all_gather(partials, 'core')  10.4 us
    all_to_all x1, starting transfers between devices, exchange(): return lax.all_to_all(copies, axis, 0, 0, tiled=True)  9.68 us
    all_gather x3, blocking collectives, shards(): given = (flags, cost, lax.all_gather(lse, 'core'), row_pot, col_pot)  6.88 us
    all_gather x1, blocking collectives, shards(): pair = lax.all_gather(valid_pack, 'zl', axis=0)  5.59 us
  transfers between devices with their start and end apart: 5, of which 3 were waited for; matrix products, arithmetic and copies ran while one was open for 0% of the time, Pallas kernels for 1%

profile of v16, /device:TPU:1, one launch (start us, length us, event | category | flops | bytes accessed | tf_op | source)
XLA Modules:
  0.0 142.5 jit_solution(1840290487793018402)
XLA Ops:
  0.0 1.7 %shard_map.64 = (bf16[32,16,384]{2,1,0:T(8,128)(2,1)}, bf16[144,256]{1,0:T(8,128)(2,1)}) custom-call(s32[16]{0:T(128)} %train_label_hbm.1, bf16[16,256]{1,0:T(8,128)(2,1)} %train_hbm.1, bf16[128,256]{1,0:T(8,128)(2,1)} %valid_hbm.1, s32[1,128]{1,0:T(1,128)} %bitcast.30), custom_call_target="tpu_custom_call" | custom-call | flops 16777216 | bytes 4194304 | tf_op jit(solution)/shard_map/pallas_call | solution.py:273
  1.7 5.6 %all-gather = bf16[288,256]{1,0:T(8,128)(2,1)S(1)} all-gather(bf16[144,256]{1,0:T(8,128)(2,1)} %get-tuple-element.23), channel_id=2, replica_groups=mesh['zh'=4,'zl'=2,'core'=2,'y'=8,'x'=4] {'zl'}, dimensions={0}, use_global_device_ids=true | all-gather | bytes 221184 | tf_op jit(solution)/shard_map/all_gather | solution.py:308
  7.3 5.8 %collective-permute-start = (bf16[2,144,256]{2,1,0:T(8,128)(2,1)S(1)}, bf16[2,144,256]{2,1,0:T(8,128)(2,1)S(1)}, u32[]{:S(2)}, u32[]{:S(2)}) collective-permute-start(bf16[2,144,256]{2,1,0:T(8,128)(2,1)S(1)} %bitcast.23), channel_id=1, source_target_pairs={{0,128},{128,256},{256,384},{384,0},{1,129},{129,257},{257,385},{3... | collective-permute-start | bytes 442376 | tf_op jit(solution)/shard_map/ppermute | solution.py:311
  13.1 8.2 %collective-permute-start.1 = (bf16[2,144,256]{2,1,0:T(8,128)(2,1)S(1)}, bf16[2,144,256]{2,1,0:T(8,128)(2,1)S(1)}, u32[]{:S(2)}, u32[]{:S(2)}) collective-permute-start(bf16[2,144,256]{2,1,0:T(8,128)(2,1)S(1)} %bitcast.24), channel_id=1, source_target_pairs={{0,256},{128,384},{256,0},{384,128},{1,257},{129,385},{257,1},{385... | collective-permute-start | bytes 442376 | tf_op jit(solution)/shard_map/ppermute | solution.py:311
  21.3 3.4 %collective-permute-start.2 = (bf16[2,144,256]{2,1,0:T(8,128)(2,1)S(1)}, bf16[2,144,256]{2,1,0:T(8,128)(2,1)S(1)}, u32[]{:S(2)}, u32[]{:S(2)}) collective-permute-start(bf16[2,144,256]{2,1,0:T(8,128)(2,1)S(1)} %bitcast.25), channel_id=1, source_target_pairs={{0,384},{128,0},{256,128},{384,256},{1,385},{129,1},{257,129},{385... | collective-permute-start | bytes 442376 | tf_op jit(solution)/shard_map/ppermute | solution.py:311
  24.7 9.7 %all-to-all-start = ((bf16[32,16,384]{2,1,0:T(8,128)(2,1)}), bf16[32,16,384]{2,1,0:T(8,128)(2,1)S(1)}, u32[]{:S(2)}, u32[]{:S(2)}) async-start(bf16[32,16,384]{2,1,0:T(8,128)(2,1)} %get-tuple-element.22), calls=%async_computation | async-start | bytes 786432 | tf_op jit(solution)/shard_map/all_to_all | solution.py:254
  34.4 1.6 %collective-permute-done.2 = bf16[2,144,256]{2,1,0:T(8,128)(2,1)S(1)} collective-permute-done((bf16[2,144,256]{2,1,0:T(8,128)(2,1)S(1)}, bf16[2,144,256]{2,1,0:T(8,128)(2,1)S(1)}, u32[]{:S(2)}, u32[]{:S(2)}) %collective-permute-start.2) | collective-permute-done | bytes 147488 | tf_op jit(solution)/shard_map/ppermute | solution.py:311
  36.1 3.2 %collective-permute-start.3 = (bf16[4,2,144,256]{3,2,1,0:T(8,128)(2,1)S(1)}, bf16[4,2,144,256]{3,2,1,0:T(8,128)(2,1)S(1)}, u32[]{:S(2)}, u32[]{:S(2)}) collective-permute-start(bf16[4,2,144,256]{3,2,1,0:T(8,128)(2,1)S(1)} %pad_maximum_fusion.mine_ref), channel_id=1, source_target_pairs={{0,32},{32,0},{1,33},{33,1},{2,34},{34,2},{3,35},{35,3},{4,36},{36... | collective-permute-start | bytes 1769480 | tf_op jit(solution)/shard_map/ppermute | solution.py:312
  41.0 1.3 shard_map.65
  42.2 3.6 %all-to-all-done.train_ref = bf16[32,16,384]{2,1,0:T(8,128)(2,1)S(1)} async-done(((bf16[32,16,384]{2,1,0:T(8,128)(2,1)}), bf16[32,16,384]{2,1,0:T(8,128)(2,1)S(1)}, u32[]{:S(2)}, u32[]{:S(2)}) %all-to-all-start) | async-done | bytes 393248 | tf_op jit(solution)/shard_map/all_to_all | solution.py:254
  45.8 4.2 %shard_map.66 = (f32[512,2048]{1,0:T(8,128)S(1)}, f32[24,128]{1,0:T(8,128)S(1)}) custom-call(bf16[32,16,384]{2,1,0:T(8,128)(2,1)S(1)} %all-to-all-done.train_ref, f32[128,128]{1,0:T(8,128)S(1)} %pad.4.table_ref, bf16[2048,256]{1,0:T(8,128)(2,1)S(1)} %get-tuple-element.24.valid_ref, bf16[128,2048]{1,0:T(8,128)(2,1)S(1)} %get-tuple-element.25.hot_ref, ...), custom_call_target="tpu_custom_call" | custom-call | flops 16777216 | bytes 4194304 | tf_op jit(solution)/shard_map/pallas_call | solution.py:273
  50.1 6.8 %all-gather.1 = f32[48,128]{1,0:T(8,128)S(1)} all-gather(f32[24,128]{1,0:T(8,128)S(1)} %get-tuple-element.28), channel_id=3, replica_groups=mesh['zh'=4,'zl'=2,'core'=2,'y'=8,'x'=4] {'core'}, dimensions={0}, use_global_device_ids=true | all-gather | bytes 36864 | tf_op jit(solution)/shard_map/all_gather | solution.py:360
  56.9 14.7 %all_to_all.30.parts_ref = f32[32,16,128]{2,1,0:T(8,128)S(1)} all-to-all(f32[32,16,128]{2,1,0:T(8,128)S(1)} %shard_map.67), channel_id=1, replica_groups={{0,1,2,3,4,5,6,7,8,9,10,11,12,13,14,15,16,17,18,19,20,21,22,23,24,25,26..., dimensions={0} | all-to-all | bytes 524288 | tf_op jit(solution)/shard_map/all_to_all | solution.py:362
  71.7 2.3 %all-gather.2 = f32[32,128]{1,0:T(8,128)S(1)} all-gather(f32[16,128]{1,0:T(8,128)S(1)} %shard_map.68), channel_id=4, replica_groups=mesh['zh'=4,'zl'=2,'core'=2,'y'=8,'x'=4] {'core'}, dimensions={0}, use_global_device_ids=true | all-gather | bytes 24576 | tf_op jit(solution)/shard_map/all_gather | solution.py:364
  74.0 2.0 %shard_map.69 = (f32[24,128]{1,0:T(8,128)S(1)}, f32[4,128]{1,0:T(4,128)S(1)}, f32[16,128]{1,0:T(8,128)S(1)}) custom-call(f32[5,8,128]{2,1,0:T(8,128)S(1)} %broadcast_in_dim.8.refs_0_.flags_ref, f32[512,2048]{1,0:T(8,128)S(1)} %get-tuple-element.27.refs_1_, f32[2,16,128]{2,1,0:T(8,128)S(1)} %bitcast.17, f32[4,128]{1,0:T(4,128)S(1)} %broadcast_in_dim.20.refs_3_, ...), custom_call_target="tpu_custom_call" | custom-call | flops 16777216 | bytes 4194304 | tf_op jit(solution)/shard_map/pallas_call | solution.py:273
  76.1 1.8 %all-gather.3 = f32[48,128]{1,0:T(8,128)S(1)} all-gather(f32[24,128]{1,0:T(8,128)S(1)} %get-tuple-element.29), channel_id=5, replica_groups=mesh['zh'=4,'zl'=2,'core'=2,'y'=8,'x'=4] {'core'}, dimensions={0}, use_global_device_ids=true | all-gather | bytes 36864 | tf_op jit(solution)/shard_map/all_gather | solution.py:360
  77.9 14.7 %all_to_all.31.parts_ref = f32[32,16,128]{2,1,0:T(8,128)S(1)} all-to-all(f32[32,16,128]{2,1,0:T(8,128)S(1)} %shard_map.70), channel_id=1, replica_groups={{0,1,2,3,4,5,6,7,8,9,10,11,12,13,14,15,16,17,18,19,20,21,22,23,24,25,26..., dimensions={0} | all-to-all | bytes 524288 | tf_op jit(solution)/shard_map/all_to_all | solution.py:362
  92.7 2.3 %all-gather.4 = f32[32,128]{1,0:T(8,128)S(1)} all-gather(f32[16,128]{1,0:T(8,128)S(1)} %shard_map.71), channel_id=6, replica_groups=mesh['zh'=4,'zl'=2,'core'=2,'y'=8,'x'=4] {'core'}, dimensions={0}, use_global_device_ids=true | all-gather | bytes 24576 | tf_op jit(solution)/shard_map/all_gather | solution.py:364
  95.0 2.0 %shard_map.72 = (f32[24,128]{1,0:T(8,128)S(1)}, f32[4,128]{1,0:T(4,128)S(1)}, f32[16,128]{1,0:T(8,128)S(1)}) custom-call(f32[5,8,128]{2,1,0:T(8,128)S(1)} %broadcast_in_dim.8.refs_0_.flags_ref, f32[512,2048]{1,0:T(8,128)S(1)} %get-tuple-element.27.refs_1_, f32[2,16,128]{2,1,0:T(8,128)S(1)} %bitcast.19, f32[4,128]{1,0:T(4,128)S(1)} %get-tuple-element.30.refs_3_, ...), custom_call_target="tpu_custom_call" | custom-call | flops 16777216 | bytes 4194304 | tf_op jit(solution)/shard_map/pallas_call | solution.py:273
  97.0 1.8 %all-gather.5 = f32[48,128]{1,0:T(8,128)S(1)} all-gather(f32[24,128]{1,0:T(8,128)S(1)} %get-tuple-element.32), channel_id=7, replica_groups=mesh['zh'=4,'zl'=2,'core'=2,'y'=8,'x'=4] {'core'}, dimensions={0}, use_global_device_ids=true | all-gather | bytes 36864 | tf_op jit(solution)/shard_map/all_gather | solution.py:360
  98.9 14.7 %all_to_all.32.parts_ref = f32[32,16,128]{2,1,0:T(8,128)S(1)} all-to-all(f32[32,16,128]{2,1,0:T(8,128)S(1)} %shard_map.73), channel_id=1, replica_groups={{0,1,2,3,4,5,6,7,8,9,10,11,12,13,14,15,16,17,18,19,20,21,22,23,24,25,26..., dimensions={0} | all-to-all | bytes 524288 | tf_op jit(solution)/shard_map/all_to_all | solution.py:362
  113.7 2.3 %all-gather.6 = f32[32,128]{1,0:T(8,128)S(1)} all-gather(f32[16,128]{1,0:T(8,128)S(1)} %shard_map.74), channel_id=8, replica_groups=mesh['zh'=4,'zl'=2,'core'=2,'y'=8,'x'=4] {'core'}, dimensions={0}, use_global_device_ids=true | all-gather | bytes 24576 | tf_op jit(solution)/shard_map/all_gather | solution.py:364
  117.2 12.2 %all_to_all.33.refs_0_ = f32[32,4,128]{2,1,0:T(4,128)S(1)} all-to-all(f32[32,4,128]{2,1,0:T(4,128)S(1)} %get-tuple-element.35), channel_id=1, replica_groups=mesh['zh'=4,'zl'=2,'core'=2,'y'=8,'x'=4] {'y','x'}, dimensions={0} | all-to-all | bytes 131072 | tf_op jit(solution)/shard_map/all_to_all | solution.py:254
  129.5 12.3 %all_to_all.34.refs_0_ = f32[16,4,128]{2,1,0:T(4,128)S(1)} all-to-all(f32[16,4,128]{2,1,0:T(4,128)S(1)} %get-tuple-element.37), channel_id=1, replica_groups=mesh['zh'=4,'zl'=2,'core'=2,'y'=8,'x'=4] {'zh','zl','core'}, dimensions={0} | all-to-all | bytes 65536 | tf_op jit(solution)/shard_map/all_to_all | solution.py:254
  (25 shorter events, 4.1 us)
Async XLA Ops:
  0.0 39.4 %copy-start = (s32[100,100]{1,0:T(8,128)S(1)}, s32[100,100]{1,0:T(8,128)}, u32[]{:S(2)}) copy-start(s32[100,100]{1,0:T(8,128)} %param.10) | copy-start | bytes 120004
  0.0 39.4 %copy-start.1 = (f32[4]{0:T(128)S(1)}, f32[4]{0:T(128)}, u32[]{:S(2)}) copy-start(f32[4]{0:T(128)} %param.11) | copy-start | bytes 52
  7.3 27.1 %collective-permute-start = (bf16[2,144,256]{2,1,0:T(8,128)(2,1)S(1)}, bf16[2,144,256]{2,1,0:T(8,128)(2,1)S(1)}, u32[]{:S(2)}, u32[]{:S(2)}) collective-permute-start(bf16[2,144,256]{2,1,0:T(8,128)(2,1)S(1)} %bitcast.23), channel_id=1, source_target_pairs={{0,128},{128,256},{256,384},{384,0},{1,129},{129,257},{257,385},{3... | collective-permute-start | bytes 442376 | tf_op jit(solution)/shard_map/ppermute | solution.py:311
  13.1 21.3 %collective-permute-start.1 = (bf16[2,144,256]{2,1,0:T(8,128)(2,1)S(1)}, bf16[2,144,256]{2,1,0:T(8,128)(2,1)S(1)}, u32[]{:S(2)}, u32[]{:S(2)}) collective-permute-start(bf16[2,144,256]{2,1,0:T(8,128)(2,1)S(1)} %bitcast.24), channel_id=1, source_target_pairs={{0,256},{128,384},{256,0},{384,128},{1,257},{129,385},{257,1},{385... | collective-permute-start | bytes 442376 | tf_op jit(solution)/shard_map/ppermute | solution.py:311
  21.3 14.7 %collective-permute-start.2 = (bf16[2,144,256]{2,1,0:T(8,128)(2,1)S(1)}, bf16[2,144,256]{2,1,0:T(8,128)(2,1)S(1)}, u32[]{:S(2)}, u32[]{:S(2)}) collective-permute-start(bf16[2,144,256]{2,1,0:T(8,128)(2,1)S(1)} %bitcast.25), channel_id=1, source_target_pairs={{0,384},{128,0},{256,128},{384,256},{1,385},{129,1},{257,129},{385... | collective-permute-start | bytes 442376 | tf_op jit(solution)/shard_map/ppermute | solution.py:311
  24.7 21.2 %all-to-all-start = ((bf16[32,16,384]{2,1,0:T(8,128)(2,1)}), bf16[32,16,384]{2,1,0:T(8,128)(2,1)S(1)}, u32[]{:S(2)}, u32[]{:S(2)}) async-start(bf16[32,16,384]{2,1,0:T(8,128)(2,1)} %get-tuple-element.22), calls=%async_computation | async-start | bytes 786432 | tf_op jit(solution)/shard_map/all_to_all | solution.py:254
  36.1 4.9 %collective-permute-start.3 = (bf16[4,2,144,256]{3,2,1,0:T(8,128)(2,1)S(1)}, bf16[4,2,144,256]{3,2,1,0:T(8,128)(2,1)S(1)}, u32[]{:S(2)}, u32[]{:S(2)}) collective-permute-start(bf16[4,2,144,256]{3,2,1,0:T(8,128)(2,1)S(1)} %pad_maximum_fusion.mine_ref), channel_id=1, source_target_pairs={{0,32},{32,0},{1,33},{33,1},{2,34},{34,2},{3,35},{35,3},{4,36},{36... | collective-permute-start | bytes 1769480 | tf_op jit(solution)/shard_map/ppermute | solution.py:312
